TPU v7x, 32 devices: a whole 2x2x4 slice. The times are simulated.
32 devices in a mesh: uly: 4 (over y, x), blk: 8 (over z, core).
Axes of the slice: x: 2, y: 2, z: 4, core: 2. Of those that a mesh axis runs over, the one named last changes fastest.
Arguments:
- block_input: bfloat16 [4096, 2048], P(('uly', 'blk')), may hold values from -6 to 6
- cotangent: bfloat16 [4096, 2048], P(('uly', 'blk')), may hold values from -6 to 6
- lengths: int32 [8], replicated, may hold values from 1 to 2048, 3584 in all
- seq_order: int32 [8], replicated, may hold values from 0 to 7, each once
- norm_attn: bfloat16 [2048], P(('uly', 'blk')), may hold values from 0.5 to 1.5
- w_query: bfloat16 [2048, 2048], P(('uly', 'blk')), may hold values from -0.15625 to 0.15625
- w_key: bfloat16 [2048, 2048], P(('uly', 'blk')), may hold values from -0.15625 to 0.15625
- w_value: bfloat16 [2048, 2048], P(('uly', 'blk')), may hold values from -0.125 to 0.125
- w_out: bfloat16 [2048, 2048], P(('uly', 'blk')), may hold values from -1.5 to 1.5
- norm_ffn: bfloat16 [2048], P(('uly', 'blk')), may hold values from 0.5 to 1.5
- w_gate: bfloat16 [2048, 8192], P('blk', 'uly'), may hold values from -0.125 to 0.125
- w_up: bfloat16 [2048, 8192], P('blk', 'uly'), may hold values from -0.125 to 0.125
- w_down: bfloat16 [8192, 2048], P('uly', 'blk'), may hold values from -0.0625 to 0.0625
Outputs:
- output: bfloat16 [4096, 2048], P(('uly', 'blk'))
- input_grad: float32 [4096, 2048], P(('uly', 'blk'))
- grad_norm_attn: float32 [2048], P(('uly', 'blk'))
- grad_query: float32 [2048, 2048], P(('uly', 'blk'))
- grad_key: float32 [2048, 2048], P(('uly', 'blk'))
- grad_value: float32 [2048, 2048], P(('uly', 'blk'))
- grad_out: float32 [2048, 2048], P(('uly', 'blk'))
- grad_norm_ffn: float32 [2048], P(('uly', 'blk'))
- grad_gate: float32 [2048, 8192], P('blk', 'uly')
- grad_up: float32 [2048, 8192], P('blk', 'uly')
- grad_down: float32 [8192, 2048], P('uly', 'blk')
Inputs may be any that keep to these rules, and one draw needn't show every extreme that they name: 8 lengths that sum to 3584; the longest is exactly 2048. `seq_order`: a permutation of the 8 sequences.
All inputs are finite; a program needn't handle non-finite values.
Results may differ from a plain program's by a relative error of at most 0.017.
Values may be sent and summed in bfloat16 or wider, within the bound.
No kernel may reach another device: no remote copies, remote signals or barrier semaphores. Data moves between devices by JAX's collectives and lax.ppermute only.
A program may use at most 512 MiB of HBM per device.

v0:
```python
import math

import jax
import jax.numpy as jnp
from jax import lax
from jax.sharding import PartitionSpec as P

HEADS = 16
HD = 128


norm_eps = 1e-05
rope_base = 10000.0
score_bias = -math.log(4096.0)


def seq_bounds(lengths, seq_order):
    seq_count = lengths.shape[0]
    labels = jnp.arange(seq_count, dtype=jnp.int32)
    picked = jnp.sum(
        jnp.where(seq_order[:, None] == labels[None, :], lengths[None, :], 0),
        axis=1,
        dtype=jnp.int32,
    )
    seq_ends = jnp.cumsum(picked, dtype=jnp.int32)
    return (seq_ends - picked, seq_ends)


def locate(row_ids, seq_starts, seq_ends):
    inside = (row_ids[:, None] >= seq_starts[None, :]) & (row_ids[:, None] < seq_ends[None, :])
    segment = jnp.sum(
        (row_ids[:, None] >= seq_ends[None, :]).astype(jnp.int32), axis=1, dtype=jnp.int32
    )
    offset = jnp.sum(jnp.where(inside, seq_starts[None, :], 0), axis=1, dtype=jnp.int32)
    return (segment, row_ids - offset)


def rope_tables(position, head_dim):
    half_dim = head_dim // 2
    frequency = rope_base ** (-jnp.arange(half_dim, dtype=jnp.float32) * 2.0 / head_dim)
    angles = position.astype(jnp.float32)[:, None] * frequency[None, :]
    return (jnp.cos(angles)[:, None, :], jnp.sin(angles)[:, None, :])


def rotate(values, cos_table, sin_table):
    half_dim = values.shape[-1] // 2
    leading = values[..., :half_dim]
    trailing = values[..., half_dim:]
    return jnp.concatenate(
        [leading * cos_table - trailing * sin_table, trailing * cos_table + leading * sin_table],
        axis=-1,
    )


def unrotate(gradient, cos_table, sin_table):
    half_dim = gradient.shape[-1] // 2
    leading = gradient[..., :half_dim]
    trailing = gradient[..., half_dim:]
    return jnp.concatenate(
        [leading * cos_table + trailing * sin_table, trailing * cos_table - leading * sin_table],
        axis=-1,
    )


def allowed(query_seg, query_pos, key_seg, key_pos, seq_count):
    return (
        (query_seg[:, None] == key_seg[None, :])
        & (query_seg[:, None] < seq_count)
        & (key_pos[None, :] <= query_pos[:, None])
    )


def rms_stats(values):
    scale_inv = lax.rsqrt(jnp.mean(values * values, axis=-1, keepdims=True) + norm_eps)
    return (values * scale_inv, scale_inv)


def norm_back(grad_normed, normed, scale_inv, gain):
    scaled = grad_normed * gain
    grad_rows = scale_inv * (scaled - normed * jnp.mean(scaled * normed, axis=-1, keepdims=True))
    return (grad_rows, jnp.sum(grad_normed * normed, axis=0))


def body(
    block_input,
    cotangent,
    lengths,
    seq_order,
    norm_attn,
    w_query,
    w_key,
    w_value,
    w_out,
    norm_ffn,
    w_gate,
    w_up,
    w_down,
):
    count_uly = lax.axis_size("uly")
    count_blk = lax.axis_size("blk")
    uly_index = lax.axis_index("uly")
    blk_index = lax.axis_index("blk")
    tok_rows = block_input.shape[0]
    model_dim = block_input.shape[1]
    head_dim = HD
    heads_dev = HEADS // count_uly
    group_rows = count_uly * tok_rows
    span_rows = count_blk * tok_rows
    head_scale = 1.0 / math.sqrt(head_dim)
    seq_count = lengths.shape[0]
    seq_starts, seq_ends = seq_bounds(lengths, seq_order)
    row_iota = jnp.arange(tok_rows, dtype=jnp.int32)
    uly_iota = jnp.arange(count_uly, dtype=jnp.int32)
    own_rows = (uly_index * count_blk + blk_index) * tok_rows + row_iota
    head_rows = (
        (uly_iota[:, None] * count_blk + blk_index) * tok_rows + row_iota[None, :]
    ).reshape(-1)
    own_seg, own_pos = locate(own_rows, seq_starts, seq_ends)
    head_seg, head_pos = locate(head_rows, seq_starts, seq_ends)
    own_cos, own_sin = rope_tables(own_pos, head_dim)
    head_cos, head_sin = rope_tables(head_pos, head_dim)
    gain_attn, full_query, full_key, full_value, full_out, gain_ffn = (
        lax.all_gather(norm_attn, ("uly", "blk"), axis=0, tiled=True),
        lax.all_gather(w_query, ("uly", "blk"), axis=0, tiled=True),
        lax.all_gather(w_key, ("uly", "blk"), axis=0, tiled=True),
        lax.all_gather(w_value, ("uly", "blk"), axis=0, tiled=True),
        lax.all_gather(w_out, ("uly", "blk"), axis=0, tiled=True),
        lax.all_gather(norm_ffn, ("uly", "blk"), axis=0, tiled=True),
    )
    gate_cols, up_cols, down_rows = (
        lax.all_gather(w_gate, "blk", axis=0, tiled=True),
        lax.all_gather(w_up, "blk", axis=0, tiled=True),
        lax.all_gather(w_down, "blk", axis=1, tiled=True),
    )
    gain_attn_f = gain_attn.astype(jnp.float32)
    gain_ffn_f = gain_ffn.astype(jnp.float32)
    input_f = block_input.astype(jnp.float32)
    normed_one, inv_one = rms_stats(input_f)
    hidden_one = (normed_one * gain_attn_f).astype(jnp.bfloat16)
    query_tok = rotate(
        jnp.dot(hidden_one, full_query, preferred_element_type=jnp.float32).reshape(
            tok_rows, HEADS, head_dim
        ),
        own_cos,
        own_sin,
    )
    key_tok = rotate(
        jnp.dot(hidden_one, full_key, preferred_element_type=jnp.float32).reshape(
            tok_rows, HEADS, head_dim
        ),
        own_cos,
        own_sin,
    )
    value_tok = jnp.dot(hidden_one, full_value, preferred_element_type=jnp.float32).astype(
        jnp.bfloat16
    )
    query_heads, key_heads, value_heads = (
        lax.all_to_all(
            query_tok.reshape(tok_rows, model_dim).astype(jnp.bfloat16),
            "uly",
            split_axis=1,
            concat_axis=0,
            tiled=True,
        ),
        lax.all_to_all(
            key_tok.reshape(tok_rows, model_dim).astype(jnp.bfloat16),
            "uly",
            split_axis=1,
            concat_axis=0,
            tiled=True,
        ),
        lax.all_to_all(value_tok, "uly", split_axis=1, concat_axis=0, tiled=True),
    )
    head_query = query_heads.reshape(group_rows, heads_dev, head_dim)
    key_blocks = key_heads.reshape(count_uly, tok_rows, heads_dev * head_dim)
    value_blocks = value_heads.reshape(count_uly, tok_rows, heads_dev * head_dim)

    def scores_for(key_piece):
        piece_rows = key_piece.shape[1]
        key_ids = (
            uly_iota[:, None] * span_rows + jnp.arange(piece_rows, dtype=jnp.int32)[None, :]
        ).reshape(-1)
        key_seg, key_pos = locate(key_ids, seq_starts, seq_ends)
        key_mat = key_piece.reshape(count_uly * piece_rows, heads_dev, head_dim)
        key_mask = allowed(head_seg, head_pos, key_seg, key_pos, seq_count)
        scores = (
            jnp.einsum("qhd,khd->hqk", head_query, key_mat, preferred_element_type=jnp.float32)
            * head_scale
            + score_bias
        )
        return (key_mat, key_mask, scores)

    piece_pair = (
        lax.all_gather(key_blocks, "blk", axis=1, tiled=True),
        lax.all_gather(value_blocks, "blk", axis=1, tiled=True),
    )
    key_mat, key_mask, scores = scores_for(piece_pair[0])
    value_mat = piece_pair[1].reshape(key_mat.shape)
    weights = jnp.where(key_mask[None], jax.nn.sigmoid(scores), 0.0).astype(jnp.bfloat16)
    attended_heads = (
        jnp.einsum("hqk,khd->qhd", weights, value_mat, preferred_element_type=jnp.float32)
        .reshape(group_rows, heads_dev * head_dim)
        .astype(jnp.bfloat16)
    )
    attended_tok = lax.all_to_all(attended_heads, "uly", split_axis=0, concat_axis=1, tiled=True)
    resid = input_f + jnp.dot(attended_tok, full_out, preferred_element_type=jnp.float32)
    normed_two, inv_two = rms_stats(resid)
    hidden_two = (normed_two * gain_ffn_f).astype(jnp.bfloat16)
    group_hidden, group_cot = (
        lax.all_gather(hidden_two, "uly", axis=0, tiled=True),
        lax.all_gather(cotangent, "uly", axis=0, tiled=True),
    )
    gate_act = jnp.dot(group_hidden, gate_cols, preferred_element_type=jnp.float32)
    up_act = jnp.dot(group_hidden, up_cols, preferred_element_type=jnp.float32)
    gate_sig = jax.nn.sigmoid(gate_act)
    silu_act = gate_act * gate_sig
    inner = (silu_act * up_act).astype(jnp.bfloat16)
    ffn_part = jnp.dot(inner, down_rows, preferred_element_type=jnp.float32)
    ffn_own = lax.psum_scatter(
        ffn_part.astype(jnp.bfloat16), "uly", scatter_dimension=0, tiled=True
    ).astype(jnp.float32)
    output = (resid + ffn_own).astype(jnp.bfloat16)
    grad_inner = jnp.einsum("rd,fd->rf", group_cot, down_rows, preferred_element_type=jnp.float32)
    grad_gate_act = (grad_inner * up_act * gate_sig * (1.0 + gate_act * (1.0 - gate_sig))).astype(
        jnp.bfloat16
    )
    grad_up_act = (grad_inner * silu_act).astype(jnp.bfloat16)
    grad_down_part = jnp.einsum("rf,rd->fd", inner, group_cot, preferred_element_type=jnp.float32)
    grad_gate_part = jnp.einsum(
        "rd,rf->df", group_hidden, grad_gate_act, preferred_element_type=jnp.float32
    )
    grad_up_part = jnp.einsum(
        "rd,rf->df", group_hidden, grad_up_act, preferred_element_type=jnp.float32
    )
    grad_gate, grad_up, grad_down = (
        lax.psum_scatter(
            grad_gate_part.astype(jnp.bfloat16), "blk", scatter_dimension=0, tiled=True
        ).astype(jnp.float32),
        lax.psum_scatter(
            grad_up_part.astype(jnp.bfloat16), "blk", scatter_dimension=0, tiled=True
        ).astype(jnp.float32),
        lax.psum_scatter(
            grad_down_part.astype(jnp.bfloat16), "blk", scatter_dimension=1, tiled=True
        ).astype(jnp.float32),
    )
    grad_h2_part = jnp.einsum(
        "rf,df->rd", grad_gate_act, gate_cols, preferred_element_type=jnp.float32
    ) + jnp.einsum("rf,df->rd", grad_up_act, up_cols, preferred_element_type=jnp.float32)
    grad_h2 = lax.psum_scatter(grad_h2_part, "uly", scatter_dimension=0, tiled=True)
    grad_from_ffn, grad_gain_ffn = norm_back(grad_h2, normed_two, inv_two, gain_ffn_f)
    grad_resid = cotangent.astype(jnp.float32) + grad_from_ffn
    grad_attn = grad_resid.astype(jnp.bfloat16)
    grad_out_part = jnp.einsum(
        "td,te->de", attended_tok, grad_attn, preferred_element_type=jnp.float32
    )
    grad_att_tok = jnp.einsum(
        "te,de->td", grad_attn, full_out, preferred_element_type=jnp.float32
    ).astype(jnp.bfloat16)
    grad_att_heads = lax.all_to_all(grad_att_tok, "uly", split_axis=1, concat_axis=0, tiled=True)
    grad_heads = grad_att_heads.reshape(group_rows, heads_dev, head_dim)
    piece_pair = (
        lax.all_gather(key_blocks, "blk", axis=1, tiled=True),
        lax.all_gather(value_blocks, "blk", axis=1, tiled=True),
    )
    piece_rows = piece_pair[0].shape[1]
    key_mat, key_mask, scores = scores_for(piece_pair[0])
    value_mat = piece_pair[1].reshape(key_mat.shape)
    activation = jax.nn.sigmoid(scores)
    weights = jnp.where(key_mask[None], activation, 0.0).astype(jnp.bfloat16)
    grad_weight = jnp.einsum(
        "qhd,khd->hqk", grad_heads, value_mat, preferred_element_type=jnp.float32
    )
    grad_score = jnp.where(
        key_mask[None], grad_weight * activation * (1.0 - activation), 0.0
    ).astype(jnp.bfloat16)
    grad_q = (
        jnp.einsum("hqk,khd->qhd", grad_score, key_mat, preferred_element_type=jnp.float32)
        * head_scale
    )
    key_term = (
        jnp.einsum("hqk,qhd->khd", grad_score, head_query, preferred_element_type=jnp.float32)
        * head_scale
    ).reshape(count_uly, piece_rows, heads_dev * head_dim)
    value_term = jnp.einsum(
        "hqk,qhd->khd", weights, grad_heads, preferred_element_type=jnp.float32
    ).reshape(count_uly, piece_rows, heads_dev * head_dim)
    grad_k_own, grad_v_own = (
        lax.psum_scatter(key_term, "blk", scatter_dimension=1, tiled=True),
        lax.psum_scatter(value_term, "blk", scatter_dimension=1, tiled=True),
    )
    grad_q_heads = (
        unrotate(grad_q, head_cos, head_sin)
        .reshape(group_rows, heads_dev * head_dim)
        .astype(jnp.bfloat16)
    )
    grad_k_heads = (
        unrotate(grad_k_own.reshape(group_rows, heads_dev, head_dim), head_cos, head_sin)
        .reshape(group_rows, heads_dev * head_dim)
        .astype(jnp.bfloat16)
    )
    grad_v_heads = grad_v_own.reshape(group_rows, heads_dev * head_dim).astype(jnp.bfloat16)
    grad_q_tok, grad_k_tok, grad_v_tok = (
        lax.all_to_all(grad_q_heads, "uly", split_axis=0, concat_axis=1, tiled=True),
        lax.all_to_all(grad_k_heads, "uly", split_axis=0, concat_axis=1, tiled=True),
        lax.all_to_all(grad_v_heads, "uly", split_axis=0, concat_axis=1, tiled=True),
    )
    grad_query_part = jnp.einsum(
        "td,te->de", hidden_one, grad_q_tok, preferred_element_type=jnp.float32
    )
    grad_key_part = jnp.einsum(
        "td,te->de", hidden_one, grad_k_tok, preferred_element_type=jnp.float32
    )
    grad_value_part = jnp.einsum(
        "td,te->de", hidden_one, grad_v_tok, preferred_element_type=jnp.float32
    )
    grad_h1 = jnp.einsum("te,de->td", grad_q_tok, full_query, preferred_element_type=jnp.float32)
    grad_h1 = grad_h1 + jnp.einsum(
        "te,de->td", grad_k_tok, full_key, preferred_element_type=jnp.float32
    )
    grad_h1 = grad_h1 + jnp.einsum(
        "te,de->td", grad_v_tok, full_value, preferred_element_type=jnp.float32
    )
    grad_from_attn, grad_gain_attn = norm_back(grad_h1, normed_one, inv_one, gain_attn_f)
    input_grad = grad_resid + grad_from_attn
    summed = (
        lax.psum_scatter(grad_gain_attn, ("uly", "blk"), scatter_dimension=0, tiled=True),
        lax.psum_scatter(grad_query_part, ("uly", "blk"), scatter_dimension=0, tiled=True),
        lax.psum_scatter(grad_key_part, ("uly", "blk"), scatter_dimension=0, tiled=True),
        lax.psum_scatter(grad_value_part, ("uly", "blk"), scatter_dimension=0, tiled=True),
        lax.psum_scatter(grad_out_part, ("uly", "blk"), scatter_dimension=0, tiled=True),
        lax.psum_scatter(grad_gain_ffn, ("uly", "blk"), scatter_dimension=0, tiled=True),
    )
    return (
        output,
        input_grad,
        summed[0],
        summed[1],
        summed[2],
        summed[3],
        summed[4],
        summed[5],
        grad_gate,
        grad_up,
        grad_down,
    )


def solution(mesh):
    in_specs = (
        P(("uly", "blk"), None),
        P(("uly", "blk"), None),
        P(),
        P(),
        P(("uly", "blk")),
        P(("uly", "blk"), None),
        P(("uly", "blk"), None),
        P(("uly", "blk"), None),
        P(("uly", "blk"), None),
        P(("uly", "blk")),
        P("blk", "uly"),
        P("blk", "uly"),
        P("uly", "blk"),
    )
    out_specs = (
        P(("uly", "blk"), None),
        P(("uly", "blk"), None),
        P(("uly", "blk")),
        P(("uly", "blk"), None),
        P(("uly", "blk"), None),
        P(("uly", "blk"), None),
        P(("uly", "blk"), None),
        P(("uly", "blk")),
        P("blk", "uly"),
        P("blk", "uly"),
        P("uly", "blk"),
    )
    return jax.shard_map(body, mesh=mesh, in_specs=in_specs, out_specs=out_specs, check_vma=False)
```

profile of v0, /device:TPU:0, one launch (start us, length us, event | category | flops | bytes accessed | tf_op | source)
XLA Modules:
  0.0 2433.5 jit_solution(13335937203876417332)
XLA Ops:
  11.2 42.6 %all-reduce.5 = (bf16[2048]{0:T(1024)(128)(2,1)S(1)}, bf16[2048]{0:T(1024)(128)(2,1)S(1)}) all-reduce(bf16[2048]{0:T(1024)(128)(2,1)S(1)} %dynamic-update-slice, bf16[2048]{0:T(1024)(128)(2,1)S(1)} %dynamic-update-slice.1), channel_id=1, replica_groups=mesh['uly'=4,'blk'=8] {'uly','blk'}, use_global_device_ids=true, to_apply=%add | all-reduce | flops 4096 | bytes 16384
  55.1 36.3 %all-gather.12.cloned.1.call-done = bf16[2048,2048]{1,0:T(8,128)(2,1)} async-done(((bf16[64,2048]{1,0:T(8,128)(2,1)}), bf16[2048,2048]{1,0:T(8,128)(2,1)}) %all-gather.12.cloned.1.call-update) | async-done | bytes 8388624 | tf_op jit(solution)/shard_map/all_gather | solution.py:126
  96.3 13.5 all_to_all.122
  111.8 59.8 %all-gather.16.cloned.1.call-done = bf16[2048,2048]{1,0:T(8,128)(2,1)} async-done(((bf16[64,2048]{1,0:T(8,128)(2,1)}), bf16[2048,2048]{1,0:T(8,128)(2,1)}) %all-gather.16.cloned.1.call-update) | async-done | bytes 8388624 | tf_op jit(solution)/shard_map/all_gather | solution.py:124
  178.4 72.2 %all-gather.18.cloned.1.call-done = bf16[2048,2048]{1,0:T(8,128)(2,1)} async-done(((bf16[64,2048]{1,0:T(8,128)(2,1)}), bf16[2048,2048]{1,0:T(8,128)(2,1)}) %all-gather.18.cloned.1.call-update) | async-done | bytes 8388624 | tf_op jit(solution)/shard_map/all_gather | solution.py:125
  257.8 12.3 all_to_all.123
  287.3 11.1 all-gather.14.cloned.1.call-done
  298.4 10.1 copy.84
  316.3 30.1 %all-gather.20.cloned.1.call-done = bf16[4,1024,512]{1,2,0:T(8,128)(2,1)} async-done(((bf16[4,128,512]{1,2,0:T(8,128)(2,1)}), bf16[4,1024,512]{1,2,0:T(8,128)(2,1)}) %all-gather.20.cloned.1.call-update) | async-done | bytes 4194320 | tf_op jit(solution)/shard_map/all_gather | solution.py:194
  361.6 17.5 add_divide_fusion
  379.1 15.6 fusion.8
  400.8 29.7 %all-gather.22.cloned.1.call-done = bf16[2048,2048]{1,0:T(8,128)(2,1)} async-done(((bf16[64,2048]{1,0:T(8,128)(2,1)}), bf16[2048,2048]{1,0:T(8,128)(2,1)}) %all-gather.22.cloned.1.call-update) | async-done | bytes 8388624 | tf_op jit(solution)/shard_map/all_gather | solution.py:127
  439.5 73.3 %all-gather.28.cloned.1.call-done = bf16[2048,2048]{1,0:T(8,128)(2,1)} async-done(((bf16[256,2048]{1,0:T(8,128)(2,1)}), bf16[2048,2048]{1,0:T(8,128)(2,1)}) %all-gather.28.cloned.1.call-update) | async-done | bytes 8388624 | tf_op jit(solution)/shard_map/all_gather | solution.py:132
  512.8 36.3 %all-gather.24.cloned.1.call-done = bf16[512,2048]{1,0:T(8,128)(2,1)} async-done(((bf16[128,2048]{1,0:T(8,128)(2,1)}), bf16[512,2048]{1,0:T(8,128)(2,1)}) %all-gather.24.cloned.1.call-update) | async-done | bytes 2097168 | tf_op jit(solution)/shard_map/all_gather | solution.py:210
  549.1 10.5 fusion.37
  559.6 73.2 %all-gather.26.cloned.1.call-done = bf16[2048,2048]{1,0:T(8,128)(2,1)} async-done(((bf16[256,2048]{1,0:T(8,128)(2,1)}), bf16[2048,2048]{1,0:T(8,128)(2,1)}) %all-gather.26.cloned.1.call-update) | async-done | bytes 8388624 | tf_op jit(solution)/shard_map/all_gather | solution.py:131
  632.8 10.5 fusion.36
  643.3 25.1 %all-gather.32.cloned.1.call-done = bf16[512,2048]{1,0:T(8,128)(2,1)} async-done(((bf16[128,2048]{1,0:T(8,128)(2,1)}), bf16[512,2048]{1,0:T(8,128)(2,1)}) %all-gather.32.cloned.1.call-update) | async-done | bytes 2097168 | tf_op jit(solution)/shard_map/all_gather | solution.py:211
  668.4 84.1 %all-gather.30.cloned.1.call-done = bf16[2048,2048]{1,0:T(8,128)(2,1)} async-done(((bf16[2048,256]{1,0:T(8,128)(2,1)}), bf16[2048,2048]{1,0:T(8,128)(2,1)}) %all-gather.30.cloned.1.call-update) | async-done | bytes 8388624 | tf_op jit(solution)/shard_map/all_gather | solution.py:133
  752.5 13.6 multiply_convert_fusion
  774.6 9.6 convolution_add_fusion
  784.3 9.9 convolution_convert_fusion.3
  794.3 41.0 %reduce-scatter.16.cloned.1.call-done = f32[128,2048]{1,0:T(8,128)} async-done(((f32[512,2048]{1,0:T(8,128)}), f32[128,2048]{1,0:T(8,128)}) %reduce-scatter.16.cloned.1.call-update) | async-done | bytes 1048592 | tf_op jit(solution)/shard_map/reduce_scatter | solution.py:249
  837.4 36.9 %reduce-scatter.14.cloned.1.call-done = bf16[128,2048]{1,0:T(8,128)(2,1)} async-done(((bf16[512,2048]{1,0:T(8,128)(2,1)}), bf16[128,2048]{1,0:T(8,128)(2,1)}) %reduce-scatter.14.cloned.1.call-update) | async-done | bytes 524304 | tf_op jit(solution)/shard_map/reduce_scatter | solution.py:219
  884.2 11.6 all_to_all.124
  896.3 16.8 convolution_bitcast_fusion
  913.1 10.9 reshape.421
  924.0 11.5 copy.102
  935.6 20.4 select_convert_fusion
  956.0 11.7 multiply_bitcast_fusion
  967.7 11.0 reshape.419
  978.7 118.6 %copy.104 = f32[4,1024,512]{0,2,1:T(8,128)} copy(f32[4,1024,512]{1,0,2:T(4,128)} %reshape.419) | data formatting | bytes 16777216
  1097.3 218.9 %reshape.426 = f32[1024,2048]{1,0:T(8,128)} reshape(f32[1024,512,4]{2,1,0:T(8,128)} %bitcast.26) | data formatting | bytes 16777216
  1355.9 9.5 all_to_all.125
  1374.8 13.9 fusion.6
  1388.7 16.7 reduce-scatter.34.cloned.1.call-done
  1405.4 36.8 %reshape.427 = f32[128,512,4]{2,1,0:T(8,128)} reshape(f32[128,2048]{1,0:T(8,128)} %reduce-scatter.34.cloned.1.call-done) | data formatting | bytes 2097152
  1442.2 18.7 copy.105
  1465.3 10.6 all_to_all.126
  1485.3 9.7 all_to_all.127
  1495.0 8.8 fusion.27
  1506.7 79.1 %reduce-scatter.28.cloned.1.call-done = bf16[256,2048]{1,0:T(8,128)(2,1)} async-done(((bf16[2048,2048]{1,0:T(8,128)(2,1)}), bf16[256,2048]{1,0:T(8,128)(2,1)}) %reduce-scatter.28.cloned.1.call-update) | async-done | bytes 1048592 | tf_op jit(solution)/shard_map/reduce_scatter | solution.py:236
  1588.5 87.3 %reduce-scatter.32.cloned.1.call-done = bf16[2048,256]{1,0:T(8,128)(2,1)} async-done(((bf16[2048,2048]{1,0:T(8,128)(2,1)}), bf16[2048,256]{1,0:T(8,128)(2,1)}) %reduce-scatter.32.cloned.1.call-update) | async-done | bytes 1048592 | tf_op jit(solution)/shard_map/reduce_scatter | solution.py:242
  1694.6 40.6 %all-reduce.4 = (f32[2048]{0:T(1024)S(1)}, f32[2048]{0:T(1024)S(1)}) all-reduce(f32[2048]{0:T(1024)S(1)} %get-tuple-element.13, f32[2048]{0:T(1024)S(1)} %copy-done.14), channel_id=6, replica_groups=mesh['uly'=4,'blk'=8] {'uly','blk'}, use_global_device_ids=true, to_apply=%region_16.17.clone | all-reduce | flops 4096 | bytes 32768
  1737.7 127.1 %reduce-scatter.26.cloned.1.call-done = f32[64,2048]{1,0:T(8,128)} async-done(((f32[2048,2048]{1,0:T(8,128)}), f32[64,2048]{1,0:T(8,128)}) %reduce-scatter.26.cloned.1.call-update) | async-done | bytes 524304 | tf_op jit(solution)/shard_map/reduce_scatter | solution.py:330
  1864.8 187.1 %reduce-scatter.24.cloned.1.call-done = f32[64,2048]{1,0:T(8,128)} async-done(((f32[2048,2048]{1,0:T(8,128)}), f32[64,2048]{1,0:T(8,128)}) %reduce-scatter.24.cloned.1.call-update) | async-done | bytes 524304 | tf_op jit(solution)/shard_map/reduce_scatter | solution.py:329
  2051.9 187.3 %reduce-scatter.22.cloned.1.call-done = f32[64,2048]{1,0:T(8,128)} async-done(((f32[2048,2048]{1,0:T(8,128)}), f32[64,2048]{1,0:T(8,128)}) %reduce-scatter.22.cloned.1.call-update) | async-done | bytes 524304 | tf_op jit(solution)/shard_map/reduce_scatter | solution.py:328
  2239.2 187.3 %reduce-scatter.20.cloned.1.call-done = f32[64,2048]{1,0:T(8,128)} async-done(((f32[2048,2048]{1,0:T(8,128)}), f32[64,2048]{1,0:T(8,128)}) %reduce-scatter.20.cloned.1.call-update) | async-done | bytes 524304 | tf_op jit(solution)/shard_map/reduce_scatter | solution.py:327
  (181 shorter events, 191.7 us)
Async XLA Ops:
  7.2 84.2 %all-gather.12.cloned.1.call-start = ((), (), s32[]{:S(2)}) async-start(), calls=%async_computation.19 | async-start | bytes 8650752 | tf_op jit(solution)/shard_map/all_gather | solution.py:126
  7.9 163.7 %all-gather.16.cloned.1.call-start = ((), (), s32[]{:S(2)}) async-start(), calls=%async_computation.21 | async-start | bytes 8650752 | tf_op jit(solution)/shard_map/all_gather | solution.py:124
  8.7 242.0 %all-gather.18.cloned.1.call-start = ((), (), s32[]{:S(2)}) async-start(), calls=%async_computation.22 | async-start | bytes 8650752 | tf_op jit(solution)/shard_map/all_gather | solution.py:125
  9.4 289.0 %all-gather.14.cloned.1.call-start = ((), (), s32[]{:S(2)}) async-start(), calls=%async_computation.20 | async-start | bytes 4718592 | tf_op jit(solution)/shard_map/all_gather | solution.py:195
  53.8 196.8 %copy-start.10 = (f32[2048]{0:T(1024)}, f32[2048]{0:T(1024)S(1)}, u32[]{:S(2)}) copy-start(f32[2048]{0:T(1024)S(1)} %convert_element_type.126) | copy-start | bytes 24580
  55.0 195.6 %copy-start.12 = (f32[128]{0:T(128)}, f32[128]{0:T(128)S(1)}, u32[]{:S(2)}) copy-start(f32[128]{0:T(128)S(1)} %add_rsqrt_fusion.1) | copy-start | bytes 1540
  55.0 56.1 %copy-start.20 = (s32[8]{0:T(128)S(1)}, s32[8]{0:T(128)}, u32[]{:S(2)}) copy-start(s32[8]{0:T(128)} %param.15) | copy-start | bytes 100
  55.1 56.1 %copy-start.21 = (s32[8]{0:T(128)S(1)}, s32[8]{0:T(128)}, u32[]{:S(2)}) copy-start(s32[8]{0:T(128)} %param.16) | copy-start | bytes 100
  55.1 116.6 %copy-start = (bf16[128,2048]{1,0:T(8,128)(2,1)S(1)}, bf16[128,2048]{1,0:T(8,128)(2,1)}, u32[]{:S(2)}) copy-start(bf16[128,2048]{1,0:T(8,128)(2,1)} %param.13) | copy-start | bytes 1572868
  111.0 235.4 %all-gather.20.cloned.1.call-start = ((), (), s32[]{:S(2)}) async-start(), calls=%async_computation.23 | async-start | bytes 4718592 | tf_op jit(solution)/shard_map/all_gather | solution.py:194
  111.5 145.9 %copy-start.16 = (f32[64]{0:T(128)}, f32[64]{0:T(128)S(1)}, u32[]{:S(2)}) copy-start(f32[64]{0:T(128)S(1)} %multiply_power_fusion) | copy-start | bytes 772
  270.1 160.4 %all-gather.22.cloned.1.call-start = ((), (), s32[]{:S(2)}) async-start(), calls=%async_computation.24 | async-start | bytes 8650752 | tf_op jit(solution)/shard_map/all_gather | solution.py:127
  270.7 242.1 %all-gather.28.cloned.1.call-start = ((), (), s32[]{:S(2)}) async-start(), calls=%async_computation.27 | async-start | bytes 9437184 | tf_op jit(solution)/shard_map/all_gather | solution.py:132
  273.4 11.4 all-to-all-start.1
  287.3 74.3 %copy-start.8 = (bf16[512,4,128]{0,2,1:T(8,128)(2,1)}, bf16[512,4,128]{0,2,1:T(8,128)(2,1)S(1)}, u32[]{:S(2)}) copy-start(bf16[512,4,128]{0,2,1:T(8,128)(2,1)S(1)} %reshape.428) | copy-start | bytes 1572868
  397.0 33.6 %all-to-all-start.3 = ((bf16[4,128,512]{1,2,0:T(8,128)(2,1)}), bf16[4,128,512]{1,2,0:T(8,128)(2,1)S(1)}, u32[]{:S(2)}, u32[]{:S(2)}) async-start(bf16[4,128,512]{1,2,0:T(8,128)(2,1)} %copy.93), calls=%async_computation.3 | async-start | bytes 1048576 | tf_op jit(solution)/shard_map/all_to_all | solution.py:205
  400.6 148.5 %all-gather.24.cloned.1.call-start = ((), (), s32[]{:S(2)}) async-start(), calls=%async_computation.25 | async-start | bytes 2621440 | tf_op jit(solution)/shard_map/all_gather | solution.py:210
  430.5 4.9 copy-start.6
  435.5 1.0 copy-start.4
  437.4 195.4 %all-gather.26.cloned.1.call-start = ((), (), s32[]{:S(2)}) async-start(), calls=%async_computation.26 | async-start | bytes 9437184 | tf_op jit(solution)/shard_map/all_gather | solution.py:131
  438.2 230.2 %all-gather.32.cloned.1.call-start = ((), (), s32[]{:S(2)}) async-start(), calls=%async_computation.30 | async-start | bytes 2621440 | tf_op jit(solution)/shard_map/all_gather | solution.py:211
  438.8 313.7 %all-gather.30.cloned.1.call-start = ((), (), s32[]{:S(2)}) async-start(), calls=%async_computation.28 | async-start | bytes 9437184 | tf_op jit(solution)/shard_map/all_gather | solution.py:133
  439.5 395.8 %reduce-scatter.16.cloned.1.call-start = ((), (), s32[]{:S(2)}) async-start(), calls=%async_computation.31 | async-start | bytes 5242880 | tf_op jit(solution)/shard_map/reduce_scatter | solution.py:249
  766.1 8.5 copy-start.22
  766.1 8.5 copy-start.23
  784.2 90.1 %reduce-scatter.14.cloned.1.call-start = ((), (), s32[]{:S(2)}) async-start(), calls=%async_computation.29 | async-start | bytes 2621440 | tf_op jit(solution)/shard_map/reduce_scatter | solution.py:219
  784.3 51.0 %copy-start.5 = (f32[128,2048]{1,0:T(8,128)S(1)}, f32[128,2048]{1,0:T(8,128)}, u32[]{:S(2)}) copy-start(f32[128,2048]{1,0:T(8,128)} %copy-done.4) | copy-start | bytes 3145732
  794.2 560.2 %reduce-scatter.18.cloned.1.call-start = ((), (), s32[]{:S(2)}) async-start(), calls=%async_computation.32 | async-start | bytes 9437184 | tf_op jit(solution)/shard_map/reduce_scatter | solution.py:289
  877.0 1.0 copy-start.2
  935.5 20.5 copy-start.9
  935.5 469.9 %reduce-scatter.34.cloned.1.call-start = ((), (), s32[]{:S(2)}) async-start(), calls=%async_computation.40 | async-start | bytes 9437184
  1316.2 1.6 copy-start.18
  1316.2 187.6 %reduce-scatter.30.cloned.1.call-start = ((), (), s32[]{:S(2)}) async-start(), calls=%async_computation.38 | async-start | bytes 9437184 | tf_op jit(solution)/shard_map/reduce_scatter | solution.py:239
  1326.2 259.6 %reduce-scatter.28.cloned.1.call-start = ((), (), s32[]{:S(2)}) async-start(), calls=%async_computation.37 | async-start | bytes 9437184 | tf_op jit(solution)/shard_map/reduce_scatter | solution.py:236
  1334.8 1.6 copy-start.19
  1334.8 341.0 %reduce-scatter.32.cloned.1.call-start = ((), (), s32[]{:S(2)}) async-start(), calls=%async_computation.39 | async-start | bytes 9437184 | tf_op jit(solution)/shard_map/reduce_scatter | solution.py:242
  1344.9 1.2 copy-start.3
  1344.9 1.4 copy-start.7
  1344.9 519.9 %reduce-scatter.26.cloned.1.call-start = ((), (), s32[]{:S(2)}) async-start(), calls=%async_computation.36 | async-start | bytes 17301504 | tf_op jit(solution)/shard_map/reduce_scatter | solution.py:330
  1354.3 11.1 copy-start.1
  1354.3 11.1 copy-start.11
  1354.3 11.1 copy-start.13
  1354.4 697.6 %reduce-scatter.24.cloned.1.call-start = ((), (), s32[]{:S(2)}) async-start(), calls=%async_computation.35 | async-start | bytes 17301504 | tf_op jit(solution)/shard_map/reduce_scatter | solution.py:329
  1373.6 865.6 %reduce-scatter.22.cloned.1.call-start = ((), (), s32[]{:S(2)}) async-start(), calls=%async_computation.34 | async-start | bytes 17301504 | tf_op jit(solution)/shard_map/reduce_scatter | solution.py:328
  1484.0 942.4 %reduce-scatter.20.cloned.1.call-start = ((), (), s32[]{:S(2)}) async-start(), calls=%async_computation.33 | async-start | bytes 17301504 | tf_op jit(solution)/shard_map/reduce_scatter | solution.py:327
  1678.6 12.9 slice-start
  1685.0 6.5 slice-start.1
  1691.5 3.1 copy-start.14
  (2 other events, 1.4 us)
Sparse Core Ops, SparseCore 0:
  11.0 80.3 all-gather.11
  94.4 77.2 all-gather.15
  174.6 75.9 all-gather.17
  252.7 45.7 all-gather.13
  299.9 46.5 all-gather.19
  349.3 81.2 all-gather.21
  432.1 80.6 all-gather.27
  515.2 33.8 all-gather.23
  550.7 82.0 all-gather.25
  634.5 33.8 all-gather.31
  670.0 82.4 all-gather.29
  784.3 50.8 reduce-scatter.15
  839.1 35.1 reduce-scatter.13
  935.6 89.0 reduce-scatter.17
  1316.4 89.0 reduce-scatter.33
  1407.6 87.9 reduce-scatter.29
  1497.7 87.9 reduce-scatter.27
  1587.9 87.9 reduce-scatter.31
  1678.7 186.0 reduce-scatter.25
  1867.5 184.3 reduce-scatter.23
  2054.8 184.3 reduce-scatter.21
  2242.0 184.3 reduce-scatter.19
where the time goes:
time: 2450 us; the launch traced here: 2430 us
  waiting for transfers between devices  1490 us (61%)
  local copies, waits for them, and re-layouts  478 us (20%)
  matrix products  263 us (11%)
  blocking collectives  150 us (6%)
  other arithmetic  27.2 us (1%)
    unnamed x63, local copies, waits for them, and re-layouts  402 us
    reduce_scatter x1, waiting for transfers between devices, body(): lax.psum_scatter(grad_query_part, ('uly', 'blk'), scatter_dimension=0, ti...  187 us
    reduce_scatter x1, waiting for transfers between devices, body(): lax.psum_scatter(grad_key_part, ('uly', 'blk'), scatter_dimension=0, tile...  187 us
    reduce_scatter x1, waiting for transfers between devices, body(): lax.psum_scatter(grad_value_part, ('uly', 'blk'), scatter_dimension=0, ti...  187 us
    reduce_scatter x1, waiting for transfers between devices, body(): lax.psum_scatter(grad_out_part, ('uly', 'blk'), scatter_dimension=0, tile...  127 us
    reduce_scatter x1, waiting for transfers between devices, body(): lax.psum_scatter(grad_down_part.astype(jnp.bfloat16), 'blk', scatter_dime...  87.3 us
    all_gather x1, waiting for transfers between devices, body(): lax.all_gather(w_down, 'blk', axis=1, tiled=True)  84.1 us
    unnamed x2, blocking collectives  83.2 us
  transfers between devices with their start and end apart: 24, of which 21 were waited for; matrix products, arithmetic and copies ran while one was open for 28% of the time, Pallas kernels for 0%

commit v1 on v0

v1 whole, which is shorter than its diff:
```python
import functools
import math

import jax
import jax.numpy as jnp
from jax import lax
from jax.experimental import pallas as pl
from jax.experimental.pallas import tpu as pltpu
from jax.sharding import PartitionSpec as P

HEADS = 16
HD = 128
BOTH = ("uly", "blk")
LONGEST = {4096: 2048, 16384: 4096}
LOG2E = math.log2(math.e)

norm_eps = 1e-05
rope_base = 10000.0
score_bias = -math.log(4096.0)
head_scale = 1.0 / math.sqrt(HD)

BQ = 256
BK = 512
BR = 256
VMEM = 60 * 2**20
f32 = jnp.float32
bf16 = jnp.bfloat16


def dot_t(left, right):
    return lax.dot_general(left, right, (((1,), (1,)), ((), ())), preferred_element_type=f32)


def t_dot(left, right):
    return lax.dot_general(left, right, (((0,), (0,)), ((), ())), preferred_element_type=f32)


def dot(left, right):
    return jnp.dot(left, right, preferred_element_type=f32)


def qkv_kernel(x_ref, gain_ref, w_ref, cos_ref, sin_ref, h_ref, q_ref, kv_ref):
    x = x_ref[...].astype(f32)
    inv = lax.rsqrt(jnp.mean(x * x, axis=-1, keepdims=True) + norm_eps)
    h = (x * inv * gain_ref[...]).astype(bf16)
    h_ref[...] = h
    acc = dot(h, w_ref[...])
    cos, sin = cos_ref[...], sin_ref[...]
    width = q_ref.shape[1]
    for s in range(0, width, HD):
        t = acc[:, s : s + HD]
        q_ref[:, s : s + HD] = (t * cos + pltpu.roll(t, HD // 2, 1) * sin).astype(bf16)
        t = acc[:, width + s : width + s + HD]
        kv_ref[:, s : s + HD] = (t * cos + pltpu.roll(t, HD // 2, 1) * sin).astype(bf16)
    kv_ref[:, width:] = acc[:, 2 * width :].astype(bf16)


def qkv_call(x, gain, w, cos, sin):
    rows, dim = x.shape
    width = w.shape[1] // 3
    block = lambda cols: pl.BlockSpec((BR, cols), lambda i: (i, 0))
    whole = lambda shape: pl.BlockSpec(shape, lambda i: (0, 0))
    return pl.pallas_call(
        qkv_kernel,
        grid=(rows // BR,),
        in_specs=[block(dim), whole((1, dim)), whole(w.shape), block(HD), block(HD)],
        out_specs=[block(dim), block(width), block(2 * width)],
        out_shape=[
            jax.ShapeDtypeStruct((rows, dim), bf16),
            jax.ShapeDtypeStruct((rows, width), bf16),
            jax.ShapeDtypeStruct((rows, 2 * width), bf16),
        ],
        compiler_params=pltpu.CompilerParams(vmem_limit_bytes=VMEM),
        cost_estimate=pl.CostEstimate(
            flops=2 * rows * dim * 3 * width, bytes_accessed=16 * 2**20, transcendentals=0
        ),
    )(x, gain, w, cos, sin)


def attn_fwd_kernel(count_kv, lo_ref, q_ref, start_ref, wo_ref, *refs):
    kv_refs, (att_ref, part_ref, kv_all) = refs[:count_kv], refs[count_kv:]
    rows, width = q_ref.shape
    heads = width // HD
    base = (count_kv - 1) * rows
    for i, r in enumerate(kv_refs):
        kv_all[i * rows : (i + 1) * rows, :] = r[...]
    for i in range(rows // BQ):
        at = slice(i * BQ, (i + 1) * BQ)
        start = start_ref[at, :]
        row = base + i * BQ + lax.broadcasted_iota(jnp.int32, (BQ, BK), 0)
        col = lax.broadcasted_iota(jnp.int32, (BQ, BK), 1)
        queries = [q_ref[at, h * HD : (h + 1) * HD] for h in range(heads)]

        def step(kb, sums):
            off = pl.multiple_of(kb * BK, BK)
            here = col + off
            ok = (here >= start) & (here <= row)
            out = []
            for h in range(heads):
                k = kv_all[pl.ds(off, BK), h * HD : (h + 1) * HD]
                v = kv_all[pl.ds(off, BK), width + h * HD : width + (h + 1) * HD]
                e = jnp.exp2(
                    dot_t(queries[h], k) * (-head_scale * LOG2E) - score_bias * LOG2E
                )
                weight = jnp.where(ok, 1.0 / (1.0 + e), 0.0).astype(bf16)
                out.append(sums[h] + dot(weight, v))
            return tuple(out)

        last = (base + (i + 1) * BQ - 1) // BK + 1
        sums = lax.fori_loop(
            lo_ref[i], last, step, tuple(jnp.zeros((BQ, HD), f32) for _ in range(heads))
        )
        att = jnp.concatenate([s.astype(bf16) for s in sums], axis=1)
        att_ref[at, :] = att
        part_ref[at, :] = dot(att, wo_ref[...]).astype(bf16)


def attn_fwd_call(lo, q, start, wo, kvs):
    rows, width = q.shape
    dim = wo.shape[1]
    vmem = pl.BlockSpec(memory_space=pltpu.VMEM)
    return pl.pallas_call(
        functools.partial(attn_fwd_kernel, len(kvs)),
        in_specs=[pl.BlockSpec(memory_space=pltpu.SMEM)] + [vmem] * (3 + len(kvs)),
        out_specs=[vmem, vmem],
        out_shape=[
            jax.ShapeDtypeStruct((rows, width), bf16),
            jax.ShapeDtypeStruct((rows, dim), bf16),
        ],
        scratch_shapes=[pltpu.VMEM((len(kvs) * rows, 2 * width), bf16)],
        compiler_params=pltpu.CompilerParams(vmem_limit_bytes=VMEM),
        cost_estimate=pl.CostEstimate(
            flops=10 * 10**9, bytes_accessed=12 * 2**20, transcendentals=4 * 10**6
        ),
    )(lo, q, start, wo, *kvs)


def attn_bwd_kernel(count_kv, lo_ref, q_ref, ga_ref, start_ref, wo_ref, cos_ref, sin_ref, *refs):
    kv_refs = refs[:count_kv]
    gq_ref, own_ref = refs[count_kv : count_kv + 2]
    rem_refs = refs[count_kv + 2 : 2 * count_kv + 1]
    kv_all, gkv = refs[2 * count_kv + 1 :]
    rows, width = q_ref.shape
    heads = width // HD
    base = (count_kv - 1) * rows
    for i, r in enumerate(kv_refs):
        kv_all[i * rows : (i + 1) * rows, :] = r[...]
        gkv[i * rows : (i + 1) * rows, :] = jnp.zeros((rows, 2 * width), f32)
    for i in range(rows // BQ):
        at = slice(i * BQ, (i + 1) * BQ)
        start = start_ref[:, at]
        row = base + i * BQ + lax.broadcasted_iota(jnp.int32, (BK, BQ), 1)
        col = lax.broadcasted_iota(jnp.int32, (BK, BQ), 0)
        gatt = dot_t(ga_ref[at, :], wo_ref[...]).astype(bf16)
        queries = [q_ref[at, h * HD : (h + 1) * HD] for h in range(heads)]
        gatts = [gatt[:, h * HD : (h + 1) * HD] for h in range(heads)]

        def step(kb, sums):
            off = pl.multiple_of(kb * BK, BK)
            here = col + off
            ok = (here >= start) & (here <= row)
            out = []
            for h in range(heads):
                ks = slice(h * HD, (h + 1) * HD)
                vs = slice(width + h * HD, width + (h + 1) * HD)
                k = kv_all[pl.ds(off, BK), ks]
                v = kv_all[pl.ds(off, BK), vs]
                e = jnp.exp2(
                    dot_t(k, queries[h]) * (-head_scale * LOG2E) - score_bias * LOG2E
                )
                sg = jnp.where(ok, 1.0 / (1.0 + e), 0.0)
                gs = (dot_t(v, gatts[h]) * sg * (1.0 - sg)).astype(bf16)
                gkv[pl.ds(off, BK), ks] += dot(gs, queries[h])
                gkv[pl.ds(off, BK), vs] += dot(sg.astype(bf16), gatts[h])
                out.append(sums[h] + t_dot(gs, k))
            return tuple(out)

        last = (base + (i + 1) * BQ - 1) // BK + 1
        sums = lax.fori_loop(
            lo_ref[i], last, step, tuple(jnp.zeros((BQ, HD), f32) for _ in range(heads))
        )
        cos, sin = cos_ref[at, :], sin_ref[at, :]
        for h in range(heads):
            t = sums[h] * head_scale
            gq_ref[at, h * HD : (h + 1) * HD] = (
                t * cos - pltpu.roll(t, HD // 2, 1) * sin
            ).astype(bf16)
    own_ref[:, :width] = gkv[base:, :width] * head_scale
    own_ref[:, width:] = gkv[base:, width:]
    for i, r in enumerate(rem_refs):
        r[:, :width] = (gkv[i * rows : (i + 1) * rows, :width] * head_scale).astype(bf16)
        r[:, width:] = gkv[i * rows : (i + 1) * rows, width:].astype(bf16)


def attn_bwd_call(lo, q, ga, start, wo, cos, sin, kvs):
    rows, width = q.shape
    vmem = pl.BlockSpec(memory_space=pltpu.VMEM)
    return pl.pallas_call(
        functools.partial(attn_bwd_kernel, len(kvs)),
        in_specs=[pl.BlockSpec(memory_space=pltpu.SMEM)] + [vmem] * (6 + len(kvs)),
        out_specs=[vmem] * (1 + len(kvs)),
        out_shape=[
            jax.ShapeDtypeStruct((rows, width), bf16),
            jax.ShapeDtypeStruct((rows, 2 * width), f32),
        ]
        + [jax.ShapeDtypeStruct((rows, 2 * width), bf16)] * (len(kvs) - 1),
        scratch_shapes=[
            pltpu.VMEM((len(kvs) * rows, 2 * width), bf16),
            pltpu.VMEM((len(kvs) * rows, 2 * width), f32),
        ],
        compiler_params=pltpu.CompilerParams(vmem_limit_bytes=VMEM),
        cost_estimate=pl.CostEstimate(
            flops=25 * 10**9, bytes_accessed=20 * 2**20, transcendentals=4 * 10**6
        ),
    )(lo, q, ga, start, wo, cos, sin, *kvs)


def ffn_kernel(places, blocks, h_ref, c_ref, *refs):
    count = len(places[0])
    sources = refs[: 3 * count]
    outs = refs[3 * count : 3 * count + 3 * blocks]
    y_ref, gh_ref = refs[3 * count + 3 * blocks : 3 * count + 3 * blocks + 2]
    wg, wu, wd, gates, ups, inners, sem = refs[3 * count + 3 * blocks + 2 :]
    inner_refs, gg_refs, gu_refs = outs[:blocks], outs[blocks : 2 * blocks], outs[2 * blocks :]
    width = wg.shape[1] // blocks

    def copies(which):
        found = []
        for p, (j, row) in enumerate(places[which]):
            src = sources[which * count + p]
            held = (wg, wu, wd)[which]
            if which < 2:
                dst = held.at[pl.ds(row, src.shape[0]), pl.ds(j * width, width)]
            else:
                dst = held.at[pl.ds(j * width + row, src.shape[0]), :]
            found.append(pltpu.make_async_copy(src, dst, sem.at[which, p]))
        return found

    first = pl.program_id(0) == 0

    @pl.when(first)
    def _():
        for which in range(3):
            for c in copies(which):
                c.start()
        for which in range(3):
            for c in copies(which):
                c.wait()

    h, c = h_ref[...], c_ref[...]
    for j in range(blocks):
        cols = slice(j * width, (j + 1) * width)
        gate = dot(h, wg[:, cols])
        up = dot(h, wu[:, cols])
        grad = dot_t(c, wd[cols, :])
        sig = 1.0 / (1.0 + jnp.exp2(gate * -LOG2E))
        act = gate * sig
        inner = (act * up).astype(bf16)
        gg = (grad * up * sig * (1.0 + gate * (1.0 - sig))).astype(bf16)
        gu = (grad * act).astype(bf16)
        inner_refs[j][...] = inner
        gg_refs[j][...] = gg
        gu_refs[j][...] = gu
        inners[:, cols] = inner
        gates[:, cols] = gg
        ups[:, cols] = gu
    gh_ref[...] = (dot_t(gates[...], wg[...]) + dot_t(ups[...], wu[...])).astype(bf16)
    y_ref[...] = dot(inners[...], wd[...]).astype(bf16)


def ffn_call(h, cot, gate, up, down):
    rows, dim = h.shape
    blocks = len(gate)
    width = gate[0][0].shape[1]
    if width % HD:
        merge = lambda parts: jnp.concatenate(parts, axis=0)
        gate = [[jnp.concatenate([merge(g) for g in gate], axis=1)]]
        up = [[jnp.concatenate([merge(g) for g in up], axis=1)]]
        down = [[jnp.concatenate([merge(g) for g in down], axis=0)]]
        joined, blocks, width = blocks, 1, width * blocks
    else:
        joined = 0
    places, sources = [], []
    for weight in (gate, up, down):
        place = []
        for j, parts in enumerate(weight):
            row = 0
            for part in parts:
                place.append((j, row))
                sources.append(part)
                row += part.shape[0]
        places.append(tuple(place))
    count = len(places[0])
    hidden = blocks * width
    block = lambda cols: pl.BlockSpec((BR, cols), lambda i: (i, 0))
    result = pl.pallas_call(
        functools.partial(ffn_kernel, tuple(places), blocks),
        grid=(rows // BR,),
        in_specs=[block(dim), block(dim)] + [pl.BlockSpec(memory_space=pl.ANY)] * len(sources),
        out_specs=[block(width)] * (3 * blocks) + [block(dim)] * 2,
        out_shape=[jax.ShapeDtypeStruct((rows, width), bf16)] * (3 * blocks)
        + [jax.ShapeDtypeStruct((rows, dim), bf16)] * 2,
        scratch_shapes=[
            pltpu.VMEM((dim, hidden), bf16),
            pltpu.VMEM((dim, hidden), bf16),
            pltpu.VMEM((hidden, dim), bf16),
            pltpu.VMEM((BR, hidden), bf16),
            pltpu.VMEM((BR, hidden), bf16),
            pltpu.VMEM((BR, hidden), bf16),
            pltpu.SemaphoreType.DMA((3, count)),
        ],
        compiler_params=pltpu.CompilerParams(vmem_limit_bytes=VMEM),
        cost_estimate=pl.CostEstimate(
            flops=12 * rows * dim * hidden, bytes_accessed=36 * 2**20, transcendentals=10**6
        ),
    )(h, cot, *sources)
    inner, gg, gu = result[:blocks], result[blocks : 2 * blocks], result[2 * blocks : 3 * blocks]
    if joined:
        split = lambda a: jnp.split(a[0], joined, axis=1)
        inner, gg, gu = split(inner), split(gg), split(gu)
    return inner, gg, gu, result[-2], result[-1]


def xor_permute(x, count, flip):
    return lax.ppermute(x, "uly", [(i, i ^ flip) for i in range(count)])


def gather_uly(x, count):
    if count != 4:
        return [[x]] + [[xor_permute(x, count, j)] for j in range(1, count)]
    half = x.shape[0] // 2
    one, two = xor_permute(x, count, 1), xor_permute(x, count, 2)
    low = xor_permute(one[:half], count, 2)
    high = xor_permute(two[half:], count, 1)
    return [[x], [one], [two], [low, high]]


def in_order(pieces, index):
    rows = sum(p.shape[0] for p in pieces[0])
    out = jnp.zeros((len(pieces) * rows,) + pieces[0][0].shape[1:], pieces[0][0].dtype)
    for j, parts in enumerate(pieces):
        at = (index ^ j) * rows
        for part in parts:
            out = lax.dynamic_update_slice_in_dim(out, part, at, 0)
            at = at + part.shape[0]
    return out


def scatter_uly(own, others, count):
    got = [xor_permute(block, count, j + 1) for j, block in enumerate(others)]
    for block in got:
        own = own + block.astype(f32)
    return own


def rms_stats(values):
    scale_inv = lax.rsqrt(jnp.mean(values * values, axis=-1, keepdims=True) + norm_eps)
    return (values * scale_inv, scale_inv)


def norm_back(grad_normed, normed, scale_inv, gain):
    scaled = grad_normed * gain
    return scale_inv * (scaled - normed * jnp.mean(scaled * normed, axis=-1, keepdims=True))


def body(
    block_input,
    cotangent,
    lengths,
    seq_order,
    norm_attn,
    w_query,
    w_key,
    w_value,
    w_out,
    norm_ffn,
    w_gate,
    w_up,
    w_down,
):
    count_uly = lax.axis_size("uly")
    count_blk = lax.axis_size("blk")
    devices = count_uly * count_blk
    uly_index = lax.axis_index("uly")
    tok_rows, dim = block_input.shape
    group = count_blk * tok_rows
    part = dim // count_blk
    rows_w = w_query.shape[0]
    longest = LONGEST.get(devices * tok_rows, devices * tok_rows)
    back = min(count_uly - 1, -(-(longest - 1) // group))

    labels = jnp.arange(lengths.shape[0], dtype=jnp.int32)
    picked = jnp.sum(
        jnp.where(seq_order[:, None] == labels[None, :], lengths[None, :], 0), axis=1
    )
    ends = jnp.sum(jnp.where(labels[None, :] <= labels[:, None], picked[None, :], 0), axis=1)
    starts = ends - picked
    row_ids = uly_index * group + jnp.arange(group, dtype=jnp.int32)
    inside = (row_ids[:, None] >= starts[None, :]) & (row_ids[:, None] < ends[None, :])
    seq_start = jnp.sum(jnp.where(inside, starts[None, :], 0), axis=1)
    position = row_ids - seq_start
    used = jnp.any(inside, axis=1)
    shift = (uly_index - back) * group
    begin = jnp.where(used, seq_start - shift, 1 << 30).astype(jnp.int32)
    firsts = begin[::BQ]
    ends_kb = (back * group + jnp.arange(group // BQ, dtype=jnp.int32) * BQ + BQ - 1) // BK + 1
    low_kb = jnp.minimum(firsts // BK, ends_kb).astype(jnp.int32)
    frequency = rope_base ** (-jnp.arange(HD // 2, dtype=f32) * 2.0 / HD)
    angles = position.astype(f32)[:, None] * frequency[None, :]
    cos, sin = jnp.cos(angles), jnp.sin(angles)
    cos = jnp.concatenate([cos, cos], axis=1)
    sin = jnp.concatenate([-sin, sin], axis=1)

    group_in = lax.all_gather(block_input, "blk", axis=0, tiled=True)
    gains = jnp.concatenate([norm_attn, norm_ffn])
    gains = lax.all_to_all(
        jnp.broadcast_to(gains[None], (devices, gains.shape[0])), BOTH, 0, 0, tiled=True
    )
    gain_attn = gains[:, :rows_w].reshape(1, dim).astype(f32)
    gain_ffn = gains[:, rows_w:].reshape(1, dim).astype(f32)
    qkv = jnp.stack([w.reshape(rows_w, count_blk, part) for w in (w_query, w_key, w_value)], axis=1)
    qkv = qkv.transpose(2, 0, 1, 3).reshape(count_blk * rows_w, 3 * part)
    qkv = lax.all_to_all(qkv, "blk", 0, 0, tiled=True)
    w_qkv = in_order(gather_uly(qkv, count_uly), uly_index)
    owner = [
        (i, (i % count_uly) * count_blk + i // count_uly) for i in range(devices)
    ]
    wo = lax.ppermute(w_out, BOTH, owner)
    wo = in_order(gather_uly(wo, count_uly), uly_index)

    hidden_one, query, kv = qkv_call(group_in, gain_attn, w_qkv, cos, sin)
    kvs = [
        lax.ppermute(kv, "uly", [(i, i + s) for i in range(count_uly - s)])
        for s in range(back, 0, -1)
    ] + [kv]

    group_cot = lax.all_gather(cotangent, "blk", axis=0, tiled=True)
    gate = gather_uly(lax.all_to_all(w_gate, "blk", 1, 0, tiled=True), count_uly)
    up = gather_uly(lax.all_to_all(w_up, "blk", 1, 0, tiled=True), count_uly)
    down = gather_uly(lax.all_to_all(w_down, "blk", 0, 1, tiled=True), count_uly)

    attended, out_part = attn_fwd_call(low_kb, query, begin[:, None], wo, kvs)
    input_f = block_input.astype(f32)
    resid = input_f + lax.psum_scatter(out_part, "blk", scatter_dimension=0, tiled=True).astype(f32)
    normed_two, inv_two = rms_stats(resid)
    hidden_two = (normed_two * gain_ffn).astype(bf16)
    group_hidden = lax.all_gather(hidden_two, "blk", axis=0, tiled=True)

    inner, gg, gu, y_part, gh_part = ffn_call(group_hidden, group_cot, gate, up, down)
    grad_h2 = lax.psum_scatter(gh_part, "blk", scatter_dimension=0, tiled=True).astype(f32)
    output = (
        resid + lax.psum_scatter(y_part, "blk", scatter_dimension=0, tiled=True).astype(f32)
    ).astype(bf16)
    grad_resid = cotangent.astype(f32) + norm_back(grad_h2, normed_two, inv_two, gain_ffn)
    gain_part = jnp.sum(grad_h2 * normed_two, axis=0).reshape(devices, rows_w)
    grad_gain_ffn = jnp.sum(
        lax.all_to_all(gain_part, BOTH, 0, 0, tiled=True).reshape(devices, rows_w), axis=0
    )
    group_gattn = lax.all_gather(grad_resid.astype(bf16), "blk", axis=0, tiled=True)

    def summed(term, lefts, rights):
        parts = [term(left, right) for left, right in zip(lefts, rights)]
        return scatter_uly(parts[0], [p.astype(bf16) for p in parts[1:]], count_uly).astype(bf16)

    hiddens, cots = [group_hidden] * count_uly, [group_cot] * count_uly
    grad_gate = lax.all_to_all(summed(t_dot, hiddens, gg), "blk", 0, 1, tiled=True).astype(f32)
    grad_up = lax.all_to_all(summed(t_dot, hiddens, gu), "blk", 0, 1, tiled=True).astype(f32)
    grad_down = lax.all_to_all(summed(t_dot, inner, cots), "blk", 1, 0, tiled=True).astype(f32)

    def split_rows(whole):
        rows = whole.shape[0] // count_uly
        pick = lambda j: lax.dynamic_slice_in_dim(whole, (uly_index ^ j) * rows, rows, 0)
        return scatter_uly(
            pick(0), [pick(j).astype(bf16) for j in range(1, count_uly)], count_uly
        ).astype(bf16)

    grad_out = lax.ppermute(
        split_rows(t_dot(attended, group_gattn)), BOTH, [(j, i) for i, j in owner]
    ).astype(f32)

    gq, gkv, *sent = attn_bwd_call(
        low_kb, query, group_gattn, begin[None, :], wo, cos, sin, kvs
    )
    for s, block in zip(range(back, 0, -1), sent):
        gkv = gkv + lax.ppermute(
            block, "uly", [(i, i - s) for i in range(s, count_uly)]
        ).astype(f32)
    gk = gkv[:, :part].reshape(group, part // HD, HD)
    gk = gk * cos[:, None, :] - jnp.roll(gk, HD // 2, axis=2) * sin[:, None, :]
    gqkv = jnp.concatenate(
        [gq, gk.reshape(group, part).astype(bf16), gkv[:, part:].astype(bf16)], axis=1
    )
    gh1_part = dot_t(gqkv, w_qkv).astype(bf16)
    grad_h1 = lax.psum_scatter(gh1_part, "blk", scatter_dimension=0, tiled=True).astype(f32)
    normed_one, inv_one = rms_stats(input_f)
    input_grad = grad_resid + norm_back(grad_h1, normed_one, inv_one, gain_attn)
    grads = split_rows(t_dot(hidden_one, gqkv))
    grads = lax.all_to_all(grads, "blk", 0, 0, tiled=True).astype(f32)
    grads = grads.reshape(count_blk, rows_w, 3, part).transpose(2, 1, 0, 3).reshape(3, rows_w, dim)
    grad_gain_attn = (
        jnp.sum(
            grads[0] * w_query.astype(f32)
            + grads[1] * w_key.astype(f32)
            + grads[2] * w_value.astype(f32),
            axis=1,
        )
        / norm_attn.astype(f32)
    )
    return (
        output,
        input_grad,
        grad_gain_attn,
        grads[0],
        grads[1],
        grads[2],
        grad_out,
        grad_gain_ffn,
        grad_gate,
        grad_up,
        grad_down,
    )


def solution(mesh):
    rows = P(("uly", "blk"), None)
    vector = P(("uly", "blk"))
    weights = (vector, rows, rows, rows, rows, vector, P("blk", "uly"), P("blk", "uly"), P("uly", "blk"))
    return jax.shard_map(
        body,
        mesh=mesh,
        in_specs=(rows, rows, P(), P()) + weights,
        out_specs=(rows, rows) + weights,
        check_vma=False,
    )
```

time: 2450 us -> 953 us (0.39)
  waiting for transfers between devices: 1490 us -> 573 us
  local copies, waits for them, and re-layouts: 478 us -> 48.2 us
  matrix products: 263 us -> 54.3 us
  blocking collectives: 150 us -> 46.7 us
  starting transfers between devices: 9.05 us -> 102 us
  Pallas kernels: 0 us -> 68.8 us
    reduce_scatter x10 -> x4, waiting for transfers between devices: 933 us -> 110 us  [the longest x1 60 us: body(): lax.psum_scatter(out_part, 'blk', scatter_dimension=0, tiled=True)]
    all_gather x11 -> x4, waiting for transfers between devices: 531 us -> 45.4 us  [the longest x1 45.4 us: body(): lax.all_gather(grad_resid.astype(bf16), 'blk', axis=0, tiled=True)]
    unnamed x63 -> x109, local copies, waits for them, and re-layouts: 402 us -> 10 us
    ppermute x0 -> x41, waiting for transfers between devices: none -> 275 us  [the longest x35 237 us: xor_permute(): return lax.ppermute(x, 'uly', [(i, i ^ flip) for i in range(count)])]
    dot_general x25 -> x15, matrix products: 249 us -> 54.3 us  [the longest x14 47.3 us: t_dot(): lax.dot_general(left, right, (((0,), (0,)), ((), ())), preferred_element_...]
    all_to_all x2 -> x9, waiting for transfers between devices: 4.54 us -> 141 us  [the longest x1 53.7 us: body(): lax.all_to_all(w_gate, 'blk', 1, 0, tiled=True)]
    unnamed x2 -> x0, blocking collectives: 83.2 us -> none
    pallas_call x0 -> x4, Pallas kernels: none -> 68.8 us  [the longest x1 35.3 us: ffn_call(): pl.pallas_call(functools.partial(ffn_kernel, tuple(places), blocks), grid...]
  transfers between devices with their start and end apart: 24 -> 58, of which waited for: 21 -> 26; matrix products, arithmetic and copies ran while one was open for 28% -> 10% of each run, Pallas kernels for 0% -> 1%
where the time goes in v1:
time: 953 us; the launch traced here: 940 us
  waiting for transfers between devices  573 us (60%)
  starting transfers between devices  102 us (11%)
  Pallas kernels  68.8 us (7%)
  matrix products  54.3 us (6%)
  local copies, waits for them, and re-layouts  48.2 us (5%)
  blocking collectives  46.7 us (5%)
  other arithmetic  31.5 us (3%)
  between operations  15.6 us (2%)
    ppermute x35, waiting for transfers between devices, xor_permute(): return lax.ppermute(x, 'uly', [(i, i ^ flip) for i in range(count)])  237 us
    reduce_scatter x1, waiting for transfers between devices, body(): lax.psum_scatter(out_part, 'blk', scatter_dimension=0, tiled=True)  60 us
    all_to_all x1, waiting for transfers between devices, body(): lax.all_to_all(w_gate, 'blk', 1, 0, tiled=True)  53.7 us
    ppermute x35, starting transfers between devices, xor_permute(): return lax.ppermute(x, 'uly', [(i, i ^ flip) for i in range(count)])  53.1 us
    reduce_scatter x1, waiting for transfers between devices, body(): lax.psum_scatter(gh_part, 'blk', scatter_dimension=0, tiled=True)  49.9 us
    dot_general x14, matrix products, t_dot(): lax.dot_general(left, right, (((0,), (0,)), ((), ())), preferred_element_...  47.3 us
    all_to_all x1, blocking collectives, body(): up = gather_uly(lax.all_to_all(w_up, 'blk', 1, 0, tiled=True), count_uly)  46.7 us
    all_to_all x1, waiting for transfers between devices, body(): qkv = lax.all_to_all(qkv, 'blk', 0, 0, tiled=True)  45.6 us
  transfers between devices with their start and end apart: 58, of which 26 were waited for; matrix products, arithmetic and copies ran while one was open for 10% of the time, Pallas kernels for 1%

profile of v1, /device:TPU:0, one launch (start us, length us, event | category | flops | bytes accessed | tf_op | source)
XLA Modules:
  0.0 940.2 jit_solution(6454856153623362259)
XLA Ops:
  14.8 6.3 all-to-all-start.1
  22.5 45.6 %all-to-all-done.1 = bf16[8,64,768]{2,1,0:T(8,128)(2,1)S(1)} async-done(((bf16[8,64,768]{2,1,0:T(8,128)(2,1)}), bf16[8,64,768]{2,1,0:T(8,128)(2,1)S(1)}, u32[]{:S(2)}, u32[]{:S(2)}) %all-to-all-start.1) | async-done | bytes 786464 | tf_op jit(solution)/shard_map/all_to_all | solution.py:423
  68.7 4.5 all-to-all-start
  87.6 7.1 collective-permute-done
  102.2 6.4 collective-permute-done.2
  110.2 8.5 shard_map.212
  121.9 3.6 collective-permute-start.9
  126.1 43.9 %collective-permute-done.7 = bf16[32,2048]{1,0:T(8,128)(2,1)S(1)} collective-permute-done((bf16[32,2048]{1,0:T(8,128)(2,1)S(1)}, bf16[32,2048]{1,0:T(8,128)(2,1)S(1)}, u32[]{:S(2)}, u32[]{:S(2)}) %collective-permute-start.7) | collective-permute-done | bytes 131104 | tf_op jit(solution)/shard_map/ppermute | solution.py:325
  171.4 10.6 %shard_map.213 = (bf16[1024,256]{1,0:T(8,128)(2,1)}, bf16[1024,2048]{1,0:T(8,128)(2,1)}) custom-call(s32[4]{0:T(128)} %add_minimum_fusion.lo_ref, bf16[1024,256]{1,0:T(8,128)(2,1)} %get-tuple-element.34.q_ref, s32[1024,1]{1,0:T(8,128)} %copy.97.start_ref, bf16[256,2048]{1,0:T(8,128)(2,1)} %copy-done.20, bf16[1024,512]{1,0:T(8,128)(2,1)} %collective-permute-done.9.refs_0_, ...), custom_call_target="tpu_custom_call" | custom-call | flops 10000000000 | bytes 12582912 | tf_op jit(solution)/shard_map/pallas_call | solution.py:122
  182.9 60.0 %reduce-scatter.5.cloned.1.call-done = bf16[128,2048]{1,0:T(8,128)(2,1)} async-done(((bf16[1024,2048]{1,0:T(8,128)(2,1)}), bf16[128,2048]{1,0:T(8,128)(2,1)}) %reduce-scatter.5.cloned.1.call-update) | async-done | bytes 524304 | tf_op jit(solution)/shard_map/reduce_scatter | solution.py:444
  247.3 4.3 all-to-all-start.2
  251.7 53.7 %all-to-all-done.2 = bf16[256,8,256]{2,0,1:T(8,128)(2,1)} async-done(((bf16[256,8,256]{2,0,1:T(8,128)(2,1)}), bf16[256,8,256]{2,0,1:T(8,128)(2,1)}, u32[]{:S(2)}, u32[]{:S(2)}) %all-to-all-start.2) | async-done | bytes 1048608 | tf_op jit(solution)/shard_map/all_to_all | solution.py:438
  305.4 46.7 %all_to_all.135 = bf16[256,8,256]{2,0,1:T(8,128)(2,1)S(1)} all-to-all(bf16[256,8,256]{2,0,1:T(8,128)(2,1)S(1)} %bitcast.110), channel_id=1, replica_groups=mesh['uly'=4,'blk'=8] {'blk'}, dimensions={1} | all-to-all | bytes 2097152 | tf_op jit(solution)/shard_map/all_to_all | solution.py:439
  352.2 3.6 all-to-all-start.4
  359.9 30.9 %all-to-all-done.4 = bf16[8,256,256]{2,1,0:T(8,128)(2,1)S(1)} async-done(((bf16[8,256,256]{2,1,0:T(8,128)(2,1)}), bf16[8,256,256]{2,1,0:T(8,128)(2,1)S(1)}, u32[]{:S(2)}, u32[]{:S(2)}) %all-to-all-start.4) | async-done | bytes 1048608 | tf_op jit(solution)/shard_map/all_to_all | solution.py:440
  396.8 7.8 collective-permute-done.15.refs_6_
  409.8 17.2 %collective-permute-done.19.refs_11_ = bf16[256,2048]{1,0:T(8,128)(2,1)S(1)} collective-permute-done((bf16[256,2048]{1,0:T(8,128)(2,1)S(1)}, bf16[256,2048]{1,0:T(8,128)(2,1)S(1)}, u32[]{:S(2)}, u32[]{:S(2)}) %collective-permute-start.19) | collective-permute-done | bytes 1048608 | tf_op jit(solution)/shard_map/ppermute | solution.py:325
  430.1 9.6 %collective-permute-done.13.refs_3_ = bf16[1024,256]{1,0:T(8,128)(2,1)S(1)} collective-permute-done((bf16[1024,256]{1,0:T(8,128)(2,1)S(1)}, bf16[1024,256]{1,0:T(8,128)(2,1)S(1)}, u32[]{:S(2)}, u32[]{:S(2)}) %collective-permute-start.13) | collective-permute-done | bytes 524320 | tf_op jit(solution)/shard_map/ppermute | solution.py:325
  440.3 10.7 %collective-permute-done.17.refs_8_ = bf16[1024,256]{1,0:T(8,128)(2,1)S(1)} collective-permute-done((bf16[1024,256]{1,0:T(8,128)(2,1)S(1)}, bf16[1024,256]{1,0:T(8,128)(2,1)S(1)}, u32[]{:S(2)}, u32[]{:S(2)}) %collective-permute-start.17) | collective-permute-done | bytes 524320 | tf_op jit(solution)/shard_map/ppermute | solution.py:325
  451.0 10.3 %collective-permute-done.21.refs_13_ = bf16[128,2048]{1,0:T(8,128)(2,1)S(1)} collective-permute-done((bf16[128,2048]{1,0:T(8,128)(2,1)S(1)}, bf16[128,2048]{1,0:T(8,128)(2,1)S(1)}, u32[]{:S(2)}, u32[]{:S(2)}) %collective-permute-start.21) | collective-permute-done | bytes 524320 | tf_op jit(solution)/shard_map/ppermute | solution.py:325
  462.1 35.3 %shard_map.214 = (bf16[1024,256]{1,0:T(8,128)(2,1)}, bf16[1024,256]{1,0:T(8,128)(2,1)}, bf16[1024,256]{1,0:T(8,128)(2,1)}, bf16[1024,256]{1,0:T(8,128)(2,1)}, bf...) custom-call(bf16[1024,2048]{1,0:T(8,128)(2,1)} %all-gather.7.cloned., ...), custom_call_target="tpu_custom_call" | custom-call | flops 25769803776 | bytes 37748736 | tf_op jit(solution)/shard_map/pallas_call | solution.py:296
  498.0 49.9 %reduce-scatter.9.cloned.1.call-done = bf16[128,2048]{1,0:T(8,128)(2,1)} async-done(((bf16[1024,2048]{1,0:T(8,128)(2,1)}), bf16[128,2048]{1,0:T(8,128)(2,1)}) %reduce-scatter.9.cloned.1.call-update) | async-done | bytes 524304 | tf_op jit(solution)/shard_map/reduce_scatter | solution.py:450
  551.8 45.4 %all-gather.11.cloned.1.call-done.ga_ref = bf16[1024,2048]{1,0:T(8,128)(2,1)} async-done(((bf16[128,2048]{1,0:T(8,128)(2,1)}), bf16[1024,2048]{1,0:T(8,128)(2,1)}) %all-gather.11.cloned.1.call-update) | async-done | bytes 4194320 | tf_op jit(solution)/shard_map/all_gather | solution.py:459
  597.2 14.4 %shard_map.215 = (bf16[1024,256]{1,0:T(8,128)(2,1)}, f32[1024,512]{1,0:T(8,128)}, bf16[1024,512]{1,0:T(8,128)(2,1)}, bf16[1024,512]{1,0:T(8,128)(2,1)}) custom-call(s32[4]{0:T(128)} %add_minimum_fusion.lo_ref, bf16[1024,256]{1,0:T(8,128)(2,1)} %get-tuple-element.34.q_ref, bf16[1024,2048]{1,0:T(8,128)(2,1)} %all-gather.11.cloned.1.call-done.ga_ref, ...), custom_call_target="tpu_custom_call" | custom-call | flops 24999999488 | bytes 20971520 | tf_op jit(solution)/shard_map/pallas_call | solution.py:198
  614.1 38.3 %collective-permute-done.23 = bf16[1024,512]{1,0:T(8,128)(2,1)S(1)} collective-permute-done((bf16[1024,512]{1,0:T(8,128)(2,1)}, bf16[1024,512]{1,0:T(8,128)(2,1)S(1)}, u32[]{:S(2)}, u32[]{:S(2)}) %collective-permute-start.23) | collective-permute-done | bytes 1048608 | tf_op jit(solution)/shard_map/ppermute | solution.py:485
  664.8 7.1 convolution_convert_fusion
  672.9 3.6 convolution_convert_fusion.3
  676.5 16.0 %collective-permute-start.38 = (bf16[256,2048]{1,0:T(8,128)(2,1)S(1)}, bf16[256,2048]{1,0:T(8,128)(2,1)S(1)}, u32[]{:S(2)}, u32[]{:S(2)}) collective-permute-start(bf16[256,2048]{1,0:T(8,128)(2,1)S(1)} %convolution_convert_fusion.3), channel_id=1, source_target_pairs={{0,8},{8,0},{16,24},{24,16},{1,9},{9,1},{17,25},{25,17},{2,10},{10... | collective-permute-start | bytes 3145736 | tf_op jit(solution)/shard_map/ppermute | solution.py:325
  703.5 13.1 %collective-permute-done.38 = bf16[256,2048]{1,0:T(8,128)(2,1)S(1)} collective-permute-done((bf16[256,2048]{1,0:T(8,128)(2,1)S(1)}, bf16[256,2048]{1,0:T(8,128)(2,1)S(1)}, u32[]{:S(2)}, u32[]{:S(2)}) %collective-permute-start.38) | collective-permute-done | bytes 1048608 | tf_op jit(solution)/shard_map/ppermute | solution.py:325
  716.6 25.9 %collective-permute-done.39 = bf16[256,2048]{1,0:T(8,128)(2,1)S(1)} collective-permute-done((bf16[256,2048]{1,0:T(8,128)(2,1)S(1)}, bf16[256,2048]{1,0:T(8,128)(2,1)S(1)}, u32[]{:S(2)}, u32[]{:S(2)}) %collective-permute-start.39) | collective-permute-done | bytes 1048608 | tf_op jit(solution)/shard_map/ppermute | solution.py:325
  745.0 3.6 all-to-all-start.9
  748.9 4.6 convolution_convert_fusion.4
  753.5 4.8 convolution_convert_fusion.9
  764.1 23.3 %collective-permute-done.36 = bf16[2048,256]{1,0:T(8,128)(2,1)} collective-permute-done((bf16[2048,256]{1,0:T(8,128)(2,1)}, bf16[2048,256]{1,0:T(8,128)(2,1)}, u32[]{:S(2)}, u32[]{:S(2)}) %collective-permute-start.36) | collective-permute-done | bytes 1048608 | tf_op jit(solution)/shard_map/ppermute | solution.py:325
  787.5 4.3 fusion.7
  791.8 3.6 all-to-all-start.8
  795.4 3.8 convolution_convert_fusion.7
  799.3 7.3 collective-permute-done.32
  806.6 23.9 %collective-permute-done.33 = bf16[2048,256]{1,0:T(8,128)(2,1)} collective-permute-done((bf16[2048,256]{1,0:T(8,128)(2,1)}, bf16[2048,256]{1,0:T(8,128)(2,1)}, u32[]{:S(2)}, u32[]{:S(2)}) %collective-permute-start.33) | collective-permute-done | bytes 1048608 | tf_op jit(solution)/shard_map/ppermute | solution.py:325
  830.5 4.3 fusion.8
  834.8 4.5 all-to-all-start.7
  839.3 5.8 fusion.24
  853.4 4.9 fusion.32
  858.4 7.5 all-to-all-done.7
  869.8 16.6 %collective-permute-done.26 = bf16[512,768]{1,0:T(8,128)(2,1)} collective-permute-done((bf16[512,768]{1,0:T(8,128)(2,1)}, bf16[512,768]{1,0:T(8,128)(2,1)}, u32[]{:S(2)}, u32[]{:S(2)}) %collective-permute-start.26) | collective-permute-done | bytes 786464 | tf_op jit(solution)/shard_map/ppermute | solution.py:325
  889.8 4.8 all-to-all-start.5
  899.8 5.4 collective-permute-done.28
  905.2 6.7 collective-permute-done.29
  (292 shorter events, 144.8 us)
Async XLA Ops:
  7.2 103.0 %all-gather.5.cloned.1.call-start = ((), (), s32[]{:S(2)}) async-start(), calls=%async_computation.14 | async-start | bytes 4718592 | tf_op jit(solution)/shard_map/all_gather | solution.py:414
  14.8 53.3 %all-to-all-start.1 = ((bf16[8,64,768]{2,1,0:T(8,128)(2,1)}), bf16[8,64,768]{2,1,0:T(8,128)(2,1)S(1)}, u32[]{:S(2)}, u32[]{:S(2)}) async-start(bf16[8,64,768]{2,1,0:T(8,128)(2,1)} %all_to_all.100), calls=%async_computation.1 | async-start | bytes 1572864 | tf_op jit(solution)/shard_map/all_to_all | solution.py:423
  21.1 64.3 %collective-permute-start.4 = (bf16[64,2048]{1,0:T(8,128)(2,1)S(1)}, bf16[64,2048]{1,0:T(8,128)(2,1)S(1)}, u32[]{:S(2)}, u32[]{:S(2)}) collective-permute-start(bf16[64,2048]{1,0:T(8,128)(2,1)S(1)} %copy-done.36), channel_id=1, source_target_pairs={{0,0},{1,8},{2,16},{3,24},{4,1},{5,9},{6,17},{7,25},{8,2},{9,10},{... | collective-permute-start | bytes 786440 | tf_op jit(solution)/shard_map/ppermute | solution.py:428
  73.3 169.6 %reduce-scatter.5.cloned.1.call-start = ((), (), s32[]{:S(2)}) async-start(), calls=%async_computation.15 | async-start | bytes 4718592 | tf_op jit(solution)/shard_map/reduce_scatter | solution.py:444
  85.5 40.1 %collective-permute-start.5 = (bf16[64,2048]{1,0:T(8,128)(2,1)S(1)}, bf16[64,2048]{1,0:T(8,128)(2,1)S(1)}, u32[]{:S(2)}, u32[]{:S(2)}) collective-permute-start(bf16[64,2048]{1,0:T(8,128)(2,1)S(1)} %collective-permute-done.4), channel_id=1, source_target_pairs={{0,8},{8,0},{16,24},{24,16},{1,9},{9,1},{17,25},{25,17},{2,10},{10... | collective-permute-start | bytes 786440 | tf_op jit(solution)/shard_map/ppermute | solution.py:325
  86.3 39.4 %collective-permute-start.6 = (bf16[64,2048]{1,0:T(8,128)(2,1)S(1)}, bf16[64,2048]{1,0:T(8,128)(2,1)S(1)}, u32[]{:S(2)}, u32[]{:S(2)}) collective-permute-start(bf16[64,2048]{1,0:T(8,128)(2,1)S(1)} %collective-permute-done.4), channel_id=1, source_target_pairs={{0,16},{8,24},{16,0},{24,8},{1,17},{9,25},{17,1},{25,9},{2,18},{10... | collective-permute-start | bytes 786440 | tf_op jit(solution)/shard_map/ppermute | solution.py:325
  118.7 51.4 %collective-permute-start.10 = (bf16[1024,512]{1,0:T(8,128)(2,1)}, bf16[1024,512]{1,0:T(8,128)(2,1)S(1)}, u32[]{:S(2)}, u32[]{:S(2)}) collective-permute-start(bf16[1024,512]{1,0:T(8,128)(2,1)} %get-tuple-element.35.refs_2_), channel_id=1, source_target_pairs={{0,8},{8,16},{16,24},{1,9},{9,17},{17,25},{2,10},{10,18},{18,26},{... | collective-permute-start | bytes 3145736 | tf_op jit(solution)/shard_map/ppermute | solution.py:433
  121.9 48.2 %collective-permute-start.9 = (bf16[1024,512]{1,0:T(8,128)(2,1)}, bf16[1024,512]{1,0:T(8,128)(2,1)}, u32[]{:S(2)}, u32[]{:S(2)}) collective-permute-start(bf16[1024,512]{1,0:T(8,128)(2,1)} %get-tuple-element.35.refs_2_), channel_id=1, source_target_pairs={{0,16},{8,24},{1,17},{9,25},{2,18},{10,26},{3,19},{11,27},{4,20},{... | collective-permute-start | bytes 3145736 | tf_op jit(solution)/shard_map/ppermute | solution.py:433
  125.6 44.3 %collective-permute-start.7 = (bf16[32,2048]{1,0:T(8,128)(2,1)S(1)}, bf16[32,2048]{1,0:T(8,128)(2,1)S(1)}, u32[]{:S(2)}, u32[]{:S(2)}) collective-permute-start(bf16[32,2048]{1,0:T(8,128)(2,1)S(1)} %slice.92), channel_id=1, source_target_pairs={{0,16},{8,24},{16,0},{24,8},{1,17},{9,25},{17,1},{25,9},{2,18},{10... | collective-permute-start | bytes 393224 | tf_op jit(solution)/shard_map/ppermute | solution.py:325
  125.7 44.3 %collective-permute-start.8 = (bf16[32,2048]{1,0:T(8,128)(2,1)S(1)}, bf16[32,2048]{1,0:T(8,128)(2,1)S(1)}, u32[]{:S(2)}, u32[]{:S(2)}) collective-permute-start(bf16[32,2048]{1,0:T(8,128)(2,1)S(1)} %slice.93), channel_id=1, source_target_pairs={{0,8},{8,0},{16,24},{24,16},{1,9},{9,1},{17,25},{25,17},{2,10},{10... | collective-permute-start | bytes 393224 | tf_op jit(solution)/shard_map/ppermute | solution.py:325
  182.0 280.1 %all-gather.9.cloned.1.call-start = ((), (), s32[]{:S(2)}) async-start(), calls=%async_computation.17 | async-start | bytes 4718592 | tf_op jit(solution)/shard_map/all_gather | solution.py:437
  182.7 279.3 %all-gather.7.cloned.1.call-start = ((), (), s32[]{:S(2)}) async-start(), calls=%async_computation.16 | async-start | bytes 4718592 | tf_op jit(solution)/shard_map/all_gather | solution.py:447
  247.3 58.1 %all-to-all-start.2 = ((bf16[256,8,256]{2,0,1:T(8,128)(2,1)}), bf16[256,8,256]{2,0,1:T(8,128)(2,1)}, u32[]{:S(2)}, u32[]{:S(2)}) async-start(bf16[256,8,256]{2,0,1:T(8,128)(2,1)} %bitcast.103), calls=%async_computation.3 | async-start | bytes 2097152 | tf_op jit(solution)/shard_map/all_to_all | solution.py:438
  352.2 38.7 %all-to-all-start.4 = ((bf16[8,256,256]{2,1,0:T(8,128)(2,1)}), bf16[8,256,256]{2,1,0:T(8,128)(2,1)S(1)}, u32[]{:S(2)}, u32[]{:S(2)}) async-start(bf16[8,256,256]{2,1,0:T(8,128)(2,1)} %bitcast.135), calls=%async_computation.5 | async-start | bytes 2097152 | tf_op jit(solution)/shard_map/all_to_all | solution.py:440
  355.7 192.1 %reduce-scatter.9.cloned.1.call-start = ((), (), s32[]{:S(2)}) async-start(), calls=%async_computation.19 | async-start | bytes 4718592 | tf_op jit(solution)/shard_map/reduce_scatter | solution.py:450
  355.8 36.7 %collective-permute-start.11 = (bf16[2048,256]{1,0:T(8,128)(2,1)}, bf16[2048,256]{1,0:T(8,128)(2,1)}, u32[]{:S(2)}, u32[]{:S(2)}) collective-permute-start(bf16[2048,256]{1,0:T(8,128)(2,1)} %bitcast.4.refs_0_), channel_id=1, source_target_pairs={{0,8},{8,0},{16,24},{24,16},{1,9},{9,1},{17,25},{25,17},{2,10},{10... | collective-permute-start | bytes 3145736 | tf_op jit(solution)/shard_map/ppermute | solution.py:325
  357.3 37.7 %collective-permute-start.12 = (bf16[2048,256]{1,0:T(8,128)(2,1)}, bf16[2048,256]{1,0:T(8,128)(2,1)}, u32[]{:S(2)}, u32[]{:S(2)}) collective-permute-start(bf16[2048,256]{1,0:T(8,128)(2,1)} %bitcast.4.refs_0_), channel_id=1, source_target_pairs={{0,16},{8,24},{16,0},{24,8},{1,17},{9,25},{17,1},{25,9},{2,18},{10... | collective-permute-start | bytes 3145736 | tf_op jit(solution)/shard_map/ppermute | solution.py:325
  358.8 45.8 %collective-permute-start.15 = (bf16[2048,256]{1,0:T(8,128)(2,1)S(1)}, bf16[2048,256]{1,0:T(8,128)(2,1)}, u32[]{:S(2)}, u32[]{:S(2)}) collective-permute-start(bf16[2048,256]{1,0:T(8,128)(2,1)S(1)} %bitcast.136), channel_id=1, source_target_pairs={{0,8},{8,0},{16,24},{24,16},{1,9},{9,1},{17,25},{25,17},{2,10},{10... | collective-permute-start | bytes 3145736 | tf_op jit(solution)/shard_map/ppermute | solution.py:325
  359.3 47.8 %collective-permute-start.16 = (bf16[2048,256]{1,0:T(8,128)(2,1)S(1)}, bf16[2048,256]{1,0:T(8,128)(2,1)}, u32[]{:S(2)}, u32[]{:S(2)}) collective-permute-start(bf16[2048,256]{1,0:T(8,128)(2,1)S(1)} %bitcast.137), channel_id=1, source_target_pairs={{0,16},{8,24},{16,0},{24,8},{1,17},{9,25},{17,1},{25,9},{2,18},{10... | collective-permute-start | bytes 3145736 | tf_op jit(solution)/shard_map/ppermute | solution.py:325
  391.0 36.0 %collective-permute-start.19 = (bf16[256,2048]{1,0:T(8,128)(2,1)S(1)}, bf16[256,2048]{1,0:T(8,128)(2,1)S(1)}, u32[]{:S(2)}, u32[]{:S(2)}) collective-permute-start(bf16[256,2048]{1,0:T(8,128)(2,1)S(1)} %bitcast.139), channel_id=1, source_target_pairs={{0,8},{8,0},{16,24},{24,16},{1,9},{9,1},{17,25},{25,17},{2,10},{10... | collective-permute-start | bytes 3145736 | tf_op jit(solution)/shard_map/ppermute | solution.py:325
  392.5 36.0 %collective-permute-start.20 = (bf16[256,2048]{1,0:T(8,128)(2,1)S(1)}, bf16[256,2048]{1,0:T(8,128)(2,1)S(1)}, u32[]{:S(2)}, u32[]{:S(2)}) collective-permute-start(bf16[256,2048]{1,0:T(8,128)(2,1)S(1)} %bitcast.140), channel_id=1, source_target_pairs={{0,16},{8,24},{16,0},{24,8},{1,17},{9,25},{17,1},{25,9},{2,18},{10... | collective-permute-start | bytes 3145736 | tf_op jit(solution)/shard_map/ppermute | solution.py:325
  395.1 44.7 %collective-permute-start.13 = (bf16[1024,256]{1,0:T(8,128)(2,1)S(1)}, bf16[1024,256]{1,0:T(8,128)(2,1)S(1)}, u32[]{:S(2)}, u32[]{:S(2)}) collective-permute-start(bf16[1024,256]{1,0:T(8,128)(2,1)S(1)} %slice.95), channel_id=1, source_target_pairs={{0,16},{8,24},{16,0},{24,8},{1,17},{9,25},{17,1},{25,9},{2,18},{10... | collective-permute-start | bytes 1572872 | tf_op jit(solution)/shard_map/ppermute | solution.py:325
  404.6 35.7 %collective-permute-start.14 = (bf16[1024,256]{1,0:T(8,128)(2,1)S(1)}, bf16[1024,256]{1,0:T(8,128)(2,1)S(1)}, u32[]{:S(2)}, u32[]{:S(2)}) collective-permute-start(bf16[1024,256]{1,0:T(8,128)(2,1)S(1)} %slice.96), channel_id=1, source_target_pairs={{0,8},{8,0},{16,24},{24,16},{1,9},{9,1},{17,25},{25,17},{2,10},{10... | collective-permute-start | bytes 1572872 | tf_op jit(solution)/shard_map/ppermute | solution.py:325
  407.2 43.8 %collective-permute-start.17 = (bf16[1024,256]{1,0:T(8,128)(2,1)S(1)}, bf16[1024,256]{1,0:T(8,128)(2,1)S(1)}, u32[]{:S(2)}, u32[]{:S(2)}) collective-permute-start(bf16[1024,256]{1,0:T(8,128)(2,1)S(1)} %slice.97), channel_id=1, source_target_pairs={{0,16},{8,24},{16,0},{24,8},{1,17},{9,25},{17,1},{25,9},{2,18},{10... | collective-permute-start | bytes 1572872 | tf_op jit(solution)/shard_map/ppermute | solution.py:325
  427.0 24.0 %collective-permute-start.18 = (bf16[1024,256]{1,0:T(8,128)(2,1)S(1)}, bf16[1024,256]{1,0:T(8,128)(2,1)S(1)}, u32[]{:S(2)}, u32[]{:S(2)}) collective-permute-start(bf16[1024,256]{1,0:T(8,128)(2,1)S(1)} %slice.98), channel_id=1, source_target_pairs={{0,8},{8,0},{16,24},{24,16},{1,9},{9,1},{17,25},{25,17},{2,10},{10... | collective-permute-start | bytes 1572872 | tf_op jit(solution)/shard_map/ppermute | solution.py:325
  428.5 32.7 %collective-permute-start.21 = (bf16[128,2048]{1,0:T(8,128)(2,1)S(1)}, bf16[128,2048]{1,0:T(8,128)(2,1)S(1)}, u32[]{:S(2)}, u32[]{:S(2)}) collective-permute-start(bf16[128,2048]{1,0:T(8,128)(2,1)S(1)} %slice.99), channel_id=1, source_target_pairs={{0,16},{8,24},{16,0},{24,8},{1,17},{9,25},{17,1},{25,9},{2,18},{10... | collective-permute-start | bytes 1572872 | tf_op jit(solution)/shard_map/ppermute | solution.py:325
  439.7 22.3 %collective-permute-start.22 = (bf16[128,2048]{1,0:T(8,128)(2,1)S(1)}, bf16[128,2048]{1,0:T(8,128)(2,1)}, u32[]{:S(2)}, u32[]{:S(2)}) collective-permute-start(bf16[128,2048]{1,0:T(8,128)(2,1)S(1)} %slice.100), channel_id=1, source_target_pairs={{0,8},{8,0},{16,24},{24,16},{1,9},{9,1},{17,25},{25,17},{2,10},{10... | collective-permute-start | bytes 1572872 | tf_op jit(solution)/shard_map/ppermute | solution.py:325
  497.5 99.7 %all-gather.11.cloned.1.call-start = ((), (), s32[]{:S(2)}) async-start(), calls=%async_computation.20 | async-start | bytes 4718592 | tf_op jit(solution)/shard_map/all_gather | solution.py:459
  551.7 376.6 %reduce-scatter.11.cloned.1.call-start = ((), (), s32[]{:S(2)}) async-start(), calls=%async_computation.21 | async-start | bytes 4718592 | tf_op jit(solution)/shard_map/reduce_scatter | solution.py:494
  611.5 40.9 %collective-permute-start.23 = (bf16[1024,512]{1,0:T(8,128)(2,1)}, bf16[1024,512]{1,0:T(8,128)(2,1)S(1)}, u32[]{:S(2)}, u32[]{:S(2)}) collective-permute-start(bf16[1024,512]{1,0:T(8,128)(2,1)} %get-tuple-element.41), channel_id=1, source_target_pairs={{16,0},{24,8},{17,1},{25,9},{18,2},{26,10},{19,3},{27,11},{20,4},{... | collective-permute-start | bytes 3145736 | tf_op jit(solution)/shard_map/ppermute | solution.py:485
  612.8 39.6 %collective-permute-start.24 = (bf16[1024,512]{1,0:T(8,128)(2,1)}, bf16[1024,512]{1,0:T(8,128)(2,1)S(1)}, u32[]{:S(2)}, u32[]{:S(2)}) collective-permute-start(bf16[1024,512]{1,0:T(8,128)(2,1)} %get-tuple-element.42), channel_id=1, source_target_pairs={{8,0},{16,8},{24,16},{9,1},{17,9},{25,17},{10,2},{18,10},{26,18},{... | collective-permute-start | bytes 3145736 | tf_op jit(solution)/shard_map/ppermute | solution.py:485
  676.5 40.1 %collective-permute-start.38 = (bf16[256,2048]{1,0:T(8,128)(2,1)S(1)}, bf16[256,2048]{1,0:T(8,128)(2,1)S(1)}, u32[]{:S(2)}, u32[]{:S(2)}) collective-permute-start(bf16[256,2048]{1,0:T(8,128)(2,1)S(1)} %convolution_convert_fusion.3), channel_id=1, source_target_pairs={{0,8},{8,0},{16,24},{24,16},{1,9},{9,1},{17,25},{25,17},{2,10},{10... | collective-permute-start | bytes 3145736 | tf_op jit(solution)/shard_map/ppermute | solution.py:325
  693.8 48.6 %collective-permute-start.39 = (bf16[256,2048]{1,0:T(8,128)(2,1)S(1)}, bf16[256,2048]{1,0:T(8,128)(2,1)S(1)}, u32[]{:S(2)}, u32[]{:S(2)}) collective-permute-start(bf16[256,2048]{1,0:T(8,128)(2,1)S(1)} %convolution_convert_fusion.2), channel_id=1, source_target_pairs={{0,16},{8,24},{16,0},{24,8},{1,17},{9,25},{17,1},{25,9},{2,18},{10... | collective-permute-start | bytes 3145736 | tf_op jit(solution)/shard_map/ppermute | solution.py:325
  695.2 47.2 %collective-permute-start.40 = (bf16[256,2048]{1,0:T(8,128)(2,1)S(1)}, bf16[256,2048]{1,0:T(8,128)(2,1)S(1)}, u32[]{:S(2)}, u32[]{:S(2)}) collective-permute-start(bf16[256,2048]{1,0:T(8,128)(2,1)S(1)} %convolution_convert_fusion.1), channel_id=1, source_target_pairs={{0,24},{8,16},{16,8},{24,0},{1,25},{9,17},{17,9},{25,1},{2,26},{10... | collective-permute-start | bytes 3145736 | tf_op jit(solution)/shard_map/ppermute | solution.py:325
  699.2 64.9 %collective-permute-start.35 = (bf16[2048,256]{1,0:T(8,128)(2,1)}, bf16[2048,256]{1,0:T(8,128)(2,1)S(1)}, u32[]{:S(2)}, u32[]{:S(2)}) collective-permute-start(bf16[2048,256]{1,0:T(8,128)(2,1)} %convolution_convert_fusion.6), channel_id=1, source_target_pairs={{0,8},{8,0},{16,24},{24,16},{1,9},{9,1},{17,25},{25,17},{2,10},{10... | collective-permute-start | bytes 3145736 | tf_op jit(solution)/shard_map/ppermute | solution.py:325
  703.4 84.0 %collective-permute-start.36 = (bf16[2048,256]{1,0:T(8,128)(2,1)}, bf16[2048,256]{1,0:T(8,128)(2,1)}, u32[]{:S(2)}, u32[]{:S(2)}) collective-permute-start(bf16[2048,256]{1,0:T(8,128)(2,1)} %convolution_convert_fusion.5), channel_id=1, source_target_pairs={{0,16},{8,24},{16,0},{24,8},{1,17},{9,25},{17,1},{25,9},{2,18},{10... | collective-permute-start | bytes 3145736 | tf_op jit(solution)/shard_map/ppermute | solution.py:325
  745.0 46.7 %all-to-all-start.9 = ((bf16[256,8,256]{2,0,1:T(8,128)(2,1)}), bf16[256,8,256]{2,0,1:T(8,128)(2,1)S(1)}, u32[]{:S(2)}, u32[]{:S(2)}) async-start(bf16[256,8,256]{2,0,1:T(8,128)(2,1)} %bitcast.101), calls=%async_computation.13 | async-start | bytes 2097152 | tf_op jit(solution)/shard_map/all_to_all | solution.py:468
  748.6 181.1 %reduce-scatter.7.cloned.1.call-start = ((), (), s32[]{:S(2)}) async-start(), calls=%async_computation.18 | async-start | bytes 4718592 | tf_op jit(solution)/shard_map/reduce_scatter | solution.py:452
  753.5 34.0 %collective-permute-start.37 = (bf16[2048,256]{1,0:T(8,128)(2,1)}, bf16[2048,256]{1,0:T(8,128)(2,1)}, u32[]{:S(2)}, u32[]{:S(2)}) collective-permute-start(bf16[2048,256]{1,0:T(8,128)(2,1)} %convolution_convert_fusion.4), channel_id=1, source_target_pairs={{0,24},{8,16},{16,8},{24,0},{1,25},{9,17},{17,9},{25,1},{2,26},{10... | collective-permute-start | bytes 3145736 | tf_op jit(solution)/shard_map/ppermute | solution.py:325
  758.3 48.3 %collective-permute-start.32 = (bf16[2048,256]{1,0:T(8,128)(2,1)}, bf16[2048,256]{1,0:T(8,128)(2,1)}, u32[]{:S(2)}, u32[]{:S(2)}) collective-permute-start(bf16[2048,256]{1,0:T(8,128)(2,1)} %convolution_convert_fusion.9), channel_id=1, source_target_pairs={{0,8},{8,0},{16,24},{24,16},{1,9},{9,1},{17,25},{25,17},{2,10},{10... | collective-permute-start | bytes 3145736 | tf_op jit(solution)/shard_map/ppermute | solution.py:325
  762.1 68.4 %collective-permute-start.33 = (bf16[2048,256]{1,0:T(8,128)(2,1)}, bf16[2048,256]{1,0:T(8,128)(2,1)}, u32[]{:S(2)}, u32[]{:S(2)}) collective-permute-start(bf16[2048,256]{1,0:T(8,128)(2,1)} %convolution_convert_fusion.8), channel_id=1, source_target_pairs={{0,16},{8,24},{16,0},{24,8},{1,17},{9,25},{17,1},{25,9},{2,18},{10... | collective-permute-start | bytes 3145736 | tf_op jit(solution)/shard_map/ppermute | solution.py:325
  791.8 43.0 %all-to-all-start.8 = ((bf16[8,256,256]{2,1,0:T(8,128)(2,1)}), bf16[8,256,256]{2,1,0:T(8,128)(2,1)S(1)}, u32[]{:S(2)}, u32[]{:S(2)}) async-start(bf16[8,256,256]{2,1,0:T(8,128)(2,1)} %bitcast.143), calls=%async_computation.12 | async-start | bytes 2097152 | tf_op jit(solution)/shard_map/all_to_all | solution.py:467
  799.2 31.3 %collective-permute-start.34 = (bf16[2048,256]{1,0:T(8,128)(2,1)S(1)}, bf16[2048,256]{1,0:T(8,128)(2,1)S(1)}, u32[]{:S(2)}, u32[]{:S(2)}) collective-permute-start(bf16[2048,256]{1,0:T(8,128)(2,1)S(1)} %convolution_convert_fusion.7), channel_id=1, source_target_pairs={{0,24},{8,16},{16,8},{24,0},{1,25},{9,17},{17,9},{25,1},{2,26},{10... | collective-permute-start | bytes 3145736 | tf_op jit(solution)/shard_map/ppermute | solution.py:325
  834.8 31.1 %all-to-all-start.7 = ((bf16[8,256,256]{2,1,0:T(8,128)(2,1)}), bf16[8,256,256]{2,1,0:T(8,128)(2,1)}, u32[]{:S(2)}, u32[]{:S(2)}) async-start(bf16[8,256,256]{2,1,0:T(8,128)(2,1)} %bitcast.142), calls=%async_computation.11 | async-start | bytes 2097152 | tf_op jit(solution)/shard_map/all_to_all | solution.py:466
  849.5 36.9 %collective-permute-start.26 = (bf16[512,768]{1,0:T(8,128)(2,1)}, bf16[512,768]{1,0:T(8,128)(2,1)}, u32[]{:S(2)}, u32[]{:S(2)}) collective-permute-start(bf16[512,768]{1,0:T(8,128)(2,1)} %get-tuple-element.62), channel_id=1, source_target_pairs={{0,16},{8,24},{16,0},{24,8},{1,17},{9,25},{17,1},{25,9},{2,18},{10... | collective-permute-start | bytes 2359304 | tf_op jit(solution)/shard_map/ppermute | solution.py:325
  849.8 36.7 %collective-permute-start.27 = (bf16[512,768]{1,0:T(8,128)(2,1)}, bf16[512,768]{1,0:T(8,128)(2,1)}, u32[]{:S(2)}, u32[]{:S(2)}) collective-permute-start(bf16[512,768]{1,0:T(8,128)(2,1)} %get-tuple-element.61), channel_id=1, source_target_pairs={{0,24},{8,16},{16,8},{24,0},{1,25},{9,17},{17,9},{25,1},{2,26},{10... | collective-permute-start | bytes 2359304 | tf_op jit(solution)/shard_map/ppermute | solution.py:325
  865.9 23.9 %all-to-all-start.6 = ((f32[32,1,64]{2,1,0:T(1,128)}), f32[32,1,64]{2,1,0:T(1,128)S(1)}, u32[]{:S(2)}, u32[]{:S(2)}) async-start(f32[32,1,64]{2,1,0:T(1,128)} %all_to_all.117), calls=%async_computation.10 | async-start | bytes 32768 | tf_op jit(solution)/shard_map/all_to_all | solution.py:457
  889.8 31.3 %all-to-all-start.5 = ((bf16[8,64,768]{2,1,0:T(8,128)(2,1)}), bf16[8,64,768]{2,1,0:T(8,128)(2,1)}, u32[]{:S(2)}, u32[]{:S(2)}) async-start(bf16[8,64,768]{2,1,0:T(8,128)(2,1)} %bitcast.111), calls=%async_computation.9 | async-start | bytes 1572864 | tf_op jit(solution)/shard_map/all_to_all | solution.py:498
  (61 other events, 979.4 us)
Sparse Core Ops, SparseCore 0:
  9.6 78.1 all-gather.4
  182.1 60.6 reduce-scatter.4
  244.4 67.5 all-gather.8
  314.1 73.1 all-gather.6
  497.6 50.1 reduce-scatter.8
  551.9 45.2 all-gather.10
  672.0 62.3 reduce-scatter.10
  753.6 69.6 reduce-scatter.6

commit v2 on v1

--- a/solution.py
+++ b/solution.py
@@ -19,7 +19,7 @@
 score_bias = -math.log(4096.0)
 head_scale = 1.0 / math.sqrt(HD)
 
-BQ = 256
+BQ = 512
 BK = 512
 BR = 256
 VMEM = 60 * 2**20
@@ -37,6 +37,49 @@
 
 def dot(left, right):
     return jnp.dot(left, right, preferred_element_type=f32)
+
+
+def pack_kernel(wq_ref, wk_ref, wv_ref, gain_ref, out_ref):
+    rows = wq_ref.shape[0]
+    width = out_ref.shape[2] // 3
+    for b in range(out_ref.shape[0]):
+        for i, w in enumerate((wq_ref, wk_ref, wv_ref)):
+            out_ref[b, :rows, i * width : (i + 1) * width] = w[:, b * width : (b + 1) * width]
+        out_ref[b, rows:, :] = gain_ref[...]
+
+
+def pack_call(wq, wk, wv, gains, count):
+    rows, dim = wq.shape
+    vmem = pl.BlockSpec(memory_space=pltpu.VMEM)
+    return pl.pallas_call(
+        pack_kernel,
+        in_specs=[vmem] * 4,
+        out_specs=vmem,
+        out_shape=jax.ShapeDtypeStruct((count, rows + gains.shape[0], 3 * dim // count), bf16),
+    )(wq, wk, wv, gains)
+
+
+def unpack_kernel(got_ref, wq_ref, wk_ref, wv_ref, gain_ref, gq_ref, gk_ref, gv_ref, gg_ref):
+    width = got_ref.shape[2] // 3
+    total = jnp.zeros(gg_ref.shape, f32)
+    for i, (w, g_ref) in enumerate(((wq_ref, gq_ref), (wk_ref, gk_ref), (wv_ref, gv_ref))):
+        for b in range(got_ref.shape[0]):
+            at = slice(b * width, (b + 1) * width)
+            g = got_ref[b, :, i * width : (i + 1) * width].astype(f32)
+            g_ref[:, at] = g
+            total = total + jnp.sum(g * w[:, at].astype(f32), axis=1, keepdims=True)
+    gg_ref[...] = total / gain_ref[...]
+
+
+def unpack_call(got, wq, wk, wv, gain):
+    vmem = pl.BlockSpec(memory_space=pltpu.VMEM)
+    return pl.pallas_call(
+        unpack_kernel,
+        in_specs=[vmem] * 5,
+        out_specs=[vmem] * 4,
+        out_shape=[jax.ShapeDtypeStruct(wq.shape, f32)] * 3
+        + [jax.ShapeDtypeStruct((wq.shape[0], 1), f32)],
+    )(got, wq, wk, wv, gain)
 
 
 def qkv_kernel(x_ref, gain_ref, w_ref, cos_ref, sin_ref, h_ref, q_ref, kv_ref):
@@ -77,8 +120,8 @@
     )(x, gain, w, cos, sin)
 
 
-def attn_fwd_kernel(count_kv, lo_ref, q_ref, start_ref, wo_ref, *refs):
-    kv_refs, (att_ref, part_ref, kv_all) = refs[:count_kv], refs[count_kv:]
+def attn_fwd_kernel(count_kv, lo_ref, q_ref, start_ref, *refs):
+    kv_refs, (att_ref, kv_all) = refs[:count_kv], refs[count_kv:]
     rows, width = q_ref.shape
     heads = width // HD
     base = (count_kv - 1) * rows
@@ -110,29 +153,94 @@
         sums = lax.fori_loop(
             lo_ref[i], last, step, tuple(jnp.zeros((BQ, HD), f32) for _ in range(heads))
         )
-        att = jnp.concatenate([s.astype(bf16) for s in sums], axis=1)
-        att_ref[at, :] = att
-        part_ref[at, :] = dot(att, wo_ref[...]).astype(bf16)
-
-
-def attn_fwd_call(lo, q, start, wo, kvs):
+        att_ref[at, :] = jnp.concatenate([s.astype(bf16) for s in sums], axis=1)
+
+
+def attn_fwd_call(lo, q, start, kvs):
     rows, width = q.shape
-    dim = wo.shape[1]
     vmem = pl.BlockSpec(memory_space=pltpu.VMEM)
     return pl.pallas_call(
         functools.partial(attn_fwd_kernel, len(kvs)),
-        in_specs=[pl.BlockSpec(memory_space=pltpu.SMEM)] + [vmem] * (3 + len(kvs)),
-        out_specs=[vmem, vmem],
-        out_shape=[
-            jax.ShapeDtypeStruct((rows, width), bf16),
-            jax.ShapeDtypeStruct((rows, dim), bf16),
-        ],
+        in_specs=[pl.BlockSpec(memory_space=pltpu.SMEM)] + [vmem] * (2 + len(kvs)),
+        out_specs=vmem,
+        out_shape=jax.ShapeDtypeStruct((rows, width), bf16),
         scratch_shapes=[pltpu.VMEM((len(kvs) * rows, 2 * width), bf16)],
         compiler_params=pltpu.CompilerParams(vmem_limit_bytes=VMEM),
         cost_estimate=pl.CostEstimate(
             flops=10 * 10**9, bytes_accessed=12 * 2**20, transcendentals=4 * 10**6
         ),
-    )(lo, q, start, wo, *kvs)
+    )(lo, q, start, *kvs)
+
+
+def project_kernel(count, places, at_ref, att_ref, x_ref, gain_ref, *refs):
+    sources, (h_ref, own_ref, wo_out_ref, wo, att, sem) = refs[: len(places)], refs[len(places) :]
+    uly, blk = at_ref[0], at_ref[1]
+    heads, _, width = att_ref.shape
+    dim = wo.shape[0]
+    step = pl.program_id(0)
+
+    @pl.when(step == 0)
+    def _():
+        copies = []
+        for n, (source, (j, half, row)) in enumerate(zip(sources, places)):
+            rows = source.shape[0]
+            block = dim // count
+            at = (uly ^ j) * block + row
+            if half:
+                core = lax.rem(blk, 2)
+                at = at + (core if half == 1 else 1 - core) * (block // 2)
+            to = wo.at[pl.ds(pl.multiple_of(at, rows), rows), :]
+            copies.append(pltpu.make_async_copy(source, to, sem.at[n]))
+        for c in copies:
+            c.start()
+        for c in copies:
+            c.wait()
+        wo_out_ref[...] = wo[pl.ds(pl.multiple_of(blk * width, width), width), :]
+
+    for n in range(heads):
+        att[:, n * width : (n + 1) * width] = att_ref[n]
+    resid = x_ref[...].astype(f32) + dot(att[...], wo[...])
+    inv = lax.rsqrt(jnp.mean(resid * resid, axis=-1, keepdims=True) + norm_eps)
+    h_ref[...] = (resid * inv * gain_ref[...]).astype(bf16)
+    own = own_ref.shape[0]
+    for n in range(BR // own):
+
+        @pl.when(step * (BR // own) + n == blk)
+        def _():
+            own_ref[...] = resid[n * own : (n + 1) * own, :]
+
+
+def project_call(at, att, x, gain, sources, places, own, count):
+    heads, rows, width = att.shape
+    dim = x.shape[1]
+    block = lambda cols: pl.BlockSpec((BR, cols), lambda i: (i, 0))
+    whole = lambda *shape: pl.BlockSpec(shape, lambda i: (0, 0))
+    return pl.pallas_call(
+        functools.partial(project_kernel, count, places),
+        grid=(rows // BR,),
+        in_specs=[
+            pl.BlockSpec(memory_space=pltpu.SMEM),
+            pl.BlockSpec((heads, BR, width), lambda i: (0, i, 0)),
+            block(dim),
+            whole(1, dim),
+        ]
+        + [pl.BlockSpec(memory_space=pl.ANY)] * len(sources),
+        out_specs=[block(dim), whole(own, dim), whole(width, dim)],
+        out_shape=[
+            jax.ShapeDtypeStruct((rows, dim), bf16),
+            jax.ShapeDtypeStruct((own, dim), f32),
+            jax.ShapeDtypeStruct((width, dim), bf16),
+        ],
+        scratch_shapes=[
+            pltpu.VMEM((dim, dim), bf16),
+            pltpu.VMEM((BR, dim), bf16),
+            pltpu.SemaphoreType.DMA((len(places),)),
+        ],
+        compiler_params=pltpu.CompilerParams(vmem_limit_bytes=VMEM),
+        cost_estimate=pl.CostEstimate(
+            flops=2 * rows * dim * dim, bytes_accessed=24 * 2**20, transcendentals=0
+        ),
+    )(at, att, x, gain, *sources)
 
 
 def attn_bwd_kernel(count_kv, lo_ref, q_ref, ga_ref, start_ref, wo_ref, cos_ref, sin_ref, *refs):
@@ -215,110 +323,205 @@
     )(lo, q, ga, start, wo, cos, sin, *kvs)
 
 
-def ffn_kernel(places, blocks, h_ref, c_ref, *refs):
-    count = len(places[0])
-    sources = refs[: 3 * count]
-    outs = refs[3 * count : 3 * count + 3 * blocks]
-    y_ref, gh_ref = refs[3 * count + 3 * blocks : 3 * count + 3 * blocks + 2]
-    wg, wu, wd, gates, ups, inners, sem = refs[3 * count + 3 * blocks + 2 :]
-    inner_refs, gg_refs, gu_refs = outs[:blocks], outs[blocks : 2 * blocks], outs[2 * blocks :]
+def gqkv_kernel(count, index_ref, h_ref, gq_ref, own_ref, cos_ref, sin_ref, w_ref, *refs):
+    got, gh_ref, grad_refs, g_ref = refs[: -2 - count], refs[-2 - count], refs[-1 - count : -1], refs[-1]
+    rows, width = gq_ref.shape
+    for at in range(0, rows, BR):
+        at = slice(at, at + BR)
+        gkv = own_ref[at, :]
+        for r in got:
+            gkv = gkv + r[at, :].astype(f32)
+        cos, sin = cos_ref[at, :], sin_ref[at, :]
+        g_ref[at, :width] = gq_ref[at, :]
+        for s in range(0, width, HD):
+            t = gkv[:, s : s + HD]
+            g_ref[at, width + s : width + s + HD] = (
+                t * cos - pltpu.roll(t, HD // 2, 1) * sin
+            ).astype(bf16)
+        g_ref[at, 2 * width :] = gkv[:, width:].astype(bf16)
+        gh_ref[at, :] = dot_t(g_ref[at, :], w_ref[...]).astype(bf16)
+    size = h_ref.shape[1] // count
+    for j in list(range(1, count)) + [0]:
+        at = pl.multiple_of((index_ref[0] ^ j) * size, size)
+        grad_refs[j][...] = t_dot(h_ref[:, pl.ds(at, size)], g_ref[...]).astype(grad_refs[j].dtype)
+
+
+def gqkv_call(index, h, gq, own, got, cos, sin, w, count):
+    rows, width = gq.shape
+    dim = h.shape[1]
+    size = dim // count
+    vmem = pl.BlockSpec(memory_space=pltpu.VMEM)
+    gh, *grads = pl.pallas_call(
+        functools.partial(gqkv_kernel, count),
+        in_specs=[pl.BlockSpec(memory_space=pltpu.SMEM)] + [vmem] * (6 + len(got)),
+        out_specs=[vmem] * (1 + count),
+        out_shape=[
+            jax.ShapeDtypeStruct((rows, dim), bf16),
+            jax.ShapeDtypeStruct((size, 3 * width), f32),
+        ]
+        + [jax.ShapeDtypeStruct((size, 3 * width), bf16)] * (count - 1),
+        scratch_shapes=[pltpu.VMEM((rows, 3 * width), bf16)],
+        compiler_params=pltpu.CompilerParams(vmem_limit_bytes=VMEM),
+        cost_estimate=pl.CostEstimate(
+            flops=12 * rows * width * dim, bytes_accessed=20 * 2**20, transcendentals=0
+        ),
+    )(index, h, gq, own, cos, sin, w, *got)
+    return gh, grads
+
+
+def ffn_kernel(places, blocks, groups, h_ref, c_ref, *refs):
+    count = 1 + max(p[1] for p in places)
+    sources = refs[:count]
+    outs = refs[count : count + 3 * len(groups)]
+    inner_ref, gh_ref, wg, wu, wd, gates, ups, sem = refs[count + 3 * len(groups) :]
     width = wg.shape[1] // blocks
-
-    def copies(which):
-        found = []
-        for p, (j, row) in enumerate(places[which]):
-            src = sources[which * count + p]
-            held = (wg, wu, wd)[which]
-            if which < 2:
-                dst = held.at[pl.ds(row, src.shape[0]), pl.ds(j * width, width)]
-            else:
-                dst = held.at[pl.ds(j * width + row, src.shape[0]), :]
-            found.append(pltpu.make_async_copy(src, dst, sem.at[which, p]))
-        return found
-
+    copies = [
+        (which, pltpu.make_async_copy(sources[source].at[at], (wg, wu, wd)[which].at[to], sem.at[i]))
+        for i, (which, source, at, to) in enumerate(places)
+    ]
     first = pl.program_id(0) == 0
+
+    def wait(weight):
+        @pl.when(first)
+        def _():
+            for which, c in copies:
+                if which == weight:
+                    c.wait()
 
     @pl.when(first)
     def _():
-        for which in range(3):
-            for c in copies(which):
-                c.start()
-        for which in range(3):
-            for c in copies(which):
-                c.wait()
-
-    h, c = h_ref[...], c_ref[...]
-    for j in range(blocks):
-        cols = slice(j * width, (j + 1) * width)
-        gate = dot(h, wg[:, cols])
-        up = dot(h, wu[:, cols])
-        grad = dot_t(c, wd[cols, :])
-        sig = 1.0 / (1.0 + jnp.exp2(gate * -LOG2E))
-        act = gate * sig
-        inner = (act * up).astype(bf16)
-        gg = (grad * up * sig * (1.0 + gate * (1.0 - sig))).astype(bf16)
-        gu = (grad * act).astype(bf16)
-        inner_refs[j][...] = inner
-        gg_refs[j][...] = gg
-        gu_refs[j][...] = gu
-        inners[:, cols] = inner
-        gates[:, cols] = gg
-        ups[:, cols] = gu
+        for weight in range(3):
+            for which, c in copies:
+                if which == weight:
+                    c.start()
+
+    wait(0)
+    gate = dot(h_ref[...], wg[...])
+    wait(1)
+    up = dot(h_ref[...], wu[...])
+    wait(2)
+    grad = dot_t(c_ref[...], wd[...])
+    sig = 1.0 / (1.0 + jnp.exp2(gate * -LOG2E))
+    act = gate * sig
+    inner = (act * up).astype(bf16)
+    gg = (grad * up * sig * (1.0 + gate * (1.0 - sig))).astype(bf16)
+    gu = (grad * act).astype(bf16)
+    inner_ref[...] = inner
+    gates[...] = gg
+    ups[...] = gu
+    for n, members in enumerate(groups):
+        for m, j in enumerate(members):
+            at, to = slice(j * width, (j + 1) * width), slice(m * width, (m + 1) * width)
+            outs[n][:, to] = inner[:, at]
+            outs[len(groups) + n][:, to] = gg[:, at]
+            outs[2 * len(groups) + n][:, to] = gu[:, at]
     gh_ref[...] = (dot_t(gates[...], wg[...]) + dot_t(ups[...], wu[...])).astype(bf16)
-    y_ref[...] = dot(inners[...], wd[...]).astype(bf16)
-
-
-def ffn_call(h, cot, gate, up, down):
+
+
+def ffn_call(h, cot, sources, places, blocks, width, groups):
     rows, dim = h.shape
-    blocks = len(gate)
-    width = gate[0][0].shape[1]
-    if width % HD:
-        merge = lambda parts: jnp.concatenate(parts, axis=0)
-        gate = [[jnp.concatenate([merge(g) for g in gate], axis=1)]]
-        up = [[jnp.concatenate([merge(g) for g in up], axis=1)]]
-        down = [[jnp.concatenate([merge(g) for g in down], axis=0)]]
-        joined, blocks, width = blocks, 1, width * blocks
-    else:
-        joined = 0
-    places, sources = [], []
-    for weight in (gate, up, down):
-        place = []
-        for j, parts in enumerate(weight):
-            row = 0
-            for part in parts:
-                place.append((j, row))
-                sources.append(part)
-                row += part.shape[0]
-        places.append(tuple(place))
-    count = len(places[0])
     hidden = blocks * width
     block = lambda cols: pl.BlockSpec((BR, cols), lambda i: (i, 0))
+    sizes = [len(members) * width for members in groups] * 3 + [hidden, dim]
     result = pl.pallas_call(
-        functools.partial(ffn_kernel, tuple(places), blocks),
+        functools.partial(ffn_kernel, places, blocks, groups),
         grid=(rows // BR,),
         in_specs=[block(dim), block(dim)] + [pl.BlockSpec(memory_space=pl.ANY)] * len(sources),
-        out_specs=[block(width)] * (3 * blocks) + [block(dim)] * 2,
-        out_shape=[jax.ShapeDtypeStruct((rows, width), bf16)] * (3 * blocks)
-        + [jax.ShapeDtypeStruct((rows, dim), bf16)] * 2,
+        out_specs=[block(size) for size in sizes],
+        out_shape=[jax.ShapeDtypeStruct((rows, size), bf16) for size in sizes],
         scratch_shapes=[
             pltpu.VMEM((dim, hidden), bf16),
             pltpu.VMEM((dim, hidden), bf16),
             pltpu.VMEM((hidden, dim), bf16),
             pltpu.VMEM((BR, hidden), bf16),
             pltpu.VMEM((BR, hidden), bf16),
-            pltpu.VMEM((BR, hidden), bf16),
-            pltpu.SemaphoreType.DMA((3, count)),
+            pltpu.SemaphoreType.DMA((len(places),)),
         ],
         compiler_params=pltpu.CompilerParams(vmem_limit_bytes=VMEM),
         cost_estimate=pl.CostEstimate(
-            flops=12 * rows * dim * hidden, bytes_accessed=36 * 2**20, transcendentals=10**6
+            flops=10 * rows * dim * hidden, bytes_accessed=36 * 2**20, transcendentals=10**6
         ),
     )(h, cot, *sources)
-    inner, gg, gu = result[:blocks], result[blocks : 2 * blocks], result[2 * blocks : 3 * blocks]
-    if joined:
-        split = lambda a: jnp.split(a[0], joined, axis=1)
-        inner, gg, gu = split(inner), split(gg), split(gu)
-    return inner, gg, gu, result[-2], result[-1]
+    n = len(groups)
+    down = [p for p in places if p[0] == 2]
+    base = min(p[1] for p in down)
+    y = down_call(result[-2], sources[base:], [(p[1] - base,) + p[2:] for p in down])
+    return result[:n], result[n : 2 * n], result[2 * n : 3 * n], y, result[-1]
+
+
+def down_kernel(places, inner_ref, *refs):
+    sources, (y_ref, wd, sem) = refs[:-3], refs[-3:]
+
+    @pl.when(pl.program_id(0) == 0)
+    def _():
+        copies = [
+            pltpu.make_async_copy(sources[source].at[at], wd.at[to], sem.at[i])
+            for i, (source, at, to) in enumerate(places)
+        ]
+        for c in copies:
+            c.start()
+        for c in copies:
+            c.wait()
+
+    y_ref[...] = dot(inner_ref[...], wd[...]).astype(bf16)
+
+
+def down_call(inner, sources, places):
+    rows, hidden = inner.shape
+    dim = max(to[1].stop or 0 for _, _, to in places) or sources[0].shape[-1]
+    block = lambda cols: pl.BlockSpec((BR, cols), lambda i: (i, 0))
+    return pl.pallas_call(
+        functools.partial(down_kernel, tuple(places)),
+        grid=(rows // BR,),
+        in_specs=[block(hidden)] + [pl.BlockSpec(memory_space=pl.ANY)] * len(sources),
+        out_specs=block(dim),
+        out_shape=jax.ShapeDtypeStruct((rows, dim), bf16),
+        scratch_shapes=[
+            pltpu.VMEM((hidden, dim), bf16),
+            pltpu.SemaphoreType.DMA((len(places),)),
+        ],
+        compiler_params=pltpu.CompilerParams(vmem_limit_bytes=VMEM),
+        cost_estimate=pl.CostEstimate(
+            flops=2 * rows * dim * hidden, bytes_accessed=12 * 2**20, transcendentals=0
+        ),
+    )(inner, *sources)
+
+
+PAIRS = ((0, 2), (1, 3), (2, 3), (0, 1))
+
+
+def ffn_pieces(h, cot, gate_up, down, width):
+    sources, places = [], []
+    for pieces, kinds in ((gate_up, (0, 1)), (down, (2,))):
+        for j, parts in enumerate(pieces):
+            block = 0
+            for part in parts:
+                size = part.shape[2] if kinds == (2,) else part.shape[1] // 2
+                for i in range(part.shape[0]):
+                    rows = slice(block * size, (block + 1) * size)
+                    cols = slice(j * width, (j + 1) * width)
+                    for which in kinds:
+                        at = (i, slice(which * size, (which + 1) * size)) if which < 2 else (i,)
+                        to = (rows, cols) if which < 2 else (cols, rows)
+                        places.append((which, len(sources), at, to))
+                    block += 1
+                sources.append(part)
+    return ffn_call(h, cot, sources, tuple(places), len(down), width, PAIRS)
+
+
+def ffn_plain(h, cot, gate_up, down):
+    size = gate_up[0][0].shape[1] // 2
+    merge = lambda parts: jnp.concatenate(parts, axis=0)
+    flat = lambda p, at: merge(p)[:, at].reshape(-1, p[0].shape[-1])
+    tall = lambda p: merge(p).transpose(1, 0, 2).reshape(p[0].shape[1], -1)
+    sources = [
+        jnp.concatenate([flat(p, slice(0, size)) for p in gate_up], axis=1),
+        jnp.concatenate([flat(p, slice(size, 2 * size)) for p in gate_up], axis=1),
+        jnp.concatenate([tall(p) for p in down], axis=0),
+    ]
+    every = (slice(None), slice(None))
+    places = tuple((which, which, every, every) for which in range(3))
+    return ffn_call(h, cot, sources, places, 1, sources[0].shape[1], ((0,),))
 
 
 def xor_permute(x, count, flip):
@@ -326,10 +529,18 @@
 
 
 def gather_uly(x, count):
+    return gather_rest(gather_first(x, count), count)
+
+
+def gather_first(x, count):
+    return [x] + [xor_permute(x, count, j) for j in ((1, 2) if count == 4 else range(1, count))]
+
+
+def gather_rest(blocks, count):
     if count != 4:
-        return [[x]] + [[xor_permute(x, count, j)] for j in range(1, count)]
+        return [[block] for block in blocks]
+    x, one, two = blocks
     half = x.shape[0] // 2
-    one, two = xor_permute(x, count, 1), xor_permute(x, count, 2)
     low = xor_permute(one[:half], count, 2)
     high = xor_permute(two[half:], count, 1)
     return [[x], [one], [two], [low, high]]
@@ -351,6 +562,10 @@
     for block in got:
         own = own + block.astype(f32)
     return own
+
+
+def after(x, *earlier):
+    return lax.optimization_barrier((x,) + earlier)[0]
 
 
 def rms_stats(values):
@@ -382,10 +597,14 @@
     count_blk = lax.axis_size("blk")
     devices = count_uly * count_blk
     uly_index = lax.axis_index("uly")
+    blk_index = lax.axis_index("blk")
+    uly_at = uly_index.astype(jnp.int32).reshape(1)
+    both_at = jnp.stack([uly_index, blk_index]).astype(jnp.int32)
     tok_rows, dim = block_input.shape
     group = count_blk * tok_rows
     part = dim // count_blk
     rows_w = w_query.shape[0]
+    together = lax.optimization_barrier
     longest = LONGEST.get(devices * tok_rows, devices * tok_rows)
     back = min(count_uly - 1, -(-(longest - 1) // group))
 
@@ -411,108 +630,191 @@
     cos = jnp.concatenate([cos, cos], axis=1)
     sin = jnp.concatenate([-sin, sin], axis=1)
 
-    group_in = lax.all_gather(block_input, "blk", axis=0, tiled=True)
+    wo = lax.all_gather(w_out, "blk", axis=0, tiled=True)
     gains = jnp.concatenate([norm_attn, norm_ffn])
-    gains = lax.all_to_all(
-        jnp.broadcast_to(gains[None], (devices, gains.shape[0])), BOTH, 0, 0, tiled=True
-    )
+    gains = jnp.pad(gains[None], ((0, 15), (0, 3 * part - 2 * rows_w)))
+    qkv = pack_call(w_query, w_key, w_value, gains, count_blk)
+    qkv = lax.all_to_all(qkv, "blk", 0, 0, tiled=True)
+    group_in = lax.all_gather(after(block_input, qkv, wo), "blk", axis=0, tiled=True)
+    qkv_pieces = gather_uly(qkv, count_uly)
+    cut = lambda f: in_order([[f(p) for p in parts] for parts in qkv_pieces], uly_index)
+    w_qkv = cut(lambda p: p[:, :rows_w].reshape(-1, 3 * part))
+    gains = cut(lambda p: p[:, rows_w, : 2 * rows_w])
     gain_attn = gains[:, :rows_w].reshape(1, dim).astype(f32)
     gain_ffn = gains[:, rows_w:].reshape(1, dim).astype(f32)
-    qkv = jnp.stack([w.reshape(rows_w, count_blk, part) for w in (w_query, w_key, w_value)], axis=1)
-    qkv = qkv.transpose(2, 0, 1, 3).reshape(count_blk * rows_w, 3 * part)
-    qkv = lax.all_to_all(qkv, "blk", 0, 0, tiled=True)
-    w_qkv = in_order(gather_uly(qkv, count_uly), uly_index)
-    owner = [
-        (i, (i % count_uly) * count_blk + i // count_uly) for i in range(devices)
-    ]
-    wo = lax.ppermute(w_out, BOTH, owner)
-    wo = in_order(gather_uly(wo, count_uly), uly_index)
-
+
+    rows_d, width = w_gate.shape[0], w_gate.shape[1] // count_blk
+    columns = lambda w: w.reshape(rows_d, count_blk, width).transpose(1, 0, 2)
+    to_hidden = lambda w: lax.all_to_all(w, "blk", 0, 0, tiled=True)
+    gate_up = jnp.concatenate([columns(w_gate), columns(w_up)], axis=1)
+    down = to_hidden(after(w_down.reshape(count_blk, width, rows_d), qkv))
+    if count_uly == 4:
+        size = wo.shape[0] // 2
+        half = lax.dynamic_slice_in_dim(wo, lax.rem(blk_index, 2) * size, size, 0)
+        halves = gather_uly(after(half, qkv_pieces[3][-1]), count_uly)[1:]
+    else:
+        halves = gather_uly(wo, count_uly)[1:]
+    halves, group_in, down, gate_up = together((halves, group_in, down, gate_up))
+    wos, places = [wo], [(0, 0, 0)]
+    for j, parts in enumerate(halves, 1):
+        row = 0
+        for piece in parts:
+            if count_uly == 4:
+                swapped = lax.ppermute(piece, "blk", [(i, i ^ 1) for i in range(count_blk)])
+                wos += [piece, swapped]
+                places += [(j, 1, row), (j, 2, row)]
+            else:
+                wos += [piece]
+                places += [(j, 0, 0)]
+            row += piece.shape[0]
     hidden_one, query, kv = qkv_call(group_in, gain_attn, w_qkv, cos, sin)
     kvs = [
         lax.ppermute(kv, "uly", [(i, i + s) for i in range(count_uly - s)])
         for s in range(back, 0, -1)
     ] + [kv]
 
-    group_cot = lax.all_gather(cotangent, "blk", axis=0, tiled=True)
-    gate = gather_uly(lax.all_to_all(w_gate, "blk", 1, 0, tiled=True), count_uly)
-    up = gather_uly(lax.all_to_all(w_up, "blk", 1, 0, tiled=True), count_uly)
-    down = gather_uly(lax.all_to_all(w_down, "blk", 0, 1, tiled=True), count_uly)
-
-    attended, out_part = attn_fwd_call(low_kb, query, begin[:, None], wo, kvs)
+    gate_up = to_hidden(after(gate_up, kv))
+    group_cot = lax.all_gather(after(cotangent, kv), "blk", axis=0, tiled=True)
+    down = gather_uly(after(down, kv), count_uly)
+    query, gate_up, down, group_cot = together((query, gate_up, down, group_cot))
+    gate_up = gather_first(gate_up, count_uly)
+    attended = attn_fwd_call(low_kb, query, begin[:, None], kvs)
+    group_att = lax.all_gather(attended, "blk", axis=0, tiled=True)
+    gate_up, group_att = together((gate_up, group_att))
+    gate_up = gather_rest(gate_up, count_uly)
+    group_hidden, resid, wo = project_call(
+        both_at,
+        group_att.reshape(count_blk, group, part),
+        group_in,
+        gain_ffn,
+        wos,
+        tuple(places),
+        tok_rows,
+        count_uly,
+    )
     input_f = block_input.astype(f32)
-    resid = input_f + lax.psum_scatter(out_part, "blk", scatter_dimension=0, tiled=True).astype(f32)
     normed_two, inv_two = rms_stats(resid)
-    hidden_two = (normed_two * gain_ffn).astype(bf16)
-    group_hidden = lax.all_gather(hidden_two, "blk", axis=0, tiled=True)
-
-    inner, gg, gu, y_part, gh_part = ffn_call(group_hidden, group_cot, gate, up, down)
-    grad_h2 = lax.psum_scatter(gh_part, "blk", scatter_dimension=0, tiled=True).astype(f32)
-    output = (
-        resid + lax.psum_scatter(y_part, "blk", scatter_dimension=0, tiled=True).astype(f32)
-    ).astype(bf16)
+
+    pairs = count_uly == 4 and width % HD == 0
+    if pairs:
+        ffn = ffn_pieces(group_hidden, group_cot, gate_up, down, width)
+    else:
+        ffn = ffn_plain(group_hidden, group_cot, gate_up, down)
+    inner, gg, gu, y_part, gh_part = ffn
+    grad_h2 = lax.psum_scatter(gh_part, "blk", scatter_dimension=0, tiled=True)
+
+    def products(lefts, rights, rows):
+        half = dim // 2
+        if rows:
+            halves = (rights[:, :half], rights[:, half:])
+            term = [t_dot(lefts[n], halves[n // 2]) for n in range(4)]
+        else:
+            halves = (lefts[:, :half], lefts[:, half:])
+            term = [t_dot(halves[n // 2], rights[n]) for n in range(4)]
+        return [term[1].astype(bf16), term[2].astype(bf16), term[0], term[3]]
+
+    def first_phase(term):
+        return [
+            xor_permute(term[0], count_uly, 1),
+            xor_permute(term[1], count_uly, 2),
+            term[2],
+            term[3],
+        ]
+
+    def second_phase(term, rows):
+        axis = 0 if rows else 1
+        one, two = (k + g.astype(f32) for k, g in zip(term[2:], term[:2]))
+        mine = [lax.slice_in_dim(t, 0, width, axis=axis) for t in (one, two)]
+        rest = [lax.slice_in_dim(t, width, 2 * width, axis=axis).astype(bf16) for t in (one, two)]
+        mine[0] = mine[0] + xor_permute(rest[0], count_uly, 2).astype(f32)
+        mine[1] = mine[1] + xor_permute(rest[1], count_uly, 1).astype(f32)
+        return jnp.concatenate(mine, axis=1 - axis).astype(bf16)
+
+    def direct(lefts, rights, rows):
+        cut = lambda a: [a[0][:, j * width : (j + 1) * width] for j in range(count_uly)]
+        if rows:
+            terms = [t_dot(left, rights) for left in cut(lefts)]
+        else:
+            terms = [t_dot(lefts, right) for right in cut(rights)]
+        return scatter_uly(terms[0], [t.astype(bf16) for t in terms[1:]], count_uly).astype(bf16)
+
+    if pairs:
+        sum_gate = second_phase(first_phase(products(group_hidden, gg, False)), False)
+        sum_up = products(group_hidden, gu, False)
+        sum_down = products(inner, group_cot, True)
+    else:
+        sum_gate = direct(group_hidden, gg, False)
+        sum_up = direct(group_hidden, gu, False)
+        sum_down = direct(inner, group_cot, True)
+    grad_h2, sum_gate, sum_up, sum_down, y_part = together((grad_h2, sum_gate, sum_up, sum_down, y_part))
+    if pairs:
+        sum_up = second_phase(first_phase(sum_up), False)
+        sum_down = second_phase(first_phase(sum_down), True)
+    grad_h2 = grad_h2.astype(f32)
     grad_resid = cotangent.astype(f32) + norm_back(grad_h2, normed_two, inv_two, gain_ffn)
-    gain_part = jnp.sum(grad_h2 * normed_two, axis=0).reshape(devices, rows_w)
-    grad_gain_ffn = jnp.sum(
-        lax.all_to_all(gain_part, BOTH, 0, 0, tiled=True).reshape(devices, rows_w), axis=0
+    group_gattn = lax.all_gather(grad_resid.astype(bf16), "blk", axis=0, tiled=True)
+    blocks_of = lambda w: w.reshape(count_blk, rows_d, width)
+    gain_part = jnp.sum(grad_h2 * normed_two, axis=0).astype(bf16).reshape(count_blk, -1, width)
+    gain_rows = gain_part.shape[1]
+    gain_part = jnp.pad(gain_part, ((0, 0), (0, -gain_rows % 8), (0, 0)))
+    grad_gate = to_hidden(jnp.concatenate([blocks_of(sum_gate), gain_part], axis=1))
+    gattn, sum_up, sum_down, grad_gate = together((group_gattn, sum_up, sum_down, grad_gate))
+
+    down_blocks = sum_down.reshape(width, count_blk, rows_d).transpose(1, 0, 2)
+    grads_ud = to_hidden(
+        jnp.concatenate(
+            [blocks_of(sum_up), down_blocks.reshape(count_blk, rows_d, width)], axis=1
+        )
     )
-    group_gattn = lax.all_gather(grad_resid.astype(bf16), "blk", axis=0, tiled=True)
-
-    def summed(term, lefts, rights):
-        parts = [term(left, right) for left, right in zip(lefts, rights)]
-        return scatter_uly(parts[0], [p.astype(bf16) for p in parts[1:]], count_uly).astype(bf16)
-
-    hiddens, cots = [group_hidden] * count_uly, [group_cot] * count_uly
-    grad_gate = lax.all_to_all(summed(t_dot, hiddens, gg), "blk", 0, 1, tiled=True).astype(f32)
-    grad_up = lax.all_to_all(summed(t_dot, hiddens, gu), "blk", 0, 1, tiled=True).astype(f32)
-    grad_down = lax.all_to_all(summed(t_dot, inner, cots), "blk", 1, 0, tiled=True).astype(f32)
-
+    gq, gkv, *sent = attn_bwd_call(
+        low_kb, query, gattn, begin[None, :], wo, cos, sin, kvs
+    )
+    got = [
+        lax.ppermute(block, "uly", [(i, i - s) for i in range(s, count_uly)])
+        for s, block in zip(range(back, 0, -1), sent)
+    ]
+    y_own = lax.psum_scatter(after(y_part, gattn), "blk", scatter_dimension=0, tiled=True)
     def split_rows(whole):
         rows = whole.shape[0] // count_uly
         pick = lambda j: lax.dynamic_slice_in_dim(whole, (uly_index ^ j) * rows, rows, 0)
         return scatter_uly(
-            pick(0), [pick(j).astype(bf16) for j in range(1, count_uly)], count_uly
+            pick(0).astype(f32), [pick(j) for j in range(1, count_uly)], count_uly
         ).astype(bf16)
 
-    grad_out = lax.ppermute(
-        split_rows(t_dot(attended, group_gattn)), BOTH, [(j, i) for i, j in owner]
-    ).astype(f32)
-
-    gq, gkv, *sent = attn_bwd_call(
-        low_kb, query, group_gattn, begin[None, :], wo, cos, sin, kvs
+    gain_sum = jnp.sum(grad_gate[:, rows_d:][:, :gain_rows].astype(f32), axis=0)
+    gain_sum = jnp.pad(gain_sum.reshape(part, 1), ((0, 0), (0, HD - 1)))
+    outs = jnp.concatenate([t_dot(attended, gattn), gain_sum], axis=1).astype(bf16)
+    outs = split_rows(after(outs, gq))
+    gkv, y_own, grads_ud, outs = together((gkv, y_own, grads_ud, outs))
+    output = (resid + y_own.astype(f32)).astype(bf16)
+    gh1_part, grads = gqkv_call(
+        uly_at, hidden_one, gq, gkv, got, cos, sin, w_qkv, count_uly
     )
-    for s, block in zip(range(back, 0, -1), sent):
-        gkv = gkv + lax.ppermute(
-            block, "uly", [(i, i - s) for i in range(s, count_uly)]
-        ).astype(f32)
-    gk = gkv[:, :part].reshape(group, part // HD, HD)
-    gk = gk * cos[:, None, :] - jnp.roll(gk, HD // 2, axis=2) * sin[:, None, :]
-    gqkv = jnp.concatenate(
-        [gq, gk.reshape(group, part).astype(bf16), gkv[:, part:].astype(bf16)], axis=1
-    )
-    gh1_part = dot_t(gqkv, w_qkv).astype(bf16)
     grad_h1 = lax.psum_scatter(gh1_part, "blk", scatter_dimension=0, tiled=True).astype(f32)
     normed_one, inv_one = rms_stats(input_f)
     input_grad = grad_resid + norm_back(grad_h1, normed_one, inv_one, gain_attn)
-    grads = split_rows(t_dot(hidden_one, gqkv))
-    grads = lax.all_to_all(grads, "blk", 0, 0, tiled=True).astype(f32)
-    grads = grads.reshape(count_blk, rows_w, 3, part).transpose(2, 1, 0, 3).reshape(3, rows_w, dim)
-    grad_gain_attn = (
-        jnp.sum(
-            grads[0] * w_query.astype(f32)
-            + grads[1] * w_key.astype(f32)
-            + grads[2] * w_value.astype(f32),
-            axis=1,
-        )
-        / norm_attn.astype(f32)
+
+    grads = scatter_uly(grads[0], grads[1:], count_uly).astype(bf16)
+    owner = [((i % count_uly) * count_blk + i // count_uly, i) for i in range(devices)]
+    outs = lax.ppermute(after(outs, gh1_part), BOTH, owner)
+    grads, outs = together((grads, outs))
+    outs = outs.astype(f32)
+    grad_out, grad_gain_ffn = outs[:, :dim], outs[:, dim]
+    grads = lax.all_to_all(grads.reshape(count_blk, rows_w, 3 * part), "blk", 0, 0, tiled=True)
+    grad_gate = grad_gate[:, :rows_d].astype(f32).transpose(1, 0, 2).reshape(w_gate.shape)
+    grad_up = grads_ud[:, :rows_d].astype(f32).transpose(1, 0, 2).reshape(w_up.shape)
+    grad_down = grads_ud[:, rows_d:].astype(f32).reshape(w_down.shape)
+    grads, *_ = together((grads, grad_gate, grad_up, grad_down, input_grad, grad_out, grad_gain_ffn))
+    grad_query, grad_key, grad_value, grad_gain_attn = unpack_call(
+        grads, w_query, w_key, w_value, norm_attn.astype(f32)[:, None]
     )
     return (
         output,
         input_grad,
-        grad_gain_attn,
-        grads[0],
-        grads[1],
-        grads[2],
+        grad_gain_attn[:, 0],
+        grad_query,
+        grad_key,
+        grad_value,
         grad_out,
         grad_gain_ffn,
         grad_gate,

time: 953 us -> 699 us (0.73)
  waiting for transfers between devices: 573 us -> 321 us
  Pallas kernels: 68.8 us -> 107 us
  matrix products: 54.3 us -> 35.1 us
  local copies, waits for them, and re-layouts: 48.2 us -> 32.1 us
  starting transfers between devices: 102 us -> 91.4 us
    all_to_all x9 -> x5, waiting for transfers between devices: 141 us -> 21.6 us  [the longest x1 11.1 us: body(): lax.all_to_all(grads.reshape(count_blk, rows_w, 3 * part), 'blk', 0, 0, t...]
    reduce_scatter x3 -> x2, waiting for transfers between devices: 110 us -> 5.99 us  [the longest x1 5.99 us: body(): lax.psum_scatter(after(y_part, gattn), 'blk', scatter_dimension=0, tiled=...]
    ppermute x35 -> x34, waiting for transfers between devices: 237 us -> 290 us  [xor_permute(): return lax.ppermute(x, 'uly', [(i, i ^ flip) for i in range(count)])]
    all_gather x1, waiting for transfers between devices: 45.4 us -> 0.25 us  [body(): lax.all_gather(grad_resid.astype(bf16), 'blk', axis=0, tiled=True)]
    pallas_call x1 -> x6, Pallas kernels: 35.3 us -> 76 us  [the longest x1 30.8 us: ffn_call(): pl.pallas_call(functools.partial(ffn_kernel, places, blocks, groups), gri...]
    ppermute x2, waiting for transfers between devices: 38.3 us -> 0.01 us  [body(): lax.ppermute(block, 'uly', [(i, i - s) for i in range(s, count_uly)])]
    all_to_all x9 -> x5, starting transfers between devices: 37.6 us -> 19.3 us  [the longest x4 15 us: body(): to_hidden = lambda w: lax.all_to_all(w, 'blk', 0, 0, tiled=True)]
    dot_general x14 -> x13, matrix products: 47.3 us -> 35.1 us  [t_dot(): lax.dot_general(left, right, (((0,), (0,)), ((), ())), preferred_element_...]
  transfers between devices with their start and end apart: 58 -> 56, of which waited for: 26 -> 30; matrix products, arithmetic and copies ran while one was open for 10% -> 14% of each run, Pallas kernels for 1% -> 6%
where the time goes in v2:
time: 699 us; the launch traced here: 691 us
  waiting for transfers between devices  321 us (46%)
  Pallas kernels  107 us (15%)
  starting transfers between devices  91.4 us (13%)
  blocking collectives  48.5 us (7%)
  other arithmetic  40.6 us (6%)
  matrix products  35.1 us (5%)
  local copies, waits for them, and re-layouts  32.1 us (5%)
  between operations  15.4 us (2%)
    ppermute x34, waiting for transfers between devices, xor_permute(): return lax.ppermute(x, 'uly', [(i, i ^ flip) for i in range(count)])  290 us
    ppermute x34, starting transfers between devices, xor_permute(): return lax.ppermute(x, 'uly', [(i, i ^ flip) for i in range(count)])  57.9 us
    all_to_all x1, blocking collectives, body(): qkv = lax.all_to_all(qkv, 'blk', 0, 0, tiled=True)  48.5 us
    dot_general x13, matrix products, t_dot(): lax.dot_general(left, right, (((0,), (0,)), ((), ())), preferred_element_...  35.1 us
    pallas_call x1, Pallas kernels, ffn_call(): pl.pallas_call(functools.partial(ffn_kernel, places, blocks, groups), gri...  30.8 us
    pallas_call x1, Pallas kernels, project_call(): pl.pallas_call(functools.partial(project_kernel, count, places), grid=(ro...  17.6 us
    all_to_all x4, starting transfers between devices, body(): to_hidden = lambda w: lax.all_to_all(w, 'blk', 0, 0, tiled=True)  15 us
    pallas_call x1, Pallas kernels, attn_bwd_call(): pl.pallas_call(functools.partial(attn_bwd_kernel, len(kvs)), in_specs=[pl...  14.9 us
  transfers between devices with their start and end apart: 56, of which 30 were waited for; matrix products, arithmetic and copies ran while one was open for 14% of the time, Pallas kernels for 6%

profile of v2, /device:TPU:0, one launch (start us, length us, event | category | flops | bytes accessed | tf_op | source)
XLA Modules:
  0.0 691.3 jit_solution(14688180100923278498)
XLA Ops:
  11.5 48.5 %all_to_all.30 = bf16[8,80,768]{2,1,0:T(8,128)(2,1)} all-to-all(bf16[8,80,768]{2,1,0:T(8,128)(2,1)} %shard_map.212), channel_id=1, replica_groups=mesh['uly'=4,'blk'=8] {'blk'}, dimensions={0} | all-to-all | bytes 1966080 | tf_op jit(solution)/shard_map/all_to_all | solution.py:637
  69.9 17.5 %collective-permute-done = bf16[8,80,768]{2,1,0:T(8,128)(2,1)S(1)} collective-permute-done((bf16[8,80,768]{2,1,0:T(8,128)(2,1)}, bf16[8,80,768]{2,1,0:T(8,128)(2,1)S(1)}, u32[]{:S(2)}, u32[]{:S(2)}) %collective-permute-start) | collective-permute-done | bytes 983072 | tf_op jit(solution)/shard_map/ppermute | solution.py:528
  92.0 3.6 all-to-all-start.1
  97.1 5.1 collective-permute-done.1
  109.1 28.5 %collective-permute-done.7 = bf16[4,80,768]{2,1,0:T(8,128)(2,1)S(1)} collective-permute-done((bf16[4,80,768]{2,1,0:T(8,128)(2,1)S(1)}, bf16[4,80,768]{2,1,0:T(8,128)(2,1)S(1)}, u32[]{:S(2)}, u32[]{:S(2)}) %collective-permute-start.7) | collective-permute-done | bytes 491552 | tf_op jit(solution)/shard_map/ppermute | solution.py:528
  144.6 4.4 collective-permute-done.4.refs_5_
  150.3 8.5 %shard_map.213 = (bf16[1024,2048]{1,0:T(8,128)(2,1)}, bf16[1024,256]{1,0:T(8,128)(2,1)}, bf16[1024,512]{1,0:T(8,128)(2,1)}) custom-call(bf16[1024,2048]{1,0:T(8,128)(2,1)} %all-gather.8.cloned.1.call-done.x_ref, f32[1,2048]{1,0:T(1,128)} %reshape.239.gain_ref, bf16[2048,768]{1,0:T(8,128)(2,1)} %constant_dynamic-update-slice_fusion.w_ref, ...), custom_call_target="tpu_custom_call" | custom-call | flops 3221225472 | bytes 16777216 | tf_op jit(solution)/shard_map/pallas_call | solution.py:106
  158.8 3.6 all-to-all-start.2
  163.7 4.4 collective-permute-start.14
  168.1 4.3 collective-permute-start.15
  172.4 16.1 %collective-permute-done.8.refs_6_.refs_1_ = bf16[8,256,256]{2,1,0:T(8,128)(2,1)S(1)} collective-permute-done((bf16[8,256,256]{2,1,0:T(8,128)(2,1)S(1)}, bf16[8,256,256]{2,1,0:T(8,128)(2,1)S(1)}, u32[]{:S(2)}, u32[]{:S(2)}) %collective-permute-start.8) | collective-permute-done | bytes 1048608 | tf_op jit(solution)/shard_map/ppermute | solution.py:528
  192.3 50.3 %collective-permute-done.10.refs_8_.refs_3_ = bf16[4,256,256]{2,1,0:T(8,128)(2,1)} collective-permute-done((bf16[4,256,256]{2,1,0:T(8,128)(2,1)}, bf16[4,256,256]{2,1,0:T(8,128)(2,1)}, u32[]{:S(2)}, u32[]{:S(2)}) %collective-permute-start.10) | collective-permute-done | bytes 524320 | tf_op jit(solution)/shard_map/ppermute | solution.py:528
  245.2 7.5 %shard_map.214 = bf16[1024,256]{1,0:T(8,128)(2,1)} custom-call(s32[2]{0:T(128)} %add_minimum_fusion.lo_ref, bf16[1024,256]{1,0:T(8,128)(2,1)} %get-tuple-element.106.q_ref, s32[1024,1]{1,0:T(8,128)} %copy.43.start_ref, bf16[1024,512]{1,0:T(8,128)(2,1)} %collective-permute-done.14.refs_0_, bf16[1024,512]{1,0:T(8,128)(2,1)} %collective-permute-done.15.refs_1_, ...), custom_call_target="tpu_custom_call" | custom-call | flops 10000000000 | bytes 12582912 | tf_op jit(solution)/shard_map/pallas_call | solution.py:162
  253.0 4.9 collective-permute-start.12
  258.6 44.8 %collective-permute-done.12.refs_1_ = bf16[8,512,256]{2,1,0:T(8,128)(2,1)S(1)} collective-permute-done((bf16[8,512,256]{2,1,0:T(8,128)(2,1)S(1)}, bf16[8,512,256]{2,1,0:T(8,128)(2,1)S(1)}, u32[]{:S(2)}, u32[]{:S(2)}) %collective-permute-start.12) | collective-permute-done | bytes 2097184 | tf_op jit(solution)/shard_map/ppermute | solution.py:528
  310.9 17.6 %shard_map.215 = (bf16[1024,2048]{1,0:T(8,128)(2,1)}, f32[128,2048]{1,0:T(8,128)}, bf16[256,2048]{1,0:T(8,128)(2,1)}) custom-call(s32[2]{0:T(128)} %pad_add_fusion.at_ref, bf16[8,1024,256]{2,1,0:T(8,128)(2,1)} %bitcast.82, bf16[1024,2048]{1,0:T(8,128)(2,1)} %all-gather.8.cloned.1.call-done.x_ref, f32[1,2048]{1,0:T(1,128)} %reshape.240.gain_ref, ...), custom_call_target="tpu_custom_call" | custom-call | flops 8589934592 | bytes 25165824 | tf_op jit(solution)/shard_map/pallas_call | solution.py:218
  328.6 3.1 collective-permute-done.20.refs_3_
  331.7 2.8 collective-permute-done.21.refs_4_
  334.6 30.8 %shard_map.216 = (bf16[1024,512]{1,0:T(8,128)(2,1)}, bf16[1024,512]{1,0:T(8,128)(2,1)}, bf16[1024,512]{1,0:T(8,128)(2,1)}, bf16[1024,512]{1,0:T(8,128)(2,1)}, bf...) custom-call(bf16[1024,2048]{1,0:T(8,128)(2,1)} %get-tuple-element.11, ...), custom_call_target="tpu_custom_call" | custom-call | flops 21474836480 | bytes 37748736 | tf_op jit(solution)/shard_map/pallas_call | solution.py:426
  366.7 4.3 convolution_convert_fusion.3
  377.6 2.7 fusion.21
  380.3 2.6 fusion.16
  391.0 10.0 %shard_map.217 = bf16[1024,2048]{1,0:T(8,128)(2,1)} custom-call(bf16[1024,1024]{1,0:T(8,128)(2,1)} %get-tuple-element.136.inner_ref, bf16[8,256,256]{2,1,0:T(8,128)(2,1)} %copy-done.21, bf16[8,256,256]{2,1,0:T(8,128)(2,1)} %copy-done.28, bf16[8,256,256]{2,1,0:T(8,128)(2,1)} %copy-done.29, bf16[4,256,256]{2,1,0:T(8,128)(2,1)} %collective-permute-done.10.refs_8_.refs_3_, ...), custom_call_target="tpu_custom_call" | custom-call | flops 4294967296 | bytes 12582912 | tf_op jit(solution)/shard_map/pallas_call | solution.py:473
  401.0 3.6 convert_add_fusion.4
  405.5 2.7 convert_add_fusion.5
  409.7 2.6 fusion.2
  412.3 5.2 collective-permute-done.25
  417.7 3.3 collective-permute-done.23
  432.4 4.2 all-to-all-start.3
  436.7 15.8 %collective-permute-done.28 = bf16[1024,512]{1,0:T(8,128)(2,1)} collective-permute-done((bf16[1024,512]{1,0:T(8,128)(2,1)}, bf16[1024,512]{1,0:T(8,128)(2,1)}, u32[]{:S(2)}, u32[]{:S(2)}) %collective-permute-start.28) | collective-permute-done | bytes 1048608 | tf_op jit(solution)/shard_map/ppermute | solution.py:528
  458.6 16.4 %collective-permute-done.32 = bf16[512,1024]{1,0:T(8,128)(2,1)} collective-permute-done((bf16[512,1024]{1,0:T(8,128)(2,1)}, bf16[512,1024]{1,0:T(8,128)(2,1)}, u32[]{:S(2)}, u32[]{:S(2)}) %collective-permute-start.32) | collective-permute-done | bytes 1048608 | tf_op jit(solution)/shard_map/ppermute | solution.py:528
  480.5 6.7 collective-permute-done.29
  487.7 7.1 %collective-permute-done.33 = bf16[256,1024]{1,0:T(8,128)(2,1)S(1)} collective-permute-done((bf16[256,1024]{1,0:T(8,128)(2,1)S(1)}, bf16[256,1024]{1,0:T(8,128)(2,1)S(1)}, u32[]{:S(2)}, u32[]{:S(2)}) %collective-permute-start.33) | collective-permute-done | bytes 524320 | tf_op jit(solution)/shard_map/ppermute | solution.py:528
  497.1 3.6 all-to-all-start.4
  501.7 3.9 convolution_convert_fusion
  506.7 14.9 %shard_map.218 = (bf16[1024,256]{1,0:T(8,128)(2,1)}, f32[1024,512]{1,0:T(8,128)}, bf16[1024,512]{1,0:T(8,128)(2,1)}, bf16[1024,512]{1,0:T(8,128)(2,1)}) custom-call(s32[2]{0:T(128)} %add_minimum_fusion.lo_ref, bf16[1024,256]{1,0:T(8,128)(2,1)} %get-tuple-element.106.q_ref, bf16[1024,2048]{1,0:T(8,128)(2,1)} %all-gather.14.cloned.1.call-done.ga_ref, ...), custom_call_target="tpu_custom_call" | custom-call | flops 24999999488 | bytes 20971520 | tf_op jit(solution)/shard_map/pallas_call | solution.py:306
  526.2 13.7 %collective-permute-start.36 = (bf16[64,2176]{1,0:T(8,128)(2,1)}, bf16[64,2176]{1,0:T(8,128)(2,1)S(1)}, u32[]{:S(2)}, u32[]{:S(2)}) collective-permute-start(bf16[64,2176]{1,0:T(8,128)(2,1)} %get-tuple-element.182), channel_id=1, source_target_pairs={{0,24},{8,16},{16,8},{24,0},{1,25},{9,17},{17,9},{25,1},{2,26},{10... | collective-permute-start | bytes 835592 | tf_op jit(solution)/shard_map/ppermute | solution.py:528
  540.5 26.6 %collective-permute-done.36 = bf16[64,2176]{1,0:T(8,128)(2,1)S(1)} collective-permute-done((bf16[64,2176]{1,0:T(8,128)(2,1)}, bf16[64,2176]{1,0:T(8,128)(2,1)S(1)}, u32[]{:S(2)}, u32[]{:S(2)}) %collective-permute-start.36) | collective-permute-done | bytes 278560 | tf_op jit(solution)/shard_map/ppermute | solution.py:528
  572.4 8.0 %all-to-all-done.4 = bf16[8,512,256]{2,1,0:T(8,128)(2,1)S(1)} async-done(((bf16[8,512,256]{2,1,0:T(8,128)(2,1)}), bf16[8,512,256]{2,1,0:T(8,128)(2,1)S(1)}, u32[]{:S(2)}, u32[]{:S(2)}) %all-to-all-start.4) | async-done | bytes 2097184 | tf_op jit(solution)/shard_map/all_to_all | solution.py:648
  580.3 6.0 reduce-scatter.6.cloned.1.call-done
  586.3 12.9 %shard_map.219 = (bf16[1024,2048]{1,0:T(8,128)(2,1)}, f32[512,768]{1,0:T(8,128)}, bf16[512,768]{1,0:T(8,128)(2,1)}, bf16[512,768]{1,0:T(8,128)(2,1)}, bf16[512,768]{1,0:T(8,128)(2,1)}) custom-call(s32[1]{0:T(128)} %bitcast.index_ref, bf16[1024,2048]{1,0:T(8,128)(2,1)} %get-tuple-element.158.h_ref, bf16[1024,256]{1,0:T(8,128)(2,1)} %get-tuple-element.155.gq_ref, ...), custom_call_target="tpu_custom_call" | custom-call | flops 6442450944 | bytes 20971520 | tf_op jit(solution)/shard_map/pallas_call | solution.py:354
  600.8 8.7 %collective-permute-start.41 = (bf16[512,768]{1,0:T(8,128)(2,1)}, bf16[512,768]{1,0:T(8,128)(2,1)S(1)}, u32[]{:S(2)}, u32[]{:S(2)}) collective-permute-start(bf16[512,768]{1,0:T(8,128)(2,1)} %get-tuple-element.166), channel_id=1, source_target_pairs={{0,24},{8,16},{16,8},{24,0},{1,25},{9,17},{17,9},{25,1},{2,26},{10... | collective-permute-start | bytes 2359304 | tf_op jit(solution)/shard_map/ppermute | solution.py:528
  618.3 13.2 %collective-permute-done.41 = bf16[512,768]{1,0:T(8,128)(2,1)S(1)} collective-permute-done((bf16[512,768]{1,0:T(8,128)(2,1)}, bf16[512,768]{1,0:T(8,128)(2,1)S(1)}, u32[]{:S(2)}, u32[]{:S(2)}) %collective-permute-start.41) | collective-permute-done | bytes 786464 | tf_op jit(solution)/shard_map/ppermute | solution.py:528
  631.6 18.4 %collective-permute-done.40 = bf16[512,768]{1,0:T(8,128)(2,1)} collective-permute-done((bf16[512,768]{1,0:T(8,128)(2,1)}, bf16[512,768]{1,0:T(8,128)(2,1)}, u32[]{:S(2)}, u32[]{:S(2)}) %collective-permute-start.40) | collective-permute-done | bytes 786464 | tf_op jit(solution)/shard_map/ppermute | solution.py:528
  650.2 2.7 add_convert_fusion
  652.9 4.3 all-to-all-start.5
  665.3 2.9 fusion.35
  668.2 11.1 %all-to-all-done.5.got_ref = bf16[8,64,768]{2,1,0:T(8,128)(2,1)S(1)} async-done(((bf16[8,64,768]{2,1,0:T(8,128)(2,1)}), bf16[8,64,768]{2,1,0:T(8,128)(2,1)S(1)}, u32[]{:S(2)}, u32[]{:S(2)}) %all-to-all-start.5) | async-done | bytes 786464 | tf_op jit(solution)/shard_map/all_to_all | solution.py:803
  (295 shorter events, 131.7 us)
Async XLA Ops:
  7.2 53.4 %all-gather.6.cloned.1.call-start = ((), (), s32[]{:S(2)}) async-start(), calls=%async_computation.9 | async-start | bytes 2359296 | tf_op jit(solution)/shard_map/all_gather | solution.py:633
  7.9 142.4 %all-gather.8.cloned.1.call-start = ((), (), s32[]{:S(2)}) async-start(), calls=%async_computation.10 | async-start | bytes 4718592 | tf_op jit(solution)/shard_map/all_gather | solution.py:638
  63.3 24.2 %collective-permute-start = (bf16[8,80,768]{2,1,0:T(8,128)(2,1)}, bf16[8,80,768]{2,1,0:T(8,128)(2,1)S(1)}, u32[]{:S(2)}, u32[]{:S(2)}) collective-permute-start(bf16[8,80,768]{2,1,0:T(8,128)(2,1)} %all_to_all.30), channel_id=1, source_target_pairs={{0,16},{8,24},{16,0},{24,8},{1,17},{9,25},{17,1},{25,9},{2,18},{10... | collective-permute-start | bytes 2949128 | tf_op jit(solution)/shard_map/ppermute | solution.py:528
  66.5 38.9 %collective-permute-start.6 = (bf16[8,80,768]{2,1,0:T(8,128)(2,1)S(1)}, bf16[8,80,768]{2,1,0:T(8,128)(2,1)S(1)}, u32[]{:S(2)}, u32[]{:S(2)}) collective-permute-start(bf16[8,80,768]{2,1,0:T(8,128)(2,1)S(1)} %copy-done.9), channel_id=1, source_target_pairs={{0,8},{8,0},{16,24},{24,16},{1,9},{9,1},{17,25},{25,17},{2,10},{10... | collective-permute-start | bytes 2949128 | tf_op jit(solution)/shard_map/ppermute | solution.py:528
  92.0 52.6 %all-to-all-start.1 = ((bf16[8,256,256]{2,1,0:T(8,128)(2,1)}), bf16[8,256,256]{2,1,0:T(8,128)(2,1)S(1)}, u32[]{:S(2)}, u32[]{:S(2)}) async-start(bf16[8,256,256]{2,1,0:T(8,128)(2,1)} %bitcast.3), calls=%async_computation.1 | async-start | bytes 2097152 | tf_op jit(solution)/shard_map/all_to_all | solution.py:648
  95.6 149.6 %all-gather.10.cloned.1.call-start = ((), (), s32[]{:S(2)}) async-start(), calls=%async_computation.11 | async-start | bytes 4718592 | tf_op jit(solution)/shard_map/all_gather | solution.py:677
  102.2 35.4 %collective-permute-start.2 = (bf16[256,2048]{1,0:T(8,128)(2,1)S(1)}, bf16[256,2048]{1,0:T(8,128)(2,1)S(1)}, u32[]{:S(2)}, u32[]{:S(2)}) collective-permute-start(bf16[256,2048]{1,0:T(8,128)(2,1)S(1)} %constant_dynamic-slice_fusion.3), channel_id=1, source_target_pairs={{0,8},{8,0},{16,24},{24,16},{1,9},{9,1},{17,25},{25,17},{2,10},{10... | collective-permute-start | bytes 3145736 | tf_op jit(solution)/shard_map/ppermute | solution.py:528
  103.6 35.5 %collective-permute-start.3 = (bf16[256,2048]{1,0:T(8,128)(2,1)S(1)}, bf16[256,2048]{1,0:T(8,128)(2,1)S(1)}, u32[]{:S(2)}, u32[]{:S(2)}) collective-permute-start(bf16[256,2048]{1,0:T(8,128)(2,1)S(1)} %constant_dynamic-slice_fusion.3), channel_id=1, source_target_pairs={{0,16},{8,24},{16,0},{24,8},{1,17},{9,25},{17,1},{25,9},{2,18},{10... | collective-permute-start | bytes 3145736 | tf_op jit(solution)/shard_map/ppermute | solution.py:528
  105.5 32.1 %collective-permute-start.7 = (bf16[4,80,768]{2,1,0:T(8,128)(2,1)S(1)}, bf16[4,80,768]{2,1,0:T(8,128)(2,1)S(1)}, u32[]{:S(2)}, u32[]{:S(2)}) collective-permute-start(bf16[4,80,768]{2,1,0:T(8,128)(2,1)S(1)} %slice.188), channel_id=1, source_target_pairs={{0,16},{8,24},{16,0},{24,8},{1,17},{9,25},{17,1},{25,9},{2,18},{10... | collective-permute-start | bytes 1474568 | tf_op jit(solution)/shard_map/ppermute | solution.py:528
  158.8 86.3 %all-to-all-start.2 = ((bf16[8,512,256]{2,1,0:T(8,128)(2,1)}), bf16[8,512,256]{2,1,0:T(8,128)(2,1)S(1)}, u32[]{:S(2)}, u32[]{:S(2)}) async-start(bf16[8,512,256]{2,1,0:T(8,128)(2,1)} %pad_maximum_fusion), calls=%async_computation.2 | async-start | bytes 4194304 | tf_op jit(solution)/shard_map/all_to_all | solution.py:648
  162.5 142.5 %all-gather.12.cloned.1.call-start = ((), (), s32[]{:S(2)}) async-start(), calls=%async_computation.12 | async-start | bytes 4718592 | tf_op jit(solution)/shard_map/all_gather | solution.py:682
  162.5 26.0 %collective-permute-start.8 = (bf16[8,256,256]{2,1,0:T(8,128)(2,1)S(1)}, bf16[8,256,256]{2,1,0:T(8,128)(2,1)S(1)}, u32[]{:S(2)}, u32[]{:S(2)}) collective-permute-start(bf16[8,256,256]{2,1,0:T(8,128)(2,1)S(1)} %all-to-all-done.1.refs_5_.refs_0_), channel_id=1, source_target_pairs={{0,8},{8,0},{16,24},{24,16},{1,9},{9,1},{17,25},{25,17},{2,10},{10... | collective-permute-start | bytes 3145736 | tf_op jit(solution)/shard_map/ppermute | solution.py:528
  163.2 26.3 %collective-permute-start.9 = (bf16[8,256,256]{2,1,0:T(8,128)(2,1)S(1)}, bf16[8,256,256]{2,1,0:T(8,128)(2,1)S(1)}, u32[]{:S(2)}, u32[]{:S(2)}) collective-permute-start(bf16[8,256,256]{2,1,0:T(8,128)(2,1)S(1)} %all-to-all-done.1.refs_5_.refs_0_), channel_id=1, source_target_pairs={{0,16},{8,24},{16,0},{24,8},{1,17},{9,25},{17,1},{25,9},{2,18},{10... | collective-permute-start | bytes 3145736 | tf_op jit(solution)/shard_map/ppermute | solution.py:528
  163.7 81.5 %collective-permute-start.14 = (bf16[1024,512]{1,0:T(8,128)(2,1)}, bf16[1024,512]{1,0:T(8,128)(2,1)}, u32[]{:S(2)}, u32[]{:S(2)}) collective-permute-start(bf16[1024,512]{1,0:T(8,128)(2,1)} %get-tuple-element.100.refs_2_), channel_id=1, source_target_pairs={{0,16},{8,24},{1,17},{9,25},{2,18},{10,26},{3,19},{11,27},{4,20},{... | collective-permute-start | bytes 3145736 | tf_op jit(solution)/shard_map/ppermute | solution.py:672
  168.1 77.1 %collective-permute-start.15 = (bf16[1024,512]{1,0:T(8,128)(2,1)}, bf16[1024,512]{1,0:T(8,128)(2,1)}, u32[]{:S(2)}, u32[]{:S(2)}) collective-permute-start(bf16[1024,512]{1,0:T(8,128)(2,1)} %get-tuple-element.100.refs_2_), channel_id=1, source_target_pairs={{0,8},{8,16},{16,24},{1,9},{9,17},{17,25},{2,10},{10,18},{18,26},{... | collective-permute-start | bytes 3145736 | tf_op jit(solution)/shard_map/ppermute | solution.py:672
  189.4 53.1 %collective-permute-start.10 = (bf16[4,256,256]{2,1,0:T(8,128)(2,1)}, bf16[4,256,256]{2,1,0:T(8,128)(2,1)}, u32[]{:S(2)}, u32[]{:S(2)}) collective-permute-start(bf16[4,256,256]{2,1,0:T(8,128)(2,1)} %slice.197), channel_id=1, source_target_pairs={{0,16},{8,24},{16,0},{24,8},{1,17},{9,25},{17,1},{25,9},{2,18},{10... | collective-permute-start | bytes 1572872 | tf_op jit(solution)/shard_map/ppermute | solution.py:528
  189.5 53.1 %collective-permute-start.11 = (bf16[4,256,256]{2,1,0:T(8,128)(2,1)S(1)}, bf16[4,256,256]{2,1,0:T(8,128)(2,1)S(1)}, u32[]{:S(2)}, u32[]{:S(2)}) collective-permute-start(bf16[4,256,256]{2,1,0:T(8,128)(2,1)S(1)} %slice.198), channel_id=1, source_target_pairs={{0,8},{8,0},{16,24},{24,16},{1,9},{9,1},{17,25},{25,17},{2,10},{10... | collective-permute-start | bytes 1572872 | tf_op jit(solution)/shard_map/ppermute | solution.py:528
  252.7 169.5 %reduce-scatter.4.cloned.1.call-start = ((), (), s32[]{:S(2)}) async-start(), calls=%async_computation.13 | async-start | bytes 4718592 | tf_op jit(solution)/shard_map/reduce_scatter | solution.py:704
  253.0 50.4 %collective-permute-start.12 = (bf16[8,512,256]{2,1,0:T(8,128)(2,1)S(1)}, bf16[8,512,256]{2,1,0:T(8,128)(2,1)S(1)}, u32[]{:S(2)}, u32[]{:S(2)}) collective-permute-start(bf16[8,512,256]{2,1,0:T(8,128)(2,1)S(1)} %all-to-all-done.2.refs_0_), channel_id=1, source_target_pairs={{0,8},{8,0},{16,24},{24,16},{1,9},{9,1},{17,25},{25,17},{2,10},{10... | collective-permute-start | bytes 6291464 | tf_op jit(solution)/shard_map/ppermute | solution.py:528
  257.9 47.0 %collective-permute-start.13 = (bf16[8,512,256]{2,1,0:T(8,128)(2,1)S(1)}, bf16[8,512,256]{2,1,0:T(8,128)(2,1)}, u32[]{:S(2)}, u32[]{:S(2)}) collective-permute-start(bf16[8,512,256]{2,1,0:T(8,128)(2,1)S(1)} %all-to-all-done.2.refs_0_), channel_id=1, source_target_pairs={{0,16},{8,24},{16,0},{24,8},{1,17},{9,25},{17,1},{25,9},{2,18},{10... | collective-permute-start | bytes 6291464 | tf_op jit(solution)/shard_map/ppermute | solution.py:528
  258.0 53.0 %collective-permute-start.16 = (bf16[256,2048]{1,0:T(8,128)(2,1)S(1)}, bf16[256,2048]{1,0:T(8,128)(2,1)}, u32[]{:S(2)}, u32[]{:S(2)}) collective-permute-start(bf16[256,2048]{1,0:T(8,128)(2,1)S(1)} %copy-done.26), channel_id=1, source_target_pairs={{0,1},{1,0},{2,3},{3,2},{4,5},{5,4},{6,7},{7,6},{8,9},{9,8},{10,11... | collective-permute-start | bytes 3145736 | tf_op jit(solution)/shard_map/ppermute | solution.py:663
  258.0 52.9 %collective-permute-start.17 = (bf16[256,2048]{1,0:T(8,128)(2,1)}, bf16[256,2048]{1,0:T(8,128)(2,1)}, u32[]{:S(2)}, u32[]{:S(2)}) collective-permute-start(bf16[256,2048]{1,0:T(8,128)(2,1)} %copy-done.27), channel_id=1, source_target_pairs={{0,1},{1,0},{2,3},{3,2},{4,5},{5,4},{6,7},{7,6},{8,9},{9,8},{10,11... | collective-permute-start | bytes 3145736 | tf_op jit(solution)/shard_map/ppermute | solution.py:663
  258.5 50.6 %collective-permute-start.18 = (bf16[128,2048]{1,0:T(8,128)(2,1)}, bf16[128,2048]{1,0:T(8,128)(2,1)}, u32[]{:S(2)}, u32[]{:S(2)}) collective-permute-start(bf16[128,2048]{1,0:T(8,128)(2,1)} %copy-done.31), channel_id=1, source_target_pairs={{0,1},{1,0},{2,3},{3,2},{4,5},{5,4},{6,7},{7,6},{8,9},{9,8},{10,11... | collective-permute-start | bytes 1572872 | tf_op jit(solution)/shard_map/ppermute | solution.py:663
  306.2 25.5 %collective-permute-start.20 = (bf16[4,512,256]{2,1,0:T(8,128)(2,1)S(1)}, bf16[4,512,256]{2,1,0:T(8,128)(2,1)}, u32[]{:S(2)}, u32[]{:S(2)}) collective-permute-start(bf16[4,512,256]{2,1,0:T(8,128)(2,1)S(1)} %slice.158), channel_id=1, source_target_pairs={{0,16},{8,24},{16,0},{24,8},{1,17},{9,25},{17,1},{25,9},{2,18},{10... | collective-permute-start | bytes 3145736 | tf_op jit(solution)/shard_map/ppermute | solution.py:528
  309.1 25.5 %collective-permute-start.21 = (bf16[4,512,256]{2,1,0:T(8,128)(2,1)S(1)}, bf16[4,512,256]{2,1,0:T(8,128)(2,1)}, u32[]{:S(2)}, u32[]{:S(2)}) collective-permute-start(bf16[4,512,256]{2,1,0:T(8,128)(2,1)S(1)} %slice.159), channel_id=1, source_target_pairs={{0,8},{8,0},{16,24},{24,16},{1,9},{9,1},{17,25},{25,17},{2,10},{10... | collective-permute-start | bytes 3145736 | tf_op jit(solution)/shard_map/ppermute | solution.py:528
  365.3 130.2 %all-gather.14.cloned.1.call-start = ((), (), s32[]{:S(2)}) async-start(), calls=%async_computation.14 | async-start | bytes 4718592 | tf_op jit(solution)/shard_map/all_gather | solution.py:755
  371.0 30.0 %collective-permute-start.24 = (bf16[1024,512]{1,0:T(8,128)(2,1)}, bf16[1024,512]{1,0:T(8,128)(2,1)}, u32[]{:S(2)}, u32[]{:S(2)}) collective-permute-start(bf16[1024,512]{1,0:T(8,128)(2,1)} %convolution_convert_fusion.3), channel_id=1, source_target_pairs={{0,16},{8,24},{16,0},{24,8},{1,17},{9,25},{17,1},{25,9},{2,18},{10... | collective-permute-start | bytes 3145736 | tf_op jit(solution)/shard_map/ppermute | solution.py:528
  373.6 31.9 %collective-permute-start.22 = (bf16[1024,512]{1,0:T(8,128)(2,1)}, bf16[1024,512]{1,0:T(8,128)(2,1)}, u32[]{:S(2)}, u32[]{:S(2)}) collective-permute-start(bf16[1024,512]{1,0:T(8,128)(2,1)} %convolution_convert_fusion.4), channel_id=1, source_target_pairs={{0,8},{8,0},{16,24},{24,16},{1,9},{9,1},{17,25},{25,17},{2,10},{10... | collective-permute-start | bytes 3145736 | tf_op jit(solution)/shard_map/ppermute | solution.py:528
  426.0 26.5 %collective-permute-start.28 = (bf16[1024,512]{1,0:T(8,128)(2,1)}, bf16[1024,512]{1,0:T(8,128)(2,1)}, u32[]{:S(2)}, u32[]{:S(2)}) collective-permute-start(bf16[1024,512]{1,0:T(8,128)(2,1)} %convolution_convert_fusion.1), channel_id=1, source_target_pairs={{0,16},{8,24},{16,0},{24,8},{1,17},{9,25},{17,1},{25,9},{2,18},{10... | collective-permute-start | bytes 3145736 | tf_op jit(solution)/shard_map/ppermute | solution.py:528
  427.2 28.8 %collective-permute-start.26 = (bf16[1024,512]{1,0:T(8,128)(2,1)}, bf16[1024,512]{1,0:T(8,128)(2,1)}, u32[]{:S(2)}, u32[]{:S(2)}) collective-permute-start(bf16[1024,512]{1,0:T(8,128)(2,1)} %convolution_convert_fusion.2), channel_id=1, source_target_pairs={{0,8},{8,0},{16,24},{24,16},{1,9},{9,1},{17,25},{25,17},{2,10},{10... | collective-permute-start | bytes 3145736 | tf_op jit(solution)/shard_map/ppermute | solution.py:528
  428.1 46.9 %collective-permute-start.32 = (bf16[512,1024]{1,0:T(8,128)(2,1)}, bf16[512,1024]{1,0:T(8,128)(2,1)}, u32[]{:S(2)}, u32[]{:S(2)}) collective-permute-start(bf16[512,1024]{1,0:T(8,128)(2,1)} %fusion.13), channel_id=1, source_target_pairs={{0,16},{8,24},{16,0},{24,8},{1,17},{9,25},{17,1},{25,9},{2,18},{10... | collective-permute-start | bytes 3145736 | tf_op jit(solution)/shard_map/ppermute | solution.py:528
  429.3 48.7 %collective-permute-start.30 = (bf16[512,1024]{1,0:T(8,128)(2,1)}, bf16[512,1024]{1,0:T(8,128)(2,1)}, u32[]{:S(2)}, u32[]{:S(2)}) collective-permute-start(bf16[512,1024]{1,0:T(8,128)(2,1)} %fusion.10), channel_id=1, source_target_pairs={{0,8},{8,0},{16,24},{24,16},{1,9},{9,1},{17,25},{25,17},{2,10},{10... | collective-permute-start | bytes 3145736 | tf_op jit(solution)/shard_map/ppermute | solution.py:528
  432.4 62.8 %all-to-all-start.3 = ((bf16[8,264,256]{2,1,0:T(8,128)(2,1)}), bf16[8,264,256]{2,1,0:T(8,128)(2,1)}, u32[]{:S(2)}, u32[]{:S(2)}) async-start(bf16[8,264,256]{2,1,0:T(8,128)(2,1)} %fusion.31), calls=%async_computation.4 | async-start | bytes 2162688 | tf_op jit(solution)/shard_map/all_to_all | solution.py:648
  436.7 149.6 %reduce-scatter.6.cloned.1.call-start = ((), (), s32[]{:S(2)}) async-start(), calls=%async_computation.15 | async-start | bytes 4718592 | tf_op jit(solution)/shard_map/reduce_scatter | solution.py:776
  454.8 32.5 %collective-permute-start.29 = (bf16[1024,256]{1,0:T(8,128)(2,1)S(1)}, bf16[1024,256]{1,0:T(8,128)(2,1)S(1)}, u32[]{:S(2)}, u32[]{:S(2)}) collective-permute-start(bf16[1024,256]{1,0:T(8,128)(2,1)S(1)} %slice.274), channel_id=1, source_target_pairs={{0,8},{8,0},{16,24},{24,16},{1,9},{9,1},{17,25},{25,17},{2,10},{10... | collective-permute-start | bytes 1572872 | tf_op jit(solution)/shard_map/ppermute | solution.py:528
  457.7 29.8 %collective-permute-start.27 = (bf16[1024,256]{1,0:T(8,128)(2,1)S(1)}, bf16[1024,256]{1,0:T(8,128)(2,1)S(1)}, u32[]{:S(2)}, u32[]{:S(2)}) collective-permute-start(bf16[1024,256]{1,0:T(8,128)(2,1)S(1)} %slice.275), channel_id=1, source_target_pairs={{0,16},{8,24},{16,0},{24,8},{1,17},{9,25},{17,1},{25,9},{2,18},{10... | collective-permute-start | bytes 1572872 | tf_op jit(solution)/shard_map/ppermute | solution.py:528
  497.1 83.2 %all-to-all-start.4 = ((bf16[8,512,256]{2,1,0:T(8,128)(2,1)}), bf16[8,512,256]{2,1,0:T(8,128)(2,1)S(1)}, u32[]{:S(2)}, u32[]{:S(2)}) async-start(bf16[8,512,256]{2,1,0:T(8,128)(2,1)} %pad_maximum_fusion.1), calls=%async_computation.6 | async-start | bytes 4194304 | tf_op jit(solution)/shard_map/all_to_all | solution.py:648
  500.7 163.2 %reduce-scatter.8.cloned.1.call-start = ((), (), s32[]{:S(2)}) async-start(), calls=%async_computation.16 | async-start | bytes 4718592 | tf_op jit(solution)/shard_map/reduce_scatter | solution.py:793
  521.6 64.8 %collective-permute-start.37 = (bf16[1024,512]{1,0:T(8,128)(2,1)}, bf16[1024,512]{1,0:T(8,128)(2,1)}, u32[]{:S(2)}, u32[]{:S(2)}) collective-permute-start(bf16[1024,512]{1,0:T(8,128)(2,1)} %get-tuple-element.160), channel_id=1, source_target_pairs={{16,0},{24,8},{17,1},{25,9},{18,2},{26,10},{19,3},{27,11},{20,4},{... | collective-permute-start | bytes 3145736 | tf_op jit(solution)/shard_map/ppermute | solution.py:773
  522.9 63.5 %collective-permute-start.38 = (bf16[1024,512]{1,0:T(8,128)(2,1)}, bf16[1024,512]{1,0:T(8,128)(2,1)}, u32[]{:S(2)}, u32[]{:S(2)}) collective-permute-start(bf16[1024,512]{1,0:T(8,128)(2,1)} %get-tuple-element.161), channel_id=1, source_target_pairs={{8,0},{16,8},{24,16},{9,1},{17,9},{25,17},{10,2},{18,10},{26,18},{... | collective-permute-start | bytes 3145736 | tf_op jit(solution)/shard_map/ppermute | solution.py:773
  526.2 40.9 %collective-permute-start.36 = (bf16[64,2176]{1,0:T(8,128)(2,1)}, bf16[64,2176]{1,0:T(8,128)(2,1)S(1)}, u32[]{:S(2)}, u32[]{:S(2)}) collective-permute-start(bf16[64,2176]{1,0:T(8,128)(2,1)} %get-tuple-element.182), channel_id=1, source_target_pairs={{0,24},{8,16},{16,8},{24,0},{1,25},{9,17},{17,9},{25,1},{2,26},{10... | collective-permute-start | bytes 835592 | tf_op jit(solution)/shard_map/ppermute | solution.py:528
  539.9 28.5 %collective-permute-start.35 = (bf16[64,2176]{1,0:T(8,128)(2,1)}, bf16[64,2176]{1,0:T(8,128)(2,1)}, u32[]{:S(2)}, u32[]{:S(2)}) collective-permute-start(bf16[64,2176]{1,0:T(8,128)(2,1)} %get-tuple-element.183), channel_id=1, source_target_pairs={{0,16},{8,24},{16,0},{24,8},{1,17},{9,25},{17,1},{25,9},{2,18},{10... | collective-permute-start | bytes 835592 | tf_op jit(solution)/shard_map/ppermute | solution.py:528
  539.9 30.4 %collective-permute-start.34 = (bf16[64,2176]{1,0:T(8,128)(2,1)}, bf16[64,2176]{1,0:T(8,128)(2,1)}, u32[]{:S(2)}, u32[]{:S(2)}) collective-permute-start(bf16[64,2176]{1,0:T(8,128)(2,1)} %get-tuple-element.181), channel_id=1, source_target_pairs={{0,8},{8,0},{16,24},{24,16},{1,9},{9,1},{17,25},{25,17},{2,10},{10... | collective-permute-start | bytes 835592 | tf_op jit(solution)/shard_map/ppermute | solution.py:528
  600.8 30.8 %collective-permute-start.41 = (bf16[512,768]{1,0:T(8,128)(2,1)}, bf16[512,768]{1,0:T(8,128)(2,1)S(1)}, u32[]{:S(2)}, u32[]{:S(2)}) collective-permute-start(bf16[512,768]{1,0:T(8,128)(2,1)} %get-tuple-element.166), channel_id=1, source_target_pairs={{0,24},{8,16},{16,8},{24,0},{1,25},{9,17},{17,9},{25,1},{2,26},{10... | collective-permute-start | bytes 2359304 | tf_op jit(solution)/shard_map/ppermute | solution.py:528
  609.5 40.4 %collective-permute-start.40 = (bf16[512,768]{1,0:T(8,128)(2,1)}, bf16[512,768]{1,0:T(8,128)(2,1)}, u32[]{:S(2)}, u32[]{:S(2)}) collective-permute-start(bf16[512,768]{1,0:T(8,128)(2,1)} %get-tuple-element.165), channel_id=1, source_target_pairs={{0,16},{8,24},{16,0},{24,8},{1,17},{9,25},{17,1},{25,9},{2,18},{10... | collective-permute-start | bytes 2359304 | tf_op jit(solution)/shard_map/ppermute | solution.py:528
  612.0 38.2 %collective-permute-start.39 = (bf16[512,768]{1,0:T(8,128)(2,1)}, bf16[512,768]{1,0:T(8,128)(2,1)}, u32[]{:S(2)}, u32[]{:S(2)}) collective-permute-start(bf16[512,768]{1,0:T(8,128)(2,1)} %get-tuple-element.164), channel_id=1, source_target_pairs={{0,8},{8,0},{16,24},{24,16},{1,9},{9,1},{17,25},{25,17},{2,10},{10... | collective-permute-start | bytes 2359304 | tf_op jit(solution)/shard_map/ppermute | solution.py:528
  615.1 37.8 %collective-permute-start.42 = (bf16[64,2176]{1,0:T(8,128)(2,1)S(1)}, bf16[64,2176]{1,0:T(8,128)(2,1)}, u32[]{:S(2)}, u32[]{:S(2)}) collective-permute-start(bf16[64,2176]{1,0:T(8,128)(2,1)S(1)} %copy-done.24), channel_id=1, source_target_pairs={{0,0},{8,1},{16,2},{24,3},{1,4},{9,5},{17,6},{25,7},{2,8},{10,9},{... | collective-permute-start | bytes 835592 | tf_op jit(solution)/shard_map/ppermute | solution.py:799
  652.9 26.3 %all-to-all-start.5 = ((bf16[8,64,768]{2,1,0:T(8,128)(2,1)}), bf16[8,64,768]{2,1,0:T(8,128)(2,1)S(1)}, u32[]{:S(2)}, u32[]{:S(2)}) async-start(bf16[8,64,768]{2,1,0:T(8,128)(2,1)} %bitcast.19), calls=%async_computation.8 | async-start | bytes 1572864 | tf_op jit(solution)/shard_map/all_to_all | solution.py:803
  (55 other events, 515.7 us)
Sparse Core Ops, SparseCore 0:
  9.6 50.9 all-gather.5
  62.2 52.3 all-gather.7
  159.0 82.6 all-gather.9
  252.8 50.1 all-gather.11
  365.5 48.3 reduce-scatter.3
  426.1 69.3 all-gather.13
  497.8 88.4 reduce-scatter.5
  599.4 64.4 reduce-scatter.7

commit v3 on v2

--- a/solution.py
+++ b/solution.py
@@ -120,8 +120,8 @@
     )(x, gain, w, cos, sin)
 
 
-def attn_fwd_kernel(count_kv, lo_ref, q_ref, start_ref, *refs):
-    kv_refs, (att_ref, kv_all) = refs[:count_kv], refs[count_kv:]
+def attn_fwd_kernel(count_kv, lo_ref, q_ref, start_ref, wo_ref, *refs):
+    kv_refs, (att_ref, part_ref, kv_all) = refs[:count_kv], refs[count_kv:]
     rows, width = q_ref.shape
     heads = width // HD
     base = (count_kv - 1) * rows
@@ -153,94 +153,29 @@
         sums = lax.fori_loop(
             lo_ref[i], last, step, tuple(jnp.zeros((BQ, HD), f32) for _ in range(heads))
         )
-        att_ref[at, :] = jnp.concatenate([s.astype(bf16) for s in sums], axis=1)
-
-
-def attn_fwd_call(lo, q, start, kvs):
+        att = jnp.concatenate([s.astype(bf16) for s in sums], axis=1)
+        att_ref[at, :] = att
+        part_ref[at, :] = dot(att, wo_ref[...]).astype(bf16)
+
+
+def attn_fwd_call(lo, q, start, wo, kvs):
     rows, width = q.shape
+    dim = wo.shape[1]
     vmem = pl.BlockSpec(memory_space=pltpu.VMEM)
     return pl.pallas_call(
         functools.partial(attn_fwd_kernel, len(kvs)),
-        in_specs=[pl.BlockSpec(memory_space=pltpu.SMEM)] + [vmem] * (2 + len(kvs)),
-        out_specs=vmem,
-        out_shape=jax.ShapeDtypeStruct((rows, width), bf16),
+        in_specs=[pl.BlockSpec(memory_space=pltpu.SMEM)] + [vmem] * (3 + len(kvs)),
+        out_specs=[vmem, vmem],
+        out_shape=[
+            jax.ShapeDtypeStruct((rows, width), bf16),
+            jax.ShapeDtypeStruct((rows, dim), bf16),
+        ],
         scratch_shapes=[pltpu.VMEM((len(kvs) * rows, 2 * width), bf16)],
         compiler_params=pltpu.CompilerParams(vmem_limit_bytes=VMEM),
         cost_estimate=pl.CostEstimate(
-            flops=10 * 10**9, bytes_accessed=12 * 2**20, transcendentals=4 * 10**6
+            flops=10**6, bytes_accessed=10**6, transcendentals=0
         ),
-    )(lo, q, start, *kvs)
-
-
-def project_kernel(count, places, at_ref, att_ref, x_ref, gain_ref, *refs):
-    sources, (h_ref, own_ref, wo_out_ref, wo, att, sem) = refs[: len(places)], refs[len(places) :]
-    uly, blk = at_ref[0], at_ref[1]
-    heads, _, width = att_ref.shape
-    dim = wo.shape[0]
-    step = pl.program_id(0)
-
-    @pl.when(step == 0)
-    def _():
-        copies = []
-        for n, (source, (j, half, row)) in enumerate(zip(sources, places)):
-            rows = source.shape[0]
-            block = dim // count
-            at = (uly ^ j) * block + row
-            if half:
-                core = lax.rem(blk, 2)
-                at = at + (core if half == 1 else 1 - core) * (block // 2)
-            to = wo.at[pl.ds(pl.multiple_of(at, rows), rows), :]
-            copies.append(pltpu.make_async_copy(source, to, sem.at[n]))
-        for c in copies:
-            c.start()
-        for c in copies:
-            c.wait()
-        wo_out_ref[...] = wo[pl.ds(pl.multiple_of(blk * width, width), width), :]
-
-    for n in range(heads):
-        att[:, n * width : (n + 1) * width] = att_ref[n]
-    resid = x_ref[...].astype(f32) + dot(att[...], wo[...])
-    inv = lax.rsqrt(jnp.mean(resid * resid, axis=-1, keepdims=True) + norm_eps)
-    h_ref[...] = (resid * inv * gain_ref[...]).astype(bf16)
-    own = own_ref.shape[0]
-    for n in range(BR // own):
-
-        @pl.when(step * (BR // own) + n == blk)
-        def _():
-            own_ref[...] = resid[n * own : (n + 1) * own, :]
-
-
-def project_call(at, att, x, gain, sources, places, own, count):
-    heads, rows, width = att.shape
-    dim = x.shape[1]
-    block = lambda cols: pl.BlockSpec((BR, cols), lambda i: (i, 0))
-    whole = lambda *shape: pl.BlockSpec(shape, lambda i: (0, 0))
-    return pl.pallas_call(
-        functools.partial(project_kernel, count, places),
-        grid=(rows // BR,),
-        in_specs=[
-            pl.BlockSpec(memory_space=pltpu.SMEM),
-            pl.BlockSpec((heads, BR, width), lambda i: (0, i, 0)),
-            block(dim),
-            whole(1, dim),
-        ]
-        + [pl.BlockSpec(memory_space=pl.ANY)] * len(sources),
-        out_specs=[block(dim), whole(own, dim), whole(width, dim)],
-        out_shape=[
-            jax.ShapeDtypeStruct((rows, dim), bf16),
-            jax.ShapeDtypeStruct((own, dim), f32),
-            jax.ShapeDtypeStruct((width, dim), bf16),
-        ],
-        scratch_shapes=[
-            pltpu.VMEM((dim, dim), bf16),
-            pltpu.VMEM((BR, dim), bf16),
-            pltpu.SemaphoreType.DMA((len(places),)),
-        ],
-        compiler_params=pltpu.CompilerParams(vmem_limit_bytes=VMEM),
-        cost_estimate=pl.CostEstimate(
-            flops=2 * rows * dim * dim, bytes_accessed=24 * 2**20, transcendentals=0
-        ),
-    )(at, att, x, gain, *sources)
+    )(lo, q, start, wo, *kvs)
 
 
 def attn_bwd_kernel(count_kv, lo_ref, q_ref, ga_ref, start_ref, wo_ref, cos_ref, sin_ref, *refs):
@@ -597,9 +532,7 @@
     count_blk = lax.axis_size("blk")
     devices = count_uly * count_blk
     uly_index = lax.axis_index("uly")
-    blk_index = lax.axis_index("blk")
     uly_at = uly_index.astype(jnp.int32).reshape(1)
-    both_at = jnp.stack([uly_index, blk_index]).astype(jnp.int32)
     tok_rows, dim = block_input.shape
     group = count_blk * tok_rows
     part = dim // count_blk
@@ -630,7 +563,8 @@
     cos = jnp.concatenate([cos, cos], axis=1)
     sin = jnp.concatenate([-sin, sin], axis=1)
 
-    wo = lax.all_gather(w_out, "blk", axis=0, tiled=True)
+    owner = [(i, (i % count_uly) * count_blk + i // count_uly) for i in range(devices)]
+    wo = lax.ppermute(w_out, BOTH, owner)
     gains = jnp.concatenate([norm_attn, norm_ffn])
     gains = jnp.pad(gains[None], ((0, 15), (0, 3 * part - 2 * rows_w)))
     qkv = pack_call(w_query, w_key, w_value, gains, count_blk)
@@ -647,53 +581,42 @@
     columns = lambda w: w.reshape(rows_d, count_blk, width).transpose(1, 0, 2)
     to_hidden = lambda w: lax.all_to_all(w, "blk", 0, 0, tiled=True)
     gate_up = jnp.concatenate([columns(w_gate), columns(w_up)], axis=1)
-    down = to_hidden(after(w_down.reshape(count_blk, width, rows_d), qkv))
-    if count_uly == 4:
-        size = wo.shape[0] // 2
-        half = lax.dynamic_slice_in_dim(wo, lax.rem(blk_index, 2) * size, size, 0)
-        halves = gather_uly(after(half, qkv_pieces[3][-1]), count_uly)[1:]
+    down = to_hidden(
+        after(w_down.reshape(count_blk, width, rows_d), *[p[0] for p in qkv_pieces[1:3]])
+    )
+    wo = in_order(gather_uly(after(wo, qkv_pieces[3][-1]), count_uly), uly_index)
+    group_in, down, gate_up, wo = together((group_in, down, gate_up, wo))
+    hidden_one, query, kv = qkv_call(group_in, gain_attn, w_qkv, cos, sin)
+    if count_uly == 4 and back == 2:
+        half = group // 2
+        two = lax.ppermute(kv, "uly", [(0, 2), (1, 3)])
+        one = lax.ppermute(kv, "uly", [(0, 1), (2, 3)])
+        over = lax.ppermute(kv[:half], "uly", [(1, 0)])
+        over = lax.ppermute(over, "uly", [(0, 2)])
+        under = lax.ppermute(two[half:], "uly", [(3, 2)])
+        kvs = [two, one + jnp.concatenate([over, under]), kv]
     else:
-        halves = gather_uly(wo, count_uly)[1:]
-    halves, group_in, down, gate_up = together((halves, group_in, down, gate_up))
-    wos, places = [wo], [(0, 0, 0)]
-    for j, parts in enumerate(halves, 1):
-        row = 0
-        for piece in parts:
-            if count_uly == 4:
-                swapped = lax.ppermute(piece, "blk", [(i, i ^ 1) for i in range(count_blk)])
-                wos += [piece, swapped]
-                places += [(j, 1, row), (j, 2, row)]
-            else:
-                wos += [piece]
-                places += [(j, 0, 0)]
-            row += piece.shape[0]
-    hidden_one, query, kv = qkv_call(group_in, gain_attn, w_qkv, cos, sin)
-    kvs = [
-        lax.ppermute(kv, "uly", [(i, i + s) for i in range(count_uly - s)])
-        for s in range(back, 0, -1)
-    ] + [kv]
+        kvs = [
+            lax.ppermute(kv, "uly", [(i, i + s) for i in range(count_uly - s)])
+            for s in range(back, 0, -1)
+        ] + [kv]
 
     gate_up = to_hidden(after(gate_up, kv))
     group_cot = lax.all_gather(after(cotangent, kv), "blk", axis=0, tiled=True)
-    down = gather_uly(after(down, kv), count_uly)
-    query, gate_up, down, group_cot = together((query, gate_up, down, group_cot))
+    down = gather_first(after(down, kv), count_uly)
+    query, down = together((query, down))
+    attended, out_part = attn_fwd_call(low_kb, query, begin[:, None], wo, kvs)
+    out_part, gate_up, group_cot = together((out_part, gate_up, group_cot))
     gate_up = gather_first(gate_up, count_uly)
-    attended = attn_fwd_call(low_kb, query, begin[:, None], kvs)
-    group_att = lax.all_gather(attended, "blk", axis=0, tiled=True)
-    gate_up, group_att = together((gate_up, group_att))
+    out_own = lax.psum_scatter(out_part, "blk", scatter_dimension=0, tiled=True)
+    out_own, gate_up = together((out_own, gate_up))
     gate_up = gather_rest(gate_up, count_uly)
-    group_hidden, resid, wo = project_call(
-        both_at,
-        group_att.reshape(count_blk, group, part),
-        group_in,
-        gain_ffn,
-        wos,
-        tuple(places),
-        tok_rows,
-        count_uly,
-    )
+    down = gather_rest(down, count_uly)
     input_f = block_input.astype(f32)
+    resid = input_f + out_own.astype(f32)
     normed_two, inv_two = rms_stats(resid)
+    hidden_two = (normed_two * gain_ffn).astype(bf16)
+    group_hidden = lax.all_gather(hidden_two, "blk", axis=0, tiled=True)
 
     pairs = count_uly == 4 and width % HD == 0
     if pairs:
@@ -795,8 +718,7 @@
     input_grad = grad_resid + norm_back(grad_h1, normed_one, inv_one, gain_attn)
 
     grads = scatter_uly(grads[0], grads[1:], count_uly).astype(bf16)
-    owner = [((i % count_uly) * count_blk + i // count_uly, i) for i in range(devices)]
-    outs = lax.ppermute(after(outs, gh1_part), BOTH, owner)
+    outs = lax.ppermute(after(outs, gh1_part), BOTH, [(j, i) for i, j in owner])
     grads, outs = together((grads, outs))
     outs = outs.astype(f32)
     grad_out, grad_gain_ffn = outs[:, :dim], outs[:, dim]

time: 699 us -> 677 us (0.969)
  blocking collectives: 48.5 us -> 0 us
  waiting for transfers between devices: 321 us -> 353 us
  Pallas kernels: 107 us -> 91.7 us
  starting transfers between devices: 91.4 us -> 99.5 us
    ppermute x34, waiting for transfers between devices: 290 us -> 225 us  [xor_permute(): return lax.ppermute(x, 'uly', [(i, i ^ flip) for i in range(count)])]
    all_to_all x1 -> x0, blocking collectives: 48.5 us -> none  [body(): qkv = lax.all_to_all(qkv, 'blk', 0, 0, tiled=True)]
    ppermute x7, waiting for transfers between devices: 0.02 us -> 38.9 us  [the longest x1 28.3 us: body(): over = lax.ppermute(kv[:half], 'uly', [(1, 0)])]
    all_to_all x0 -> x1, waiting for transfers between devices: none -> 30.5 us  [body(): qkv = lax.all_to_all(qkv, 'blk', 0, 0, tiled=True)]
    all_to_all x4, waiting for transfers between devices: 10.5 us -> 31.6 us  [body(): to_hidden = lambda w: lax.all_to_all(w, 'blk', 0, 0, tiled=True)]
    pallas_call x1 -> x0, Pallas kernels: 17.6 us -> none  [project_call(): pl.pallas_call(functools.partial(project_kernel, count, places), grid=(ro...]
    ppermute x34, starting transfers between devices: 57.9 us -> 45.2 us  [xor_permute(): return lax.ppermute(x, 'uly', [(i, i ^ flip) for i in range(count)])]
    all_to_all x4, starting transfers between devices: 15 us -> 22.8 us  [body(): to_hidden = lambda w: lax.all_to_all(w, 'blk', 0, 0, tiled=True)]
  transfers between devices with their start and end apart: 56 -> 57, of which waited for: 30 -> 35; matrix products, arithmetic and copies ran while one was open for 14% -> 14% of each run, Pallas kernels for 6% -> 5%
where the time goes in v3:
time: 677 us; the launch traced here: 667 us
  waiting for transfers between devices  353 us (52%)
  starting transfers between devices  99.5 us (15%)
  Pallas kernels  91.7 us (14%)
  other arithmetic  44.6 us (7%)
  matrix products  34.5 us (5%)
  local copies, waits for them, and re-layouts  27.9 us (4%)
  between operations  15.5 us (2%)
    ppermute x34, waiting for transfers between devices, xor_permute(): return lax.ppermute(x, 'uly', [(i, i ^ flip) for i in range(count)])  225 us
    ppermute x34, starting transfers between devices, xor_permute(): return lax.ppermute(x, 'uly', [(i, i ^ flip) for i in range(count)])  45.2 us
    dot_general x13, matrix products, t_dot(): lax.dot_general(left, right, (((0,), (0,)), ((), ())), preferred_element_...  34.5 us
    all_to_all x4, waiting for transfers between devices, body(): to_hidden = lambda w: lax.all_to_all(w, 'blk', 0, 0, tiled=True)  31.6 us
    pallas_call x1, Pallas kernels, ffn_call(): pl.pallas_call(functools.partial(ffn_kernel, places, blocks, groups), gri...  30.7 us
    all_to_all x1, waiting for transfers between devices, body(): qkv = lax.all_to_all(qkv, 'blk', 0, 0, tiled=True)  30.5 us
    ppermute x1, waiting for transfers between devices, body(): over = lax.ppermute(kv[:half], 'uly', [(1, 0)])  28.3 us
    all_to_all x4, starting transfers between devices, body(): to_hidden = lambda w: lax.all_to_all(w, 'blk', 0, 0, tiled=True)  22.8 us
  transfers between devices with their start and end apart: 57, of which 35 were waited for; matrix products, arithmetic and copies ran while one was open for 14% of the time, Pallas kernels for 5%

profile of v3, /device:TPU:0, one launch (start us, length us, event | category | flops | bytes accessed | tf_op | source)
XLA Modules:
  0.0 666.8 jit_solution(8916458116532648302)
XLA Ops:
  10.8 6.3 all-to-all-start
  17.9 30.5 %all-to-all-done = bf16[8,80,768]{2,1,0:T(8,128)(2,1)S(1)} async-done(((bf16[8,80,768]{2,1,0:T(8,128)(2,1)}), bf16[8,80,768]{2,1,0:T(8,128)(2,1)S(1)}, u32[]{:S(2)}, u32[]{:S(2)}) %all-to-all-start) | async-done | bytes 983072 | tf_op jit(solution)/shard_map/all_to_all | solution.py:571
  61.5 11.7 %collective-permute-done.1 = bf16[8,80,768]{2,1,0:T(8,128)(2,1)S(1)} collective-permute-done((bf16[8,80,768]{2,1,0:T(8,128)(2,1)}, bf16[8,80,768]{2,1,0:T(8,128)(2,1)S(1)}, u32[]{:S(2)}, u32[]{:S(2)}) %collective-permute-start.1) | collective-permute-done | bytes 983072 | tf_op jit(solution)/shard_map/ppermute | solution.py:463
  75.4 10.4 %all-to-all-start.1 = ((bf16[8,256,256]{2,1,0:T(8,128)(2,1)}), bf16[8,256,256]{2,1,0:T(8,128)(2,1)}, u32[]{:S(2)}, u32[]{:S(2)}) async-start(bf16[8,256,256]{2,1,0:T(8,128)(2,1)} %bitcast.1), calls=%async_computation.1 | async-start | bytes 2097152 | tf_op jit(solution)/shard_map/all_to_all | solution.py:582
  91.1 8.5 %collective-permute-done.3 = bf16[4,80,768]{2,1,0:T(8,128)(2,1)S(1)} collective-permute-done((bf16[4,80,768]{2,1,0:T(8,128)(2,1)S(1)}, bf16[4,80,768]{2,1,0:T(8,128)(2,1)S(1)}, u32[]{:S(2)}, u32[]{:S(2)}) %collective-permute-start.3) | collective-permute-done | bytes 491552 | tf_op jit(solution)/shard_map/ppermute | solution.py:463
  104.8 2.8 collective-permute-done.4
  113.9 6.8 %all-to-all-done.1.refs_5_.refs_0_ = bf16[8,256,256]{2,1,0:T(8,128)(2,1)} async-done(((bf16[8,256,256]{2,1,0:T(8,128)(2,1)}), bf16[8,256,256]{2,1,0:T(8,128)(2,1)}, u32[]{:S(2)}, u32[]{:S(2)}) %all-to-all-start.1) | async-done | bytes 1048608 | tf_op jit(solution)/shard_map/all_to_all | solution.py:582
  120.7 8.5 %shard_map.213 = (bf16[1024,2048]{1,0:T(8,128)(2,1)}, bf16[1024,256]{1,0:T(8,128)(2,1)}, bf16[1024,512]{1,0:T(8,128)(2,1)}) custom-call(bf16[1024,2048]{1,0:T(8,128)(2,1)} %all-gather.5.cloned.1.call-done.x_ref, f32[1,2048]{1,0:T(1,128)} %reshape.230.gain_ref, bf16[2048,768]{1,0:T(8,128)(2,1)} %constant_dynamic-update-slice_fusion.w_ref, ...), custom_call_target="tpu_custom_call" | custom-call | flops 3221225472 | bytes 16777216 | tf_op jit(solution)/shard_map/pallas_call | solution.py:106
  129.2 4.5 all-to-all-start.2
  133.8 3.5 collective-permute-start.11
  140.3 5.4 collective-permute-start.12
  145.7 28.3 %collective-permute-done.13 = bf16[512,512]{1,0:T(8,128)(2,1)} collective-permute-done((bf16[512,512]{1,0:T(8,128)(2,1)S(1)}, bf16[512,512]{1,0:T(8,128)(2,1)}, u32[]{:S(2)}, u32[]{:S(2)}) %collective-permute-start.13) | collective-permute-done | bytes 524320 | tf_op jit(solution)/shard_map/ppermute | solution.py:594
  180.1 3.2 collective-permute-done.10.refs_7_.refs_2_
  184.3 9.6 %collective-permute-done.14 = bf16[512,512]{1,0:T(8,128)(2,1)} collective-permute-done((bf16[512,512]{1,0:T(8,128)(2,1)}, bf16[512,512]{1,0:T(8,128)(2,1)}, u32[]{:S(2)}, u32[]{:S(2)}) %collective-permute-start.14) | collective-permute-done | bytes 524320 | tf_op jit(solution)/shard_map/ppermute | solution.py:595
  196.4 9.9 %shard_map.214 = (bf16[1024,256]{1,0:T(8,128)(2,1)}, bf16[1024,2048]{1,0:T(8,128)(2,1)}) custom-call(s32[2]{0:T(128)} %add_minimum_fusion.lo_ref, bf16[1024,256]{1,0:T(8,128)(2,1)} %get-tuple-element.97.q_ref, s32[1024,1]{1,0:T(8,128)} %copy.43.start_ref, bf16[256,2048]{1,0:T(8,128)(2,1)} %copy-done.8, bf16[1024,512]{1,0:T(8,128)(2,1)} %copy-done.17, ...), custom_call_target="tpu_custom_call" | custom-call | flops 1000000 | bytes 1000000 | tf_op jit(solution)/shard_map/pallas_call | solution.py:165
  206.3 10.2 %all-to-all-done.2.refs_0_ = bf16[8,512,256]{2,1,0:T(8,128)(2,1)} async-done(((bf16[8,512,256]{2,1,0:T(8,128)(2,1)}), bf16[8,512,256]{2,1,0:T(8,128)(2,1)}, u32[]{:S(2)}, u32[]{:S(2)}) %all-to-all-start.2) | async-done | bytes 2097184 | tf_op jit(solution)/shard_map/all_to_all | solution.py:582
  219.9 44.1 %collective-permute-done.16.refs_1_ = bf16[8,512,256]{2,1,0:T(8,128)(2,1)S(1)} collective-permute-done((bf16[8,512,256]{2,1,0:T(8,128)(2,1)}, bf16[8,512,256]{2,1,0:T(8,128)(2,1)S(1)}, u32[]{:S(2)}, u32[]{:S(2)}) %collective-permute-start.16) | collective-permute-done | bytes 2097184 | tf_op jit(solution)/shard_map/ppermute | solution.py:463
  277.0 26.7 %collective-permute-done.20.refs_8_.refs_3_ = bf16[4,256,256]{2,1,0:T(8,128)(2,1)S(1)} collective-permute-done((bf16[4,256,256]{2,1,0:T(8,128)(2,1)S(1)}, bf16[4,256,256]{2,1,0:T(8,128)(2,1)S(1)}, u32[]{:S(2)}, u32[]{:S(2)}) %collective-permute-start.20) | collective-permute-done | bytes 524320 | tf_op jit(solution)/shard_map/ppermute | solution.py:463
  303.7 2.7 collective-permute-done.21.refs_9_.refs_4_
  307.4 7.4 %all-gather.9.cloned.1.call-done.h_ref = bf16[1024,2048]{1,0:T(8,128)(2,1)} async-done(((bf16[128,2048]{1,0:T(8,128)(2,1)}), bf16[1024,2048]{1,0:T(8,128)(2,1)}) %all-gather.9.cloned.1.call-update) | async-done | bytes 4194320 | tf_op jit(solution)/shard_map/all_gather | solution.py:619
  314.8 30.7 %shard_map.215 = (bf16[1024,512]{1,0:T(8,128)(2,1)}, bf16[1024,512]{1,0:T(8,128)(2,1)}, bf16[1024,512]{1,0:T(8,128)(2,1)}, bf16[1024,512]{1,0:T(8,128)(2,1)}, bf...) custom-call(bf16[1024,2048]{1,0:T(8,128)(2,1)} %all-gather.9.cloned., ...), custom_call_target="tpu_custom_call" | custom-call | flops 21474836480 | bytes 37748736 | tf_op jit(solution)/shard_map/pallas_call | solution.py:361
  346.8 4.0 convolution_convert_fusion.3
  360.9 2.6 fusion.16
  371.7 10.0 %shard_map.216 = bf16[1024,2048]{1,0:T(8,128)(2,1)} custom-call(bf16[1024,1024]{1,0:T(8,128)(2,1)} %get-tuple-element.126.inner_ref, bf16[8,256,256]{2,1,0:T(8,128)(2,1)} %all-to-all-done.1.refs_5_.refs_0_, bf16[8,256,256]{2,1,0:T(8,128)(2,1)} %collective-permute-done.9.refs_6_.refs_1_, bf16[8,256,256]{2,1,0:T(8,128)(2,1)} %collective-permute-done.10.refs_7_.refs_2_, ...), custom_call_target="tpu_custom_call" | custom-call | flops 4294967296 | bytes 12582912 | tf_op jit(solution)/shard_map/pallas_call | solution.py:408
  381.7 3.6 convert_add_fusion.4
  386.1 2.7 convert_add_fusion.5
  392.1 6.9 %collective-permute-done.25 = bf16[1024,256]{1,0:T(8,128)(2,1)S(1)} collective-permute-done((bf16[1024,256]{1,0:T(8,128)(2,1)S(1)}, bf16[1024,256]{1,0:T(8,128)(2,1)S(1)}, u32[]{:S(2)}, u32[]{:S(2)}) %collective-permute-start.25) | collective-permute-done | bytes 524320 | tf_op jit(solution)/shard_map/ppermute | solution.py:463
  399.2 3.2 collective-permute-done.23
  414.2 4.2 all-to-all-start.3
  418.5 15.7 %collective-permute-done.28 = bf16[1024,512]{1,0:T(8,128)(2,1)} collective-permute-done((bf16[1024,512]{1,0:T(8,128)(2,1)}, bf16[1024,512]{1,0:T(8,128)(2,1)}, u32[]{:S(2)}, u32[]{:S(2)}) %collective-permute-start.28) | collective-permute-done | bytes 1048608 | tf_op jit(solution)/shard_map/ppermute | solution.py:463
  440.0 16.7 %collective-permute-done.32 = bf16[512,1024]{1,0:T(8,128)(2,1)} collective-permute-done((bf16[512,1024]{1,0:T(8,128)(2,1)}, bf16[512,1024]{1,0:T(8,128)(2,1)}, u32[]{:S(2)}, u32[]{:S(2)}) %collective-permute-start.32) | collective-permute-done | bytes 1048608 | tf_op jit(solution)/shard_map/ppermute | solution.py:463
  461.9 6.4 collective-permute-done.29
  468.9 8.2 %collective-permute-done.33 = bf16[256,1024]{1,0:T(8,128)(2,1)S(1)} collective-permute-done((bf16[256,1024]{1,0:T(8,128)(2,1)S(1)}, bf16[256,1024]{1,0:T(8,128)(2,1)S(1)}, u32[]{:S(2)}, u32[]{:S(2)}) %collective-permute-start.33) | collective-permute-done | bytes 524320 | tf_op jit(solution)/shard_map/ppermute | solution.py:463
  479.1 3.6 all-to-all-start.4
  483.7 3.6 convolution_convert_fusion
  488.4 14.9 %shard_map.217 = (bf16[1024,256]{1,0:T(8,128)(2,1)}, f32[1024,512]{1,0:T(8,128)}, bf16[1024,512]{1,0:T(8,128)(2,1)}, bf16[1024,512]{1,0:T(8,128)(2,1)}) custom-call(s32[2]{0:T(128)} %add_minimum_fusion.lo_ref, bf16[1024,256]{1,0:T(8,128)(2,1)} %get-tuple-element.97.q_ref, bf16[1024,2048]{1,0:T(8,128)(2,1)} %all-gather.11.cloned.1.call-done.ga_ref, ...), custom_call_target="tpu_custom_call" | custom-call | flops 24999999488 | bytes 20971520 | tf_op jit(solution)/shard_map/pallas_call | solution.py:241
  507.1 9.7 %collective-permute-start.36 = (bf16[64,2176]{1,0:T(8,128)(2,1)S(1)}, bf16[64,2176]{1,0:T(8,128)(2,1)S(1)}, u32[]{:S(2)}, u32[]{:S(2)}) collective-permute-start(bf16[64,2176]{1,0:T(8,128)(2,1)S(1)} %get-tuple-element.173), channel_id=1, source_target_pairs={{0,24},{8,16},{16,8},{24,0},{1,25},{9,17},{17,9},{25,1},{2,26},{10... | collective-permute-start | bytes 835592 | tf_op jit(solution)/shard_map/ppermute | solution.py:463
  517.4 27.3 %collective-permute-done.36 = bf16[64,2176]{1,0:T(8,128)(2,1)S(1)} collective-permute-done((bf16[64,2176]{1,0:T(8,128)(2,1)S(1)}, bf16[64,2176]{1,0:T(8,128)(2,1)S(1)}, u32[]{:S(2)}, u32[]{:S(2)}) %collective-permute-start.36) | collective-permute-done | bytes 278560 | tf_op jit(solution)/shard_map/ppermute | solution.py:463
  547.7 14.6 %all-to-all-done.4 = bf16[8,512,256]{2,1,0:T(8,128)(2,1)S(1)} async-done(((bf16[8,512,256]{2,1,0:T(8,128)(2,1)}), bf16[8,512,256]{2,1,0:T(8,128)(2,1)S(1)}, u32[]{:S(2)}, u32[]{:S(2)}) %all-to-all-start.4) | async-done | bytes 2097184 | tf_op jit(solution)/shard_map/all_to_all | solution.py:582
  562.3 3.9 reduce-scatter.9.cloned.1.call-done
  566.3 12.9 %shard_map.218 = (bf16[1024,2048]{1,0:T(8,128)(2,1)}, f32[512,768]{1,0:T(8,128)}, bf16[512,768]{1,0:T(8,128)(2,1)}, bf16[512,768]{1,0:T(8,128)(2,1)}, bf16[512,768]{1,0:T(8,128)(2,1)}) custom-call(s32[1]{0:T(128)} %bitcast.16.index_ref, bf16[1024,2048]{1,0:T(8,128)(2,1)} %get-tuple-element.148.h_ref, bf16[1024,256]{1,0:T(8,128)(2,1)} %get-tuple-element.145.gq_ref, ...), custom_call_target="tpu_custom_call" | custom-call | flops 6442450944 | bytes 20971520 | tf_op jit(solution)/shard_map/pallas_call | solution.py:289
  580.6 3.1 collective-permute-start.41
  591.3 13.6 %collective-permute-done.41 = bf16[512,768]{1,0:T(8,128)(2,1)S(1)} collective-permute-done((bf16[512,768]{1,0:T(8,128)(2,1)}, bf16[512,768]{1,0:T(8,128)(2,1)S(1)}, u32[]{:S(2)}, u32[]{:S(2)}) %collective-permute-start.41) | collective-permute-done | bytes 786464 | tf_op jit(solution)/shard_map/ppermute | solution.py:463
  604.9 19.1 %collective-permute-done.40 = bf16[512,768]{1,0:T(8,128)(2,1)S(1)} collective-permute-done((bf16[512,768]{1,0:T(8,128)(2,1)}, bf16[512,768]{1,0:T(8,128)(2,1)S(1)}, u32[]{:S(2)}, u32[]{:S(2)}) %collective-permute-start.40) | collective-permute-done | bytes 786464 | tf_op jit(solution)/shard_map/ppermute | solution.py:463
  625.3 6.8 %all-to-all-start.5 = ((bf16[8,64,768]{2,1,0:T(8,128)(2,1)}), bf16[8,64,768]{2,1,0:T(8,128)(2,1)S(1)}, u32[]{:S(2)}, u32[]{:S(2)}) async-start(bf16[8,64,768]{2,1,0:T(8,128)(2,1)} %bitcast.17), calls=%async_computation.9 | async-start | bytes 1572864 | tf_op jit(solution)/shard_map/all_to_all | solution.py:725
  635.2 4.9 reduce-scatter.11.cloned.1.call-done
  641.4 3.2 fusion.35
  644.6 10.1 %all-to-all-done.5.got_ref = bf16[8,64,768]{2,1,0:T(8,128)(2,1)S(1)} async-done(((bf16[8,64,768]{2,1,0:T(8,128)(2,1)}), bf16[8,64,768]{2,1,0:T(8,128)(2,1)S(1)}, u32[]{:S(2)}, u32[]{:S(2)}) %all-to-all-start.5) | async-done | bytes 786464 | tf_op jit(solution)/shard_map/all_to_all | solution.py:725
  (302 shorter events, 144.2 us)
Async XLA Ops:
  10.8 37.6 %all-to-all-start = ((bf16[8,80,768]{2,1,0:T(8,128)(2,1)}), bf16[8,80,768]{2,1,0:T(8,128)(2,1)S(1)}, u32[]{:S(2)}, u32[]{:S(2)}) async-start(bf16[8,80,768]{2,1,0:T(8,128)(2,1)} %shard_map.212), calls=%async_computation | async-start | bytes 1966080 | tf_op jit(solution)/shard_map/all_to_all | solution.py:571
  17.1 103.6 %all-gather.5.cloned.1.call-start = ((), (), s32[]{:S(2)}) async-start(), calls=%async_computation.10 | async-start | bytes 4718592 | tf_op jit(solution)/shard_map/all_gather | solution.py:572
  52.3 20.8 %collective-permute-start.1 = (bf16[8,80,768]{2,1,0:T(8,128)(2,1)}, bf16[8,80,768]{2,1,0:T(8,128)(2,1)S(1)}, u32[]{:S(2)}, u32[]{:S(2)}) collective-permute-start(bf16[8,80,768]{2,1,0:T(8,128)(2,1)} %copy-done.9), channel_id=1, source_target_pairs={{0,8},{8,0},{16,24},{24,16},{1,9},{9,1},{17,25},{25,17},{2,10},{10... | collective-permute-start | bytes 2949128 | tf_op jit(solution)/shard_map/ppermute | solution.py:463
  53.8 21.6 %collective-permute-start.2 = (bf16[8,80,768]{2,1,0:T(8,128)(2,1)}, bf16[8,80,768]{2,1,0:T(8,128)(2,1)S(1)}, u32[]{:S(2)}, u32[]{:S(2)}) collective-permute-start(bf16[8,80,768]{2,1,0:T(8,128)(2,1)} %copy-done.9), channel_id=1, source_target_pairs={{0,16},{8,24},{16,0},{24,8},{1,17},{9,25},{17,1},{25,9},{2,18},{10... | collective-permute-start | bytes 2949128 | tf_op jit(solution)/shard_map/ppermute | solution.py:463
  75.4 45.3 %all-to-all-start.1 = ((bf16[8,256,256]{2,1,0:T(8,128)(2,1)}), bf16[8,256,256]{2,1,0:T(8,128)(2,1)}, u32[]{:S(2)}, u32[]{:S(2)}) async-start(bf16[8,256,256]{2,1,0:T(8,128)(2,1)} %bitcast.1), calls=%async_computation.1 | async-start | bytes 2097152 | tf_op jit(solution)/shard_map/all_to_all | solution.py:582
  85.9 130.6 %all-gather.7.cloned.1.call-start = ((), (), s32[]{:S(2)}) async-start(), calls=%async_computation.11 | async-start | bytes 4718592 | tf_op jit(solution)/shard_map/all_gather | solution.py:605
  129.2 87.3 %all-to-all-start.2 = ((bf16[8,512,256]{2,1,0:T(8,128)(2,1)}), bf16[8,512,256]{2,1,0:T(8,128)(2,1)}, u32[]{:S(2)}, u32[]{:S(2)}) async-start(bf16[8,512,256]{2,1,0:T(8,128)(2,1)} %pad_maximum_fusion), calls=%async_computation.2 | async-start | bytes 4194304 | tf_op jit(solution)/shard_map/all_to_all | solution.py:582
  133.7 132.0 %reduce-scatter.5.cloned.1.call-start = ((), (), s32[]{:S(2)}) async-start(), calls=%async_computation.12 | async-start | bytes 4718592 | tf_op jit(solution)/shard_map/reduce_scatter | solution.py:611
  133.8 42.4 %collective-permute-start.11 = (bf16[1024,512]{1,0:T(8,128)(2,1)S(1)}, bf16[1024,512]{1,0:T(8,128)(2,1)S(1)}, u32[]{:S(2)}, u32[]{:S(2)}) collective-permute-start(bf16[1024,512]{1,0:T(8,128)(2,1)S(1)} %copy-done.16), channel_id=1, source_target_pairs={{0,16},{8,24},{1,17},{9,25},{2,18},{10,26},{3,19},{11,27},{4,20},{... | collective-permute-start | bytes 3145736 | tf_op jit(solution)/shard_map/ppermute | solution.py:592
  137.3 42.8 %collective-permute-start.9 = (bf16[8,256,256]{2,1,0:T(8,128)(2,1)}, bf16[8,256,256]{2,1,0:T(8,128)(2,1)}, u32[]{:S(2)}, u32[]{:S(2)}) collective-permute-start(bf16[8,256,256]{2,1,0:T(8,128)(2,1)} %all-to-all-done.1.refs_5_.refs_0_), channel_id=1, source_target_pairs={{0,8},{8,0},{16,24},{24,16},{1,9},{9,1},{17,25},{25,17},{2,10},{10... | collective-permute-start | bytes 3145736 | tf_op jit(solution)/shard_map/ppermute | solution.py:463
  139.0 44.3 %collective-permute-start.10 = (bf16[8,256,256]{2,1,0:T(8,128)(2,1)}, bf16[8,256,256]{2,1,0:T(8,128)(2,1)}, u32[]{:S(2)}, u32[]{:S(2)}) collective-permute-start(bf16[8,256,256]{2,1,0:T(8,128)(2,1)} %all-to-all-done.1.refs_5_.refs_0_), channel_id=1, source_target_pairs={{0,16},{8,24},{16,0},{24,8},{1,17},{9,25},{17,1},{25,9},{2,18},{10... | collective-permute-start | bytes 3145736 | tf_op jit(solution)/shard_map/ppermute | solution.py:463
  139.0 35.0 %collective-permute-start.13 = (bf16[512,512]{1,0:T(8,128)(2,1)S(1)}, bf16[512,512]{1,0:T(8,128)(2,1)}, u32[]{:S(2)}, u32[]{:S(2)}) collective-permute-start(bf16[512,512]{1,0:T(8,128)(2,1)S(1)} %slice.161), channel_id=1, source_target_pairs={{8,0},{9,1},{10,2},{11,3},{12,4},{13,5},{14,6},{15,7}} | collective-permute-start | bytes 1572872 | tf_op jit(solution)/shard_map/ppermute | solution.py:594
  140.3 44.0 %collective-permute-start.12 = (bf16[1024,512]{1,0:T(8,128)(2,1)S(1)}, bf16[1024,512]{1,0:T(8,128)(2,1)S(1)}, u32[]{:S(2)}, u32[]{:S(2)}) collective-permute-start(bf16[1024,512]{1,0:T(8,128)(2,1)S(1)} %copy-done.16), channel_id=1, source_target_pairs={{0,8},{16,24},{1,9},{17,25},{2,10},{18,26},{3,11},{19,27},{4,12},{... | collective-permute-start | bytes 3145736 | tf_op jit(solution)/shard_map/ppermute | solution.py:593
  174.0 19.9 %collective-permute-start.14 = (bf16[512,512]{1,0:T(8,128)(2,1)}, bf16[512,512]{1,0:T(8,128)(2,1)}, u32[]{:S(2)}, u32[]{:S(2)}) collective-permute-start(bf16[512,512]{1,0:T(8,128)(2,1)} %collective-permute-done.13), channel_id=1, source_target_pairs={{0,16},{1,17},{2,18},{3,19},{4,20},{5,21},{6,22},{7,23}} | collective-permute-start | bytes 1572872 | tf_op jit(solution)/shard_map/ppermute | solution.py:595
  177.0 16.9 %collective-permute-start.15 = (bf16[512,512]{1,0:T(8,128)(2,1)}, bf16[512,512]{1,0:T(8,128)(2,1)}, u32[]{:S(2)}, u32[]{:S(2)}) collective-permute-start(bf16[512,512]{1,0:T(8,128)(2,1)} %slice.205), channel_id=1, source_target_pairs={{24,16},{25,17},{26,18},{27,19},{28,20},{29,21},{30,22},{31,23}} | collective-permute-start | bytes 1572872 | tf_op jit(solution)/shard_map/ppermute | solution.py:596
  216.5 98.3 %all-gather.9.cloned.1.call-start = ((), (), s32[]{:S(2)}) async-start(), calls=%async_computation.13 | async-start | bytes 4718592 | tf_op jit(solution)/shard_map/all_gather | solution.py:619
  216.5 47.4 %collective-permute-start.16 = (bf16[8,512,256]{2,1,0:T(8,128)(2,1)}, bf16[8,512,256]{2,1,0:T(8,128)(2,1)S(1)}, u32[]{:S(2)}, u32[]{:S(2)}) collective-permute-start(bf16[8,512,256]{2,1,0:T(8,128)(2,1)} %all-to-all-done.2.refs_0_), channel_id=1, source_target_pairs={{0,8},{8,0},{16,24},{24,16},{1,9},{9,1},{17,25},{25,17},{2,10},{10... | collective-permute-start | bytes 6291464 | tf_op jit(solution)/shard_map/ppermute | solution.py:463
  218.2 47.2 %collective-permute-start.17 = (bf16[8,512,256]{2,1,0:T(8,128)(2,1)}, bf16[8,512,256]{2,1,0:T(8,128)(2,1)}, u32[]{:S(2)}, u32[]{:S(2)}) collective-permute-start(bf16[8,512,256]{2,1,0:T(8,128)(2,1)} %all-to-all-done.2.refs_0_), channel_id=1, source_target_pairs={{0,16},{8,24},{16,0},{24,8},{1,17},{9,25},{17,1},{25,9},{2,18},{10... | collective-permute-start | bytes 6291464 | tf_op jit(solution)/shard_map/ppermute | solution.py:463
  269.1 134.6 %reduce-scatter.7.cloned.1.call-start = ((), (), s32[]{:S(2)}) async-start(), calls=%async_computation.14 | async-start | bytes 4718592 | tf_op jit(solution)/shard_map/reduce_scatter | solution.py:627
  269.2 37.2 %collective-permute-start.18 = (bf16[4,512,256]{2,1,0:T(8,128)(2,1)S(1)}, bf16[4,512,256]{2,1,0:T(8,128)(2,1)S(1)}, u32[]{:S(2)}, u32[]{:S(2)}) collective-permute-start(bf16[4,512,256]{2,1,0:T(8,128)(2,1)S(1)} %slice.164), channel_id=1, source_target_pairs={{0,16},{8,24},{16,0},{24,8},{1,17},{9,25},{17,1},{25,9},{2,18},{10... | collective-permute-start | bytes 3145736 | tf_op jit(solution)/shard_map/ppermute | solution.py:463
  272.1 35.4 %collective-permute-start.19 = (bf16[4,512,256]{2,1,0:T(8,128)(2,1)S(1)}, bf16[4,512,256]{2,1,0:T(8,128)(2,1)S(1)}, u32[]{:S(2)}, u32[]{:S(2)}) collective-permute-start(bf16[4,512,256]{2,1,0:T(8,128)(2,1)S(1)} %slice.165), channel_id=1, source_target_pairs={{0,8},{8,0},{16,24},{24,16},{1,9},{9,1},{17,25},{25,17},{2,10},{10... | collective-permute-start | bytes 3145736 | tf_op jit(solution)/shard_map/ppermute | solution.py:463
  274.7 29.0 %collective-permute-start.20 = (bf16[4,256,256]{2,1,0:T(8,128)(2,1)S(1)}, bf16[4,256,256]{2,1,0:T(8,128)(2,1)S(1)}, u32[]{:S(2)}, u32[]{:S(2)}) collective-permute-start(bf16[4,256,256]{2,1,0:T(8,128)(2,1)S(1)} %slice.166), channel_id=1, source_target_pairs={{0,16},{8,24},{16,0},{24,8},{1,17},{9,25},{17,1},{25,9},{2,18},{10... | collective-permute-start | bytes 1572872 | tf_op jit(solution)/shard_map/ppermute | solution.py:463
  276.4 30.0 %collective-permute-start.21 = (bf16[4,256,256]{2,1,0:T(8,128)(2,1)S(1)}, bf16[4,256,256]{2,1,0:T(8,128)(2,1)S(1)}, u32[]{:S(2)}, u32[]{:S(2)}) collective-permute-start(bf16[4,256,256]{2,1,0:T(8,128)(2,1)S(1)} %slice.167), channel_id=1, source_target_pairs={{0,8},{8,0},{16,24},{24,16},{1,9},{9,1},{17,25},{25,17},{2,10},{10... | collective-permute-start | bytes 1572872 | tf_op jit(solution)/shard_map/ppermute | solution.py:463
  345.6 132.0 %all-gather.11.cloned.1.call-start = ((), (), s32[]{:S(2)}) async-start(), calls=%async_computation.15 | async-start | bytes 4718592 | tf_op jit(solution)/shard_map/all_gather | solution.py:678
  350.8 30.9 %collective-permute-start.24 = (bf16[1024,512]{1,0:T(8,128)(2,1)}, bf16[1024,512]{1,0:T(8,128)(2,1)}, u32[]{:S(2)}, u32[]{:S(2)}) collective-permute-start(bf16[1024,512]{1,0:T(8,128)(2,1)} %convolution_convert_fusion.3), channel_id=1, source_target_pairs={{0,16},{8,24},{16,0},{24,8},{1,17},{9,25},{17,1},{25,9},{2,18},{10... | collective-permute-start | bytes 3145736 | tf_op jit(solution)/shard_map/ppermute | solution.py:463
  354.5 31.5 %collective-permute-start.22 = (bf16[1024,512]{1,0:T(8,128)(2,1)}, bf16[1024,512]{1,0:T(8,128)(2,1)}, u32[]{:S(2)}, u32[]{:S(2)}) collective-permute-start(bf16[1024,512]{1,0:T(8,128)(2,1)} %convolution_convert_fusion.4), channel_id=1, source_target_pairs={{0,8},{8,0},{16,24},{24,16},{1,9},{9,1},{17,25},{25,17},{2,10},{10... | collective-permute-start | bytes 3145736 | tf_op jit(solution)/shard_map/ppermute | solution.py:463
  407.7 26.5 %collective-permute-start.28 = (bf16[1024,512]{1,0:T(8,128)(2,1)}, bf16[1024,512]{1,0:T(8,128)(2,1)}, u32[]{:S(2)}, u32[]{:S(2)}) collective-permute-start(bf16[1024,512]{1,0:T(8,128)(2,1)} %convolution_convert_fusion.1), channel_id=1, source_target_pairs={{0,16},{8,24},{16,0},{24,8},{1,17},{9,25},{17,1},{25,9},{2,18},{10... | collective-permute-start | bytes 3145736 | tf_op jit(solution)/shard_map/ppermute | solution.py:463
  408.4 29.4 %collective-permute-start.26 = (bf16[1024,512]{1,0:T(8,128)(2,1)}, bf16[1024,512]{1,0:T(8,128)(2,1)}, u32[]{:S(2)}, u32[]{:S(2)}) collective-permute-start(bf16[1024,512]{1,0:T(8,128)(2,1)} %convolution_convert_fusion.2), channel_id=1, source_target_pairs={{0,8},{8,0},{16,24},{24,16},{1,9},{9,1},{17,25},{25,17},{2,10},{10... | collective-permute-start | bytes 3145736 | tf_op jit(solution)/shard_map/ppermute | solution.py:463
  409.6 47.1 %collective-permute-start.32 = (bf16[512,1024]{1,0:T(8,128)(2,1)}, bf16[512,1024]{1,0:T(8,128)(2,1)}, u32[]{:S(2)}, u32[]{:S(2)}) collective-permute-start(bf16[512,1024]{1,0:T(8,128)(2,1)} %fusion.13), channel_id=1, source_target_pairs={{0,16},{8,24},{16,0},{24,8},{1,17},{9,25},{17,1},{25,9},{2,18},{10... | collective-permute-start | bytes 3145736 | tf_op jit(solution)/shard_map/ppermute | solution.py:463
  411.0 48.7 %collective-permute-start.30 = (bf16[512,1024]{1,0:T(8,128)(2,1)}, bf16[512,1024]{1,0:T(8,128)(2,1)}, u32[]{:S(2)}, u32[]{:S(2)}) collective-permute-start(bf16[512,1024]{1,0:T(8,128)(2,1)} %fusion.10), channel_id=1, source_target_pairs={{0,8},{8,0},{16,24},{24,16},{1,9},{9,1},{17,25},{25,17},{2,10},{10... | collective-permute-start | bytes 3145736 | tf_op jit(solution)/shard_map/ppermute | solution.py:463
  414.2 63.3 %all-to-all-start.3 = ((bf16[8,264,256]{2,1,0:T(8,128)(2,1)}), bf16[8,264,256]{2,1,0:T(8,128)(2,1)}, u32[]{:S(2)}, u32[]{:S(2)}) async-start(bf16[8,264,256]{2,1,0:T(8,128)(2,1)} %fusion.31), calls=%async_computation.5 | async-start | bytes 2162688 | tf_op jit(solution)/shard_map/all_to_all | solution.py:582
  418.5 147.8 %reduce-scatter.9.cloned.1.call-start = ((), (), s32[]{:S(2)}) async-start(), calls=%async_computation.16 | async-start | bytes 4718592 | tf_op jit(solution)/shard_map/reduce_scatter | solution.py:699
  436.5 31.9 %collective-permute-start.29 = (bf16[1024,256]{1,0:T(8,128)(2,1)S(1)}, bf16[1024,256]{1,0:T(8,128)(2,1)S(1)}, u32[]{:S(2)}, u32[]{:S(2)}) collective-permute-start(bf16[1024,256]{1,0:T(8,128)(2,1)S(1)} %slice.283), channel_id=1, source_target_pairs={{0,8},{8,0},{16,24},{24,16},{1,9},{9,1},{17,25},{25,17},{2,10},{10... | collective-permute-start | bytes 1572872 | tf_op jit(solution)/shard_map/ppermute | solution.py:463
  439.4 29.2 %collective-permute-start.27 = (bf16[1024,256]{1,0:T(8,128)(2,1)S(1)}, bf16[1024,256]{1,0:T(8,128)(2,1)S(1)}, u32[]{:S(2)}, u32[]{:S(2)}) collective-permute-start(bf16[1024,256]{1,0:T(8,128)(2,1)S(1)} %slice.284), channel_id=1, source_target_pairs={{0,16},{8,24},{16,0},{24,8},{1,17},{9,25},{17,1},{25,9},{2,18},{10... | collective-permute-start | bytes 1572872 | tf_op jit(solution)/shard_map/ppermute | solution.py:463
  458.5 18.6 %collective-permute-start.33 = (bf16[256,1024]{1,0:T(8,128)(2,1)S(1)}, bf16[256,1024]{1,0:T(8,128)(2,1)S(1)}, u32[]{:S(2)}, u32[]{:S(2)}) collective-permute-start(bf16[256,1024]{1,0:T(8,128)(2,1)S(1)} %slice.281), channel_id=1, source_target_pairs={{0,8},{8,0},{16,24},{24,16},{1,9},{9,1},{17,25},{25,17},{2,10},{10... | collective-permute-start | bytes 1572872 | tf_op jit(solution)/shard_map/ppermute | solution.py:463
  461.3 15.9 %collective-permute-start.31 = (bf16[256,1024]{1,0:T(8,128)(2,1)S(1)}, bf16[256,1024]{1,0:T(8,128)(2,1)S(1)}, u32[]{:S(2)}, u32[]{:S(2)}) collective-permute-start(bf16[256,1024]{1,0:T(8,128)(2,1)S(1)} %slice.282), channel_id=1, source_target_pairs={{0,16},{8,24},{16,0},{24,8},{1,17},{9,25},{17,1},{25,9},{2,18},{10... | collective-permute-start | bytes 1572872 | tf_op jit(solution)/shard_map/ppermute | solution.py:463
  479.1 83.2 %all-to-all-start.4 = ((bf16[8,512,256]{2,1,0:T(8,128)(2,1)}), bf16[8,512,256]{2,1,0:T(8,128)(2,1)S(1)}, u32[]{:S(2)}, u32[]{:S(2)}) async-start(bf16[8,512,256]{2,1,0:T(8,128)(2,1)} %pad_maximum_fusion.1), calls=%async_computation.7 | async-start | bytes 4194304 | tf_op jit(solution)/shard_map/all_to_all | solution.py:582
  482.7 157.3 %reduce-scatter.11.cloned.1.call-start = ((), (), s32[]{:S(2)}) async-start(), calls=%async_computation.17 | async-start | bytes 4718592 | tf_op jit(solution)/shard_map/reduce_scatter | solution.py:716
  503.3 63.0 %collective-permute-start.37 = (bf16[1024,512]{1,0:T(8,128)(2,1)}, bf16[1024,512]{1,0:T(8,128)(2,1)}, u32[]{:S(2)}, u32[]{:S(2)}) collective-permute-start(bf16[1024,512]{1,0:T(8,128)(2,1)} %get-tuple-element.150), channel_id=1, source_target_pairs={{16,0},{24,8},{17,1},{25,9},{18,2},{26,10},{19,3},{27,11},{20,4},{... | collective-permute-start | bytes 3145736 | tf_op jit(solution)/shard_map/ppermute | solution.py:696
  504.6 61.7 %collective-permute-start.38 = (bf16[1024,512]{1,0:T(8,128)(2,1)}, bf16[1024,512]{1,0:T(8,128)(2,1)}, u32[]{:S(2)}, u32[]{:S(2)}) collective-permute-start(bf16[1024,512]{1,0:T(8,128)(2,1)} %get-tuple-element.151), channel_id=1, source_target_pairs={{8,0},{16,8},{24,16},{9,1},{17,9},{25,17},{10,2},{18,10},{26,18},{... | collective-permute-start | bytes 3145736 | tf_op jit(solution)/shard_map/ppermute | solution.py:696
  507.1 37.6 %collective-permute-start.36 = (bf16[64,2176]{1,0:T(8,128)(2,1)S(1)}, bf16[64,2176]{1,0:T(8,128)(2,1)S(1)}, u32[]{:S(2)}, u32[]{:S(2)}) collective-permute-start(bf16[64,2176]{1,0:T(8,128)(2,1)S(1)} %get-tuple-element.173), channel_id=1, source_target_pairs={{0,24},{8,16},{16,8},{24,0},{1,25},{9,17},{17,9},{25,1},{2,26},{10... | collective-permute-start | bytes 835592 | tf_op jit(solution)/shard_map/ppermute | solution.py:463
  516.8 29.2 %collective-permute-start.35 = (bf16[64,2176]{1,0:T(8,128)(2,1)S(1)}, bf16[64,2176]{1,0:T(8,128)(2,1)S(1)}, u32[]{:S(2)}, u32[]{:S(2)}) collective-permute-start(bf16[64,2176]{1,0:T(8,128)(2,1)S(1)} %get-tuple-element.174), channel_id=1, source_target_pairs={{0,16},{8,24},{16,0},{24,8},{1,17},{9,25},{17,1},{25,9},{2,18},{10... | collective-permute-start | bytes 835592 | tf_op jit(solution)/shard_map/ppermute | solution.py:463
  516.8 29.2 %collective-permute-start.34 = (bf16[64,2176]{1,0:T(8,128)(2,1)S(1)}, bf16[64,2176]{1,0:T(8,128)(2,1)S(1)}, u32[]{:S(2)}, u32[]{:S(2)}) collective-permute-start(bf16[64,2176]{1,0:T(8,128)(2,1)S(1)} %get-tuple-element.172), channel_id=1, source_target_pairs={{0,8},{8,0},{16,24},{24,16},{1,9},{9,1},{17,25},{25,17},{2,10},{10... | collective-permute-start | bytes 835592 | tf_op jit(solution)/shard_map/ppermute | solution.py:463
  580.6 24.3 %collective-permute-start.41 = (bf16[512,768]{1,0:T(8,128)(2,1)}, bf16[512,768]{1,0:T(8,128)(2,1)S(1)}, u32[]{:S(2)}, u32[]{:S(2)}) collective-permute-start(bf16[512,768]{1,0:T(8,128)(2,1)} %get-tuple-element.156), channel_id=1, source_target_pairs={{0,24},{8,16},{16,8},{24,0},{1,25},{9,17},{17,9},{25,1},{2,26},{10... | collective-permute-start | bytes 2359304 | tf_op jit(solution)/shard_map/ppermute | solution.py:463
  583.7 40.3 %collective-permute-start.40 = (bf16[512,768]{1,0:T(8,128)(2,1)}, bf16[512,768]{1,0:T(8,128)(2,1)S(1)}, u32[]{:S(2)}, u32[]{:S(2)}) collective-permute-start(bf16[512,768]{1,0:T(8,128)(2,1)} %get-tuple-element.155), channel_id=1, source_target_pairs={{0,16},{8,24},{16,0},{24,8},{1,17},{9,25},{17,1},{25,9},{2,18},{10... | collective-permute-start | bytes 2359304 | tf_op jit(solution)/shard_map/ppermute | solution.py:463
  584.8 39.2 %collective-permute-start.39 = (bf16[512,768]{1,0:T(8,128)(2,1)}, bf16[512,768]{1,0:T(8,128)(2,1)S(1)}, u32[]{:S(2)}, u32[]{:S(2)}) collective-permute-start(bf16[512,768]{1,0:T(8,128)(2,1)} %get-tuple-element.154), channel_id=1, source_target_pairs={{0,8},{8,0},{16,24},{24,16},{1,9},{9,1},{17,25},{25,17},{2,10},{10... | collective-permute-start | bytes 2359304 | tf_op jit(solution)/shard_map/ppermute | solution.py:463
  587.8 37.5 %collective-permute-start.42 = (bf16[64,2176]{1,0:T(8,128)(2,1)S(1)}, bf16[64,2176]{1,0:T(8,128)(2,1)S(1)}, u32[]{:S(2)}, u32[]{:S(2)}) collective-permute-start(bf16[64,2176]{1,0:T(8,128)(2,1)S(1)} %copy-done.25), channel_id=1, source_target_pairs={{0,0},{8,1},{16,2},{24,3},{1,4},{9,5},{17,6},{25,7},{2,8},{10,9},{... | collective-permute-start | bytes 835592 | tf_op jit(solution)/shard_map/ppermute | solution.py:721
  625.3 29.5 %all-to-all-start.5 = ((bf16[8,64,768]{2,1,0:T(8,128)(2,1)}), bf16[8,64,768]{2,1,0:T(8,128)(2,1)S(1)}, u32[]{:S(2)}, u32[]{:S(2)}) async-start(bf16[8,64,768]{2,1,0:T(8,128)(2,1)} %bitcast.17), calls=%async_computation.9 | async-start | bytes 1572864 | tf_op jit(solution)/shard_map/all_to_all | solution.py:725
  (57 other events, 576.2 us)
Sparse Core Ops, SparseCore 0:
  48.6 59.0 all-gather.4
  129.3 84.3 all-gather.6
  216.6 49.0 reduce-scatter.4
  269.2 45.5 all-gather.8
  345.7 48.7 reduce-scatter.6
  407.9 67.6 all-gather.10
  477.8 88.4 reduce-scatter.8
  579.3 60.6 reduce-scatter.10

commit v4 on v3

--- a/solution.py
+++ b/solution.py
@@ -258,50 +258,111 @@
     )(lo, q, ga, start, wo, cos, sin, *kvs)
 
 
-def gqkv_kernel(count, index_ref, h_ref, gq_ref, own_ref, cos_ref, sin_ref, w_ref, *refs):
-    got, gh_ref, grad_refs, g_ref = refs[: -2 - count], refs[-2 - count], refs[-1 - count : -1], refs[-1]
-    rows, width = gq_ref.shape
-    for at in range(0, rows, BR):
-        at = slice(at, at + BR)
-        gkv = own_ref[at, :]
-        for r in got:
-            gkv = gkv + r[at, :].astype(f32)
-        cos, sin = cos_ref[at, :], sin_ref[at, :]
-        g_ref[at, :width] = gq_ref[at, :]
-        for s in range(0, width, HD):
-            t = gkv[:, s : s + HD]
-            g_ref[at, width + s : width + s + HD] = (
-                t * cos - pltpu.roll(t, HD // 2, 1) * sin
-            ).astype(bf16)
-        g_ref[at, 2 * width :] = gkv[:, width:].astype(bf16)
-        gh_ref[at, :] = dot_t(g_ref[at, :], w_ref[...]).astype(bf16)
-    size = h_ref.shape[1] // count
-    for j in list(range(1, count)) + [0]:
-        at = pl.multiple_of((index_ref[0] ^ j) * size, size)
-        grad_refs[j][...] = t_dot(h_ref[:, pl.ds(at, size)], g_ref[...]).astype(grad_refs[j].dtype)
-
-
-def gqkv_call(index, h, gq, own, got, cos, sin, w, count):
+def norm_kernel(gh_ref, cot_ref, resid_ref, gain_ref, grad_ref, low_ref, part_ref):
+    gh, resid, gain = gh_ref[...].astype(f32), resid_ref[...], gain_ref[...]
+    inv = lax.rsqrt(jnp.mean(resid * resid, axis=-1, keepdims=True) + norm_eps)
+    normed = resid * inv
+    scaled = gh * gain
+    grad = cot_ref[...].astype(f32) + inv * (
+        scaled - normed * jnp.mean(scaled * normed, axis=-1, keepdims=True)
+    )
+    grad_ref[...] = grad
+    low_ref[...] = grad.astype(bf16)
+    part_ref[...] = jnp.sum(gh * normed, axis=0, keepdims=True)
+
+
+def norm_call(gh, cot, resid, gain):
+    vmem = pl.BlockSpec(memory_space=pltpu.VMEM)
+    return pl.pallas_call(
+        norm_kernel,
+        in_specs=[vmem] * 4,
+        out_specs=[vmem] * 3,
+        out_shape=[
+            jax.ShapeDtypeStruct(resid.shape, f32),
+            jax.ShapeDtypeStruct(resid.shape, bf16),
+            jax.ShapeDtypeStruct(gain.shape, f32),
+        ],
+    )(gh, cot, resid, gain)
+
+
+def gqkv_kernel(gq_ref, own_ref, cos_ref, sin_ref, w_ref, *refs):
+    got, g_ref, gh_ref = refs[:-2], refs[-2], refs[-1]
+    width = gq_ref.shape[1]
+    gkv = own_ref[...]
+    for r in got:
+        gkv = gkv + r[...].astype(f32)
+    cos, sin = cos_ref[...], sin_ref[...]
+    g_ref[:, :width] = gq_ref[...]
+    for s in range(0, width, HD):
+        t = gkv[:, s : s + HD]
+        g_ref[:, width + s : width + s + HD] = (
+            t * cos - pltpu.roll(t, HD // 2, 1) * sin
+        ).astype(bf16)
+    g_ref[:, 2 * width :] = gkv[:, width:].astype(bf16)
+    gh_ref[...] = dot_t(g_ref[...], w_ref[...]).astype(bf16)
+
+
+def gqkv_call(gq, own, got, cos, sin, w):
     rows, width = gq.shape
-    dim = h.shape[1]
-    size = dim // count
-    vmem = pl.BlockSpec(memory_space=pltpu.VMEM)
-    gh, *grads = pl.pallas_call(
-        functools.partial(gqkv_kernel, count),
-        in_specs=[pl.BlockSpec(memory_space=pltpu.SMEM)] + [vmem] * (6 + len(got)),
-        out_specs=[vmem] * (1 + count),
+    dim = w.shape[0]
+    block = lambda cols: pl.BlockSpec((BR, cols), lambda i: (i, 0))
+    return pl.pallas_call(
+        gqkv_kernel,
+        grid=(rows // BR,),
+        in_specs=[
+            block(width),
+            block(2 * width),
+            block(HD),
+            block(HD),
+            pl.BlockSpec(w.shape, lambda i: (0, 0)),
+        ]
+        + [block(2 * width)] * len(got),
+        out_specs=[block(3 * width), block(dim)],
         out_shape=[
+            jax.ShapeDtypeStruct((rows, 3 * width), bf16),
             jax.ShapeDtypeStruct((rows, dim), bf16),
-            jax.ShapeDtypeStruct((size, 3 * width), f32),
-        ]
-        + [jax.ShapeDtypeStruct((size, 3 * width), bf16)] * (count - 1),
-        scratch_shapes=[pltpu.VMEM((rows, 3 * width), bf16)],
+        ],
         compiler_params=pltpu.CompilerParams(vmem_limit_bytes=VMEM),
         cost_estimate=pl.CostEstimate(
-            flops=12 * rows * width * dim, bytes_accessed=20 * 2**20, transcendentals=0
+            flops=2 * rows * dim * 3 * width, bytes_accessed=16 * 2**20, transcendentals=0
         ),
-    )(index, h, gq, own, cos, sin, w, *got)
-    return gh, grads
+    )(gq, own, cos, sin, w, *got)
+
+
+def grads_kernel(groups, index_ref, h_ref, g_ref, *refs):
+    size = refs[0].shape[1]
+    for j in range(h_ref.shape[1] // size):
+        at = pl.multiple_of((index_ref[0] ^ j) * size, size)
+        grad = t_dot(h_ref[:, pl.ds(at, size)], g_ref[...])
+        for ref, (first, columns, members) in zip(refs, groups):
+            if j in members:
+                ref[members.index(j)] = grad[:, first : first + columns].astype(ref.dtype)
+
+
+def grads_call(index, h, g, count):
+    rows, width = g.shape
+    size = h.shape[1] // count
+    if count == 4:
+        half = width // 2
+        groups = [(0, half, (1, 3)), (half, half, (2, 3)), (0, half, (0, 2)), (half, half, (0, 1))]
+        kinds = [bf16, bf16, f32, f32]
+    else:
+        groups = [(0, width, (j,)) for j in range(count)]
+        kinds = [f32] + [bf16] * (count - 1)
+    vmem = pl.BlockSpec(memory_space=pltpu.VMEM)
+    return pl.pallas_call(
+        functools.partial(grads_kernel, groups),
+        in_specs=[pl.BlockSpec(memory_space=pltpu.SMEM), vmem, vmem],
+        out_specs=[vmem] * len(groups),
+        out_shape=[
+            jax.ShapeDtypeStruct((len(members), size, columns), kind)
+            for (_, columns, members), kind in zip(groups, kinds)
+        ],
+        compiler_params=pltpu.CompilerParams(vmem_limit_bytes=VMEM),
+        cost_estimate=pl.CostEstimate(
+            flops=2 * rows * width * h.shape[1], bytes_accessed=9 * 2**20, transcendentals=0
+        ),
+    )(index, h, g)
 
 
 def ffn_kernel(places, blocks, groups, h_ref, c_ref, *refs):
@@ -380,8 +441,10 @@
     n = len(groups)
     down = [p for p in places if p[0] == 2]
     base = min(p[1] for p in down)
-    y = down_call(result[-2], sources[base:], [(p[1] - base,) + p[2:] for p in down])
-    return result[:n], result[n : 2 * n], result[2 * n : 3 * n], y, result[-1]
+    project = functools.partial(
+        down_call, sources=sources[base:], places=[(p[1] - base,) + p[2:] for p in down]
+    )
+    return result[:n], result[n : 2 * n], result[2 * n : 3 * n], result[-2], project, result[-1]
 
 
 def down_kernel(places, inner_ref, *refs):
@@ -614,8 +677,7 @@
     down = gather_rest(down, count_uly)
     input_f = block_input.astype(f32)
     resid = input_f + out_own.astype(f32)
-    normed_two, inv_two = rms_stats(resid)
-    hidden_two = (normed_two * gain_ffn).astype(bf16)
+    hidden_two = (rms_stats(resid)[0] * gain_ffn).astype(bf16)
     group_hidden = lax.all_gather(hidden_two, "blk", axis=0, tiled=True)
 
     pairs = count_uly == 4 and width % HD == 0
@@ -623,7 +685,7 @@
         ffn = ffn_pieces(group_hidden, group_cot, gate_up, down, width)
     else:
         ffn = ffn_plain(group_hidden, group_cot, gate_up, down)
-    inner, gg, gu, y_part, gh_part = ffn
+    inner, gg, gu, inner_all, project, gh_part = ffn
     grad_h2 = lax.psum_scatter(gh_part, "blk", scatter_dimension=0, tiled=True)
 
     def products(lefts, rights, rows):
@@ -669,19 +731,23 @@
         sum_gate = direct(group_hidden, gg, False)
         sum_up = direct(group_hidden, gu, False)
         sum_down = direct(inner, group_cot, True)
-    grad_h2, sum_gate, sum_up, sum_down, y_part = together((grad_h2, sum_gate, sum_up, sum_down, y_part))
+    grad_h2, sum_gate, sum_up, sum_down, inner_all = together(
+        (grad_h2, sum_gate, sum_up, sum_down, inner_all)
+    )
+    y_part = project(inner_all)
     if pairs:
         sum_up = second_phase(first_phase(sum_up), False)
         sum_down = second_phase(first_phase(sum_down), True)
-    grad_h2 = grad_h2.astype(f32)
-    grad_resid = cotangent.astype(f32) + norm_back(grad_h2, normed_two, inv_two, gain_ffn)
-    group_gattn = lax.all_gather(grad_resid.astype(bf16), "blk", axis=0, tiled=True)
+    grad_resid, grad_low, gain_part = norm_call(grad_h2, cotangent, resid, gain_ffn)
+    group_gattn = lax.all_gather(grad_low, "blk", axis=0, tiled=True)
     blocks_of = lambda w: w.reshape(count_blk, rows_d, width)
-    gain_part = jnp.sum(grad_h2 * normed_two, axis=0).astype(bf16).reshape(count_blk, -1, width)
+    gain_part = gain_part.astype(bf16).reshape(count_blk, -1, width)
     gain_rows = gain_part.shape[1]
     gain_part = jnp.pad(gain_part, ((0, 0), (0, -gain_rows % 8), (0, 0)))
     grad_gate = to_hidden(jnp.concatenate([blocks_of(sum_gate), gain_part], axis=1))
-    gattn, sum_up, sum_down, grad_gate = together((group_gattn, sum_up, sum_down, grad_gate))
+    gattn, sum_up, sum_down, grad_gate, y_part = together(
+        (group_gattn, sum_up, sum_down, grad_gate, y_part)
+    )
 
     down_blocks = sum_down.reshape(width, count_blk, rows_d).transpose(1, 0, 2)
     grads_ud = to_hidden(
@@ -706,20 +772,25 @@
 
     gain_sum = jnp.sum(grad_gate[:, rows_d:][:, :gain_rows].astype(f32), axis=0)
     gain_sum = jnp.pad(gain_sum.reshape(part, 1), ((0, 0), (0, HD - 1)))
-    outs = jnp.concatenate([t_dot(attended, gattn), gain_sum], axis=1).astype(bf16)
+    outs = jnp.concatenate([t_dot(after(attended, gq), gattn), gain_sum], axis=1).astype(bf16)
     outs = split_rows(after(outs, gq))
     gkv, y_own, grads_ud, outs = together((gkv, y_own, grads_ud, outs))
     output = (resid + y_own.astype(f32)).astype(bf16)
-    gh1_part, grads = gqkv_call(
-        uly_at, hidden_one, gq, gkv, got, cos, sin, w_qkv, count_uly
-    )
+    gqkv, gh1_part = gqkv_call(gq, gkv, got, cos, sin, w_qkv)
+    grads = grads_call(uly_at, hidden_one, gqkv, count_uly)
     grad_h1 = lax.psum_scatter(gh1_part, "blk", scatter_dimension=0, tiled=True).astype(f32)
     normed_one, inv_one = rms_stats(input_f)
     input_grad = grad_resid + norm_back(grad_h1, normed_one, inv_one, gain_attn)
 
-    grads = scatter_uly(grads[0], grads[1:], count_uly).astype(bf16)
-    outs = lax.ppermute(after(outs, gh1_part), BOTH, [(j, i) for i, j in owner])
-    grads, outs = together((grads, outs))
+    if count_uly == 4:
+        one = grads[2] + xor_permute(grads[0], count_uly, 1).astype(f32)
+        two = grads[3] + xor_permute(grads[1], count_uly, 2).astype(f32)
+        one = one[0] + xor_permute(one[1].astype(bf16), count_uly, 2).astype(f32)
+        two = two[0] + xor_permute(two[1].astype(bf16), count_uly, 1).astype(f32)
+        grads = jnp.concatenate([one, two], axis=1).astype(bf16)
+    else:
+        grads = scatter_uly(grads[0][0], [g[0] for g in grads[1:]], count_uly).astype(bf16)
+    outs = lax.ppermute(after(outs, grads), BOTH, [(j, i) for i, j in owner])
     outs = outs.astype(f32)
     grad_out, grad_gain_ffn = outs[:, :dim], outs[:, dim]
     grads = lax.all_to_all(grads.reshape(count_blk, rows_w, 3 * part), "blk", 0, 0, tiled=True)

time: 677 us -> 664 us (0.981)
  waiting for transfers between devices: 353 us -> 334 us
  Pallas kernels: 91.7 us -> 99.2 us
    ppermute x34 -> x35, waiting for transfers between devices: 225 us -> 208 us  [xor_permute(): return lax.ppermute(x, 'uly', [(i, i ^ flip) for i in range(count)])]
    ppermute x34 -> x35, starting transfers between devices: 45.2 us -> 52.3 us  [xor_permute(): return lax.ppermute(x, 'uly', [(i, i ^ flip) for i in range(count)])]
    pallas_call x1 -> x3, Pallas kernels: 12.9 us -> 19.8 us  [the longest x1 8.55 us: gqkv_call(): pl.pallas_call(gqkv_kernel, grid=(rows // BR,), in_specs=[block(width), b...]
  transfers between devices with their start and end apart: 57 -> 58, of which waited for: 35 -> 37; matrix products, arithmetic and copies ran while one was open for 14% -> 14% of each run, Pallas kernels for 5% -> 7%
where the time goes in v4:
time: 664 us; the launch traced here: 654 us
  waiting for transfers between devices  334 us (50%)
  starting transfers between devices  105 us (16%)
  Pallas kernels  99.2 us (15%)
  other arithmetic  40 us (6%)
  local copies, waits for them, and re-layouts  31.8 us (5%)
  matrix products  28.4 us (4%)
  between operations  15.6 us (2%)
    ppermute x35, waiting for transfers between devices, xor_permute(): return lax.ppermute(x, 'uly', [(i, i ^ flip) for i in range(count)])  208 us
    ppermute x35, starting transfers between devices, xor_permute(): return lax.ppermute(x, 'uly', [(i, i ^ flip) for i in range(count)])  52.3 us
    pallas_call x1, Pallas kernels, ffn_call(): pl.pallas_call(functools.partial(ffn_kernel, places, blocks, groups), gri...  30.8 us
    all_to_all x1, waiting for transfers between devices, body(): qkv = lax.all_to_all(qkv, 'blk', 0, 0, tiled=True)  30.5 us
    dot_general x13, matrix products, t_dot(): lax.dot_general(left, right, (((0,), (0,)), ((), ())), preferred_element_...  28.4 us
    ppermute x1, waiting for transfers between devices, body(): over = lax.ppermute(kv[:half], 'uly', [(1, 0)])  27.5 us
    all_to_all x4, waiting for transfers between devices, body(): to_hidden = lambda w: lax.all_to_all(w, 'blk', 0, 0, tiled=True)  25.9 us
    all_to_all x4, starting transfers between devices, body(): to_hidden = lambda w: lax.all_to_all(w, 'blk', 0, 0, tiled=True)  23.9 us
  transfers between devices with their start and end apart: 58, of which 37 were waited for; matrix products, arithmetic and copies ran while one was open for 14% of the time, Pallas kernels for 7%

profile of v4, /device:TPU:0, one launch (start us, length us, event | category | flops | bytes accessed | tf_op | source)
XLA Modules:
  0.0 653.8 jit_solution(12065677275275028955)
XLA Ops:
  10.8 6.3 all-to-all-start
  17.9 30.5 %all-to-all-done = bf16[8,80,768]{2,1,0:T(8,128)(2,1)S(1)} async-done(((bf16[8,80,768]{2,1,0:T(8,128)(2,1)}), bf16[8,80,768]{2,1,0:T(8,128)(2,1)S(1)}, u32[]{:S(2)}, u32[]{:S(2)}) %all-to-all-start) | async-done | bytes 983072 | tf_op jit(solution)/shard_map/all_to_all | solution.py:634
  63.3 11.4 %collective-permute-done.2 = bf16[8,80,768]{2,1,0:T(8,128)(2,1)S(1)} collective-permute-done((bf16[8,80,768]{2,1,0:T(8,128)(2,1)}, bf16[8,80,768]{2,1,0:T(8,128)(2,1)S(1)}, u32[]{:S(2)}, u32[]{:S(2)}) %collective-permute-start.2) | collective-permute-done | bytes 983072 | tf_op jit(solution)/shard_map/ppermute | solution.py:526
  76.8 11.1 %all-to-all-start.1 = ((bf16[8,256,256]{2,1,0:T(8,128)(2,1)}), bf16[8,256,256]{2,1,0:T(8,128)(2,1)S(1)}, u32[]{:S(2)}, u32[]{:S(2)}) async-start(bf16[8,256,256]{2,1,0:T(8,128)(2,1)} %bitcast.1), calls=%async_computation.1 | async-start | bytes 2097152 | tf_op jit(solution)/shard_map/all_to_all | solution.py:645
  96.9 6.2 collective-permute-done.8
  113.5 7.5 %all-to-all-done.1.refs_5_.refs_0_ = bf16[8,256,256]{2,1,0:T(8,128)(2,1)S(1)} async-done(((bf16[8,256,256]{2,1,0:T(8,128)(2,1)}), bf16[8,256,256]{2,1,0:T(8,128)(2,1)S(1)}, u32[]{:S(2)}, u32[]{:S(2)}) %all-to-all-start.1) | async-done | bytes 1048608 | tf_op jit(solution)/shard_map/all_to_all | solution.py:645
  120.9 8.8 %shard_map.213 = (bf16[1024,2048]{1,0:T(8,128)(2,1)}, bf16[1024,256]{1,0:T(8,128)(2,1)}, bf16[1024,512]{1,0:T(8,128)(2,1)}) custom-call(bf16[1024,2048]{1,0:T(8,128)(2,1)} %all-gather.5.cloned.1.call-done.x_ref, f32[1,2048]{1,0:T(1,128)} %reshape.229.gain_ref, bf16[2048,768]{1,0:T(8,128)(2,1)} %constant_dynamic-update-slice_fusion.w_ref, ...), custom_call_target="tpu_custom_call" | custom-call | flops 3221225472 | bytes 16777216 | tf_op jit(solution)/shard_map/pallas_call | solution.py:106
  129.8 4.5 all-to-all-start.2
  134.4 3.2 collective-permute-start.11
  140.6 6.3 collective-permute-start.12
  146.9 27.5 %collective-permute-done.13 = bf16[512,512]{1,0:T(8,128)(2,1)} collective-permute-done((bf16[512,512]{1,0:T(8,128)(2,1)S(1)}, bf16[512,512]{1,0:T(8,128)(2,1)}, u32[]{:S(2)}, u32[]{:S(2)}) %collective-permute-start.13) | collective-permute-done | bytes 524320 | tf_op jit(solution)/shard_map/ppermute | solution.py:657
  178.9 4.7 collective-permute-done.10.refs_7_.refs_2_
  184.5 9.7 %collective-permute-done.14 = bf16[512,512]{1,0:T(8,128)(2,1)S(1)} collective-permute-done((bf16[512,512]{1,0:T(8,128)(2,1)}, bf16[512,512]{1,0:T(8,128)(2,1)S(1)}, u32[]{:S(2)}, u32[]{:S(2)}) %collective-permute-start.14) | collective-permute-done | bytes 524320 | tf_op jit(solution)/shard_map/ppermute | solution.py:658
  196.9 10.3 %shard_map.214 = (bf16[1024,256]{1,0:T(8,128)(2,1)}, bf16[1024,2048]{1,0:T(8,128)(2,1)}) custom-call(s32[2]{0:T(128)} %add_minimum_fusion.lo_ref, bf16[1024,256]{1,0:T(8,128)(2,1)} %get-tuple-element.100.q_ref, s32[1024,1]{1,0:T(8,128)} %copy.44.start_ref, bf16[256,2048]{1,0:T(8,128)(2,1)} %copy-done.5, bf16[1024,512]{1,0:T(8,128)(2,1)} %copy-done.12, ...), custom_call_target="tpu_custom_call" | custom-call | flops 1000000 | bytes 1000000 | tf_op jit(solution)/shard_map/pallas_call | solution.py:165
  207.1 9.9 %all-to-all-done.2.refs_0_ = bf16[8,512,256]{2,1,0:T(8,128)(2,1)} async-done(((bf16[8,512,256]{2,1,0:T(8,128)(2,1)}), bf16[8,512,256]{2,1,0:T(8,128)(2,1)}, u32[]{:S(2)}, u32[]{:S(2)}) %all-to-all-start.2) | async-done | bytes 2097184 | tf_op jit(solution)/shard_map/all_to_all | solution.py:645
  220.0 44.6 %collective-permute-done.16.refs_1_ = bf16[8,512,256]{2,1,0:T(8,128)(2,1)S(1)} collective-permute-done((bf16[8,512,256]{2,1,0:T(8,128)(2,1)}, bf16[8,512,256]{2,1,0:T(8,128)(2,1)S(1)}, u32[]{:S(2)}, u32[]{:S(2)}) %collective-permute-start.16) | collective-permute-done | bytes 2097184 | tf_op jit(solution)/shard_map/ppermute | solution.py:526
  277.6 26.8 %collective-permute-done.20.refs_8_.refs_3_ = bf16[4,256,256]{2,1,0:T(8,128)(2,1)S(1)} collective-permute-done((bf16[4,256,256]{2,1,0:T(8,128)(2,1)S(1)}, bf16[4,256,256]{2,1,0:T(8,128)(2,1)S(1)}, u32[]{:S(2)}, u32[]{:S(2)}) %collective-permute-start.20) | collective-permute-done | bytes 524320 | tf_op jit(solution)/shard_map/ppermute | solution.py:526
  307.8 7.7 %all-gather.9.cloned.1.call-done.h_ref = bf16[1024,2048]{1,0:T(8,128)(2,1)} async-done(((bf16[128,2048]{1,0:T(8,128)(2,1)}), bf16[1024,2048]{1,0:T(8,128)(2,1)}) %all-gather.9.cloned.1.call-update) | async-done | bytes 4194320 | tf_op jit(solution)/shard_map/all_gather | solution.py:681
  315.5 30.8 %shard_map.215 = (bf16[1024,512]{1,0:T(8,128)(2,1)}, bf16[1024,512]{1,0:T(8,128)(2,1)}, bf16[1024,512]{1,0:T(8,128)(2,1)}, bf16[1024,512]{1,0:T(8,128)(2,1)}, bf...) custom-call(bf16[1024,2048]{1,0:T(8,128)(2,1)} %all-gather.9.cloned., ...), custom_call_target="tpu_custom_call" | custom-call | flops 21474836480 | bytes 37748736 | tf_op jit(solution)/shard_map/pallas_call | solution.py:422
  347.5 3.0 convolution_convert_fusion.4
  370.7 5.1 collective-permute-done.22
  383.9 6.7 %collective-permute-done.23 = bf16[1024,256]{1,0:T(8,128)(2,1)S(1)} collective-permute-done((bf16[1024,256]{1,0:T(8,128)(2,1)S(1)}, bf16[1024,256]{1,0:T(8,128)(2,1)S(1)}, u32[]{:S(2)}, u32[]{:S(2)}) %collective-permute-start.23) | collective-permute-done | bytes 524320 | tf_op jit(solution)/shard_map/ppermute | solution.py:526
  395.2 3.4 shard_map.216
  404.7 4.2 all-to-all-start.3
  410.2 9.8 %shard_map.217 = bf16[1024,2048]{1,0:T(8,128)(2,1)} custom-call(bf16[1024,1024]{1,0:T(8,128)(2,1)} %get-tuple-element.142.inner_ref, bf16[8,256,256]{2,1,0:T(8,128)(2,1)} %copy-done.20, bf16[8,256,256]{2,1,0:T(8,128)(2,1)} %collective-permute-done.9.refs_6_.refs_1_, bf16[8,256,256]{2,1,0:T(8,128)(2,1)} %collective-permute-done.10.refs_7_.refs_2_, ...), custom_call_target="tpu_custom_call" | custom-call | flops 4294967296 | bytes 12582912 | tf_op jit(solution)/shard_map/pallas_call | solution.py:471
  419.9 5.1 collective-permute-done.30
  432.0 15.5 %collective-permute-done.26 = bf16[1024,512]{1,0:T(8,128)(2,1)} collective-permute-done((bf16[1024,512]{1,0:T(8,128)(2,1)}, bf16[1024,512]{1,0:T(8,128)(2,1)}, u32[]{:S(2)}, u32[]{:S(2)}) %collective-permute-start.26) | collective-permute-done | bytes 1048608 | tf_op jit(solution)/shard_map/ppermute | solution.py:526
  453.9 6.3 collective-permute-done.31
  460.5 7.3 %collective-permute-done.27 = bf16[1024,256]{1,0:T(8,128)(2,1)S(1)} collective-permute-done((bf16[1024,256]{1,0:T(8,128)(2,1)S(1)}, bf16[1024,256]{1,0:T(8,128)(2,1)S(1)}, u32[]{:S(2)}, u32[]{:S(2)}) %collective-permute-start.27) | collective-permute-done | bytes 524320 | tf_op jit(solution)/shard_map/ppermute | solution.py:526
  469.9 4.1 all-to-all-start.4
  474.1 15.0 %shard_map.218 = (bf16[1024,256]{1,0:T(8,128)(2,1)}, f32[1024,512]{1,0:T(8,128)}, bf16[1024,512]{1,0:T(8,128)(2,1)}, bf16[1024,512]{1,0:T(8,128)(2,1)}) custom-call(s32[2]{0:T(128)} %add_minimum_fusion.lo_ref, bf16[1024,256]{1,0:T(8,128)(2,1)} %get-tuple-element.100.q_ref, bf16[1024,2048]{1,0:T(8,128)(2,1)} %all-gather.11.cloned.1.call-done.ga_ref, ...), custom_call_target="tpu_custom_call" | custom-call | flops 24999999488 | bytes 20971520 | tf_op jit(solution)/shard_map/pallas_call | solution.py:241
  490.0 3.5 convolution_convert_fusion
  496.3 3.7 collective-permute-start.34
  500.0 10.6 %collective-permute-start.35 = (bf16[64,2176]{1,0:T(8,128)(2,1)S(1)}, bf16[64,2176]{1,0:T(8,128)(2,1)S(1)}, u32[]{:S(2)}, u32[]{:S(2)}) collective-permute-start(bf16[64,2176]{1,0:T(8,128)(2,1)S(1)} %get-tuple-element.179), channel_id=1, source_target_pairs={{0,16},{8,24},{16,0},{24,8},{1,17},{9,25},{17,1},{25,9},{2,18},{10... | collective-permute-start | bytes 835592 | tf_op jit(solution)/shard_map/ppermute | solution.py:526
  510.6 19.4 %collective-permute-done.34 = bf16[64,2176]{1,0:T(8,128)(2,1)S(1)} collective-permute-done((bf16[64,2176]{1,0:T(8,128)(2,1)S(1)}, bf16[64,2176]{1,0:T(8,128)(2,1)S(1)}, u32[]{:S(2)}, u32[]{:S(2)}) %collective-permute-start.34) | collective-permute-done | bytes 278560 | tf_op jit(solution)/shard_map/ppermute | solution.py:526
  530.0 4.4 collective-permute-done.35
  534.4 10.0 %collective-permute-done.36 = bf16[64,2176]{1,0:T(8,128)(2,1)S(1)} collective-permute-done((bf16[64,2176]{1,0:T(8,128)(2,1)S(1)}, bf16[64,2176]{1,0:T(8,128)(2,1)S(1)}, u32[]{:S(2)}, u32[]{:S(2)}) %collective-permute-start.36) | collective-permute-done | bytes 278560 | tf_op jit(solution)/shard_map/ppermute | solution.py:526
  545.3 8.5 %all-to-all-done.4 = bf16[8,512,256]{2,1,0:T(8,128)(2,1)S(1)} async-done(((bf16[8,512,256]{2,1,0:T(8,128)(2,1)}), bf16[8,512,256]{2,1,0:T(8,128)(2,1)S(1)}, u32[]{:S(2)}, u32[]{:S(2)}) %all-to-all-start.4) | async-done | bytes 2097184 | tf_op jit(solution)/shard_map/all_to_all | solution.py:645
  553.8 4.0 reduce-scatter.9.cloned.1.call-done
  557.8 8.6 %shard_map.219 = (bf16[1024,768]{1,0:T(8,128)(2,1)}, bf16[1024,2048]{1,0:T(8,128)(2,1)}) custom-call(bf16[1024,256]{1,0:T(8,128)(2,1)} %get-tuple-element.150.gq_ref, f32[1024,512]{1,0:T(8,128)} %get-tuple-element.156.own_ref, f32[1024,128]{1,0:T(8,128)} %get-tuple-element.191.cos_ref, f32[1024,128]{1,0:T(8,128)} %get-tuple-element.192.sin_ref, ...), custom_call_target="tpu_custom_call" | custom-call | flops 3221225472 | bytes 16777216 | tf_op jit(solution)/shard_map/pallas_call | solution.py:309
  566.4 7.8 %shard_map.220 = (bf16[2,512,384]{2,1,0:T(8,128)(2,1)}, bf16[2,512,384]{2,1,0:T(8,128)(2,1)}, f32[2,512,384]{2,1,0:T(8,128)}, f32[2,512,384]{2,1,0:T(8,128)}) custom-call(s32[1]{0:T(128)} %bitcast.16.index_ref, bf16[1024,2048]{1,0:T(8,128)(2,1)} %get-tuple-element.160.h_ref, bf16[1024,768]{1,0:T(8,128)(2,1)} %get-tuple-element.161.g_ref), custom_call_target="tpu_custom_call" | custom-call | flops 3221225472 | bytes 9437184 | tf_op jit(solution)/shard_map/pallas_call | solution.py:353
  581.7 12.7 %collective-permute-done.39 = bf16[2,512,384]{2,1,0:T(8,128)(2,1)S(1)} collective-permute-done((bf16[2,512,384]{2,1,0:T(8,128)(2,1)}, bf16[2,512,384]{2,1,0:T(8,128)(2,1)S(1)}, u32[]{:S(2)}, u32[]{:S(2)}) %collective-permute-start.39) | collective-permute-done | bytes 786464 | tf_op jit(solution)/shard_map/ppermute | solution.py:526
  602.0 4.5 collective-permute-done.40
  606.6 3.4 collective-permute-done.42
  611.1 4.1 all-to-all-start.5
  618.3 10.8 %reduce-scatter.11.cloned.1.call-done = bf16[128,2048]{1,0:T(8,128)(2,1)} async-done(((bf16[1024,2048]{1,0:T(8,128)(2,1)}), bf16[128,2048]{1,0:T(8,128)(2,1)}) %reduce-scatter.11.cloned.1.call-update) | async-done | bytes 524304 | tf_op jit(solution)/shard_map/reduce_scatter | solution.py:781
  630.5 3.0 fusion.33
  633.5 8.2 %all-to-all-done.5.got_ref = bf16[8,64,768]{2,1,0:T(8,128)(2,1)S(1)} async-done(((bf16[8,64,768]{2,1,0:T(8,128)(2,1)}), bf16[8,64,768]{2,1,0:T(8,128)(2,1)S(1)}, u32[]{:S(2)}, u32[]{:S(2)}) %all-to-all-start.5) | async-done | bytes 786464 | tf_op jit(solution)/shard_map/all_to_all | solution.py:796
  (308 shorter events, 157.5 us)
Async XLA Ops:
  10.8 37.6 %all-to-all-start = ((bf16[8,80,768]{2,1,0:T(8,128)(2,1)}), bf16[8,80,768]{2,1,0:T(8,128)(2,1)S(1)}, u32[]{:S(2)}, u32[]{:S(2)}) async-start(bf16[8,80,768]{2,1,0:T(8,128)(2,1)} %shard_map.212), calls=%async_computation | async-start | bytes 1966080 | tf_op jit(solution)/shard_map/all_to_all | solution.py:634
  17.1 103.8 %all-gather.5.cloned.1.call-start = ((), (), s32[]{:S(2)}) async-start(), calls=%async_computation.10 | async-start | bytes 4718592 | tf_op jit(solution)/shard_map/all_gather | solution.py:635
  53.9 20.8 %collective-permute-start.2 = (bf16[8,80,768]{2,1,0:T(8,128)(2,1)}, bf16[8,80,768]{2,1,0:T(8,128)(2,1)S(1)}, u32[]{:S(2)}, u32[]{:S(2)}) collective-permute-start(bf16[8,80,768]{2,1,0:T(8,128)(2,1)} %copy-done.6), channel_id=1, source_target_pairs={{0,16},{8,24},{16,0},{24,8},{1,17},{9,25},{17,1},{25,9},{2,18},{10... | collective-permute-start | bytes 2949128 | tf_op jit(solution)/shard_map/ppermute | solution.py:526
  53.9 22.9 %collective-permute-start.1 = (bf16[8,80,768]{2,1,0:T(8,128)(2,1)}, bf16[8,80,768]{2,1,0:T(8,128)(2,1)}, u32[]{:S(2)}, u32[]{:S(2)}) collective-permute-start(bf16[8,80,768]{2,1,0:T(8,128)(2,1)} %copy-done.6), channel_id=1, source_target_pairs={{0,8},{8,0},{16,24},{24,16},{1,9},{9,1},{17,25},{25,17},{2,10},{10... | collective-permute-start | bytes 2949128 | tf_op jit(solution)/shard_map/ppermute | solution.py:526
  74.7 19.6 %collective-permute-start.3 = (bf16[4,80,768]{2,1,0:T(8,128)(2,1)S(1)}, bf16[4,80,768]{2,1,0:T(8,128)(2,1)}, u32[]{:S(2)}, u32[]{:S(2)}) collective-permute-start(bf16[4,80,768]{2,1,0:T(8,128)(2,1)S(1)} %slice.208), channel_id=1, source_target_pairs={{0,8},{8,0},{16,24},{24,16},{1,9},{9,1},{17,25},{25,17},{2,10},{10... | collective-permute-start | bytes 1474568 | tf_op jit(solution)/shard_map/ppermute | solution.py:526
  76.8 44.1 %all-to-all-start.1 = ((bf16[8,256,256]{2,1,0:T(8,128)(2,1)}), bf16[8,256,256]{2,1,0:T(8,128)(2,1)S(1)}, u32[]{:S(2)}, u32[]{:S(2)}) async-start(bf16[8,256,256]{2,1,0:T(8,128)(2,1)} %bitcast.1), calls=%async_computation.1 | async-start | bytes 2097152 | tf_op jit(solution)/shard_map/all_to_all | solution.py:645
  87.9 129.2 %all-gather.7.cloned.1.call-start = ((), (), s32[]{:S(2)}) async-start(), calls=%async_computation.11 | async-start | bytes 4718592 | tf_op jit(solution)/shard_map/all_gather | solution.py:668
  129.8 87.3 %all-to-all-start.2 = ((bf16[8,512,256]{2,1,0:T(8,128)(2,1)}), bf16[8,512,256]{2,1,0:T(8,128)(2,1)}, u32[]{:S(2)}, u32[]{:S(2)}) async-start(bf16[8,512,256]{2,1,0:T(8,128)(2,1)} %pad_maximum_fusion), calls=%async_computation.2 | async-start | bytes 4194304 | tf_op jit(solution)/shard_map/all_to_all | solution.py:645
  134.3 131.6 %reduce-scatter.5.cloned.1.call-start = ((), (), s32[]{:S(2)}) async-start(), calls=%async_computation.12 | async-start | bytes 4718592 | tf_op jit(solution)/shard_map/reduce_scatter | solution.py:674
  134.4 41.4 %collective-permute-start.11 = (bf16[1024,512]{1,0:T(8,128)(2,1)S(1)}, bf16[1024,512]{1,0:T(8,128)(2,1)S(1)}, u32[]{:S(2)}, u32[]{:S(2)}) collective-permute-start(bf16[1024,512]{1,0:T(8,128)(2,1)S(1)} %copy-done.11), channel_id=1, source_target_pairs={{0,16},{8,24},{1,17},{9,25},{2,18},{10,26},{3,19},{11,27},{4,20},{... | collective-permute-start | bytes 3145736 | tf_op jit(solution)/shard_map/ppermute | solution.py:655
  137.6 46.0 %collective-permute-start.10 = (bf16[8,256,256]{2,1,0:T(8,128)(2,1)}, bf16[8,256,256]{2,1,0:T(8,128)(2,1)}, u32[]{:S(2)}, u32[]{:S(2)}) collective-permute-start(bf16[8,256,256]{2,1,0:T(8,128)(2,1)} %copy-done.20), channel_id=1, source_target_pairs={{0,16},{8,24},{16,0},{24,8},{1,17},{9,25},{17,1},{25,9},{2,18},{10... | collective-permute-start | bytes 3145736 | tf_op jit(solution)/shard_map/ppermute | solution.py:526
  137.7 45.9 %collective-permute-start.9 = (bf16[8,256,256]{2,1,0:T(8,128)(2,1)}, bf16[8,256,256]{2,1,0:T(8,128)(2,1)}, u32[]{:S(2)}, u32[]{:S(2)}) collective-permute-start(bf16[8,256,256]{2,1,0:T(8,128)(2,1)} %copy-done.20), channel_id=1, source_target_pairs={{0,8},{8,0},{16,24},{24,16},{1,9},{9,1},{17,25},{25,17},{2,10},{10... | collective-permute-start | bytes 3145736 | tf_op jit(solution)/shard_map/ppermute | solution.py:526
  139.3 35.1 %collective-permute-start.13 = (bf16[512,512]{1,0:T(8,128)(2,1)S(1)}, bf16[512,512]{1,0:T(8,128)(2,1)}, u32[]{:S(2)}, u32[]{:S(2)}) collective-permute-start(bf16[512,512]{1,0:T(8,128)(2,1)S(1)} %slice.175), channel_id=1, source_target_pairs={{8,0},{9,1},{10,2},{11,3},{12,4},{13,5},{14,6},{15,7}} | collective-permute-start | bytes 1572872 | tf_op jit(solution)/shard_map/ppermute | solution.py:657
  140.6 44.0 %collective-permute-start.12 = (bf16[1024,512]{1,0:T(8,128)(2,1)S(1)}, bf16[1024,512]{1,0:T(8,128)(2,1)}, u32[]{:S(2)}, u32[]{:S(2)}) collective-permute-start(bf16[1024,512]{1,0:T(8,128)(2,1)S(1)} %copy-done.11), channel_id=1, source_target_pairs={{0,8},{16,24},{1,9},{17,25},{2,10},{18,26},{3,11},{19,27},{4,12},{... | collective-permute-start | bytes 3145736 | tf_op jit(solution)/shard_map/ppermute | solution.py:656
  174.4 19.8 %collective-permute-start.14 = (bf16[512,512]{1,0:T(8,128)(2,1)}, bf16[512,512]{1,0:T(8,128)(2,1)S(1)}, u32[]{:S(2)}, u32[]{:S(2)}) collective-permute-start(bf16[512,512]{1,0:T(8,128)(2,1)} %collective-permute-done.13), channel_id=1, source_target_pairs={{0,16},{1,17},{2,18},{3,19},{4,20},{5,21},{6,22},{7,23}} | collective-permute-start | bytes 1572872 | tf_op jit(solution)/shard_map/ppermute | solution.py:658
  175.8 18.4 %collective-permute-start.15 = (bf16[512,512]{1,0:T(8,128)(2,1)S(1)}, bf16[512,512]{1,0:T(8,128)(2,1)}, u32[]{:S(2)}, u32[]{:S(2)}) collective-permute-start(bf16[512,512]{1,0:T(8,128)(2,1)S(1)} %slice.223), channel_id=1, source_target_pairs={{24,16},{25,17},{26,18},{27,19},{28,20},{29,21},{30,22},{31,23}} | collective-permute-start | bytes 1572872 | tf_op jit(solution)/shard_map/ppermute | solution.py:659
  217.1 98.4 %all-gather.9.cloned.1.call-start = ((), (), s32[]{:S(2)}) async-start(), calls=%async_computation.13 | async-start | bytes 4718592 | tf_op jit(solution)/shard_map/all_gather | solution.py:681
  217.1 47.4 %collective-permute-start.16 = (bf16[8,512,256]{2,1,0:T(8,128)(2,1)}, bf16[8,512,256]{2,1,0:T(8,128)(2,1)S(1)}, u32[]{:S(2)}, u32[]{:S(2)}) collective-permute-start(bf16[8,512,256]{2,1,0:T(8,128)(2,1)} %all-to-all-done.2.refs_0_), channel_id=1, source_target_pairs={{0,8},{8,0},{16,24},{24,16},{1,9},{9,1},{17,25},{25,17},{2,10},{10... | collective-permute-start | bytes 6291464 | tf_op jit(solution)/shard_map/ppermute | solution.py:526
  218.5 47.2 %collective-permute-start.17 = (bf16[8,512,256]{2,1,0:T(8,128)(2,1)}, bf16[8,512,256]{2,1,0:T(8,128)(2,1)}, u32[]{:S(2)}, u32[]{:S(2)}) collective-permute-start(bf16[8,512,256]{2,1,0:T(8,128)(2,1)} %all-to-all-done.2.refs_0_), channel_id=1, source_target_pairs={{0,16},{8,24},{16,0},{24,8},{1,17},{9,25},{17,1},{25,9},{2,18},{10... | collective-permute-start | bytes 6291464 | tf_op jit(solution)/shard_map/ppermute | solution.py:526
  269.7 125.5 %reduce-scatter.7.cloned.1.call-start = ((), (), s32[]{:S(2)}) async-start(), calls=%async_computation.14 | async-start | bytes 4718592 | tf_op jit(solution)/shard_map/reduce_scatter | solution.py:689
  269.8 37.2 %collective-permute-start.18 = (bf16[4,512,256]{2,1,0:T(8,128)(2,1)S(1)}, bf16[4,512,256]{2,1,0:T(8,128)(2,1)S(1)}, u32[]{:S(2)}, u32[]{:S(2)}) collective-permute-start(bf16[4,512,256]{2,1,0:T(8,128)(2,1)S(1)} %slice.178), channel_id=1, source_target_pairs={{0,16},{8,24},{16,0},{24,8},{1,17},{9,25},{17,1},{25,9},{2,18},{10... | collective-permute-start | bytes 3145736 | tf_op jit(solution)/shard_map/ppermute | solution.py:526
  272.6 35.1 %collective-permute-start.19 = (bf16[4,512,256]{2,1,0:T(8,128)(2,1)S(1)}, bf16[4,512,256]{2,1,0:T(8,128)(2,1)S(1)}, u32[]{:S(2)}, u32[]{:S(2)}) collective-permute-start(bf16[4,512,256]{2,1,0:T(8,128)(2,1)S(1)} %slice.179), channel_id=1, source_target_pairs={{0,8},{8,0},{16,24},{24,16},{1,9},{9,1},{17,25},{25,17},{2,10},{10... | collective-permute-start | bytes 3145736 | tf_op jit(solution)/shard_map/ppermute | solution.py:526
  275.3 29.2 %collective-permute-start.20 = (bf16[4,256,256]{2,1,0:T(8,128)(2,1)S(1)}, bf16[4,256,256]{2,1,0:T(8,128)(2,1)S(1)}, u32[]{:S(2)}, u32[]{:S(2)}) collective-permute-start(bf16[4,256,256]{2,1,0:T(8,128)(2,1)S(1)} %slice.180), channel_id=1, source_target_pairs={{0,16},{8,24},{16,0},{24,8},{1,17},{9,25},{17,1},{25,9},{2,18},{10... | collective-permute-start | bytes 1572872 | tf_op jit(solution)/shard_map/ppermute | solution.py:526
  277.0 30.0 %collective-permute-start.21 = (bf16[4,256,256]{2,1,0:T(8,128)(2,1)S(1)}, bf16[4,256,256]{2,1,0:T(8,128)(2,1)S(1)}, u32[]{:S(2)}, u32[]{:S(2)}) collective-permute-start(bf16[4,256,256]{2,1,0:T(8,128)(2,1)S(1)} %slice.181), channel_id=1, source_target_pairs={{0,8},{8,0},{16,24},{24,16},{1,9},{9,1},{17,25},{25,17},{2,10},{10... | collective-permute-start | bytes 1572872 | tf_op jit(solution)/shard_map/ppermute | solution.py:526
  346.3 122.1 %all-gather.11.cloned.1.call-start = ((), (), s32[]{:S(2)}) async-start(), calls=%async_computation.15 | async-start | bytes 4718592 | tf_op jit(solution)/shard_map/all_gather | solution.py:742
  350.5 25.4 %collective-permute-start.22 = (bf16[1024,512]{1,0:T(8,128)(2,1)S(1)}, bf16[1024,512]{1,0:T(8,128)(2,1)S(1)}, u32[]{:S(2)}, u32[]{:S(2)}) collective-permute-start(bf16[1024,512]{1,0:T(8,128)(2,1)S(1)} %convolution_convert_fusion.4), channel_id=1, source_target_pairs={{0,8},{8,0},{16,24},{24,16},{1,9},{9,1},{17,25},{25,17},{2,10},{10... | collective-permute-start | bytes 3145736 | tf_op jit(solution)/shard_map/ppermute | solution.py:526
  353.3 25.4 %collective-permute-start.24 = (bf16[1024,512]{1,0:T(8,128)(2,1)S(1)}, bf16[1024,512]{1,0:T(8,128)(2,1)S(1)}, u32[]{:S(2)}, u32[]{:S(2)}) collective-permute-start(bf16[1024,512]{1,0:T(8,128)(2,1)S(1)} %convolution_convert_fusion.3), channel_id=1, source_target_pairs={{0,16},{8,24},{16,0},{24,8},{1,17},{9,25},{17,1},{25,9},{2,18},{10... | collective-permute-start | bytes 3145736 | tf_op jit(solution)/shard_map/ppermute | solution.py:526
  398.6 26.5 %collective-permute-start.30 = (bf16[512,1024]{1,0:T(8,128)(2,1)}, bf16[512,1024]{1,0:T(8,128)(2,1)}, u32[]{:S(2)}, u32[]{:S(2)}) collective-permute-start(bf16[512,1024]{1,0:T(8,128)(2,1)} %fusion.10), channel_id=1, source_target_pairs={{0,8},{8,0},{16,24},{24,16},{1,9},{9,1},{17,25},{25,17},{2,10},{10... | collective-permute-start | bytes 3145736 | tf_op jit(solution)/shard_map/ppermute | solution.py:526
  400.1 28.7 %collective-permute-start.32 = (bf16[512,1024]{1,0:T(8,128)(2,1)}, bf16[512,1024]{1,0:T(8,128)(2,1)}, u32[]{:S(2)}, u32[]{:S(2)}) collective-permute-start(bf16[512,1024]{1,0:T(8,128)(2,1)} %fusion.13), channel_id=1, source_target_pairs={{0,16},{8,24},{16,0},{24,8},{1,17},{9,25},{17,1},{25,9},{2,18},{10... | collective-permute-start | bytes 3145736 | tf_op jit(solution)/shard_map/ppermute | solution.py:526
  404.7 63.6 %all-to-all-start.3 = ((bf16[8,264,256]{2,1,0:T(8,128)(2,1)}), bf16[8,264,256]{2,1,0:T(8,128)(2,1)}, u32[]{:S(2)}, u32[]{:S(2)}) async-start(bf16[8,264,256]{2,1,0:T(8,128)(2,1)} %fusion.29), calls=%async_computation.5 | async-start | bytes 2162688 | tf_op jit(solution)/shard_map/all_to_all | solution.py:645
  409.0 148.8 %reduce-scatter.9.cloned.1.call-start = ((), (), s32[]{:S(2)}) async-start(), calls=%async_computation.16 | async-start | bytes 4718592 | tf_op jit(solution)/shard_map/reduce_scatter | solution.py:765
  409.0 38.5 %collective-permute-start.26 = (bf16[1024,512]{1,0:T(8,128)(2,1)}, bf16[1024,512]{1,0:T(8,128)(2,1)}, u32[]{:S(2)}, u32[]{:S(2)}) collective-permute-start(bf16[1024,512]{1,0:T(8,128)(2,1)} %convolution_convert_fusion.2), channel_id=1, source_target_pairs={{0,8},{8,0},{16,24},{24,16},{1,9},{9,1},{17,25},{25,17},{2,10},{10... | collective-permute-start | bytes 3145736 | tf_op jit(solution)/shard_map/ppermute | solution.py:526
  409.6 41.1 %collective-permute-start.28 = (bf16[1024,512]{1,0:T(8,128)(2,1)}, bf16[1024,512]{1,0:T(8,128)(2,1)}, u32[]{:S(2)}, u32[]{:S(2)}) collective-permute-start(bf16[1024,512]{1,0:T(8,128)(2,1)} %convolution_convert_fusion.1), channel_id=1, source_target_pairs={{0,16},{8,24},{16,0},{24,8},{1,17},{9,25},{17,1},{25,9},{2,18},{10... | collective-permute-start | bytes 3145736 | tf_op jit(solution)/shard_map/ppermute | solution.py:526
  427.3 32.8 %collective-permute-start.31 = (bf16[256,1024]{1,0:T(8,128)(2,1)S(1)}, bf16[256,1024]{1,0:T(8,128)(2,1)S(1)}, u32[]{:S(2)}, u32[]{:S(2)}) collective-permute-start(bf16[256,1024]{1,0:T(8,128)(2,1)S(1)} %slice.320), channel_id=1, source_target_pairs={{0,16},{8,24},{16,0},{24,8},{1,17},{9,25},{17,1},{25,9},{2,18},{10... | collective-permute-start | bytes 1572872 | tf_op jit(solution)/shard_map/ppermute | solution.py:526
  430.5 29.8 %collective-permute-start.33 = (bf16[256,1024]{1,0:T(8,128)(2,1)S(1)}, bf16[256,1024]{1,0:T(8,128)(2,1)S(1)}, u32[]{:S(2)}, u32[]{:S(2)}) collective-permute-start(bf16[256,1024]{1,0:T(8,128)(2,1)S(1)} %slice.319), channel_id=1, source_target_pairs={{0,8},{8,0},{16,24},{24,16},{1,9},{9,1},{17,25},{25,17},{2,10},{10... | collective-permute-start | bytes 1572872 | tf_op jit(solution)/shard_map/ppermute | solution.py:526
  449.2 18.7 %collective-permute-start.27 = (bf16[1024,256]{1,0:T(8,128)(2,1)S(1)}, bf16[1024,256]{1,0:T(8,128)(2,1)S(1)}, u32[]{:S(2)}, u32[]{:S(2)}) collective-permute-start(bf16[1024,256]{1,0:T(8,128)(2,1)S(1)} %slice.322), channel_id=1, source_target_pairs={{0,16},{8,24},{16,0},{24,8},{1,17},{9,25},{17,1},{25,9},{2,18},{10... | collective-permute-start | bytes 1572872 | tf_op jit(solution)/shard_map/ppermute | solution.py:526
  452.3 15.7 %collective-permute-start.29 = (bf16[1024,256]{1,0:T(8,128)(2,1)S(1)}, bf16[1024,256]{1,0:T(8,128)(2,1)S(1)}, u32[]{:S(2)}, u32[]{:S(2)}) collective-permute-start(bf16[1024,256]{1,0:T(8,128)(2,1)S(1)} %slice.321), channel_id=1, source_target_pairs={{0,8},{8,0},{16,24},{24,16},{1,9},{9,1},{17,25},{25,17},{2,10},{10... | collective-permute-start | bytes 1572872 | tf_op jit(solution)/shard_map/ppermute | solution.py:526
  469.9 83.8 %all-to-all-start.4 = ((bf16[8,512,256]{2,1,0:T(8,128)(2,1)}), bf16[8,512,256]{2,1,0:T(8,128)(2,1)S(1)}, u32[]{:S(2)}, u32[]{:S(2)}) async-start(bf16[8,512,256]{2,1,0:T(8,128)(2,1)} %pad_maximum_fusion.1), calls=%async_computation.7 | async-start | bytes 4194304 | tf_op jit(solution)/shard_map/all_to_all | solution.py:645
  474.0 155.1 %reduce-scatter.11.cloned.1.call-start = ((), (), s32[]{:S(2)}) async-start(), calls=%async_computation.17 | async-start | bytes 4718592 | tf_op jit(solution)/shard_map/reduce_scatter | solution.py:781
  493.6 64.2 %collective-permute-start.37 = (bf16[1024,512]{1,0:T(8,128)(2,1)}, bf16[1024,512]{1,0:T(8,128)(2,1)}, u32[]{:S(2)}, u32[]{:S(2)}) collective-permute-start(bf16[1024,512]{1,0:T(8,128)(2,1)} %get-tuple-element.157), channel_id=1, source_target_pairs={{16,0},{24,8},{17,1},{25,9},{18,2},{26,10},{19,3},{27,11},{20,4},{... | collective-permute-start | bytes 3145736 | tf_op jit(solution)/shard_map/ppermute | solution.py:762
  494.9 62.9 %collective-permute-start.38 = (bf16[1024,512]{1,0:T(8,128)(2,1)}, bf16[1024,512]{1,0:T(8,128)(2,1)}, u32[]{:S(2)}, u32[]{:S(2)}) collective-permute-start(bf16[1024,512]{1,0:T(8,128)(2,1)} %get-tuple-element.158), channel_id=1, source_target_pairs={{8,0},{16,8},{24,16},{9,1},{17,9},{25,17},{10,2},{18,10},{26,18},{... | collective-permute-start | bytes 3145736 | tf_op jit(solution)/shard_map/ppermute | solution.py:762
  496.3 33.7 %collective-permute-start.34 = (bf16[64,2176]{1,0:T(8,128)(2,1)S(1)}, bf16[64,2176]{1,0:T(8,128)(2,1)S(1)}, u32[]{:S(2)}, u32[]{:S(2)}) collective-permute-start(bf16[64,2176]{1,0:T(8,128)(2,1)S(1)} %get-tuple-element.177), channel_id=1, source_target_pairs={{0,8},{8,0},{16,24},{24,16},{1,9},{9,1},{17,25},{25,17},{2,10},{10... | collective-permute-start | bytes 835592 | tf_op jit(solution)/shard_map/ppermute | solution.py:526
  500.0 34.4 %collective-permute-start.35 = (bf16[64,2176]{1,0:T(8,128)(2,1)S(1)}, bf16[64,2176]{1,0:T(8,128)(2,1)S(1)}, u32[]{:S(2)}, u32[]{:S(2)}) collective-permute-start(bf16[64,2176]{1,0:T(8,128)(2,1)S(1)} %get-tuple-element.179), channel_id=1, source_target_pairs={{0,16},{8,24},{16,0},{24,8},{1,17},{9,25},{17,1},{25,9},{2,18},{10... | collective-permute-start | bytes 835592 | tf_op jit(solution)/shard_map/ppermute | solution.py:526
  510.6 33.8 %collective-permute-start.36 = (bf16[64,2176]{1,0:T(8,128)(2,1)S(1)}, bf16[64,2176]{1,0:T(8,128)(2,1)S(1)}, u32[]{:S(2)}, u32[]{:S(2)}) collective-permute-start(bf16[64,2176]{1,0:T(8,128)(2,1)S(1)} %get-tuple-element.178), channel_id=1, source_target_pairs={{0,24},{8,16},{16,8},{24,0},{1,25},{9,17},{17,9},{25,1},{2,26},{10... | collective-permute-start | bytes 835592 | tf_op jit(solution)/shard_map/ppermute | solution.py:526
  574.2 20.2 %collective-permute-start.39 = (bf16[2,512,384]{2,1,0:T(8,128)(2,1)}, bf16[2,512,384]{2,1,0:T(8,128)(2,1)S(1)}, u32[]{:S(2)}, u32[]{:S(2)}) collective-permute-start(bf16[2,512,384]{2,1,0:T(8,128)(2,1)} %get-tuple-element.163), channel_id=1, source_target_pairs={{0,8},{8,0},{16,24},{24,16},{1,9},{9,1},{17,25},{25,17},{2,10},{10... | collective-permute-start | bytes 2359304 | tf_op jit(solution)/shard_map/ppermute | solution.py:526
  577.8 20.1 %collective-permute-start.41 = (bf16[2,512,384]{2,1,0:T(8,128)(2,1)}, bf16[2,512,384]{2,1,0:T(8,128)(2,1)S(1)}, u32[]{:S(2)}, u32[]{:S(2)}) collective-permute-start(bf16[2,512,384]{2,1,0:T(8,128)(2,1)} %get-tuple-element.165), channel_id=1, source_target_pairs={{0,16},{8,24},{16,0},{24,8},{1,17},{9,25},{17,1},{25,9},{2,18},{10... | collective-permute-start | bytes 2359304 | tf_op jit(solution)/shard_map/ppermute | solution.py:526
  601.4 15.4 %collective-permute-start.43 = (bf16[64,2176]{1,0:T(8,128)(2,1)S(1)}, bf16[64,2176]{1,0:T(8,128)(2,1)S(1)}, u32[]{:S(2)}, u32[]{:S(2)}) collective-permute-start(bf16[64,2176]{1,0:T(8,128)(2,1)S(1)} %copy-done.23), channel_id=1, source_target_pairs={{0,0},{8,1},{16,2},{24,3},{1,4},{9,5},{17,6},{25,7},{2,8},{10,9},{... | collective-permute-start | bytes 835592 | tf_op jit(solution)/shard_map/ppermute | solution.py:793
  611.1 30.6 %all-to-all-start.5 = ((bf16[8,64,768]{2,1,0:T(8,128)(2,1)}), bf16[8,64,768]{2,1,0:T(8,128)(2,1)S(1)}, u32[]{:S(2)}, u32[]{:S(2)}) async-start(bf16[8,64,768]{2,1,0:T(8,128)(2,1)} %pad_maximum_fusion.5), calls=%async_computation.9 | async-start | bytes 1572864 | tf_op jit(solution)/shard_map/all_to_all | solution.py:796
  (56 other events, 605.0 us)
Sparse Core Ops, SparseCore 0:
  48.6 57.9 all-gather.4
  129.9 84.0 all-gather.6
  217.2 48.6 reduce-scatter.4
  269.8 45.6 all-gather.8
  346.4 48.7 reduce-scatter.6
  398.7 68.2 all-gather.10
  469.3 88.4 reduce-scatter.8
  566.5 62.5 reduce-scatter.10

commit v5 on v4

--- a/solution.py
+++ b/solution.py
@@ -648,8 +648,9 @@
         after(w_down.reshape(count_blk, width, rows_d), *[p[0] for p in qkv_pieces[1:3]])
     )
     wo = in_order(gather_uly(after(wo, qkv_pieces[3][-1]), count_uly), uly_index)
-    group_in, down, gate_up, wo = together((group_in, down, gate_up, wo))
+    group_in, gate_up, wo = together((group_in, gate_up, wo))
     hidden_one, query, kv = qkv_call(group_in, gain_attn, w_qkv, cos, sin)
+    kv, query, down = together((kv, query, down))
     if count_uly == 4 and back == 2:
         half = group // 2
         two = lax.ppermute(kv, "uly", [(0, 2), (1, 3)])

time: 664 us -> 656 us (0.988)
  waiting for transfers between devices: 334 us -> 321 us
    all_to_all x4, waiting for transfers between devices: 25.9 us -> 17.1 us  [body(): to_hidden = lambda w: lax.all_to_all(w, 'blk', 0, 0, tiled=True)]
  transfers between devices with their start and end apart: 58 -> 58, of which waited for: 37 -> 36; matrix products, arithmetic and copies ran while one was open for 14% -> 14% of each run, Pallas kernels for 7% -> 8%
where the time goes in v5:
time: 656 us; the launch traced here: 646 us
  waiting for transfers between devices  321 us (49%)
  starting transfers between devices  110 us (17%)
  Pallas kernels  99 us (15%)
  other arithmetic  40 us (6%)
  local copies, waits for them, and re-layouts  32.4 us (5%)
  matrix products  28.5 us (4%)
  between operations  15.6 us (2%)
    ppermute x35, waiting for transfers between devices, xor_permute(): return lax.ppermute(x, 'uly', [(i, i ^ flip) for i in range(count)])  204 us
    ppermute x35, starting transfers between devices, xor_permute(): return lax.ppermute(x, 'uly', [(i, i ^ flip) for i in range(count)])  56.1 us
    pallas_call x1, Pallas kernels, ffn_call(): pl.pallas_call(functools.partial(ffn_kernel, places, blocks, groups), gri...  30.7 us
    all_to_all x1, waiting for transfers between devices, body(): qkv = lax.all_to_all(qkv, 'blk', 0, 0, tiled=True)  29.9 us
    dot_general x13, matrix products, t_dot(): lax.dot_general(left, right, (((0,), (0,)), ((), ())), preferred_element_...  28.5 us
    ppermute x1, waiting for transfers between devices, body(): over = lax.ppermute(kv[:half], 'uly', [(1, 0)])  27.4 us
    all_to_all x4, starting transfers between devices, body(): to_hidden = lambda w: lax.all_to_all(w, 'blk', 0, 0, tiled=True)  24.6 us
    all_to_all x4, waiting for transfers between devices, body(): to_hidden = lambda w: lax.all_to_all(w, 'blk', 0, 0, tiled=True)  17.1 us
  transfers between devices with their start and end apart: 58, of which 36 were waited for; matrix products, arithmetic and copies ran while one was open for 14% of the time, Pallas kernels for 8%

profile of v5, /device:TPU:0, one launch (start us, length us, event | category | flops | bytes accessed | tf_op | source)
XLA Modules:
  0.0 645.9 jit_solution(5495602359801111582)
XLA Ops:
  10.8 6.3 all-to-all-start
  18.5 29.9 %all-to-all-done = bf16[8,80,768]{2,1,0:T(8,128)(2,1)S(1)} async-done(((bf16[8,80,768]{2,1,0:T(8,128)(2,1)}), bf16[8,80,768]{2,1,0:T(8,128)(2,1)S(1)}, u32[]{:S(2)}, u32[]{:S(2)}) %all-to-all-start) | async-done | bytes 983072 | tf_op jit(solution)/shard_map/all_to_all | solution.py:634
  60.8 13.8 %collective-permute-done.1 = bf16[8,80,768]{2,1,0:T(8,128)(2,1)S(1)} collective-permute-done((bf16[8,80,768]{2,1,0:T(8,128)(2,1)}, bf16[8,80,768]{2,1,0:T(8,128)(2,1)S(1)}, u32[]{:S(2)}, u32[]{:S(2)}) %collective-permute-start.1) | collective-permute-done | bytes 983072 | tf_op jit(solution)/shard_map/ppermute | solution.py:526
  78.5 11.8 %all-to-all-start.1 = ((bf16[8,256,256]{2,1,0:T(8,128)(2,1)}), bf16[8,256,256]{2,1,0:T(8,128)(2,1)S(1)}, u32[]{:S(2)}, u32[]{:S(2)}) async-start(bf16[8,256,256]{2,1,0:T(8,128)(2,1)} %bitcast.10), calls=%async_computation.1 | async-start | bytes 2097152 | tf_op jit(solution)/shard_map/all_to_all | solution.py:645
  104.7 3.2 collective-permute-done.5
  109.5 8.8 %shard_map.213 = (bf16[1024,2048]{1,0:T(8,128)(2,1)}, bf16[1024,256]{1,0:T(8,128)(2,1)}, bf16[1024,512]{1,0:T(8,128)(2,1)}) custom-call(bf16[1024,2048]{1,0:T(8,128)(2,1)} %all-gather.5.cloned.1.call-done.x_ref, f32[1,2048]{1,0:T(1,128)} %reshape.229.gain_ref, bf16[2048,768]{1,0:T(8,128)(2,1)} %constant_dynamic-update-slice_fusion.w_ref, ...), custom_call_target="tpu_custom_call" | custom-call | flops 3221225472 | bytes 16777216 | tf_op jit(solution)/shard_map/pallas_call | solution.py:106
  118.3 2.8 all-to-all-done.1.refs_5_.refs_0_
  122.1 4.4 all-to-all-start.2
  126.5 3.2 collective-permute-start.11
  132.7 6.4 collective-permute-start.12
  139.1 27.4 %collective-permute-done.13 = bf16[512,512]{1,0:T(8,128)(2,1)} collective-permute-done((bf16[512,512]{1,0:T(8,128)(2,1)S(1)}, bf16[512,512]{1,0:T(8,128)(2,1)}, u32[]{:S(2)}, u32[]{:S(2)}) %collective-permute-start.13) | collective-permute-done | bytes 524320 | tf_op jit(solution)/shard_map/ppermute | solution.py:658
  171.1 4.6 collective-permute-done.10.refs_7_.refs_2_
  176.7 9.7 %collective-permute-done.14 = bf16[512,512]{1,0:T(8,128)(2,1)S(1)} collective-permute-done((bf16[512,512]{1,0:T(8,128)(2,1)}, bf16[512,512]{1,0:T(8,128)(2,1)S(1)}, u32[]{:S(2)}, u32[]{:S(2)}) %collective-permute-start.14) | collective-permute-done | bytes 524320 | tf_op jit(solution)/shard_map/ppermute | solution.py:659
  189.0 10.3 %shard_map.214 = (bf16[1024,256]{1,0:T(8,128)(2,1)}, bf16[1024,2048]{1,0:T(8,128)(2,1)}) custom-call(s32[2]{0:T(128)} %add_minimum_fusion.lo_ref, bf16[1024,256]{1,0:T(8,128)(2,1)} %get-tuple-element.104.q_ref, s32[1024,1]{1,0:T(8,128)} %copy.44.start_ref, bf16[256,2048]{1,0:T(8,128)(2,1)} %copy-done.5, bf16[1024,512]{1,0:T(8,128)(2,1)} %copy-done.15, ...), custom_call_target="tpu_custom_call" | custom-call | flops 1000000 | bytes 1000000 | tf_op jit(solution)/shard_map/pallas_call | solution.py:165
  199.2 10.0 %all-to-all-done.2.refs_0_ = bf16[8,512,256]{2,1,0:T(8,128)(2,1)} async-done(((bf16[8,512,256]{2,1,0:T(8,128)(2,1)}), bf16[8,512,256]{2,1,0:T(8,128)(2,1)}, u32[]{:S(2)}, u32[]{:S(2)}) %all-to-all-start.2) | async-done | bytes 2097184 | tf_op jit(solution)/shard_map/all_to_all | solution.py:645
  212.2 44.6 %collective-permute-done.16.refs_1_ = bf16[8,512,256]{2,1,0:T(8,128)(2,1)S(1)} collective-permute-done((bf16[8,512,256]{2,1,0:T(8,128)(2,1)}, bf16[8,512,256]{2,1,0:T(8,128)(2,1)S(1)}, u32[]{:S(2)}, u32[]{:S(2)}) %collective-permute-start.16) | collective-permute-done | bytes 2097184 | tf_op jit(solution)/shard_map/ppermute | solution.py:526
  269.8 26.8 %collective-permute-done.20.refs_8_.refs_3_ = bf16[4,256,256]{2,1,0:T(8,128)(2,1)S(1)} collective-permute-done((bf16[4,256,256]{2,1,0:T(8,128)(2,1)S(1)}, bf16[4,256,256]{2,1,0:T(8,128)(2,1)S(1)}, u32[]{:S(2)}, u32[]{:S(2)}) %collective-permute-start.20) | collective-permute-done | bytes 524320 | tf_op jit(solution)/shard_map/ppermute | solution.py:526
  299.9 7.7 %all-gather.9.cloned.1.call-done.h_ref = bf16[1024,2048]{1,0:T(8,128)(2,1)} async-done(((bf16[128,2048]{1,0:T(8,128)(2,1)}), bf16[1024,2048]{1,0:T(8,128)(2,1)}) %all-gather.9.cloned.1.call-update) | async-done | bytes 4194320 | tf_op jit(solution)/shard_map/all_gather | solution.py:682
  307.6 30.7 %shard_map.215 = (bf16[1024,512]{1,0:T(8,128)(2,1)}, bf16[1024,512]{1,0:T(8,128)(2,1)}, bf16[1024,512]{1,0:T(8,128)(2,1)}, bf16[1024,512]{1,0:T(8,128)(2,1)}, bf...) custom-call(bf16[1024,2048]{1,0:T(8,128)(2,1)} %all-gather.9.cloned., ...), custom_call_target="tpu_custom_call" | custom-call | flops 21474836480 | bytes 37748736 | tf_op jit(solution)/shard_map/pallas_call | solution.py:422
  339.6 3.0 convolution_convert_fusion.4
  362.9 5.1 collective-permute-done.22
  376.0 6.7 %collective-permute-done.23 = bf16[1024,256]{1,0:T(8,128)(2,1)S(1)} collective-permute-done((bf16[1024,256]{1,0:T(8,128)(2,1)S(1)}, bf16[1024,256]{1,0:T(8,128)(2,1)S(1)}, u32[]{:S(2)}, u32[]{:S(2)}) %collective-permute-start.23) | collective-permute-done | bytes 524320 | tf_op jit(solution)/shard_map/ppermute | solution.py:526
  387.2 3.4 shard_map.216
  396.8 4.3 all-to-all-start.3
  402.3 9.7 %shard_map.217 = bf16[1024,2048]{1,0:T(8,128)(2,1)} custom-call(bf16[1024,1024]{1,0:T(8,128)(2,1)} %get-tuple-element.146.inner_ref, bf16[8,256,256]{2,1,0:T(8,128)(2,1)} %copy-done.23, bf16[8,256,256]{2,1,0:T(8,128)(2,1)} %collective-permute-done.9.refs_6_.refs_1_, bf16[8,256,256]{2,1,0:T(8,128)(2,1)} %collective-permute-done.10.refs_7_.refs_2_, ...), custom_call_target="tpu_custom_call" | custom-call | flops 4294967296 | bytes 12582912 | tf_op jit(solution)/shard_map/pallas_call | solution.py:471
  412.0 5.2 collective-permute-done.30
  424.1 15.5 %collective-permute-done.26 = bf16[1024,512]{1,0:T(8,128)(2,1)} collective-permute-done((bf16[1024,512]{1,0:T(8,128)(2,1)}, bf16[1024,512]{1,0:T(8,128)(2,1)}, u32[]{:S(2)}, u32[]{:S(2)}) %collective-permute-start.26) | collective-permute-done | bytes 1048608 | tf_op jit(solution)/shard_map/ppermute | solution.py:526
  446.0 6.3 collective-permute-done.31
  452.6 7.3 %collective-permute-done.27 = bf16[1024,256]{1,0:T(8,128)(2,1)S(1)} collective-permute-done((bf16[1024,256]{1,0:T(8,128)(2,1)S(1)}, bf16[1024,256]{1,0:T(8,128)(2,1)S(1)}, u32[]{:S(2)}, u32[]{:S(2)}) %collective-permute-start.27) | collective-permute-done | bytes 524320 | tf_op jit(solution)/shard_map/ppermute | solution.py:526
  462.0 4.1 all-to-all-start.4
  466.2 15.0 %shard_map.218 = (bf16[1024,256]{1,0:T(8,128)(2,1)}, f32[1024,512]{1,0:T(8,128)}, bf16[1024,512]{1,0:T(8,128)(2,1)}, bf16[1024,512]{1,0:T(8,128)(2,1)}) custom-call(s32[2]{0:T(128)} %add_minimum_fusion.lo_ref, bf16[1024,256]{1,0:T(8,128)(2,1)} %get-tuple-element.104.q_ref, bf16[1024,2048]{1,0:T(8,128)(2,1)} %all-gather.11.cloned.1.call-done.ga_ref, ...), custom_call_target="tpu_custom_call" | custom-call | flops 24999999488 | bytes 20971520 | tf_op jit(solution)/shard_map/pallas_call | solution.py:241
  482.1 3.5 convolution_convert_fusion
  488.4 5.6 collective-permute-start.34
  494.0 12.7 %collective-permute-start.35 = (bf16[64,2176]{1,0:T(8,128)(2,1)S(1)}, bf16[64,2176]{1,0:T(8,128)(2,1)S(1)}, u32[]{:S(2)}, u32[]{:S(2)}) collective-permute-start(bf16[64,2176]{1,0:T(8,128)(2,1)S(1)} %get-tuple-element.183), channel_id=1, source_target_pairs={{0,16},{8,24},{16,0},{24,8},{1,17},{9,25},{17,1},{25,9},{2,18},{10... | collective-permute-start | bytes 835592 | tf_op jit(solution)/shard_map/ppermute | solution.py:526
  506.7 17.3 %collective-permute-done.34 = bf16[64,2176]{1,0:T(8,128)(2,1)S(1)} collective-permute-done((bf16[64,2176]{1,0:T(8,128)(2,1)S(1)}, bf16[64,2176]{1,0:T(8,128)(2,1)S(1)}, u32[]{:S(2)}, u32[]{:S(2)}) %collective-permute-start.34) | collective-permute-done | bytes 278560 | tf_op jit(solution)/shard_map/ppermute | solution.py:526
  524.0 6.6 %collective-permute-done.35 = bf16[64,2176]{1,0:T(8,128)(2,1)S(1)} collective-permute-done((bf16[64,2176]{1,0:T(8,128)(2,1)S(1)}, bf16[64,2176]{1,0:T(8,128)(2,1)S(1)}, u32[]{:S(2)}, u32[]{:S(2)}) %collective-permute-start.35) | collective-permute-done | bytes 278560 | tf_op jit(solution)/shard_map/ppermute | solution.py:526
  530.6 10.1 %collective-permute-done.36 = bf16[64,2176]{1,0:T(8,128)(2,1)S(1)} collective-permute-done((bf16[64,2176]{1,0:T(8,128)(2,1)S(1)}, bf16[64,2176]{1,0:T(8,128)(2,1)S(1)}, u32[]{:S(2)}, u32[]{:S(2)}) %collective-permute-start.36) | collective-permute-done | bytes 278560 | tf_op jit(solution)/shard_map/ppermute | solution.py:526
  541.5 4.3 all-to-all-done.4
  545.9 4.2 reduce-scatter.9.cloned.1.call-done
  550.1 8.5 %shard_map.219 = (bf16[1024,768]{1,0:T(8,128)(2,1)}, bf16[1024,2048]{1,0:T(8,128)(2,1)}) custom-call(bf16[1024,256]{1,0:T(8,128)(2,1)} %get-tuple-element.154.gq_ref, f32[1024,512]{1,0:T(8,128)} %get-tuple-element.160.own_ref, f32[1024,128]{1,0:T(8,128)} %get-tuple-element.195.cos_ref, f32[1024,128]{1,0:T(8,128)} %get-tuple-element.196.sin_ref, ...), custom_call_target="tpu_custom_call" | custom-call | flops 3221225472 | bytes 16777216 | tf_op jit(solution)/shard_map/pallas_call | solution.py:309
  558.6 7.8 %shard_map.220 = (bf16[2,512,384]{2,1,0:T(8,128)(2,1)}, bf16[2,512,384]{2,1,0:T(8,128)(2,1)}, f32[2,512,384]{2,1,0:T(8,128)}, f32[2,512,384]{2,1,0:T(8,128)}) custom-call(s32[1]{0:T(128)} %bitcast.16.index_ref, bf16[1024,2048]{1,0:T(8,128)(2,1)} %get-tuple-element.164.h_ref, bf16[1024,768]{1,0:T(8,128)(2,1)} %get-tuple-element.165.g_ref), custom_call_target="tpu_custom_call" | custom-call | flops 3221225472 | bytes 9437184 | tf_op jit(solution)/shard_map/pallas_call | solution.py:353
  566.5 3.4 collective-permute-start.39
  573.9 14.2 %collective-permute-done.39 = bf16[2,512,384]{2,1,0:T(8,128)(2,1)S(1)} collective-permute-done((bf16[2,512,384]{2,1,0:T(8,128)(2,1)}, bf16[2,512,384]{2,1,0:T(8,128)(2,1)S(1)}, u32[]{:S(2)}, u32[]{:S(2)}) %collective-permute-start.39) | collective-permute-done | bytes 786464 | tf_op jit(solution)/shard_map/ppermute | solution.py:526
  595.7 4.3 collective-permute-done.40
  603.4 4.1 all-to-all-start.5
  610.5 10.4 %reduce-scatter.11.cloned.1.call-done = bf16[128,2048]{1,0:T(8,128)(2,1)} async-done(((bf16[1024,2048]{1,0:T(8,128)(2,1)}), bf16[128,2048]{1,0:T(8,128)(2,1)}) %reduce-scatter.11.cloned.1.call-update) | async-done | bytes 524304 | tf_op jit(solution)/shard_map/reduce_scatter | solution.py:782
  622.3 3.0 fusion.33
  625.4 8.4 %all-to-all-done.5.got_ref = bf16[8,64,768]{2,1,0:T(8,128)(2,1)S(1)} async-done(((bf16[8,64,768]{2,1,0:T(8,128)(2,1)}), bf16[8,64,768]{2,1,0:T(8,128)(2,1)S(1)}, u32[]{:S(2)}, u32[]{:S(2)}) %all-to-all-start.5) | async-done | bytes 786464 | tf_op jit(solution)/shard_map/all_to_all | solution.py:797
  (315 shorter events, 153.8 us)
Async XLA Ops:
  10.8 37.6 %all-to-all-start = ((bf16[8,80,768]{2,1,0:T(8,128)(2,1)}), bf16[8,80,768]{2,1,0:T(8,128)(2,1)S(1)}, u32[]{:S(2)}, u32[]{:S(2)}) async-start(bf16[8,80,768]{2,1,0:T(8,128)(2,1)} %shard_map.212), calls=%async_computation | async-start | bytes 1966080 | tf_op jit(solution)/shard_map/all_to_all | solution.py:634
  17.1 92.3 %all-gather.5.cloned.1.call-start = ((), (), s32[]{:S(2)}) async-start(), calls=%async_computation.10 | async-start | bytes 4718592 | tf_op jit(solution)/shard_map/all_gather | solution.py:635
  53.9 20.7 %collective-permute-start.1 = (bf16[8,80,768]{2,1,0:T(8,128)(2,1)}, bf16[8,80,768]{2,1,0:T(8,128)(2,1)S(1)}, u32[]{:S(2)}, u32[]{:S(2)}) collective-permute-start(bf16[8,80,768]{2,1,0:T(8,128)(2,1)} %copy-done.6), channel_id=1, source_target_pairs={{0,16},{8,24},{16,0},{24,8},{1,17},{9,25},{17,1},{25,9},{2,18},{10... | collective-permute-start | bytes 2949128 | tf_op jit(solution)/shard_map/ppermute | solution.py:526
  53.9 23.5 %collective-permute-start.7 = (bf16[8,80,768]{2,1,0:T(8,128)(2,1)}, bf16[8,80,768]{2,1,0:T(8,128)(2,1)S(1)}, u32[]{:S(2)}, u32[]{:S(2)}) collective-permute-start(bf16[8,80,768]{2,1,0:T(8,128)(2,1)} %copy-done.6), channel_id=1, source_target_pairs={{0,8},{8,0},{16,24},{24,16},{1,9},{9,1},{17,25},{25,17},{2,10},{10... | collective-permute-start | bytes 2949128 | tf_op jit(solution)/shard_map/ppermute | solution.py:526
  75.4 18.0 %collective-permute-start.2 = (bf16[4,80,768]{2,1,0:T(8,128)(2,1)}, bf16[4,80,768]{2,1,0:T(8,128)(2,1)}, u32[]{:S(2)}, u32[]{:S(2)}) collective-permute-start(bf16[4,80,768]{2,1,0:T(8,128)(2,1)} %slice.208), channel_id=1, source_target_pairs={{0,8},{8,0},{16,24},{24,16},{1,9},{9,1},{17,25},{25,17},{2,10},{10... | collective-permute-start | bytes 1474568 | tf_op jit(solution)/shard_map/ppermute | solution.py:526
  78.4 17.7 %collective-permute-start.8 = (bf16[4,80,768]{2,1,0:T(8,128)(2,1)S(1)}, bf16[4,80,768]{2,1,0:T(8,128)(2,1)}, u32[]{:S(2)}, u32[]{:S(2)}) collective-permute-start(bf16[4,80,768]{2,1,0:T(8,128)(2,1)S(1)} %slice.214), channel_id=1, source_target_pairs={{0,16},{8,24},{16,0},{24,8},{1,17},{9,25},{17,1},{25,9},{2,18},{10... | collective-permute-start | bytes 1474568 | tf_op jit(solution)/shard_map/ppermute | solution.py:526
  78.5 42.5 %all-to-all-start.1 = ((bf16[8,256,256]{2,1,0:T(8,128)(2,1)}), bf16[8,256,256]{2,1,0:T(8,128)(2,1)S(1)}, u32[]{:S(2)}, u32[]{:S(2)}) async-start(bf16[8,256,256]{2,1,0:T(8,128)(2,1)} %bitcast.10), calls=%async_computation.1 | async-start | bytes 2097152 | tf_op jit(solution)/shard_map/all_to_all | solution.py:645
  90.4 118.9 %all-gather.7.cloned.1.call-start = ((), (), s32[]{:S(2)}) async-start(), calls=%async_computation.11 | async-start | bytes 4718592 | tf_op jit(solution)/shard_map/all_gather | solution.py:669
  122.1 87.2 %all-to-all-start.2 = ((bf16[8,512,256]{2,1,0:T(8,128)(2,1)}), bf16[8,512,256]{2,1,0:T(8,128)(2,1)}, u32[]{:S(2)}, u32[]{:S(2)}) async-start(bf16[8,512,256]{2,1,0:T(8,128)(2,1)} %pad_maximum_fusion), calls=%async_computation.2 | async-start | bytes 4194304 | tf_op jit(solution)/shard_map/all_to_all | solution.py:645
  126.5 131.6 %reduce-scatter.5.cloned.1.call-start = ((), (), s32[]{:S(2)}) async-start(), calls=%async_computation.12 | async-start | bytes 4718592 | tf_op jit(solution)/shard_map/reduce_scatter | solution.py:675
  126.5 41.3 %collective-permute-start.11 = (bf16[1024,512]{1,0:T(8,128)(2,1)S(1)}, bf16[1024,512]{1,0:T(8,128)(2,1)S(1)}, u32[]{:S(2)}, u32[]{:S(2)}) collective-permute-start(bf16[1024,512]{1,0:T(8,128)(2,1)S(1)} %copy-done.14), channel_id=1, source_target_pairs={{0,16},{8,24},{1,17},{9,25},{2,18},{10,26},{3,19},{11,27},{4,20},{... | collective-permute-start | bytes 3145736 | tf_op jit(solution)/shard_map/ppermute | solution.py:656
  129.7 46.0 %collective-permute-start.10 = (bf16[8,256,256]{2,1,0:T(8,128)(2,1)}, bf16[8,256,256]{2,1,0:T(8,128)(2,1)}, u32[]{:S(2)}, u32[]{:S(2)}) collective-permute-start(bf16[8,256,256]{2,1,0:T(8,128)(2,1)} %copy-done.23), channel_id=1, source_target_pairs={{0,16},{8,24},{16,0},{24,8},{1,17},{9,25},{17,1},{25,9},{2,18},{10... | collective-permute-start | bytes 3145736 | tf_op jit(solution)/shard_map/ppermute | solution.py:526
  129.8 45.9 %collective-permute-start.9 = (bf16[8,256,256]{2,1,0:T(8,128)(2,1)}, bf16[8,256,256]{2,1,0:T(8,128)(2,1)}, u32[]{:S(2)}, u32[]{:S(2)}) collective-permute-start(bf16[8,256,256]{2,1,0:T(8,128)(2,1)} %copy-done.23), channel_id=1, source_target_pairs={{0,8},{8,0},{16,24},{24,16},{1,9},{9,1},{17,25},{25,17},{2,10},{10... | collective-permute-start | bytes 3145736 | tf_op jit(solution)/shard_map/ppermute | solution.py:526
  131.4 35.1 %collective-permute-start.13 = (bf16[512,512]{1,0:T(8,128)(2,1)S(1)}, bf16[512,512]{1,0:T(8,128)(2,1)}, u32[]{:S(2)}, u32[]{:S(2)}) collective-permute-start(bf16[512,512]{1,0:T(8,128)(2,1)S(1)} %slice.175), channel_id=1, source_target_pairs={{8,0},{9,1},{10,2},{11,3},{12,4},{13,5},{14,6},{15,7}} | collective-permute-start | bytes 1572872 | tf_op jit(solution)/shard_map/ppermute | solution.py:658
  132.7 44.0 %collective-permute-start.12 = (bf16[1024,512]{1,0:T(8,128)(2,1)S(1)}, bf16[1024,512]{1,0:T(8,128)(2,1)}, u32[]{:S(2)}, u32[]{:S(2)}) collective-permute-start(bf16[1024,512]{1,0:T(8,128)(2,1)S(1)} %copy-done.14), channel_id=1, source_target_pairs={{0,8},{16,24},{1,9},{17,25},{2,10},{18,26},{3,11},{19,27},{4,12},{... | collective-permute-start | bytes 3145736 | tf_op jit(solution)/shard_map/ppermute | solution.py:657
  166.5 19.8 %collective-permute-start.14 = (bf16[512,512]{1,0:T(8,128)(2,1)}, bf16[512,512]{1,0:T(8,128)(2,1)S(1)}, u32[]{:S(2)}, u32[]{:S(2)}) collective-permute-start(bf16[512,512]{1,0:T(8,128)(2,1)} %collective-permute-done.13), channel_id=1, source_target_pairs={{0,16},{1,17},{2,18},{3,19},{4,20},{5,21},{6,22},{7,23}} | collective-permute-start | bytes 1572872 | tf_op jit(solution)/shard_map/ppermute | solution.py:659
  167.9 18.4 %collective-permute-start.15 = (bf16[512,512]{1,0:T(8,128)(2,1)S(1)}, bf16[512,512]{1,0:T(8,128)(2,1)}, u32[]{:S(2)}, u32[]{:S(2)}) collective-permute-start(bf16[512,512]{1,0:T(8,128)(2,1)S(1)} %slice.223), channel_id=1, source_target_pairs={{24,16},{25,17},{26,18},{27,19},{28,20},{29,21},{30,22},{31,23}} | collective-permute-start | bytes 1572872 | tf_op jit(solution)/shard_map/ppermute | solution.py:660
  209.3 98.3 %all-gather.9.cloned.1.call-start = ((), (), s32[]{:S(2)}) async-start(), calls=%async_computation.13 | async-start | bytes 4718592 | tf_op jit(solution)/shard_map/all_gather | solution.py:682
  209.3 47.4 %collective-permute-start.16 = (bf16[8,512,256]{2,1,0:T(8,128)(2,1)}, bf16[8,512,256]{2,1,0:T(8,128)(2,1)S(1)}, u32[]{:S(2)}, u32[]{:S(2)}) collective-permute-start(bf16[8,512,256]{2,1,0:T(8,128)(2,1)} %all-to-all-done.2.refs_0_), channel_id=1, source_target_pairs={{0,8},{8,0},{16,24},{24,16},{1,9},{9,1},{17,25},{25,17},{2,10},{10... | collective-permute-start | bytes 6291464 | tf_op jit(solution)/shard_map/ppermute | solution.py:526
  210.6 47.2 %collective-permute-start.17 = (bf16[8,512,256]{2,1,0:T(8,128)(2,1)}, bf16[8,512,256]{2,1,0:T(8,128)(2,1)}, u32[]{:S(2)}, u32[]{:S(2)}) collective-permute-start(bf16[8,512,256]{2,1,0:T(8,128)(2,1)} %all-to-all-done.2.refs_0_), channel_id=1, source_target_pairs={{0,16},{8,24},{16,0},{24,8},{1,17},{9,25},{17,1},{25,9},{2,18},{10... | collective-permute-start | bytes 6291464 | tf_op jit(solution)/shard_map/ppermute | solution.py:526
  261.8 125.4 %reduce-scatter.7.cloned.1.call-start = ((), (), s32[]{:S(2)}) async-start(), calls=%async_computation.14 | async-start | bytes 4718592 | tf_op jit(solution)/shard_map/reduce_scatter | solution.py:690
  262.0 37.2 %collective-permute-start.18 = (bf16[4,512,256]{2,1,0:T(8,128)(2,1)S(1)}, bf16[4,512,256]{2,1,0:T(8,128)(2,1)S(1)}, u32[]{:S(2)}, u32[]{:S(2)}) collective-permute-start(bf16[4,512,256]{2,1,0:T(8,128)(2,1)S(1)} %slice.178), channel_id=1, source_target_pairs={{0,16},{8,24},{16,0},{24,8},{1,17},{9,25},{17,1},{25,9},{2,18},{10... | collective-permute-start | bytes 3145736 | tf_op jit(solution)/shard_map/ppermute | solution.py:526
  264.8 35.2 %collective-permute-start.19 = (bf16[4,512,256]{2,1,0:T(8,128)(2,1)S(1)}, bf16[4,512,256]{2,1,0:T(8,128)(2,1)S(1)}, u32[]{:S(2)}, u32[]{:S(2)}) collective-permute-start(bf16[4,512,256]{2,1,0:T(8,128)(2,1)S(1)} %slice.179), channel_id=1, source_target_pairs={{0,8},{8,0},{16,24},{24,16},{1,9},{9,1},{17,25},{25,17},{2,10},{10... | collective-permute-start | bytes 3145736 | tf_op jit(solution)/shard_map/ppermute | solution.py:526
  267.4 29.2 %collective-permute-start.20 = (bf16[4,256,256]{2,1,0:T(8,128)(2,1)S(1)}, bf16[4,256,256]{2,1,0:T(8,128)(2,1)S(1)}, u32[]{:S(2)}, u32[]{:S(2)}) collective-permute-start(bf16[4,256,256]{2,1,0:T(8,128)(2,1)S(1)} %slice.180), channel_id=1, source_target_pairs={{0,16},{8,24},{16,0},{24,8},{1,17},{9,25},{17,1},{25,9},{2,18},{10... | collective-permute-start | bytes 1572872 | tf_op jit(solution)/shard_map/ppermute | solution.py:526
  269.1 30.0 %collective-permute-start.21 = (bf16[4,256,256]{2,1,0:T(8,128)(2,1)S(1)}, bf16[4,256,256]{2,1,0:T(8,128)(2,1)S(1)}, u32[]{:S(2)}, u32[]{:S(2)}) collective-permute-start(bf16[4,256,256]{2,1,0:T(8,128)(2,1)S(1)} %slice.181), channel_id=1, source_target_pairs={{0,8},{8,0},{16,24},{24,16},{1,9},{9,1},{17,25},{25,17},{2,10},{10... | collective-permute-start | bytes 1572872 | tf_op jit(solution)/shard_map/ppermute | solution.py:526
  338.4 122.1 %all-gather.11.cloned.1.call-start = ((), (), s32[]{:S(2)}) async-start(), calls=%async_computation.15 | async-start | bytes 4718592 | tf_op jit(solution)/shard_map/all_gather | solution.py:743
  342.6 25.4 %collective-permute-start.22 = (bf16[1024,512]{1,0:T(8,128)(2,1)S(1)}, bf16[1024,512]{1,0:T(8,128)(2,1)S(1)}, u32[]{:S(2)}, u32[]{:S(2)}) collective-permute-start(bf16[1024,512]{1,0:T(8,128)(2,1)S(1)} %convolution_convert_fusion.4), channel_id=1, source_target_pairs={{0,8},{8,0},{16,24},{24,16},{1,9},{9,1},{17,25},{25,17},{2,10},{10... | collective-permute-start | bytes 3145736 | tf_op jit(solution)/shard_map/ppermute | solution.py:526
  345.4 25.4 %collective-permute-start.24 = (bf16[1024,512]{1,0:T(8,128)(2,1)S(1)}, bf16[1024,512]{1,0:T(8,128)(2,1)S(1)}, u32[]{:S(2)}, u32[]{:S(2)}) collective-permute-start(bf16[1024,512]{1,0:T(8,128)(2,1)S(1)} %convolution_convert_fusion.3), channel_id=1, source_target_pairs={{0,16},{8,24},{16,0},{24,8},{1,17},{9,25},{17,1},{25,9},{2,18},{10... | collective-permute-start | bytes 3145736 | tf_op jit(solution)/shard_map/ppermute | solution.py:526
  390.7 26.5 %collective-permute-start.30 = (bf16[512,1024]{1,0:T(8,128)(2,1)}, bf16[512,1024]{1,0:T(8,128)(2,1)}, u32[]{:S(2)}, u32[]{:S(2)}) collective-permute-start(bf16[512,1024]{1,0:T(8,128)(2,1)} %fusion.10), channel_id=1, source_target_pairs={{0,8},{8,0},{16,24},{24,16},{1,9},{9,1},{17,25},{25,17},{2,10},{10... | collective-permute-start | bytes 3145736 | tf_op jit(solution)/shard_map/ppermute | solution.py:526
  392.2 28.7 %collective-permute-start.32 = (bf16[512,1024]{1,0:T(8,128)(2,1)}, bf16[512,1024]{1,0:T(8,128)(2,1)}, u32[]{:S(2)}, u32[]{:S(2)}) collective-permute-start(bf16[512,1024]{1,0:T(8,128)(2,1)} %fusion.13), channel_id=1, source_target_pairs={{0,16},{8,24},{16,0},{24,8},{1,17},{9,25},{17,1},{25,9},{2,18},{10... | collective-permute-start | bytes 3145736 | tf_op jit(solution)/shard_map/ppermute | solution.py:526
  396.8 63.6 %all-to-all-start.3 = ((bf16[8,264,256]{2,1,0:T(8,128)(2,1)}), bf16[8,264,256]{2,1,0:T(8,128)(2,1)}, u32[]{:S(2)}, u32[]{:S(2)}) async-start(bf16[8,264,256]{2,1,0:T(8,128)(2,1)} %fusion.29), calls=%async_computation.5 | async-start | bytes 2162688 | tf_op jit(solution)/shard_map/all_to_all | solution.py:645
  401.1 149.0 %reduce-scatter.9.cloned.1.call-start = ((), (), s32[]{:S(2)}) async-start(), calls=%async_computation.16 | async-start | bytes 4718592 | tf_op jit(solution)/shard_map/reduce_scatter | solution.py:766
  401.1 38.5 %collective-permute-start.26 = (bf16[1024,512]{1,0:T(8,128)(2,1)}, bf16[1024,512]{1,0:T(8,128)(2,1)}, u32[]{:S(2)}, u32[]{:S(2)}) collective-permute-start(bf16[1024,512]{1,0:T(8,128)(2,1)} %convolution_convert_fusion.2), channel_id=1, source_target_pairs={{0,8},{8,0},{16,24},{24,16},{1,9},{9,1},{17,25},{25,17},{2,10},{10... | collective-permute-start | bytes 3145736 | tf_op jit(solution)/shard_map/ppermute | solution.py:526
  401.7 41.1 %collective-permute-start.28 = (bf16[1024,512]{1,0:T(8,128)(2,1)}, bf16[1024,512]{1,0:T(8,128)(2,1)}, u32[]{:S(2)}, u32[]{:S(2)}) collective-permute-start(bf16[1024,512]{1,0:T(8,128)(2,1)} %convolution_convert_fusion.1), channel_id=1, source_target_pairs={{0,16},{8,24},{16,0},{24,8},{1,17},{9,25},{17,1},{25,9},{2,18},{10... | collective-permute-start | bytes 3145736 | tf_op jit(solution)/shard_map/ppermute | solution.py:526
  419.4 32.8 %collective-permute-start.31 = (bf16[256,1024]{1,0:T(8,128)(2,1)S(1)}, bf16[256,1024]{1,0:T(8,128)(2,1)S(1)}, u32[]{:S(2)}, u32[]{:S(2)}) collective-permute-start(bf16[256,1024]{1,0:T(8,128)(2,1)S(1)} %slice.320), channel_id=1, source_target_pairs={{0,16},{8,24},{16,0},{24,8},{1,17},{9,25},{17,1},{25,9},{2,18},{10... | collective-permute-start | bytes 1572872 | tf_op jit(solution)/shard_map/ppermute | solution.py:526
  422.6 29.8 %collective-permute-start.33 = (bf16[256,1024]{1,0:T(8,128)(2,1)S(1)}, bf16[256,1024]{1,0:T(8,128)(2,1)S(1)}, u32[]{:S(2)}, u32[]{:S(2)}) collective-permute-start(bf16[256,1024]{1,0:T(8,128)(2,1)S(1)} %slice.319), channel_id=1, source_target_pairs={{0,8},{8,0},{16,24},{24,16},{1,9},{9,1},{17,25},{25,17},{2,10},{10... | collective-permute-start | bytes 1572872 | tf_op jit(solution)/shard_map/ppermute | solution.py:526
  441.2 18.7 %collective-permute-start.27 = (bf16[1024,256]{1,0:T(8,128)(2,1)S(1)}, bf16[1024,256]{1,0:T(8,128)(2,1)S(1)}, u32[]{:S(2)}, u32[]{:S(2)}) collective-permute-start(bf16[1024,256]{1,0:T(8,128)(2,1)S(1)} %slice.322), channel_id=1, source_target_pairs={{0,16},{8,24},{16,0},{24,8},{1,17},{9,25},{17,1},{25,9},{2,18},{10... | collective-permute-start | bytes 1572872 | tf_op jit(solution)/shard_map/ppermute | solution.py:526
  444.4 15.7 %collective-permute-start.29 = (bf16[1024,256]{1,0:T(8,128)(2,1)S(1)}, bf16[1024,256]{1,0:T(8,128)(2,1)S(1)}, u32[]{:S(2)}, u32[]{:S(2)}) collective-permute-start(bf16[1024,256]{1,0:T(8,128)(2,1)S(1)} %slice.321), channel_id=1, source_target_pairs={{0,8},{8,0},{16,24},{24,16},{1,9},{9,1},{17,25},{25,17},{2,10},{10... | collective-permute-start | bytes 1572872 | tf_op jit(solution)/shard_map/ppermute | solution.py:526
  462.0 83.8 %all-to-all-start.4 = ((bf16[8,512,256]{2,1,0:T(8,128)(2,1)}), bf16[8,512,256]{2,1,0:T(8,128)(2,1)S(1)}, u32[]{:S(2)}, u32[]{:S(2)}) async-start(bf16[8,512,256]{2,1,0:T(8,128)(2,1)} %pad_maximum_fusion.1), calls=%async_computation.7 | async-start | bytes 4194304 | tf_op jit(solution)/shard_map/all_to_all | solution.py:645
  466.1 154.8 %reduce-scatter.11.cloned.1.call-start = ((), (), s32[]{:S(2)}) async-start(), calls=%async_computation.17 | async-start | bytes 4718592 | tf_op jit(solution)/shard_map/reduce_scatter | solution.py:782
  485.7 64.4 %collective-permute-start.37 = (bf16[1024,512]{1,0:T(8,128)(2,1)}, bf16[1024,512]{1,0:T(8,128)(2,1)}, u32[]{:S(2)}, u32[]{:S(2)}) collective-permute-start(bf16[1024,512]{1,0:T(8,128)(2,1)} %get-tuple-element.161), channel_id=1, source_target_pairs={{16,0},{24,8},{17,1},{25,9},{18,2},{26,10},{19,3},{27,11},{20,4},{... | collective-permute-start | bytes 3145736 | tf_op jit(solution)/shard_map/ppermute | solution.py:763
  487.0 63.1 %collective-permute-start.38 = (bf16[1024,512]{1,0:T(8,128)(2,1)}, bf16[1024,512]{1,0:T(8,128)(2,1)}, u32[]{:S(2)}, u32[]{:S(2)}) collective-permute-start(bf16[1024,512]{1,0:T(8,128)(2,1)} %get-tuple-element.162), channel_id=1, source_target_pairs={{8,0},{16,8},{24,16},{9,1},{17,9},{25,17},{10,2},{18,10},{26,18},{... | collective-permute-start | bytes 3145736 | tf_op jit(solution)/shard_map/ppermute | solution.py:763
  488.4 35.7 %collective-permute-start.34 = (bf16[64,2176]{1,0:T(8,128)(2,1)S(1)}, bf16[64,2176]{1,0:T(8,128)(2,1)S(1)}, u32[]{:S(2)}, u32[]{:S(2)}) collective-permute-start(bf16[64,2176]{1,0:T(8,128)(2,1)S(1)} %get-tuple-element.181), channel_id=1, source_target_pairs={{0,8},{8,0},{16,24},{24,16},{1,9},{9,1},{17,25},{25,17},{2,10},{10... | collective-permute-start | bytes 835592 | tf_op jit(solution)/shard_map/ppermute | solution.py:526
  494.0 36.6 %collective-permute-start.35 = (bf16[64,2176]{1,0:T(8,128)(2,1)S(1)}, bf16[64,2176]{1,0:T(8,128)(2,1)S(1)}, u32[]{:S(2)}, u32[]{:S(2)}) collective-permute-start(bf16[64,2176]{1,0:T(8,128)(2,1)S(1)} %get-tuple-element.183), channel_id=1, source_target_pairs={{0,16},{8,24},{16,0},{24,8},{1,17},{9,25},{17,1},{25,9},{2,18},{10... | collective-permute-start | bytes 835592 | tf_op jit(solution)/shard_map/ppermute | solution.py:526
  506.7 34.0 %collective-permute-start.36 = (bf16[64,2176]{1,0:T(8,128)(2,1)S(1)}, bf16[64,2176]{1,0:T(8,128)(2,1)S(1)}, u32[]{:S(2)}, u32[]{:S(2)}) collective-permute-start(bf16[64,2176]{1,0:T(8,128)(2,1)S(1)} %get-tuple-element.182), channel_id=1, source_target_pairs={{0,24},{8,16},{16,8},{24,0},{1,25},{9,17},{17,9},{25,1},{2,26},{10... | collective-permute-start | bytes 835592 | tf_op jit(solution)/shard_map/ppermute | solution.py:526
  566.5 21.7 %collective-permute-start.39 = (bf16[2,512,384]{2,1,0:T(8,128)(2,1)}, bf16[2,512,384]{2,1,0:T(8,128)(2,1)S(1)}, u32[]{:S(2)}, u32[]{:S(2)}) collective-permute-start(bf16[2,512,384]{2,1,0:T(8,128)(2,1)} %get-tuple-element.167), channel_id=1, source_target_pairs={{0,8},{8,0},{16,24},{24,16},{1,9},{9,1},{17,25},{25,17},{2,10},{10... | collective-permute-start | bytes 2359304 | tf_op jit(solution)/shard_map/ppermute | solution.py:526
  570.7 20.3 %collective-permute-start.41 = (bf16[2,512,384]{2,1,0:T(8,128)(2,1)}, bf16[2,512,384]{2,1,0:T(8,128)(2,1)S(1)}, u32[]{:S(2)}, u32[]{:S(2)}) collective-permute-start(bf16[2,512,384]{2,1,0:T(8,128)(2,1)} %get-tuple-element.169), channel_id=1, source_target_pairs={{0,16},{8,24},{16,0},{24,8},{1,17},{9,25},{17,1},{25,9},{2,18},{10... | collective-permute-start | bytes 2359304 | tf_op jit(solution)/shard_map/ppermute | solution.py:526
  603.4 30.4 %all-to-all-start.5 = ((bf16[8,64,768]{2,1,0:T(8,128)(2,1)}), bf16[8,64,768]{2,1,0:T(8,128)(2,1)S(1)}, u32[]{:S(2)}, u32[]{:S(2)}) async-start(bf16[8,64,768]{2,1,0:T(8,128)(2,1)} %pad_maximum_fusion.5), calls=%async_computation.9 | async-start | bytes 1572864 | tf_op jit(solution)/shard_map/all_to_all | solution.py:797
  (60 other events, 597.7 us)
Sparse Core Ops, SparseCore 0:
  48.6 55.3 all-gather.4
  121.2 84.8 all-gather.6
  209.4 48.6 reduce-scatter.4
  261.9 45.6 all-gather.8
  338.5 48.7 reduce-scatter.6
  390.8 68.2 all-gather.10
  461.3 88.6 reduce-scatter.8
  558.8 62.1 reduce-scatter.10

commit v6 on v5

--- a/solution.py
+++ b/solution.py
@@ -21,6 +21,7 @@
 
 BQ = 512
 BK = 512
+BB = 384
 BR = 256
 VMEM = 60 * 2**20
 f32 = jnp.float32
@@ -192,33 +193,33 @@
     for i in range(rows // BQ):
         at = slice(i * BQ, (i + 1) * BQ)
         start = start_ref[:, at]
-        row = base + i * BQ + lax.broadcasted_iota(jnp.int32, (BK, BQ), 1)
-        col = lax.broadcasted_iota(jnp.int32, (BK, BQ), 0)
+        row = base + i * BQ + lax.broadcasted_iota(jnp.int32, (BB, BQ), 1)
+        col = lax.broadcasted_iota(jnp.int32, (BB, BQ), 0)
         gatt = dot_t(ga_ref[at, :], wo_ref[...]).astype(bf16)
         queries = [q_ref[at, h * HD : (h + 1) * HD] for h in range(heads)]
         gatts = [gatt[:, h * HD : (h + 1) * HD] for h in range(heads)]
 
         def step(kb, sums):
-            off = pl.multiple_of(kb * BK, BK)
+            off = pl.multiple_of(kb * BB, BB)
             here = col + off
             ok = (here >= start) & (here <= row)
             out = []
             for h in range(heads):
                 ks = slice(h * HD, (h + 1) * HD)
                 vs = slice(width + h * HD, width + (h + 1) * HD)
-                k = kv_all[pl.ds(off, BK), ks]
-                v = kv_all[pl.ds(off, BK), vs]
+                k = kv_all[pl.ds(off, BB), ks]
+                v = kv_all[pl.ds(off, BB), vs]
                 e = jnp.exp2(
                     dot_t(k, queries[h]) * (-head_scale * LOG2E) - score_bias * LOG2E
                 )
                 sg = jnp.where(ok, 1.0 / (1.0 + e), 0.0)
                 gs = (dot_t(v, gatts[h]) * sg * (1.0 - sg)).astype(bf16)
-                gkv[pl.ds(off, BK), ks] += dot(gs, queries[h])
-                gkv[pl.ds(off, BK), vs] += dot(sg.astype(bf16), gatts[h])
+                gkv[pl.ds(off, BB), ks] += dot(gs, queries[h])
+                gkv[pl.ds(off, BB), vs] += dot(sg.astype(bf16), gatts[h])
                 out.append(sums[h] + t_dot(gs, k))
             return tuple(out)
 
-        last = (base + (i + 1) * BQ - 1) // BK + 1
+        last = (base + (i + 1) * BQ - 1) // BB + 1
         sums = lax.fori_loop(
             lo_ref[i], last, step, tuple(jnp.zeros((BQ, HD), f32) for _ in range(heads))
         )
@@ -618,8 +619,10 @@
     shift = (uly_index - back) * group
     begin = jnp.where(used, seq_start - shift, 1 << 30).astype(jnp.int32)
     firsts = begin[::BQ]
-    ends_kb = (back * group + jnp.arange(group // BQ, dtype=jnp.int32) * BQ + BQ - 1) // BK + 1
-    low_kb = jnp.minimum(firsts // BK, ends_kb).astype(jnp.int32)
+    finals = back * group + jnp.arange(group // BQ, dtype=jnp.int32) * BQ + BQ - 1
+    low_kb, low_bb = (
+        jnp.minimum(firsts // size, finals // size + 1).astype(jnp.int32) for size in (BK, BB)
+    )
     frequency = rope_base ** (-jnp.arange(HD // 2, dtype=f32) * 2.0 / HD)
     angles = position.astype(f32)[:, None] * frequency[None, :]
     cos, sin = jnp.cos(angles), jnp.sin(angles)
@@ -757,7 +760,7 @@
         )
     )
     gq, gkv, *sent = attn_bwd_call(
-        low_kb, query, gattn, begin[None, :], wo, cos, sin, kvs
+        low_bb, query, gattn, begin[None, :], wo, cos, sin, kvs
     )
     got = [
         lax.ppermute(block, "uly", [(i, i - s) for i in range(s, count_uly)])

time: 656 us -> 659 us (level)
  transfers between devices with their start and end apart: 58 -> 58, of which waited for: 36 -> 35; matrix products, arithmetic and copies ran while one was open for 14% -> 14% of each run, Pallas kernels for 8% -> 8%
where the time goes in v6:
time: 659 us; the launch traced here: 651 us
  waiting for transfers between devices  318 us (48%)
  starting transfers between devices  116 us (18%)
  Pallas kernels  101 us (15%)
  other arithmetic  40 us (6%)
  local copies, waits for them, and re-layouts  32.4 us (5%)
  matrix products  28.4 us (4%)
  between operations  15.6 us (2%)
    ppermute x35, waiting for transfers between devices, xor_permute(): return lax.ppermute(x, 'uly', [(i, i ^ flip) for i in range(count)])  201 us
    ppermute x35, starting transfers between devices, xor_permute(): return lax.ppermute(x, 'uly', [(i, i ^ flip) for i in range(count)])  58.8 us
    pallas_call x1, Pallas kernels, ffn_call(): pl.pallas_call(functools.partial(ffn_kernel, places, blocks, groups), gri...  30.7 us
    all_to_all x1, waiting for transfers between devices, body(): qkv = lax.all_to_all(qkv, 'blk', 0, 0, tiled=True)  29.9 us
    dot_general x13, matrix products, t_dot(): lax.dot_general(left, right, (((0,), (0,)), ((), ())), preferred_element_...  28.4 us
    ppermute x1, waiting for transfers between devices, body(): over = lax.ppermute(kv[:half], 'uly', [(1, 0)])  27.5 us
    all_to_all x4, starting transfers between devices, body(): to_hidden = lambda w: lax.all_to_all(w, 'blk', 0, 0, tiled=True)  24.5 us
    all_to_all x4, waiting for transfers between devices, body(): to_hidden = lambda w: lax.all_to_all(w, 'blk', 0, 0, tiled=True)  19.2 us
  transfers between devices with their start and end apart: 58, of which 35 were waited for; matrix products, arithmetic and copies ran while one was open for 14% of the time, Pallas kernels for 8%

profile of v6, /device:TPU:0, one launch (start us, length us, event | category | flops | bytes accessed | tf_op | source)
XLA Modules:
  0.0 651.0 jit_solution(12844143772416454001)
XLA Ops:
  10.8 6.3 all-to-all-start
  18.6 29.9 %all-to-all-done = bf16[8,80,768]{2,1,0:T(8,128)(2,1)S(1)} async-done(((bf16[8,80,768]{2,1,0:T(8,128)(2,1)}), bf16[8,80,768]{2,1,0:T(8,128)(2,1)S(1)}, u32[]{:S(2)}, u32[]{:S(2)}) %all-to-all-start) | async-done | bytes 983072 | tf_op jit(solution)/shard_map/all_to_all | solution.py:637
  60.8 13.8 %collective-permute-done.1 = bf16[8,80,768]{2,1,0:T(8,128)(2,1)S(1)} collective-permute-done((bf16[8,80,768]{2,1,0:T(8,128)(2,1)}, bf16[8,80,768]{2,1,0:T(8,128)(2,1)S(1)}, u32[]{:S(2)}, u32[]{:S(2)}) %collective-permute-start.1) | collective-permute-done | bytes 983072 | tf_op jit(solution)/shard_map/ppermute | solution.py:527
  78.5 11.8 %all-to-all-start.1 = ((bf16[8,256,256]{2,1,0:T(8,128)(2,1)}), bf16[8,256,256]{2,1,0:T(8,128)(2,1)S(1)}, u32[]{:S(2)}, u32[]{:S(2)}) async-start(bf16[8,256,256]{2,1,0:T(8,128)(2,1)} %bitcast.10), calls=%async_computation.1 | async-start | bytes 2097152 | tf_op jit(solution)/shard_map/all_to_all | solution.py:648
  104.7 3.2 collective-permute-done.5
  109.5 8.8 %shard_map.213 = (bf16[1024,2048]{1,0:T(8,128)(2,1)}, bf16[1024,256]{1,0:T(8,128)(2,1)}, bf16[1024,512]{1,0:T(8,128)(2,1)}) custom-call(bf16[1024,2048]{1,0:T(8,128)(2,1)} %all-gather.5.cloned.1.call-done.x_ref, f32[1,2048]{1,0:T(1,128)} %reshape.229.gain_ref, bf16[2048,768]{1,0:T(8,128)(2,1)} %constant_dynamic-update-slice_fusion.w_ref, ...), custom_call_target="tpu_custom_call" | custom-call | flops 3221225472 | bytes 16777216 | tf_op jit(solution)/shard_map/pallas_call | solution.py:107
  118.3 2.8 all-to-all-done.1.refs_5_.refs_0_
  122.1 4.4 all-to-all-start.2
  126.5 3.2 collective-permute-start.11
  132.7 6.3 collective-permute-start.12
  139.0 27.5 %collective-permute-done.13 = bf16[512,512]{1,0:T(8,128)(2,1)} collective-permute-done((bf16[512,512]{1,0:T(8,128)(2,1)S(1)}, bf16[512,512]{1,0:T(8,128)(2,1)}, u32[]{:S(2)}, u32[]{:S(2)}) %collective-permute-start.13) | collective-permute-done | bytes 524320 | tf_op jit(solution)/shard_map/ppermute | solution.py:661
  171.1 4.6 collective-permute-done.10.refs_7_.refs_2_
  176.7 9.7 %collective-permute-done.14 = bf16[512,512]{1,0:T(8,128)(2,1)S(1)} collective-permute-done((bf16[512,512]{1,0:T(8,128)(2,1)}, bf16[512,512]{1,0:T(8,128)(2,1)S(1)}, u32[]{:S(2)}, u32[]{:S(2)}) %collective-permute-start.14) | collective-permute-done | bytes 524320 | tf_op jit(solution)/shard_map/ppermute | solution.py:662
  188.9 10.3 %shard_map.214 = (bf16[1024,256]{1,0:T(8,128)(2,1)}, bf16[1024,2048]{1,0:T(8,128)(2,1)}) custom-call(s32[2]{0:T(128)} %get-tuple-element.195.lo_ref, bf16[1024,256]{1,0:T(8,128)(2,1)} %get-tuple-element.104.q_ref, s32[1024,1]{1,0:T(8,128)} %copy.44.start_ref, bf16[256,2048]{1,0:T(8,128)(2,1)} %copy-done.5, bf16[1024,512]{1,0:T(8,128)(2,1)} %copy-done.15, ...), custom_call_target="tpu_custom_call" | custom-call | flops 1000000 | bytes 1000000 | tf_op jit(solution)/shard_map/pallas_call | solution.py:166
  199.2 10.0 %all-to-all-done.2.refs_0_ = bf16[8,512,256]{2,1,0:T(8,128)(2,1)} async-done(((bf16[8,512,256]{2,1,0:T(8,128)(2,1)}), bf16[8,512,256]{2,1,0:T(8,128)(2,1)}, u32[]{:S(2)}, u32[]{:S(2)}) %all-to-all-start.2) | async-done | bytes 2097184 | tf_op jit(solution)/shard_map/all_to_all | solution.py:648
  212.1 44.6 %collective-permute-done.16.refs_1_ = bf16[8,512,256]{2,1,0:T(8,128)(2,1)S(1)} collective-permute-done((bf16[8,512,256]{2,1,0:T(8,128)(2,1)}, bf16[8,512,256]{2,1,0:T(8,128)(2,1)S(1)}, u32[]{:S(2)}, u32[]{:S(2)}) %collective-permute-start.16) | collective-permute-done | bytes 2097184 | tf_op jit(solution)/shard_map/ppermute | solution.py:527
  269.7 26.8 %collective-permute-done.20.refs_8_.refs_3_ = bf16[4,256,256]{2,1,0:T(8,128)(2,1)S(1)} collective-permute-done((bf16[4,256,256]{2,1,0:T(8,128)(2,1)S(1)}, bf16[4,256,256]{2,1,0:T(8,128)(2,1)S(1)}, u32[]{:S(2)}, u32[]{:S(2)}) %collective-permute-start.20) | collective-permute-done | bytes 524320 | tf_op jit(solution)/shard_map/ppermute | solution.py:527
  299.9 7.7 %all-gather.9.cloned.1.call-done.h_ref = bf16[1024,2048]{1,0:T(8,128)(2,1)} async-done(((bf16[128,2048]{1,0:T(8,128)(2,1)}), bf16[1024,2048]{1,0:T(8,128)(2,1)}) %all-gather.9.cloned.1.call-update) | async-done | bytes 4194320 | tf_op jit(solution)/shard_map/all_gather | solution.py:685
  307.6 30.7 %shard_map.215 = (bf16[1024,512]{1,0:T(8,128)(2,1)}, bf16[1024,512]{1,0:T(8,128)(2,1)}, bf16[1024,512]{1,0:T(8,128)(2,1)}, bf16[1024,512]{1,0:T(8,128)(2,1)}, bf...) custom-call(bf16[1024,2048]{1,0:T(8,128)(2,1)} %all-gather.9.cloned., ...), custom_call_target="tpu_custom_call" | custom-call | flops 21474836480 | bytes 37748736 | tf_op jit(solution)/shard_map/pallas_call | solution.py:423
  339.5 3.0 convolution_convert_fusion.4
  350.8 2.6 fusion.21
  362.9 5.1 collective-permute-done.22
  376.0 6.7 %collective-permute-done.23 = bf16[1024,256]{1,0:T(8,128)(2,1)S(1)} collective-permute-done((bf16[1024,256]{1,0:T(8,128)(2,1)S(1)}, bf16[1024,256]{1,0:T(8,128)(2,1)S(1)}, u32[]{:S(2)}, u32[]{:S(2)}) %collective-permute-start.23) | collective-permute-done | bytes 524320 | tf_op jit(solution)/shard_map/ppermute | solution.py:527
  387.2 3.4 shard_map.216
  396.8 4.2 all-to-all-start.3
  402.2 9.7 %shard_map.217 = bf16[1024,2048]{1,0:T(8,128)(2,1)} custom-call(bf16[1024,1024]{1,0:T(8,128)(2,1)} %get-tuple-element.146.inner_ref, bf16[8,256,256]{2,1,0:T(8,128)(2,1)} %copy-done.23, bf16[8,256,256]{2,1,0:T(8,128)(2,1)} %collective-permute-done.9.refs_6_.refs_1_, bf16[8,256,256]{2,1,0:T(8,128)(2,1)} %collective-permute-done.10.refs_7_.refs_2_, ...), custom_call_target="tpu_custom_call" | custom-call | flops 4294967296 | bytes 12582912 | tf_op jit(solution)/shard_map/pallas_call | solution.py:472
  411.9 5.2 collective-permute-done.30
  424.1 15.5 %collective-permute-done.26 = bf16[1024,512]{1,0:T(8,128)(2,1)} collective-permute-done((bf16[1024,512]{1,0:T(8,128)(2,1)}, bf16[1024,512]{1,0:T(8,128)(2,1)}, u32[]{:S(2)}, u32[]{:S(2)}) %collective-permute-start.26) | collective-permute-done | bytes 1048608 | tf_op jit(solution)/shard_map/ppermute | solution.py:527
  445.9 6.3 collective-permute-done.31
  452.6 7.3 %collective-permute-done.27 = bf16[1024,256]{1,0:T(8,128)(2,1)S(1)} collective-permute-done((bf16[1024,256]{1,0:T(8,128)(2,1)S(1)}, bf16[1024,256]{1,0:T(8,128)(2,1)S(1)}, u32[]{:S(2)}, u32[]{:S(2)}) %collective-permute-start.27) | collective-permute-done | bytes 524320 | tf_op jit(solution)/shard_map/ppermute | solution.py:527
  462.0 4.1 all-to-all-start.4
  466.1 16.6 %shard_map.218 = (bf16[1024,256]{1,0:T(8,128)(2,1)}, f32[1024,512]{1,0:T(8,128)}, bf16[1024,512]{1,0:T(8,128)(2,1)}, bf16[1024,512]{1,0:T(8,128)(2,1)}) custom-call(s32[2]{0:T(128)} %get-tuple-element.196.lo_ref, bf16[1024,256]{1,0:T(8,128)(2,1)} %get-tuple-element.104.q_ref, bf16[1024,2048]{1,0:T(8,128)(2,1)} %all-gather.11.cloned.1.call-done.ga_ref, ...), custom_call_target="tpu_custom_call" | custom-call | flops 24999999488 | bytes 20971520 | tf_op jit(solution)/shard_map/pallas_call | solution.py:242
  483.7 3.5 convolution_convert_fusion
  489.9 10.9 %collective-permute-start.34 = (bf16[64,2176]{1,0:T(8,128)(2,1)S(1)}, bf16[64,2176]{1,0:T(8,128)(2,1)S(1)}, u32[]{:S(2)}, u32[]{:S(2)}) collective-permute-start(bf16[64,2176]{1,0:T(8,128)(2,1)S(1)} %get-tuple-element.181), channel_id=1, source_target_pairs={{0,8},{8,0},{16,24},{24,16},{1,9},{9,1},{17,25},{25,17},{2,10},{10... | collective-permute-start | bytes 835592 | tf_op jit(solution)/shard_map/ppermute | solution.py:527
  500.8 4.0 collective-permute-start.35
  504.7 26.0 %collective-permute-done.34 = bf16[64,2176]{1,0:T(8,128)(2,1)S(1)} collective-permute-done((bf16[64,2176]{1,0:T(8,128)(2,1)S(1)}, bf16[64,2176]{1,0:T(8,128)(2,1)S(1)}, u32[]{:S(2)}, u32[]{:S(2)}) %collective-permute-start.34) | collective-permute-done | bytes 278560 | tf_op jit(solution)/shard_map/ppermute | solution.py:527
  530.8 7.8 %collective-permute-done.36 = bf16[64,2176]{1,0:T(8,128)(2,1)S(1)} collective-permute-done((bf16[64,2176]{1,0:T(8,128)(2,1)S(1)}, bf16[64,2176]{1,0:T(8,128)(2,1)S(1)}, u32[]{:S(2)}, u32[]{:S(2)}) %collective-permute-start.36) | collective-permute-done | bytes 278560 | tf_op jit(solution)/shard_map/ppermute | solution.py:527
  539.4 6.4 all-to-all-done.4
  545.8 4.2 reduce-scatter.9.cloned.1.call-done
  550.1 8.5 %shard_map.219 = (bf16[1024,768]{1,0:T(8,128)(2,1)}, bf16[1024,2048]{1,0:T(8,128)(2,1)}) custom-call(bf16[1024,256]{1,0:T(8,128)(2,1)} %get-tuple-element.154.gq_ref, f32[1024,512]{1,0:T(8,128)} %get-tuple-element.160.own_ref, f32[1024,128]{1,0:T(8,128)} %get-tuple-element.197.cos_ref, f32[1024,128]{1,0:T(8,128)} %get-tuple-element.198.sin_ref, ...), custom_call_target="tpu_custom_call" | custom-call | flops 3221225472 | bytes 16777216 | tf_op jit(solution)/shard_map/pallas_call | solution.py:310
  558.6 7.8 %shard_map.220 = (bf16[2,512,384]{2,1,0:T(8,128)(2,1)}, bf16[2,512,384]{2,1,0:T(8,128)(2,1)}, f32[2,512,384]{2,1,0:T(8,128)}, f32[2,512,384]{2,1,0:T(8,128)}) custom-call(s32[1]{0:T(128)} %bitcast.16.index_ref, bf16[1024,2048]{1,0:T(8,128)(2,1)} %get-tuple-element.164.h_ref, bf16[1024,768]{1,0:T(8,128)(2,1)} %get-tuple-element.165.g_ref), custom_call_target="tpu_custom_call" | custom-call | flops 3221225472 | bytes 9437184 | tf_op jit(solution)/shard_map/pallas_call | solution.py:354
  566.4 10.2 %collective-permute-start.39 = (bf16[2,512,384]{2,1,0:T(8,128)(2,1)}, bf16[2,512,384]{2,1,0:T(8,128)(2,1)S(1)}, u32[]{:S(2)}, u32[]{:S(2)}) collective-permute-start(bf16[2,512,384]{2,1,0:T(8,128)(2,1)} %get-tuple-element.167), channel_id=1, source_target_pairs={{0,8},{8,0},{16,24},{24,16},{1,9},{9,1},{17,25},{25,17},{2,10},{10... | collective-permute-start | bytes 2359304 | tf_op jit(solution)/shard_map/ppermute | solution.py:527
  580.4 13.7 %collective-permute-done.39 = bf16[2,512,384]{2,1,0:T(8,128)(2,1)S(1)} collective-permute-done((bf16[2,512,384]{2,1,0:T(8,128)(2,1)}, bf16[2,512,384]{2,1,0:T(8,128)(2,1)S(1)}, u32[]{:S(2)}, u32[]{:S(2)}) %collective-permute-start.39) | collective-permute-done | bytes 786464 | tf_op jit(solution)/shard_map/ppermute | solution.py:527
  601.1 3.7 collective-permute-done.40
  607.1 7.8 %all-to-all-start.5 = ((bf16[8,64,768]{2,1,0:T(8,128)(2,1)}), bf16[8,64,768]{2,1,0:T(8,128)(2,1)S(1)}, u32[]{:S(2)}, u32[]{:S(2)}) async-start(bf16[8,64,768]{2,1,0:T(8,128)(2,1)} %pad_maximum_fusion.5), calls=%async_computation.9 | async-start | bytes 1572864 | tf_op jit(solution)/shard_map/all_to_all | solution.py:800
  618.0 7.6 %reduce-scatter.11.cloned.1.call-done = bf16[128,2048]{1,0:T(8,128)(2,1)} async-done(((bf16[1024,2048]{1,0:T(8,128)(2,1)}), bf16[128,2048]{1,0:T(8,128)(2,1)}) %reduce-scatter.11.cloned.1.call-update) | async-done | bytes 524304 | tf_op jit(solution)/shard_map/reduce_scatter | solution.py:785
  627.0 3.0 fusion.33
  630.0 8.9 %all-to-all-done.5.got_ref = bf16[8,64,768]{2,1,0:T(8,128)(2,1)S(1)} async-done(((bf16[8,64,768]{2,1,0:T(8,128)(2,1)}), bf16[8,64,768]{2,1,0:T(8,128)(2,1)S(1)}, u32[]{:S(2)}, u32[]{:S(2)}) %all-to-all-start.5) | async-done | bytes 786464 | tf_op jit(solution)/shard_map/all_to_all | solution.py:800
  (315 shorter events, 149.4 us)
Async XLA Ops:
  10.8 37.6 %all-to-all-start = ((bf16[8,80,768]{2,1,0:T(8,128)(2,1)}), bf16[8,80,768]{2,1,0:T(8,128)(2,1)S(1)}, u32[]{:S(2)}, u32[]{:S(2)}) async-start(bf16[8,80,768]{2,1,0:T(8,128)(2,1)} %shard_map.212), calls=%async_computation | async-start | bytes 1966080 | tf_op jit(solution)/shard_map/all_to_all | solution.py:637
  17.1 92.3 %all-gather.5.cloned.1.call-start = ((), (), s32[]{:S(2)}) async-start(), calls=%async_computation.10 | async-start | bytes 4718592 | tf_op jit(solution)/shard_map/all_gather | solution.py:638
  53.9 20.7 %collective-permute-start.1 = (bf16[8,80,768]{2,1,0:T(8,128)(2,1)}, bf16[8,80,768]{2,1,0:T(8,128)(2,1)S(1)}, u32[]{:S(2)}, u32[]{:S(2)}) collective-permute-start(bf16[8,80,768]{2,1,0:T(8,128)(2,1)} %copy-done.6), channel_id=1, source_target_pairs={{0,16},{8,24},{16,0},{24,8},{1,17},{9,25},{17,1},{25,9},{2,18},{10... | collective-permute-start | bytes 2949128 | tf_op jit(solution)/shard_map/ppermute | solution.py:527
  53.9 23.5 %collective-permute-start.7 = (bf16[8,80,768]{2,1,0:T(8,128)(2,1)}, bf16[8,80,768]{2,1,0:T(8,128)(2,1)S(1)}, u32[]{:S(2)}, u32[]{:S(2)}) collective-permute-start(bf16[8,80,768]{2,1,0:T(8,128)(2,1)} %copy-done.6), channel_id=1, source_target_pairs={{0,8},{8,0},{16,24},{24,16},{1,9},{9,1},{17,25},{25,17},{2,10},{10... | collective-permute-start | bytes 2949128 | tf_op jit(solution)/shard_map/ppermute | solution.py:527
  75.4 18.0 %collective-permute-start.2 = (bf16[4,80,768]{2,1,0:T(8,128)(2,1)}, bf16[4,80,768]{2,1,0:T(8,128)(2,1)}, u32[]{:S(2)}, u32[]{:S(2)}) collective-permute-start(bf16[4,80,768]{2,1,0:T(8,128)(2,1)} %slice.208), channel_id=1, source_target_pairs={{0,8},{8,0},{16,24},{24,16},{1,9},{9,1},{17,25},{25,17},{2,10},{10... | collective-permute-start | bytes 1474568 | tf_op jit(solution)/shard_map/ppermute | solution.py:527
  78.4 17.7 %collective-permute-start.8 = (bf16[4,80,768]{2,1,0:T(8,128)(2,1)S(1)}, bf16[4,80,768]{2,1,0:T(8,128)(2,1)}, u32[]{:S(2)}, u32[]{:S(2)}) collective-permute-start(bf16[4,80,768]{2,1,0:T(8,128)(2,1)S(1)} %slice.214), channel_id=1, source_target_pairs={{0,16},{8,24},{16,0},{24,8},{1,17},{9,25},{17,1},{25,9},{2,18},{10... | collective-permute-start | bytes 1474568 | tf_op jit(solution)/shard_map/ppermute | solution.py:527
  78.5 42.5 %all-to-all-start.1 = ((bf16[8,256,256]{2,1,0:T(8,128)(2,1)}), bf16[8,256,256]{2,1,0:T(8,128)(2,1)S(1)}, u32[]{:S(2)}, u32[]{:S(2)}) async-start(bf16[8,256,256]{2,1,0:T(8,128)(2,1)} %bitcast.10), calls=%async_computation.1 | async-start | bytes 2097152 | tf_op jit(solution)/shard_map/all_to_all | solution.py:648
  90.4 118.8 %all-gather.7.cloned.1.call-start = ((), (), s32[]{:S(2)}) async-start(), calls=%async_computation.11 | async-start | bytes 4718592 | tf_op jit(solution)/shard_map/all_gather | solution.py:672
  122.1 87.1 %all-to-all-start.2 = ((bf16[8,512,256]{2,1,0:T(8,128)(2,1)}), bf16[8,512,256]{2,1,0:T(8,128)(2,1)}, u32[]{:S(2)}, u32[]{:S(2)}) async-start(bf16[8,512,256]{2,1,0:T(8,128)(2,1)} %pad_maximum_fusion), calls=%async_computation.2 | async-start | bytes 4194304 | tf_op jit(solution)/shard_map/all_to_all | solution.py:648
  126.4 131.6 %reduce-scatter.5.cloned.1.call-start = ((), (), s32[]{:S(2)}) async-start(), calls=%async_computation.12 | async-start | bytes 4718592 | tf_op jit(solution)/shard_map/reduce_scatter | solution.py:678
  126.5 41.3 %collective-permute-start.11 = (bf16[1024,512]{1,0:T(8,128)(2,1)S(1)}, bf16[1024,512]{1,0:T(8,128)(2,1)S(1)}, u32[]{:S(2)}, u32[]{:S(2)}) collective-permute-start(bf16[1024,512]{1,0:T(8,128)(2,1)S(1)} %copy-done.14), channel_id=1, source_target_pairs={{0,16},{8,24},{1,17},{9,25},{2,18},{10,26},{3,19},{11,27},{4,20},{... | collective-permute-start | bytes 3145736 | tf_op jit(solution)/shard_map/ppermute | solution.py:659
  129.7 46.0 %collective-permute-start.10 = (bf16[8,256,256]{2,1,0:T(8,128)(2,1)}, bf16[8,256,256]{2,1,0:T(8,128)(2,1)}, u32[]{:S(2)}, u32[]{:S(2)}) collective-permute-start(bf16[8,256,256]{2,1,0:T(8,128)(2,1)} %copy-done.23), channel_id=1, source_target_pairs={{0,16},{8,24},{16,0},{24,8},{1,17},{9,25},{17,1},{25,9},{2,18},{10... | collective-permute-start | bytes 3145736 | tf_op jit(solution)/shard_map/ppermute | solution.py:527
  129.8 45.9 %collective-permute-start.9 = (bf16[8,256,256]{2,1,0:T(8,128)(2,1)}, bf16[8,256,256]{2,1,0:T(8,128)(2,1)}, u32[]{:S(2)}, u32[]{:S(2)}) collective-permute-start(bf16[8,256,256]{2,1,0:T(8,128)(2,1)} %copy-done.23), channel_id=1, source_target_pairs={{0,8},{8,0},{16,24},{24,16},{1,9},{9,1},{17,25},{25,17},{2,10},{10... | collective-permute-start | bytes 3145736 | tf_op jit(solution)/shard_map/ppermute | solution.py:527
  131.4 35.1 %collective-permute-start.13 = (bf16[512,512]{1,0:T(8,128)(2,1)S(1)}, bf16[512,512]{1,0:T(8,128)(2,1)}, u32[]{:S(2)}, u32[]{:S(2)}) collective-permute-start(bf16[512,512]{1,0:T(8,128)(2,1)S(1)} %slice.175), channel_id=1, source_target_pairs={{8,0},{9,1},{10,2},{11,3},{12,4},{13,5},{14,6},{15,7}} | collective-permute-start | bytes 1572872 | tf_op jit(solution)/shard_map/ppermute | solution.py:661
  132.7 44.0 %collective-permute-start.12 = (bf16[1024,512]{1,0:T(8,128)(2,1)S(1)}, bf16[1024,512]{1,0:T(8,128)(2,1)}, u32[]{:S(2)}, u32[]{:S(2)}) collective-permute-start(bf16[1024,512]{1,0:T(8,128)(2,1)S(1)} %copy-done.14), channel_id=1, source_target_pairs={{0,8},{16,24},{1,9},{17,25},{2,10},{18,26},{3,11},{19,27},{4,12},{... | collective-permute-start | bytes 3145736 | tf_op jit(solution)/shard_map/ppermute | solution.py:660
  166.5 19.8 %collective-permute-start.14 = (bf16[512,512]{1,0:T(8,128)(2,1)}, bf16[512,512]{1,0:T(8,128)(2,1)S(1)}, u32[]{:S(2)}, u32[]{:S(2)}) collective-permute-start(bf16[512,512]{1,0:T(8,128)(2,1)} %collective-permute-done.13), channel_id=1, source_target_pairs={{0,16},{1,17},{2,18},{3,19},{4,20},{5,21},{6,22},{7,23}} | collective-permute-start | bytes 1572872 | tf_op jit(solution)/shard_map/ppermute | solution.py:662
  167.9 18.4 %collective-permute-start.15 = (bf16[512,512]{1,0:T(8,128)(2,1)S(1)}, bf16[512,512]{1,0:T(8,128)(2,1)}, u32[]{:S(2)}, u32[]{:S(2)}) collective-permute-start(bf16[512,512]{1,0:T(8,128)(2,1)S(1)} %slice.223), channel_id=1, source_target_pairs={{24,16},{25,17},{26,18},{27,19},{28,20},{29,21},{30,22},{31,23}} | collective-permute-start | bytes 1572872 | tf_op jit(solution)/shard_map/ppermute | solution.py:663
  209.2 98.3 %all-gather.9.cloned.1.call-start = ((), (), s32[]{:S(2)}) async-start(), calls=%async_computation.13 | async-start | bytes 4718592 | tf_op jit(solution)/shard_map/all_gather | solution.py:685
  209.3 47.4 %collective-permute-start.16 = (bf16[8,512,256]{2,1,0:T(8,128)(2,1)}, bf16[8,512,256]{2,1,0:T(8,128)(2,1)S(1)}, u32[]{:S(2)}, u32[]{:S(2)}) collective-permute-start(bf16[8,512,256]{2,1,0:T(8,128)(2,1)} %all-to-all-done.2.refs_0_), channel_id=1, source_target_pairs={{0,8},{8,0},{16,24},{24,16},{1,9},{9,1},{17,25},{25,17},{2,10},{10... | collective-permute-start | bytes 6291464 | tf_op jit(solution)/shard_map/ppermute | solution.py:527
  210.6 47.2 %collective-permute-start.17 = (bf16[8,512,256]{2,1,0:T(8,128)(2,1)}, bf16[8,512,256]{2,1,0:T(8,128)(2,1)}, u32[]{:S(2)}, u32[]{:S(2)}) collective-permute-start(bf16[8,512,256]{2,1,0:T(8,128)(2,1)} %all-to-all-done.2.refs_0_), channel_id=1, source_target_pairs={{0,16},{8,24},{16,0},{24,8},{1,17},{9,25},{17,1},{25,9},{2,18},{10... | collective-permute-start | bytes 6291464 | tf_op jit(solution)/shard_map/ppermute | solution.py:527
  261.8 125.4 %reduce-scatter.7.cloned.1.call-start = ((), (), s32[]{:S(2)}) async-start(), calls=%async_computation.14 | async-start | bytes 4718592 | tf_op jit(solution)/shard_map/reduce_scatter | solution.py:693
  261.9 37.2 %collective-permute-start.18 = (bf16[4,512,256]{2,1,0:T(8,128)(2,1)S(1)}, bf16[4,512,256]{2,1,0:T(8,128)(2,1)S(1)}, u32[]{:S(2)}, u32[]{:S(2)}) collective-permute-start(bf16[4,512,256]{2,1,0:T(8,128)(2,1)S(1)} %slice.178), channel_id=1, source_target_pairs={{0,16},{8,24},{16,0},{24,8},{1,17},{9,25},{17,1},{25,9},{2,18},{10... | collective-permute-start | bytes 3145736 | tf_op jit(solution)/shard_map/ppermute | solution.py:527
  264.8 35.2 %collective-permute-start.19 = (bf16[4,512,256]{2,1,0:T(8,128)(2,1)S(1)}, bf16[4,512,256]{2,1,0:T(8,128)(2,1)S(1)}, u32[]{:S(2)}, u32[]{:S(2)}) collective-permute-start(bf16[4,512,256]{2,1,0:T(8,128)(2,1)S(1)} %slice.179), channel_id=1, source_target_pairs={{0,8},{8,0},{16,24},{24,16},{1,9},{9,1},{17,25},{25,17},{2,10},{10... | collective-permute-start | bytes 3145736 | tf_op jit(solution)/shard_map/ppermute | solution.py:527
  267.4 29.2 %collective-permute-start.20 = (bf16[4,256,256]{2,1,0:T(8,128)(2,1)S(1)}, bf16[4,256,256]{2,1,0:T(8,128)(2,1)S(1)}, u32[]{:S(2)}, u32[]{:S(2)}) collective-permute-start(bf16[4,256,256]{2,1,0:T(8,128)(2,1)S(1)} %slice.180), channel_id=1, source_target_pairs={{0,16},{8,24},{16,0},{24,8},{1,17},{9,25},{17,1},{25,9},{2,18},{10... | collective-permute-start | bytes 1572872 | tf_op jit(solution)/shard_map/ppermute | solution.py:527
  269.1 30.0 %collective-permute-start.21 = (bf16[4,256,256]{2,1,0:T(8,128)(2,1)S(1)}, bf16[4,256,256]{2,1,0:T(8,128)(2,1)S(1)}, u32[]{:S(2)}, u32[]{:S(2)}) collective-permute-start(bf16[4,256,256]{2,1,0:T(8,128)(2,1)S(1)} %slice.181), channel_id=1, source_target_pairs={{0,8},{8,0},{16,24},{24,16},{1,9},{9,1},{17,25},{25,17},{2,10},{10... | collective-permute-start | bytes 1572872 | tf_op jit(solution)/shard_map/ppermute | solution.py:527
  338.3 122.1 %all-gather.11.cloned.1.call-start = ((), (), s32[]{:S(2)}) async-start(), calls=%async_computation.15 | async-start | bytes 4718592 | tf_op jit(solution)/shard_map/all_gather | solution.py:746
  342.6 25.4 %collective-permute-start.22 = (bf16[1024,512]{1,0:T(8,128)(2,1)S(1)}, bf16[1024,512]{1,0:T(8,128)(2,1)S(1)}, u32[]{:S(2)}, u32[]{:S(2)}) collective-permute-start(bf16[1024,512]{1,0:T(8,128)(2,1)S(1)} %convolution_convert_fusion.4), channel_id=1, source_target_pairs={{0,8},{8,0},{16,24},{24,16},{1,9},{9,1},{17,25},{25,17},{2,10},{10... | collective-permute-start | bytes 3145736 | tf_op jit(solution)/shard_map/ppermute | solution.py:527
  345.4 25.4 %collective-permute-start.24 = (bf16[1024,512]{1,0:T(8,128)(2,1)S(1)}, bf16[1024,512]{1,0:T(8,128)(2,1)S(1)}, u32[]{:S(2)}, u32[]{:S(2)}) collective-permute-start(bf16[1024,512]{1,0:T(8,128)(2,1)S(1)} %convolution_convert_fusion.3), channel_id=1, source_target_pairs={{0,16},{8,24},{16,0},{24,8},{1,17},{9,25},{17,1},{25,9},{2,18},{10... | collective-permute-start | bytes 3145736 | tf_op jit(solution)/shard_map/ppermute | solution.py:527
  390.6 26.5 %collective-permute-start.30 = (bf16[512,1024]{1,0:T(8,128)(2,1)}, bf16[512,1024]{1,0:T(8,128)(2,1)}, u32[]{:S(2)}, u32[]{:S(2)}) collective-permute-start(bf16[512,1024]{1,0:T(8,128)(2,1)} %fusion.10), channel_id=1, source_target_pairs={{0,8},{8,0},{16,24},{24,16},{1,9},{9,1},{17,25},{25,17},{2,10},{10... | collective-permute-start | bytes 3145736 | tf_op jit(solution)/shard_map/ppermute | solution.py:527
  392.2 28.7 %collective-permute-start.32 = (bf16[512,1024]{1,0:T(8,128)(2,1)}, bf16[512,1024]{1,0:T(8,128)(2,1)}, u32[]{:S(2)}, u32[]{:S(2)}) collective-permute-start(bf16[512,1024]{1,0:T(8,128)(2,1)} %fusion.13), channel_id=1, source_target_pairs={{0,16},{8,24},{16,0},{24,8},{1,17},{9,25},{17,1},{25,9},{2,18},{10... | collective-permute-start | bytes 3145736 | tf_op jit(solution)/shard_map/ppermute | solution.py:527
  396.8 63.6 %all-to-all-start.3 = ((bf16[8,264,256]{2,1,0:T(8,128)(2,1)}), bf16[8,264,256]{2,1,0:T(8,128)(2,1)}, u32[]{:S(2)}, u32[]{:S(2)}) async-start(bf16[8,264,256]{2,1,0:T(8,128)(2,1)} %fusion.29), calls=%async_computation.5 | async-start | bytes 2162688 | tf_op jit(solution)/shard_map/all_to_all | solution.py:648
  401.0 149.0 %reduce-scatter.9.cloned.1.call-start = ((), (), s32[]{:S(2)}) async-start(), calls=%async_computation.16 | async-start | bytes 4718592 | tf_op jit(solution)/shard_map/reduce_scatter | solution.py:769
  401.1 38.5 %collective-permute-start.26 = (bf16[1024,512]{1,0:T(8,128)(2,1)}, bf16[1024,512]{1,0:T(8,128)(2,1)}, u32[]{:S(2)}, u32[]{:S(2)}) collective-permute-start(bf16[1024,512]{1,0:T(8,128)(2,1)} %convolution_convert_fusion.2), channel_id=1, source_target_pairs={{0,8},{8,0},{16,24},{24,16},{1,9},{9,1},{17,25},{25,17},{2,10},{10... | collective-permute-start | bytes 3145736 | tf_op jit(solution)/shard_map/ppermute | solution.py:527
  401.7 41.1 %collective-permute-start.28 = (bf16[1024,512]{1,0:T(8,128)(2,1)}, bf16[1024,512]{1,0:T(8,128)(2,1)}, u32[]{:S(2)}, u32[]{:S(2)}) collective-permute-start(bf16[1024,512]{1,0:T(8,128)(2,1)} %convolution_convert_fusion.1), channel_id=1, source_target_pairs={{0,16},{8,24},{16,0},{24,8},{1,17},{9,25},{17,1},{25,9},{2,18},{10... | collective-permute-start | bytes 3145736 | tf_op jit(solution)/shard_map/ppermute | solution.py:527
  419.4 32.8 %collective-permute-start.31 = (bf16[256,1024]{1,0:T(8,128)(2,1)S(1)}, bf16[256,1024]{1,0:T(8,128)(2,1)S(1)}, u32[]{:S(2)}, u32[]{:S(2)}) collective-permute-start(bf16[256,1024]{1,0:T(8,128)(2,1)S(1)} %slice.320), channel_id=1, source_target_pairs={{0,16},{8,24},{16,0},{24,8},{1,17},{9,25},{17,1},{25,9},{2,18},{10... | collective-permute-start | bytes 1572872 | tf_op jit(solution)/shard_map/ppermute | solution.py:527
  422.6 29.8 %collective-permute-start.33 = (bf16[256,1024]{1,0:T(8,128)(2,1)S(1)}, bf16[256,1024]{1,0:T(8,128)(2,1)S(1)}, u32[]{:S(2)}, u32[]{:S(2)}) collective-permute-start(bf16[256,1024]{1,0:T(8,128)(2,1)S(1)} %slice.319), channel_id=1, source_target_pairs={{0,8},{8,0},{16,24},{24,16},{1,9},{9,1},{17,25},{25,17},{2,10},{10... | collective-permute-start | bytes 1572872 | tf_op jit(solution)/shard_map/ppermute | solution.py:527
  441.2 18.7 %collective-permute-start.27 = (bf16[1024,256]{1,0:T(8,128)(2,1)S(1)}, bf16[1024,256]{1,0:T(8,128)(2,1)S(1)}, u32[]{:S(2)}, u32[]{:S(2)}) collective-permute-start(bf16[1024,256]{1,0:T(8,128)(2,1)S(1)} %slice.322), channel_id=1, source_target_pairs={{0,16},{8,24},{16,0},{24,8},{1,17},{9,25},{17,1},{25,9},{2,18},{10... | collective-permute-start | bytes 1572872 | tf_op jit(solution)/shard_map/ppermute | solution.py:527
  462.0 83.8 %all-to-all-start.4 = ((bf16[8,512,256]{2,1,0:T(8,128)(2,1)}), bf16[8,512,256]{2,1,0:T(8,128)(2,1)S(1)}, u32[]{:S(2)}, u32[]{:S(2)}) async-start(bf16[8,512,256]{2,1,0:T(8,128)(2,1)} %pad_maximum_fusion.1), calls=%async_computation.7 | async-start | bytes 4194304 | tf_op jit(solution)/shard_map/all_to_all | solution.py:648
  466.1 159.5 %reduce-scatter.11.cloned.1.call-start = ((), (), s32[]{:S(2)}) async-start(), calls=%async_computation.17 | async-start | bytes 4718592 | tf_op jit(solution)/shard_map/reduce_scatter | solution.py:785
  487.2 62.9 %collective-permute-start.37 = (bf16[1024,512]{1,0:T(8,128)(2,1)}, bf16[1024,512]{1,0:T(8,128)(2,1)}, u32[]{:S(2)}, u32[]{:S(2)}) collective-permute-start(bf16[1024,512]{1,0:T(8,128)(2,1)} %get-tuple-element.161), channel_id=1, source_target_pairs={{16,0},{24,8},{17,1},{25,9},{18,2},{26,10},{19,3},{27,11},{20,4},{... | collective-permute-start | bytes 3145736 | tf_op jit(solution)/shard_map/ppermute | solution.py:766
  488.5 61.6 %collective-permute-start.38 = (bf16[1024,512]{1,0:T(8,128)(2,1)}, bf16[1024,512]{1,0:T(8,128)(2,1)}, u32[]{:S(2)}, u32[]{:S(2)}) collective-permute-start(bf16[1024,512]{1,0:T(8,128)(2,1)} %get-tuple-element.162), channel_id=1, source_target_pairs={{8,0},{16,8},{24,16},{9,1},{17,9},{25,17},{10,2},{18,10},{26,18},{... | collective-permute-start | bytes 3145736 | tf_op jit(solution)/shard_map/ppermute | solution.py:766
  489.9 40.9 %collective-permute-start.34 = (bf16[64,2176]{1,0:T(8,128)(2,1)S(1)}, bf16[64,2176]{1,0:T(8,128)(2,1)S(1)}, u32[]{:S(2)}, u32[]{:S(2)}) collective-permute-start(bf16[64,2176]{1,0:T(8,128)(2,1)S(1)} %get-tuple-element.181), channel_id=1, source_target_pairs={{0,8},{8,0},{16,24},{24,16},{1,9},{9,1},{17,25},{25,17},{2,10},{10... | collective-permute-start | bytes 835592 | tf_op jit(solution)/shard_map/ppermute | solution.py:527
  500.8 30.0 %collective-permute-start.35 = (bf16[64,2176]{1,0:T(8,128)(2,1)S(1)}, bf16[64,2176]{1,0:T(8,128)(2,1)S(1)}, u32[]{:S(2)}, u32[]{:S(2)}) collective-permute-start(bf16[64,2176]{1,0:T(8,128)(2,1)S(1)} %get-tuple-element.183), channel_id=1, source_target_pairs={{0,16},{8,24},{16,0},{24,8},{1,17},{9,25},{17,1},{25,9},{2,18},{10... | collective-permute-start | bytes 835592 | tf_op jit(solution)/shard_map/ppermute | solution.py:527
  504.7 33.8 %collective-permute-start.36 = (bf16[64,2176]{1,0:T(8,128)(2,1)S(1)}, bf16[64,2176]{1,0:T(8,128)(2,1)S(1)}, u32[]{:S(2)}, u32[]{:S(2)}) collective-permute-start(bf16[64,2176]{1,0:T(8,128)(2,1)S(1)} %get-tuple-element.182), channel_id=1, source_target_pairs={{0,24},{8,16},{16,8},{24,0},{1,25},{9,17},{17,9},{25,1},{2,26},{10... | collective-permute-start | bytes 835592 | tf_op jit(solution)/shard_map/ppermute | solution.py:527
  566.4 27.6 %collective-permute-start.39 = (bf16[2,512,384]{2,1,0:T(8,128)(2,1)}, bf16[2,512,384]{2,1,0:T(8,128)(2,1)S(1)}, u32[]{:S(2)}, u32[]{:S(2)}) collective-permute-start(bf16[2,512,384]{2,1,0:T(8,128)(2,1)} %get-tuple-element.167), channel_id=1, source_target_pairs={{0,8},{8,0},{16,24},{24,16},{1,9},{9,1},{17,25},{25,17},{2,10},{10... | collective-permute-start | bytes 2359304 | tf_op jit(solution)/shard_map/ppermute | solution.py:527
  577.4 19.2 %collective-permute-start.41 = (bf16[2,512,384]{2,1,0:T(8,128)(2,1)}, bf16[2,512,384]{2,1,0:T(8,128)(2,1)S(1)}, u32[]{:S(2)}, u32[]{:S(2)}) collective-permute-start(bf16[2,512,384]{2,1,0:T(8,128)(2,1)} %get-tuple-element.169), channel_id=1, source_target_pairs={{0,16},{8,24},{16,0},{24,8},{1,17},{9,25},{17,1},{25,9},{2,18},{10... | collective-permute-start | bytes 2359304 | tf_op jit(solution)/shard_map/ppermute | solution.py:527
  600.4 16.1 %collective-permute-start.43 = (bf16[64,2176]{1,0:T(8,128)(2,1)S(1)}, bf16[64,2176]{1,0:T(8,128)(2,1)S(1)}, u32[]{:S(2)}, u32[]{:S(2)}) collective-permute-start(bf16[64,2176]{1,0:T(8,128)(2,1)S(1)} %copy-done.26), channel_id=1, source_target_pairs={{0,0},{8,1},{16,2},{24,3},{1,4},{9,5},{17,6},{25,7},{2,8},{10,9},{... | collective-permute-start | bytes 835592 | tf_op jit(solution)/shard_map/ppermute | solution.py:797
  607.1 31.8 %all-to-all-start.5 = ((bf16[8,64,768]{2,1,0:T(8,128)(2,1)}), bf16[8,64,768]{2,1,0:T(8,128)(2,1)S(1)}, u32[]{:S(2)}, u32[]{:S(2)}) async-start(bf16[8,64,768]{2,1,0:T(8,128)(2,1)} %pad_maximum_fusion.5), calls=%async_computation.9 | async-start | bytes 1572864 | tf_op jit(solution)/shard_map/all_to_all | solution.py:800
  (60 other events, 601.0 us)
Sparse Core Ops, SparseCore 0:
  48.6 55.3 all-gather.4
  121.2 84.8 all-gather.6
  209.4 48.6 reduce-scatter.4
  261.9 45.6 all-gather.8
  338.5 48.7 reduce-scatter.6
  390.8 68.2 all-gather.10
  461.3 88.6 reduce-scatter.8
  558.7 66.8 reduce-scatter.10

commit v7 on v6

--- a/solution.py
+++ b/solution.py
@@ -254,7 +254,7 @@
         ],
         compiler_params=pltpu.CompilerParams(vmem_limit_bytes=VMEM),
         cost_estimate=pl.CostEstimate(
-            flops=25 * 10**9, bytes_accessed=20 * 2**20, transcendentals=4 * 10**6
+            flops=10**6, bytes_accessed=10**6, transcendentals=0
         ),
     )(lo, q, ga, start, wo, cos, sin, *kvs)
 

time: 659 us -> 659 us (level)
  no operation moved by 1% of the time
where the time goes in v7:
time: 659 us; the launch traced here: 651 us
  waiting for transfers between devices  318 us (48%)
  starting transfers between devices  116 us (18%)
  Pallas kernels  101 us (15%)
  other arithmetic  40 us (6%)
  local copies, waits for them, and re-layouts  32.4 us (5%)
  matrix products  28.4 us (4%)
  between operations  15.6 us (2%)
    ppermute x35, waiting for transfers between devices, xor_permute(): return lax.ppermute(x, 'uly', [(i, i ^ flip) for i in range(count)])  201 us
    ppermute x35, starting transfers between devices, xor_permute(): return lax.ppermute(x, 'uly', [(i, i ^ flip) for i in range(count)])  58.8 us
    pallas_call x1, Pallas kernels, ffn_call(): pl.pallas_call(functools.partial(ffn_kernel, places, blocks, groups), gri...  30.7 us
    all_to_all x1, waiting for transfers between devices, body(): qkv = lax.all_to_all(qkv, 'blk', 0, 0, tiled=True)  29.9 us
    dot_general x13, matrix products, t_dot(): lax.dot_general(left, right, (((0,), (0,)), ((), ())), preferred_element_...  28.4 us
    ppermute x1, waiting for transfers between devices, body(): over = lax.ppermute(kv[:half], 'uly', [(1, 0)])  27.5 us
    all_to_all x4, starting transfers between devices, body(): to_hidden = lambda w: lax.all_to_all(w, 'blk', 0, 0, tiled=True)  24.5 us
    all_to_all x4, waiting for transfers between devices, body(): to_hidden = lambda w: lax.all_to_all(w, 'blk', 0, 0, tiled=True)  19.2 us
  transfers between devices with their start and end apart: 58, of which 35 were waited for; matrix products, arithmetic and copies ran while one was open for 14% of the time, Pallas kernels for 8%

profile of v7, /device:TPU:0, one launch (start us, length us, event | category | flops | bytes accessed | tf_op | source)
XLA Modules:
  0.0 651.0 jit_solution(17528414059320193879)
XLA Ops:
  10.8 6.3 all-to-all-start
  18.6 29.9 %all-to-all-done = bf16[8,80,768]{2,1,0:T(8,128)(2,1)S(1)} async-done(((bf16[8,80,768]{2,1,0:T(8,128)(2,1)}), bf16[8,80,768]{2,1,0:T(8,128)(2,1)S(1)}, u32[]{:S(2)}, u32[]{:S(2)}) %all-to-all-start) | async-done | bytes 983072 | tf_op jit(solution)/shard_map/all_to_all | solution.py:637
  60.8 13.8 %collective-permute-done.1 = bf16[8,80,768]{2,1,0:T(8,128)(2,1)S(1)} collective-permute-done((bf16[8,80,768]{2,1,0:T(8,128)(2,1)}, bf16[8,80,768]{2,1,0:T(8,128)(2,1)S(1)}, u32[]{:S(2)}, u32[]{:S(2)}) %collective-permute-start.1) | collective-permute-done | bytes 983072 | tf_op jit(solution)/shard_map/ppermute | solution.py:527
  78.5 11.8 %all-to-all-start.1 = ((bf16[8,256,256]{2,1,0:T(8,128)(2,1)}), bf16[8,256,256]{2,1,0:T(8,128)(2,1)S(1)}, u32[]{:S(2)}, u32[]{:S(2)}) async-start(bf16[8,256,256]{2,1,0:T(8,128)(2,1)} %bitcast.10), calls=%async_computation.1 | async-start | bytes 2097152 | tf_op jit(solution)/shard_map/all_to_all | solution.py:648
  104.7 3.2 collective-permute-done.5
  109.5 8.8 %shard_map.213 = (bf16[1024,2048]{1,0:T(8,128)(2,1)}, bf16[1024,256]{1,0:T(8,128)(2,1)}, bf16[1024,512]{1,0:T(8,128)(2,1)}) custom-call(bf16[1024,2048]{1,0:T(8,128)(2,1)} %all-gather.5.cloned.1.call-done.x_ref, f32[1,2048]{1,0:T(1,128)} %reshape.229.gain_ref, bf16[2048,768]{1,0:T(8,128)(2,1)} %constant_dynamic-update-slice_fusion.w_ref, ...), custom_call_target="tpu_custom_call" | custom-call | flops 3221225472 | bytes 16777216 | tf_op jit(solution)/shard_map/pallas_call | solution.py:107
  118.3 2.8 all-to-all-done.1.refs_5_.refs_0_
  122.1 4.4 all-to-all-start.2
  126.5 3.2 collective-permute-start.11
  132.7 6.3 collective-permute-start.12
  139.0 27.5 %collective-permute-done.13 = bf16[512,512]{1,0:T(8,128)(2,1)} collective-permute-done((bf16[512,512]{1,0:T(8,128)(2,1)S(1)}, bf16[512,512]{1,0:T(8,128)(2,1)}, u32[]{:S(2)}, u32[]{:S(2)}) %collective-permute-start.13) | collective-permute-done | bytes 524320 | tf_op jit(solution)/shard_map/ppermute | solution.py:661
  171.1 4.6 collective-permute-done.10.refs_7_.refs_2_
  176.7 9.7 %collective-permute-done.14 = bf16[512,512]{1,0:T(8,128)(2,1)S(1)} collective-permute-done((bf16[512,512]{1,0:T(8,128)(2,1)}, bf16[512,512]{1,0:T(8,128)(2,1)S(1)}, u32[]{:S(2)}, u32[]{:S(2)}) %collective-permute-start.14) | collective-permute-done | bytes 524320 | tf_op jit(solution)/shard_map/ppermute | solution.py:662
  188.9 10.3 %shard_map.214 = (bf16[1024,256]{1,0:T(8,128)(2,1)}, bf16[1024,2048]{1,0:T(8,128)(2,1)}) custom-call(s32[2]{0:T(128)} %get-tuple-element.195.lo_ref, bf16[1024,256]{1,0:T(8,128)(2,1)} %get-tuple-element.104.q_ref, s32[1024,1]{1,0:T(8,128)} %copy.44.start_ref, bf16[256,2048]{1,0:T(8,128)(2,1)} %copy-done.1, bf16[1024,512]{1,0:T(8,128)(2,1)} %copy-done.3, ...), custom_call_target="tpu_custom_call" | custom-call | flops 1000000 | bytes 1000000 | tf_op jit(solution)/shard_map/pallas_call | solution.py:166
  199.2 10.0 %all-to-all-done.2.refs_0_ = bf16[8,512,256]{2,1,0:T(8,128)(2,1)} async-done(((bf16[8,512,256]{2,1,0:T(8,128)(2,1)}), bf16[8,512,256]{2,1,0:T(8,128)(2,1)}, u32[]{:S(2)}, u32[]{:S(2)}) %all-to-all-start.2) | async-done | bytes 2097184 | tf_op jit(solution)/shard_map/all_to_all | solution.py:648
  212.1 44.6 %collective-permute-done.16.refs_1_ = bf16[8,512,256]{2,1,0:T(8,128)(2,1)S(1)} collective-permute-done((bf16[8,512,256]{2,1,0:T(8,128)(2,1)}, bf16[8,512,256]{2,1,0:T(8,128)(2,1)S(1)}, u32[]{:S(2)}, u32[]{:S(2)}) %collective-permute-start.16) | collective-permute-done | bytes 2097184 | tf_op jit(solution)/shard_map/ppermute | solution.py:527
  269.7 26.8 %collective-permute-done.20.refs_8_.refs_3_ = bf16[4,256,256]{2,1,0:T(8,128)(2,1)S(1)} collective-permute-done((bf16[4,256,256]{2,1,0:T(8,128)(2,1)S(1)}, bf16[4,256,256]{2,1,0:T(8,128)(2,1)S(1)}, u32[]{:S(2)}, u32[]{:S(2)}) %collective-permute-start.20) | collective-permute-done | bytes 524320 | tf_op jit(solution)/shard_map/ppermute | solution.py:527
  299.9 7.7 %all-gather.9.cloned.1.call-done.h_ref = bf16[1024,2048]{1,0:T(8,128)(2,1)} async-done(((bf16[128,2048]{1,0:T(8,128)(2,1)}), bf16[1024,2048]{1,0:T(8,128)(2,1)}) %all-gather.9.cloned.1.call-update) | async-done | bytes 4194320 | tf_op jit(solution)/shard_map/all_gather | solution.py:685
  307.6 30.7 %shard_map.215 = (bf16[1024,512]{1,0:T(8,128)(2,1)}, bf16[1024,512]{1,0:T(8,128)(2,1)}, bf16[1024,512]{1,0:T(8,128)(2,1)}, bf16[1024,512]{1,0:T(8,128)(2,1)}, bf...) custom-call(bf16[1024,2048]{1,0:T(8,128)(2,1)} %all-gather.9.cloned., ...), custom_call_target="tpu_custom_call" | custom-call | flops 21474836480 | bytes 37748736 | tf_op jit(solution)/shard_map/pallas_call | solution.py:423
  339.5 3.0 convolution_convert_fusion.4
  350.8 2.6 fusion.21
  362.9 5.1 collective-permute-done.22
  376.0 6.7 %collective-permute-done.23 = bf16[1024,256]{1,0:T(8,128)(2,1)S(1)} collective-permute-done((bf16[1024,256]{1,0:T(8,128)(2,1)S(1)}, bf16[1024,256]{1,0:T(8,128)(2,1)S(1)}, u32[]{:S(2)}, u32[]{:S(2)}) %collective-permute-start.23) | collective-permute-done | bytes 524320 | tf_op jit(solution)/shard_map/ppermute | solution.py:527
  387.2 3.4 shard_map.216
  396.8 4.2 all-to-all-start.3
  402.2 9.7 %shard_map.217 = bf16[1024,2048]{1,0:T(8,128)(2,1)} custom-call(bf16[1024,1024]{1,0:T(8,128)(2,1)} %get-tuple-element.146.inner_ref, bf16[8,256,256]{2,1,0:T(8,128)(2,1)} %copy-done.23, bf16[8,256,256]{2,1,0:T(8,128)(2,1)} %collective-permute-done.9.refs_6_.refs_1_, bf16[8,256,256]{2,1,0:T(8,128)(2,1)} %collective-permute-done.10.refs_7_.refs_2_, ...), custom_call_target="tpu_custom_call" | custom-call | flops 4294967296 | bytes 12582912 | tf_op jit(solution)/shard_map/pallas_call | solution.py:472
  411.9 5.2 collective-permute-done.30
  424.1 15.5 %collective-permute-done.26 = bf16[1024,512]{1,0:T(8,128)(2,1)} collective-permute-done((bf16[1024,512]{1,0:T(8,128)(2,1)}, bf16[1024,512]{1,0:T(8,128)(2,1)}, u32[]{:S(2)}, u32[]{:S(2)}) %collective-permute-start.26) | collective-permute-done | bytes 1048608 | tf_op jit(solution)/shard_map/ppermute | solution.py:527
  445.9 6.3 collective-permute-done.31
  452.6 7.3 %collective-permute-done.27 = bf16[1024,256]{1,0:T(8,128)(2,1)S(1)} collective-permute-done((bf16[1024,256]{1,0:T(8,128)(2,1)S(1)}, bf16[1024,256]{1,0:T(8,128)(2,1)S(1)}, u32[]{:S(2)}, u32[]{:S(2)}) %collective-permute-start.27) | collective-permute-done | bytes 524320 | tf_op jit(solution)/shard_map/ppermute | solution.py:527
  462.0 4.1 all-to-all-start.4
  466.1 16.6 %shard_map.218 = (bf16[1024,256]{1,0:T(8,128)(2,1)}, f32[1024,512]{1,0:T(8,128)}, bf16[1024,512]{1,0:T(8,128)(2,1)}, bf16[1024,512]{1,0:T(8,128)(2,1)}) custom-call(s32[2]{0:T(128)} %get-tuple-element.196.lo_ref, bf16[1024,256]{1,0:T(8,128)(2,1)} %get-tuple-element.104.q_ref, bf16[1024,2048]{1,0:T(8,128)(2,1)} %all-gather.11.cloned.1.call-done.ga_ref, ...), custom_call_target="tpu_custom_call" | custom-call | flops 1000000 | bytes 1000000 | tf_op jit(solution)/shard_map/pallas_call | solution.py:242
  483.7 3.5 convolution_convert_fusion
  489.9 10.9 %collective-permute-start.34 = (bf16[64,2176]{1,0:T(8,128)(2,1)S(1)}, bf16[64,2176]{1,0:T(8,128)(2,1)S(1)}, u32[]{:S(2)}, u32[]{:S(2)}) collective-permute-start(bf16[64,2176]{1,0:T(8,128)(2,1)S(1)} %get-tuple-element.181), channel_id=1, source_target_pairs={{0,8},{8,0},{16,24},{24,16},{1,9},{9,1},{17,25},{25,17},{2,10},{10... | collective-permute-start | bytes 835592 | tf_op jit(solution)/shard_map/ppermute | solution.py:527
  500.8 4.0 collective-permute-start.35
  504.7 26.0 %collective-permute-done.34 = bf16[64,2176]{1,0:T(8,128)(2,1)S(1)} collective-permute-done((bf16[64,2176]{1,0:T(8,128)(2,1)S(1)}, bf16[64,2176]{1,0:T(8,128)(2,1)S(1)}, u32[]{:S(2)}, u32[]{:S(2)}) %collective-permute-start.34) | collective-permute-done | bytes 278560 | tf_op jit(solution)/shard_map/ppermute | solution.py:527
  530.8 7.8 %collective-permute-done.36 = bf16[64,2176]{1,0:T(8,128)(2,1)S(1)} collective-permute-done((bf16[64,2176]{1,0:T(8,128)(2,1)S(1)}, bf16[64,2176]{1,0:T(8,128)(2,1)S(1)}, u32[]{:S(2)}, u32[]{:S(2)}) %collective-permute-start.36) | collective-permute-done | bytes 278560 | tf_op jit(solution)/shard_map/ppermute | solution.py:527
  539.4 6.4 all-to-all-done.4
  545.8 4.2 reduce-scatter.9.cloned.1.call-done
  550.1 8.5 %shard_map.219 = (bf16[1024,768]{1,0:T(8,128)(2,1)}, bf16[1024,2048]{1,0:T(8,128)(2,1)}) custom-call(bf16[1024,256]{1,0:T(8,128)(2,1)} %get-tuple-element.154.gq_ref, f32[1024,512]{1,0:T(8,128)} %get-tuple-element.160.own_ref, f32[1024,128]{1,0:T(8,128)} %get-tuple-element.197.cos_ref, f32[1024,128]{1,0:T(8,128)} %get-tuple-element.198.sin_ref, ...), custom_call_target="tpu_custom_call" | custom-call | flops 3221225472 | bytes 16777216 | tf_op jit(solution)/shard_map/pallas_call | solution.py:310
  558.6 7.8 %shard_map.220 = (bf16[2,512,384]{2,1,0:T(8,128)(2,1)}, bf16[2,512,384]{2,1,0:T(8,128)(2,1)}, f32[2,512,384]{2,1,0:T(8,128)}, f32[2,512,384]{2,1,0:T(8,128)}) custom-call(s32[1]{0:T(128)} %bitcast.16.index_ref, bf16[1024,2048]{1,0:T(8,128)(2,1)} %get-tuple-element.164.h_ref, bf16[1024,768]{1,0:T(8,128)(2,1)} %get-tuple-element.165.g_ref), custom_call_target="tpu_custom_call" | custom-call | flops 3221225472 | bytes 9437184 | tf_op jit(solution)/shard_map/pallas_call | solution.py:354
  566.4 10.2 %collective-permute-start.39 = (bf16[2,512,384]{2,1,0:T(8,128)(2,1)}, bf16[2,512,384]{2,1,0:T(8,128)(2,1)S(1)}, u32[]{:S(2)}, u32[]{:S(2)}) collective-permute-start(bf16[2,512,384]{2,1,0:T(8,128)(2,1)} %get-tuple-element.167), channel_id=1, source_target_pairs={{0,8},{8,0},{16,24},{24,16},{1,9},{9,1},{17,25},{25,17},{2,10},{10... | collective-permute-start | bytes 2359304 | tf_op jit(solution)/shard_map/ppermute | solution.py:527
  580.4 13.7 %collective-permute-done.39 = bf16[2,512,384]{2,1,0:T(8,128)(2,1)S(1)} collective-permute-done((bf16[2,512,384]{2,1,0:T(8,128)(2,1)}, bf16[2,512,384]{2,1,0:T(8,128)(2,1)S(1)}, u32[]{:S(2)}, u32[]{:S(2)}) %collective-permute-start.39) | collective-permute-done | bytes 786464 | tf_op jit(solution)/shard_map/ppermute | solution.py:527
  601.1 3.7 collective-permute-done.40
  607.1 7.8 %all-to-all-start.5 = ((bf16[8,64,768]{2,1,0:T(8,128)(2,1)}), bf16[8,64,768]{2,1,0:T(8,128)(2,1)S(1)}, u32[]{:S(2)}, u32[]{:S(2)}) async-start(bf16[8,64,768]{2,1,0:T(8,128)(2,1)} %pad_maximum_fusion.5), calls=%async_computation.9 | async-start | bytes 1572864 | tf_op jit(solution)/shard_map/all_to_all | solution.py:800
  618.0 7.6 %reduce-scatter.11.cloned.1.call-done = bf16[128,2048]{1,0:T(8,128)(2,1)} async-done(((bf16[1024,2048]{1,0:T(8,128)(2,1)}), bf16[128,2048]{1,0:T(8,128)(2,1)}) %reduce-scatter.11.cloned.1.call-update) | async-done | bytes 524304 | tf_op jit(solution)/shard_map/reduce_scatter | solution.py:785
  627.0 3.0 fusion.33
  630.0 8.9 %all-to-all-done.5.got_ref = bf16[8,64,768]{2,1,0:T(8,128)(2,1)S(1)} async-done(((bf16[8,64,768]{2,1,0:T(8,128)(2,1)}), bf16[8,64,768]{2,1,0:T(8,128)(2,1)S(1)}, u32[]{:S(2)}, u32[]{:S(2)}) %all-to-all-start.5) | async-done | bytes 786464 | tf_op jit(solution)/shard_map/all_to_all | solution.py:800
  (315 shorter events, 149.4 us)
Async XLA Ops:
  10.8 37.6 %all-to-all-start = ((bf16[8,80,768]{2,1,0:T(8,128)(2,1)}), bf16[8,80,768]{2,1,0:T(8,128)(2,1)S(1)}, u32[]{:S(2)}, u32[]{:S(2)}) async-start(bf16[8,80,768]{2,1,0:T(8,128)(2,1)} %shard_map.212), calls=%async_computation | async-start | bytes 1966080 | tf_op jit(solution)/shard_map/all_to_all | solution.py:637
  17.1 92.3 %all-gather.5.cloned.1.call-start = ((), (), s32[]{:S(2)}) async-start(), calls=%async_computation.10 | async-start | bytes 4718592 | tf_op jit(solution)/shard_map/all_gather | solution.py:638
  53.9 20.7 %collective-permute-start.1 = (bf16[8,80,768]{2,1,0:T(8,128)(2,1)}, bf16[8,80,768]{2,1,0:T(8,128)(2,1)S(1)}, u32[]{:S(2)}, u32[]{:S(2)}) collective-permute-start(bf16[8,80,768]{2,1,0:T(8,128)(2,1)} %copy-done.8), channel_id=1, source_target_pairs={{0,16},{8,24},{16,0},{24,8},{1,17},{9,25},{17,1},{25,9},{2,18},{10... | collective-permute-start | bytes 2949128 | tf_op jit(solution)/shard_map/ppermute | solution.py:527
  53.9 23.5 %collective-permute-start.7 = (bf16[8,80,768]{2,1,0:T(8,128)(2,1)}, bf16[8,80,768]{2,1,0:T(8,128)(2,1)S(1)}, u32[]{:S(2)}, u32[]{:S(2)}) collective-permute-start(bf16[8,80,768]{2,1,0:T(8,128)(2,1)} %copy-done.8), channel_id=1, source_target_pairs={{0,8},{8,0},{16,24},{24,16},{1,9},{9,1},{17,25},{25,17},{2,10},{10... | collective-permute-start | bytes 2949128 | tf_op jit(solution)/shard_map/ppermute | solution.py:527
  75.4 18.0 %collective-permute-start.2 = (bf16[4,80,768]{2,1,0:T(8,128)(2,1)}, bf16[4,80,768]{2,1,0:T(8,128)(2,1)}, u32[]{:S(2)}, u32[]{:S(2)}) collective-permute-start(bf16[4,80,768]{2,1,0:T(8,128)(2,1)} %slice.208), channel_id=1, source_target_pairs={{0,8},{8,0},{16,24},{24,16},{1,9},{9,1},{17,25},{25,17},{2,10},{10... | collective-permute-start | bytes 1474568 | tf_op jit(solution)/shard_map/ppermute | solution.py:527
  78.4 17.7 %collective-permute-start.8 = (bf16[4,80,768]{2,1,0:T(8,128)(2,1)S(1)}, bf16[4,80,768]{2,1,0:T(8,128)(2,1)}, u32[]{:S(2)}, u32[]{:S(2)}) collective-permute-start(bf16[4,80,768]{2,1,0:T(8,128)(2,1)S(1)} %slice.214), channel_id=1, source_target_pairs={{0,16},{8,24},{16,0},{24,8},{1,17},{9,25},{17,1},{25,9},{2,18},{10... | collective-permute-start | bytes 1474568 | tf_op jit(solution)/shard_map/ppermute | solution.py:527
  78.5 42.5 %all-to-all-start.1 = ((bf16[8,256,256]{2,1,0:T(8,128)(2,1)}), bf16[8,256,256]{2,1,0:T(8,128)(2,1)S(1)}, u32[]{:S(2)}, u32[]{:S(2)}) async-start(bf16[8,256,256]{2,1,0:T(8,128)(2,1)} %bitcast.10), calls=%async_computation.1 | async-start | bytes 2097152 | tf_op jit(solution)/shard_map/all_to_all | solution.py:648
  90.4 118.8 %all-gather.7.cloned.1.call-start = ((), (), s32[]{:S(2)}) async-start(), calls=%async_computation.11 | async-start | bytes 4718592 | tf_op jit(solution)/shard_map/all_gather | solution.py:672
  122.1 87.1 %all-to-all-start.2 = ((bf16[8,512,256]{2,1,0:T(8,128)(2,1)}), bf16[8,512,256]{2,1,0:T(8,128)(2,1)}, u32[]{:S(2)}, u32[]{:S(2)}) async-start(bf16[8,512,256]{2,1,0:T(8,128)(2,1)} %pad_maximum_fusion), calls=%async_computation.2 | async-start | bytes 4194304 | tf_op jit(solution)/shard_map/all_to_all | solution.py:648
  126.4 131.6 %reduce-scatter.5.cloned.1.call-start = ((), (), s32[]{:S(2)}) async-start(), calls=%async_computation.12 | async-start | bytes 4718592 | tf_op jit(solution)/shard_map/reduce_scatter | solution.py:678
  126.5 41.3 %collective-permute-start.11 = (bf16[1024,512]{1,0:T(8,128)(2,1)S(1)}, bf16[1024,512]{1,0:T(8,128)(2,1)S(1)}, u32[]{:S(2)}, u32[]{:S(2)}) collective-permute-start(bf16[1024,512]{1,0:T(8,128)(2,1)S(1)} %copy-done.2), channel_id=1, source_target_pairs={{0,16},{8,24},{1,17},{9,25},{2,18},{10,26},{3,19},{11,27},{4,20},{... | collective-permute-start | bytes 3145736 | tf_op jit(solution)/shard_map/ppermute | solution.py:659
  129.7 46.0 %collective-permute-start.10 = (bf16[8,256,256]{2,1,0:T(8,128)(2,1)}, bf16[8,256,256]{2,1,0:T(8,128)(2,1)}, u32[]{:S(2)}, u32[]{:S(2)}) collective-permute-start(bf16[8,256,256]{2,1,0:T(8,128)(2,1)} %copy-done.23), channel_id=1, source_target_pairs={{0,16},{8,24},{16,0},{24,8},{1,17},{9,25},{17,1},{25,9},{2,18},{10... | collective-permute-start | bytes 3145736 | tf_op jit(solution)/shard_map/ppermute | solution.py:527
  129.8 45.9 %collective-permute-start.9 = (bf16[8,256,256]{2,1,0:T(8,128)(2,1)}, bf16[8,256,256]{2,1,0:T(8,128)(2,1)}, u32[]{:S(2)}, u32[]{:S(2)}) collective-permute-start(bf16[8,256,256]{2,1,0:T(8,128)(2,1)} %copy-done.23), channel_id=1, source_target_pairs={{0,8},{8,0},{16,24},{24,16},{1,9},{9,1},{17,25},{25,17},{2,10},{10... | collective-permute-start | bytes 3145736 | tf_op jit(solution)/shard_map/ppermute | solution.py:527
  131.4 35.1 %collective-permute-start.13 = (bf16[512,512]{1,0:T(8,128)(2,1)S(1)}, bf16[512,512]{1,0:T(8,128)(2,1)}, u32[]{:S(2)}, u32[]{:S(2)}) collective-permute-start(bf16[512,512]{1,0:T(8,128)(2,1)S(1)} %slice.175), channel_id=1, source_target_pairs={{8,0},{9,1},{10,2},{11,3},{12,4},{13,5},{14,6},{15,7}} | collective-permute-start | bytes 1572872 | tf_op jit(solution)/shard_map/ppermute | solution.py:661
  132.7 44.0 %collective-permute-start.12 = (bf16[1024,512]{1,0:T(8,128)(2,1)S(1)}, bf16[1024,512]{1,0:T(8,128)(2,1)}, u32[]{:S(2)}, u32[]{:S(2)}) collective-permute-start(bf16[1024,512]{1,0:T(8,128)(2,1)S(1)} %copy-done.2), channel_id=1, source_target_pairs={{0,8},{16,24},{1,9},{17,25},{2,10},{18,26},{3,11},{19,27},{4,12},{... | collective-permute-start | bytes 3145736 | tf_op jit(solution)/shard_map/ppermute | solution.py:660
  166.5 19.8 %collective-permute-start.14 = (bf16[512,512]{1,0:T(8,128)(2,1)}, bf16[512,512]{1,0:T(8,128)(2,1)S(1)}, u32[]{:S(2)}, u32[]{:S(2)}) collective-permute-start(bf16[512,512]{1,0:T(8,128)(2,1)} %collective-permute-done.13), channel_id=1, source_target_pairs={{0,16},{1,17},{2,18},{3,19},{4,20},{5,21},{6,22},{7,23}} | collective-permute-start | bytes 1572872 | tf_op jit(solution)/shard_map/ppermute | solution.py:662
  167.9 18.4 %collective-permute-start.15 = (bf16[512,512]{1,0:T(8,128)(2,1)S(1)}, bf16[512,512]{1,0:T(8,128)(2,1)}, u32[]{:S(2)}, u32[]{:S(2)}) collective-permute-start(bf16[512,512]{1,0:T(8,128)(2,1)S(1)} %slice.223), channel_id=1, source_target_pairs={{24,16},{25,17},{26,18},{27,19},{28,20},{29,21},{30,22},{31,23}} | collective-permute-start | bytes 1572872 | tf_op jit(solution)/shard_map/ppermute | solution.py:663
  209.2 98.3 %all-gather.9.cloned.1.call-start = ((), (), s32[]{:S(2)}) async-start(), calls=%async_computation.13 | async-start | bytes 4718592 | tf_op jit(solution)/shard_map/all_gather | solution.py:685
  209.3 47.4 %collective-permute-start.16 = (bf16[8,512,256]{2,1,0:T(8,128)(2,1)}, bf16[8,512,256]{2,1,0:T(8,128)(2,1)S(1)}, u32[]{:S(2)}, u32[]{:S(2)}) collective-permute-start(bf16[8,512,256]{2,1,0:T(8,128)(2,1)} %all-to-all-done.2.refs_0_), channel_id=1, source_target_pairs={{0,8},{8,0},{16,24},{24,16},{1,9},{9,1},{17,25},{25,17},{2,10},{10... | collective-permute-start | bytes 6291464 | tf_op jit(solution)/shard_map/ppermute | solution.py:527
  210.6 47.2 %collective-permute-start.17 = (bf16[8,512,256]{2,1,0:T(8,128)(2,1)}, bf16[8,512,256]{2,1,0:T(8,128)(2,1)}, u32[]{:S(2)}, u32[]{:S(2)}) collective-permute-start(bf16[8,512,256]{2,1,0:T(8,128)(2,1)} %all-to-all-done.2.refs_0_), channel_id=1, source_target_pairs={{0,16},{8,24},{16,0},{24,8},{1,17},{9,25},{17,1},{25,9},{2,18},{10... | collective-permute-start | bytes 6291464 | tf_op jit(solution)/shard_map/ppermute | solution.py:527
  261.8 125.4 %reduce-scatter.7.cloned.1.call-start = ((), (), s32[]{:S(2)}) async-start(), calls=%async_computation.14 | async-start | bytes 4718592 | tf_op jit(solution)/shard_map/reduce_scatter | solution.py:693
  261.9 37.2 %collective-permute-start.18 = (bf16[4,512,256]{2,1,0:T(8,128)(2,1)S(1)}, bf16[4,512,256]{2,1,0:T(8,128)(2,1)S(1)}, u32[]{:S(2)}, u32[]{:S(2)}) collective-permute-start(bf16[4,512,256]{2,1,0:T(8,128)(2,1)S(1)} %slice.178), channel_id=1, source_target_pairs={{0,16},{8,24},{16,0},{24,8},{1,17},{9,25},{17,1},{25,9},{2,18},{10... | collective-permute-start | bytes 3145736 | tf_op jit(solution)/shard_map/ppermute | solution.py:527
  264.8 35.2 %collective-permute-start.19 = (bf16[4,512,256]{2,1,0:T(8,128)(2,1)S(1)}, bf16[4,512,256]{2,1,0:T(8,128)(2,1)S(1)}, u32[]{:S(2)}, u32[]{:S(2)}) collective-permute-start(bf16[4,512,256]{2,1,0:T(8,128)(2,1)S(1)} %slice.179), channel_id=1, source_target_pairs={{0,8},{8,0},{16,24},{24,16},{1,9},{9,1},{17,25},{25,17},{2,10},{10... | collective-permute-start | bytes 3145736 | tf_op jit(solution)/shard_map/ppermute | solution.py:527
  267.4 29.2 %collective-permute-start.20 = (bf16[4,256,256]{2,1,0:T(8,128)(2,1)S(1)}, bf16[4,256,256]{2,1,0:T(8,128)(2,1)S(1)}, u32[]{:S(2)}, u32[]{:S(2)}) collective-permute-start(bf16[4,256,256]{2,1,0:T(8,128)(2,1)S(1)} %slice.180), channel_id=1, source_target_pairs={{0,16},{8,24},{16,0},{24,8},{1,17},{9,25},{17,1},{25,9},{2,18},{10... | collective-permute-start | bytes 1572872 | tf_op jit(solution)/shard_map/ppermute | solution.py:527
  269.1 30.0 %collective-permute-start.21 = (bf16[4,256,256]{2,1,0:T(8,128)(2,1)S(1)}, bf16[4,256,256]{2,1,0:T(8,128)(2,1)S(1)}, u32[]{:S(2)}, u32[]{:S(2)}) collective-permute-start(bf16[4,256,256]{2,1,0:T(8,128)(2,1)S(1)} %slice.181), channel_id=1, source_target_pairs={{0,8},{8,0},{16,24},{24,16},{1,9},{9,1},{17,25},{25,17},{2,10},{10... | collective-permute-start | bytes 1572872 | tf_op jit(solution)/shard_map/ppermute | solution.py:527
  338.3 122.1 %all-gather.11.cloned.1.call-start = ((), (), s32[]{:S(2)}) async-start(), calls=%async_computation.15 | async-start | bytes 4718592 | tf_op jit(solution)/shard_map/all_gather | solution.py:746
  342.6 25.4 %collective-permute-start.22 = (bf16[1024,512]{1,0:T(8,128)(2,1)S(1)}, bf16[1024,512]{1,0:T(8,128)(2,1)S(1)}, u32[]{:S(2)}, u32[]{:S(2)}) collective-permute-start(bf16[1024,512]{1,0:T(8,128)(2,1)S(1)} %convolution_convert_fusion.4), channel_id=1, source_target_pairs={{0,8},{8,0},{16,24},{24,16},{1,9},{9,1},{17,25},{25,17},{2,10},{10... | collective-permute-start | bytes 3145736 | tf_op jit(solution)/shard_map/ppermute | solution.py:527
  345.4 25.4 %collective-permute-start.24 = (bf16[1024,512]{1,0:T(8,128)(2,1)S(1)}, bf16[1024,512]{1,0:T(8,128)(2,1)S(1)}, u32[]{:S(2)}, u32[]{:S(2)}) collective-permute-start(bf16[1024,512]{1,0:T(8,128)(2,1)S(1)} %convolution_convert_fusion.3), channel_id=1, source_target_pairs={{0,16},{8,24},{16,0},{24,8},{1,17},{9,25},{17,1},{25,9},{2,18},{10... | collective-permute-start | bytes 3145736 | tf_op jit(solution)/shard_map/ppermute | solution.py:527
  390.6 26.5 %collective-permute-start.30 = (bf16[512,1024]{1,0:T(8,128)(2,1)}, bf16[512,1024]{1,0:T(8,128)(2,1)}, u32[]{:S(2)}, u32[]{:S(2)}) collective-permute-start(bf16[512,1024]{1,0:T(8,128)(2,1)} %fusion.10), channel_id=1, source_target_pairs={{0,8},{8,0},{16,24},{24,16},{1,9},{9,1},{17,25},{25,17},{2,10},{10... | collective-permute-start | bytes 3145736 | tf_op jit(solution)/shard_map/ppermute | solution.py:527
  392.2 28.7 %collective-permute-start.32 = (bf16[512,1024]{1,0:T(8,128)(2,1)}, bf16[512,1024]{1,0:T(8,128)(2,1)}, u32[]{:S(2)}, u32[]{:S(2)}) collective-permute-start(bf16[512,1024]{1,0:T(8,128)(2,1)} %fusion.13), channel_id=1, source_target_pairs={{0,16},{8,24},{16,0},{24,8},{1,17},{9,25},{17,1},{25,9},{2,18},{10... | collective-permute-start | bytes 3145736 | tf_op jit(solution)/shard_map/ppermute | solution.py:527
  396.8 63.6 %all-to-all-start.3 = ((bf16[8,264,256]{2,1,0:T(8,128)(2,1)}), bf16[8,264,256]{2,1,0:T(8,128)(2,1)}, u32[]{:S(2)}, u32[]{:S(2)}) async-start(bf16[8,264,256]{2,1,0:T(8,128)(2,1)} %fusion.29), calls=%async_computation.5 | async-start | bytes 2162688 | tf_op jit(solution)/shard_map/all_to_all | solution.py:648
  401.0 149.0 %reduce-scatter.9.cloned.1.call-start = ((), (), s32[]{:S(2)}) async-start(), calls=%async_computation.16 | async-start | bytes 4718592 | tf_op jit(solution)/shard_map/reduce_scatter | solution.py:769
  401.1 38.5 %collective-permute-start.26 = (bf16[1024,512]{1,0:T(8,128)(2,1)}, bf16[1024,512]{1,0:T(8,128)(2,1)}, u32[]{:S(2)}, u32[]{:S(2)}) collective-permute-start(bf16[1024,512]{1,0:T(8,128)(2,1)} %convolution_convert_fusion.2), channel_id=1, source_target_pairs={{0,8},{8,0},{16,24},{24,16},{1,9},{9,1},{17,25},{25,17},{2,10},{10... | collective-permute-start | bytes 3145736 | tf_op jit(solution)/shard_map/ppermute | solution.py:527
  401.7 41.1 %collective-permute-start.28 = (bf16[1024,512]{1,0:T(8,128)(2,1)}, bf16[1024,512]{1,0:T(8,128)(2,1)}, u32[]{:S(2)}, u32[]{:S(2)}) collective-permute-start(bf16[1024,512]{1,0:T(8,128)(2,1)} %convolution_convert_fusion.1), channel_id=1, source_target_pairs={{0,16},{8,24},{16,0},{24,8},{1,17},{9,25},{17,1},{25,9},{2,18},{10... | collective-permute-start | bytes 3145736 | tf_op jit(solution)/shard_map/ppermute | solution.py:527
  419.4 32.8 %collective-permute-start.31 = (bf16[256,1024]{1,0:T(8,128)(2,1)S(1)}, bf16[256,1024]{1,0:T(8,128)(2,1)S(1)}, u32[]{:S(2)}, u32[]{:S(2)}) collective-permute-start(bf16[256,1024]{1,0:T(8,128)(2,1)S(1)} %slice.320), channel_id=1, source_target_pairs={{0,16},{8,24},{16,0},{24,8},{1,17},{9,25},{17,1},{25,9},{2,18},{10... | collective-permute-start | bytes 1572872 | tf_op jit(solution)/shard_map/ppermute | solution.py:527
  422.6 29.8 %collective-permute-start.33 = (bf16[256,1024]{1,0:T(8,128)(2,1)S(1)}, bf16[256,1024]{1,0:T(8,128)(2,1)S(1)}, u32[]{:S(2)}, u32[]{:S(2)}) collective-permute-start(bf16[256,1024]{1,0:T(8,128)(2,1)S(1)} %slice.319), channel_id=1, source_target_pairs={{0,8},{8,0},{16,24},{24,16},{1,9},{9,1},{17,25},{25,17},{2,10},{10... | collective-permute-start | bytes 1572872 | tf_op jit(solution)/shard_map/ppermute | solution.py:527
  441.2 18.7 %collective-permute-start.27 = (bf16[1024,256]{1,0:T(8,128)(2,1)S(1)}, bf16[1024,256]{1,0:T(8,128)(2,1)S(1)}, u32[]{:S(2)}, u32[]{:S(2)}) collective-permute-start(bf16[1024,256]{1,0:T(8,128)(2,1)S(1)} %slice.322), channel_id=1, source_target_pairs={{0,16},{8,24},{16,0},{24,8},{1,17},{9,25},{17,1},{25,9},{2,18},{10... | collective-permute-start | bytes 1572872 | tf_op jit(solution)/shard_map/ppermute | solution.py:527
  462.0 83.8 %all-to-all-start.4 = ((bf16[8,512,256]{2,1,0:T(8,128)(2,1)}), bf16[8,512,256]{2,1,0:T(8,128)(2,1)S(1)}, u32[]{:S(2)}, u32[]{:S(2)}) async-start(bf16[8,512,256]{2,1,0:T(8,128)(2,1)} %pad_maximum_fusion.1), calls=%async_computation.7 | async-start | bytes 4194304 | tf_op jit(solution)/shard_map/all_to_all | solution.py:648
  466.1 159.5 %reduce-scatter.11.cloned.1.call-start = ((), (), s32[]{:S(2)}) async-start(), calls=%async_computation.17 | async-start | bytes 4718592 | tf_op jit(solution)/shard_map/reduce_scatter | solution.py:785
  487.2 62.9 %collective-permute-start.37 = (bf16[1024,512]{1,0:T(8,128)(2,1)}, bf16[1024,512]{1,0:T(8,128)(2,1)}, u32[]{:S(2)}, u32[]{:S(2)}) collective-permute-start(bf16[1024,512]{1,0:T(8,128)(2,1)} %get-tuple-element.161), channel_id=1, source_target_pairs={{16,0},{24,8},{17,1},{25,9},{18,2},{26,10},{19,3},{27,11},{20,4},{... | collective-permute-start | bytes 3145736 | tf_op jit(solution)/shard_map/ppermute | solution.py:766
  488.5 61.6 %collective-permute-start.38 = (bf16[1024,512]{1,0:T(8,128)(2,1)}, bf16[1024,512]{1,0:T(8,128)(2,1)}, u32[]{:S(2)}, u32[]{:S(2)}) collective-permute-start(bf16[1024,512]{1,0:T(8,128)(2,1)} %get-tuple-element.162), channel_id=1, source_target_pairs={{8,0},{16,8},{24,16},{9,1},{17,9},{25,17},{10,2},{18,10},{26,18},{... | collective-permute-start | bytes 3145736 | tf_op jit(solution)/shard_map/ppermute | solution.py:766
  489.9 40.9 %collective-permute-start.34 = (bf16[64,2176]{1,0:T(8,128)(2,1)S(1)}, bf16[64,2176]{1,0:T(8,128)(2,1)S(1)}, u32[]{:S(2)}, u32[]{:S(2)}) collective-permute-start(bf16[64,2176]{1,0:T(8,128)(2,1)S(1)} %get-tuple-element.181), channel_id=1, source_target_pairs={{0,8},{8,0},{16,24},{24,16},{1,9},{9,1},{17,25},{25,17},{2,10},{10... | collective-permute-start | bytes 835592 | tf_op jit(solution)/shard_map/ppermute | solution.py:527
  500.8 30.0 %collective-permute-start.35 = (bf16[64,2176]{1,0:T(8,128)(2,1)S(1)}, bf16[64,2176]{1,0:T(8,128)(2,1)S(1)}, u32[]{:S(2)}, u32[]{:S(2)}) collective-permute-start(bf16[64,2176]{1,0:T(8,128)(2,1)S(1)} %get-tuple-element.183), channel_id=1, source_target_pairs={{0,16},{8,24},{16,0},{24,8},{1,17},{9,25},{17,1},{25,9},{2,18},{10... | collective-permute-start | bytes 835592 | tf_op jit(solution)/shard_map/ppermute | solution.py:527
  504.7 33.8 %collective-permute-start.36 = (bf16[64,2176]{1,0:T(8,128)(2,1)S(1)}, bf16[64,2176]{1,0:T(8,128)(2,1)S(1)}, u32[]{:S(2)}, u32[]{:S(2)}) collective-permute-start(bf16[64,2176]{1,0:T(8,128)(2,1)S(1)} %get-tuple-element.182), channel_id=1, source_target_pairs={{0,24},{8,16},{16,8},{24,0},{1,25},{9,17},{17,9},{25,1},{2,26},{10... | collective-permute-start | bytes 835592 | tf_op jit(solution)/shard_map/ppermute | solution.py:527
  566.4 27.6 %collective-permute-start.39 = (bf16[2,512,384]{2,1,0:T(8,128)(2,1)}, bf16[2,512,384]{2,1,0:T(8,128)(2,1)S(1)}, u32[]{:S(2)}, u32[]{:S(2)}) collective-permute-start(bf16[2,512,384]{2,1,0:T(8,128)(2,1)} %get-tuple-element.167), channel_id=1, source_target_pairs={{0,8},{8,0},{16,24},{24,16},{1,9},{9,1},{17,25},{25,17},{2,10},{10... | collective-permute-start | bytes 2359304 | tf_op jit(solution)/shard_map/ppermute | solution.py:527
  577.4 19.2 %collective-permute-start.41 = (bf16[2,512,384]{2,1,0:T(8,128)(2,1)}, bf16[2,512,384]{2,1,0:T(8,128)(2,1)S(1)}, u32[]{:S(2)}, u32[]{:S(2)}) collective-permute-start(bf16[2,512,384]{2,1,0:T(8,128)(2,1)} %get-tuple-element.169), channel_id=1, source_target_pairs={{0,16},{8,24},{16,0},{24,8},{1,17},{9,25},{17,1},{25,9},{2,18},{10... | collective-permute-start | bytes 2359304 | tf_op jit(solution)/shard_map/ppermute | solution.py:527
  600.4 16.1 %collective-permute-start.43 = (bf16[64,2176]{1,0:T(8,128)(2,1)S(1)}, bf16[64,2176]{1,0:T(8,128)(2,1)S(1)}, u32[]{:S(2)}, u32[]{:S(2)}) collective-permute-start(bf16[64,2176]{1,0:T(8,128)(2,1)S(1)} %copy-done.26), channel_id=1, source_target_pairs={{0,0},{8,1},{16,2},{24,3},{1,4},{9,5},{17,6},{25,7},{2,8},{10,9},{... | collective-permute-start | bytes 835592 | tf_op jit(solution)/shard_map/ppermute | solution.py:797
  607.1 31.8 %all-to-all-start.5 = ((bf16[8,64,768]{2,1,0:T(8,128)(2,1)}), bf16[8,64,768]{2,1,0:T(8,128)(2,1)S(1)}, u32[]{:S(2)}, u32[]{:S(2)}) async-start(bf16[8,64,768]{2,1,0:T(8,128)(2,1)} %pad_maximum_fusion.5), calls=%async_computation.9 | async-start | bytes 1572864 | tf_op jit(solution)/shard_map/all_to_all | solution.py:800
  (60 other events, 601.0 us)
Sparse Core Ops, SparseCore 0:
  48.6 55.3 all-gather.4
  121.2 84.8 all-gather.6
  209.4 48.6 reduce-scatter.4
  261.9 45.6 all-gather.8
  338.5 48.7 reduce-scatter.6
  390.8 68.2 all-gather.10
  461.3 88.6 reduce-scatter.8
  558.7 66.8 reduce-scatter.10
